TPU v7x, 32 devices: a whole 2x2x4 slice. The times are simulated.
32 devices in a mesh: section: 2 (over core), dp: 16 (over z, y, x).
Axes of the slice: x: 2, y: 2, z: 4, core: 2. Of those that a mesh axis runs over, the one named last changes fastest.
Arguments:
- stream_in: float32 [2, 16, 384, 512], P(None, 'dp'), may hold values from -6 to 6, as said below
- cotangent: float32 [2, 16, 384, 512], P(None, 'dp'), may hold values from -6 to 6, as said below
- segment_ids: int32 [2, 16, 384], P(None, 'dp'), may hold values from 0 to 5, never falling along the last dimension, each value on 1 to 192 neighbouring positions
- pad_mask: int32 [2, 16, 384], P(None, 'dp'), may hold values 0 or 1
- w_query: bfloat16 [2, 512, 512], P('section'), may hold values from -0.25 to 0.25
- w_key: bfloat16 [2, 512, 512], P('section'), may hold values from -0.25 to 0.25
- w_value: bfloat16 [2, 512, 512], P('section'), may hold values from -0.25 to 0.25
- w_out: bfloat16 [2, 512, 512], P('section'), may hold values from -0.75 to 0.75
- w_in: bfloat16 [2, 512, 2048], P('section'), may hold values from -0.25 to 0.25
- w_back: bfloat16 [2, 2048, 512], P('section'), may hold values from -0.125 to 0.125
- alphas: float32 [2, 2], P('section'), may hold values from 0.5 to 1.5
Outputs:
- acts: float32 [2, 2, 16, 384, 512], P('section', None, 'dp')
- input_grads: float32 [2, 2, 16, 384, 512], P('section', None, 'dp')
- grad_query: float32 [2, 512, 512], P('section')
- grad_key: float32 [2, 512, 512], P('section')
- grad_value: float32 [2, 512, 512], P('section')
- grad_out: float32 [2, 512, 512], P('section')
- grad_in: float32 [2, 512, 2048], P('section')
- grad_back: float32 [2, 2048, 512], P('section')
- grad_alphas: float32 [2, 2], P('section')
- norms: float32 [2, 3], P('section')
Inputs may be any that keep to these rules, and one draw needn't show every extreme that they name: `stream_in`: independent entries of mean 0 and deviation about 1. `cotangent`: independent entries of mean 0 and deviation about 1.
All inputs are finite; a program needn't handle non-finite values. No bound on the sum of `pad_mask` on one device may be relied on, other than what follows from the above.
Results may differ from a plain program's by a relative error of at most 0.0005.
Values sent between devices are 32-bit elements; how exact they have to be, the bound alone decides.
No kernel may reach another device: no remote copies, remote signals or barrier semaphores. Data moves between devices by JAX's collectives and lax.ppermute only.
A program may use at most 192 MiB of HBM per device.

v0:
```python
import jax
import jax.numpy as jnp
from jax import lax
from jax.sharding import PartitionSpec as P

D = 512
HEADS = 8
HEAD_DIM = 64


def passed_along(value, axis, by):
    length = lax.axis_size(axis)
    pairs = [(i, i + by) for i in range(length) if 0 <= i + by < length]
    return lax.ppermute(value, axis, pairs)


def multiply(left_side, right_side):
    return jnp.dot(left_side, right_side, precision=lax.Precision.HIGHEST)


def contract(form, left_side, right_side):
    return jnp.einsum(form, left_side, right_side, precision=lax.Precision.HIGHEST)


def layer_forward(params, stream, segment_row, valid_row):
    w_query, w_key, w_value, w_out, w_in, w_back, scales = params
    row_count = stream.shape[0]
    scale = HEAD_DIM ** (-0.5)
    query = multiply(stream, w_query).reshape(row_count, HEADS, HEAD_DIM)
    keys_all = multiply(stream, w_key).reshape(row_count, HEADS, HEAD_DIM)
    values_all = multiply(stream, w_value).reshape(row_count, HEADS, HEAD_DIM)
    scores = contract("qhd,khd->hqk", query, keys_all) * scale
    places = jnp.arange(row_count)
    allowed = (segment_row[:, None] == segment_row[None, :]) & (places[None, :] <= places[:, None])
    allowed = allowed & ((valid_row[None, :] > 0) | (places[None, :] == places[:, None]))
    scores = jnp.where(allowed[None], scores, -1e30)
    probs = jax.nn.softmax(scores, axis=-1)
    mixed = contract("hqk,khd->qhd", probs, values_all).reshape(row_count, HEADS * HEAD_DIM)
    raw_attn = multiply(mixed, w_out)
    attn_branch = scales[0] * raw_attn
    middle = stream + attn_branch
    before = multiply(middle, w_in)
    hidden = jax.nn.gelu(before)
    raw_ffn = multiply(hidden, w_back)
    ffn_branch = scales[1] * raw_ffn
    result = middle + ffn_branch
    weighting = valid_row.astype(jnp.float32)[:, None]
    squares = jnp.stack(
        [
            jnp.sum(result * result * weighting),
            jnp.sum(attn_branch * attn_branch * weighting),
            jnp.sum(ffn_branch * ffn_branch * weighting),
        ]
    )
    saved = (
        stream,
        query,
        keys_all,
        values_all,
        probs,
        mixed,
        raw_attn,
        middle,
        before,
        hidden,
        raw_ffn,
    )
    return (result, squares, saved)


def layer_backward(params, saved, upstream):
    w_query, w_key, w_value, w_out, w_in, w_back, scales = params
    stream, query, keys_all, values_all, probs, mixed, raw_attn, middle, before, hidden, raw_ffn = (
        saved
    )
    row_count = upstream.shape[0]
    scale = HEAD_DIM ** (-0.5)
    grad_beta = jnp.sum(upstream * raw_ffn)
    second_grad = scales[1] * upstream
    grad_backer = multiply(hidden.T, second_grad)
    grad_hidden = multiply(second_grad, w_back.T)
    grad_before = jax.vjp(jax.nn.gelu, before)[1](grad_hidden)[0]
    grad_inner = multiply(middle.T, grad_before)
    grad_middle = upstream + multiply(grad_before, w_in.T)
    grad_gamma = jnp.sum(grad_middle * raw_attn)
    first_grad = scales[0] * grad_middle
    grad_outer = multiply(mixed.T, first_grad)
    grad_mixed = multiply(first_grad, w_out.T).reshape(row_count, HEADS, HEAD_DIM)
    grad_probs = contract("qhd,khd->hqk", grad_mixed, values_all)
    grad_values = contract("hqk,qhd->khd", probs, grad_mixed).reshape(row_count, D)
    grad_scores = probs * (grad_probs - jnp.sum(grad_probs * probs, axis=-1, keepdims=True))
    grad_queries = (contract("hqk,khd->qhd", grad_scores, keys_all) * scale).reshape(row_count, D)
    grad_keys = (contract("hqk,qhd->khd", grad_scores, query) * scale).reshape(row_count, D)
    grad_query = multiply(stream.T, grad_queries)
    grad_key = multiply(stream.T, grad_keys)
    grad_value = multiply(stream.T, grad_values)
    grad_stream = (
        grad_middle
        + multiply(grad_queries, w_query.T)
        + multiply(grad_keys, w_key.T)
        + multiply(grad_values, w_value.T)
    )
    grads = (
        grad_query,
        grad_key,
        grad_value,
        grad_outer,
        grad_inner,
        grad_backer,
        jnp.stack([grad_gamma, grad_beta]),
    )
    return (grads, grad_stream)


def shards(
    stream_in,
    cotangent,
    segment_ids,
    pad_mask,
    w_query,
    w_key,
    w_value,
    w_out,
    w_in,
    w_back,
    alphas,
):
    section_count = lax.axis_size("section")
    section_index = lax.axis_index("section")
    params = tuple(
        (weight[0].astype(jnp.float32) for weight in (w_query, w_key, w_value, w_out, w_in, w_back))
    ) + (alphas[0],)
    inputs = stream_in[:, 0]
    targets = cotangent[:, 0]
    segment_local = segment_ids[:, 0]
    valid_local = pad_mask[:, 0]
    micro_count = inputs.shape[0]
    first_section = section_index == 0
    last_section = section_index == section_count - 1
    ticks = micro_count + section_count - 1
    received = jnp.zeros_like(inputs[0])
    outputs = jnp.zeros_like(inputs)
    sums_total = jnp.zeros((3,), jnp.float32)
    saved_list = []
    for tick in range(ticks):
        micro_index = tick - section_index
        active = (micro_index >= 0) & (micro_index < micro_count)
        chosen = jnp.clip(micro_index, 0, micro_count - 1)
        own_input = lax.dynamic_index_in_dim(inputs, chosen, 0, keepdims=False)
        stream = jnp.where(first_section, own_input, received)
        segment_row = lax.dynamic_index_in_dim(segment_local, chosen, 0, keepdims=False)
        valid_row = lax.dynamic_index_in_dim(valid_local, chosen, 0, keepdims=False)
        result, squares, saved = layer_forward(params, stream, segment_row, valid_row)
        saved_list.append(saved)
        sums_total = sums_total + active.astype(jnp.float32) * squares
        outputs = jnp.where(
            active, lax.dynamic_update_index_in_dim(outputs, result, chosen, 0), outputs
        )
        if tick < ticks - 1:
            received = passed_along(result, "section", 1)
    grad_sums = tuple((jnp.zeros(weight.shape, jnp.float32) for weight in params))
    grad_inputs = jnp.zeros_like(inputs)
    received = jnp.zeros_like(inputs[0])
    for tick in range(ticks):
        micro_index = micro_count - 1 - tick + (section_count - 1 - section_index)
        active = (micro_index >= 0) & (micro_index < micro_count)
        chosen = jnp.clip(micro_index, 0, micro_count - 1)
        own_target = lax.dynamic_index_in_dim(targets, chosen, 0, keepdims=False)
        upstream = jnp.where(last_section, own_target, received) * active.astype(jnp.float32)
        stored = saved_list[ticks - 1 - tick]
        saved = stored
        grad_params, grad_stream = layer_backward(params, saved, upstream)
        grad_sums = tuple((total + piece for total, piece in zip(grad_sums, grad_params)))
        grad_inputs = jnp.where(
            active,
            lax.dynamic_update_index_in_dim(grad_inputs, grad_stream, chosen, 0),
            grad_inputs,
        )
        if tick < ticks - 1:
            received = passed_along(grad_stream, "section", -1)
    token_count = jnp.sum(valid_local.astype(jnp.float32))
    grad_query, grad_key, grad_value, grad_outer, grad_inner, grad_backer, grad_scales = grad_sums
    summed = lax.psum(
        (
            grad_query,
            grad_key,
            grad_value,
            grad_outer,
            grad_inner,
            grad_backer,
            grad_scales,
            sums_total,
            token_count,
        ),
        "dp",
    )
    norms = jnp.sqrt(summed[7] / (jnp.maximum(summed[8], 1.0) * D))
    return (
        outputs[None, :, None],
        grad_inputs[None, :, None],
        summed[0][None],
        summed[1][None],
        summed[2][None],
        summed[3][None],
        summed[4][None],
        summed[5][None],
        summed[6][None],
        norms[None],
    )


def solution(mesh):
    in_specs = (
        P(None, "dp", None, None),
        P(None, "dp", None, None),
        P(None, "dp", None),
        P(None, "dp", None),
        P("section", None, None),
        P("section", None, None),
        P("section", None, None),
        P("section", None, None),
        P("section", None, None),
        P("section", None, None),
        P("section", None),
    )
    out_specs = (
        P("section", None, "dp", None, None),
        P("section", None, "dp", None, None),
        P("section", None, None),
        P("section", None, None),
        P("section", None, None),
        P("section", None, None),
        P("section", None, None),
        P("section", None, None),
        P("section", None),
        P("section", None),
    )
    return jax.shard_map(shards, mesh=mesh, in_specs=in_specs, out_specs=out_specs, check_vma=False)
```

profile of v0, /device:TPU:0, one launch (start us, length us, event | category | flops | bytes accessed | tf_op | source)
XLA Modules:
  0.0 723.0 jit_solution(15345359871601497712)
XLA Ops:
  13.5 3.4 fusion.119
  16.8 3.0 fusion.121
  24.1 6.0 fusion
  31.1 4.1 fusion.246
  35.3 2.6 bitcast_add_fusion
  37.9 4.3 fusion.55
  42.4 7.0 bitcast_dynamic-update-slice_fusion.2
  50.6 3.7 collective-permute-start
  62.0 4.6 fusion.1
  67.6 4.1 fusion.240
  71.8 2.6 multiply_add_fusion.3
  74.4 2.7 fusion.53
  77.1 5.4 fusion.112
  83.6 3.3 collective-permute-start.1
  88.8 2.7 copy.79
  94.8 4.4 fusion.2
  100.1 4.2 fusion.234
  104.4 2.5 multiply_add_fusion.1
  106.9 2.6 fusion.51
  109.5 4.8 fusion.26
  114.3 2.6 fusion.86
  118.6 6.0 fusion.231
  124.6 5.2 multiply_reduce_fusion.2
  129.8 6.3 fusion.77
  136.1 4.2 fusion.76
  140.3 8.5 %fusion.64 = f32[2048,512]{1,0:T(8,128)S(1)} fusion(f32[384,2048]{1,0:T(8,128)S(1)} %fusion.51, f32[]{:T(128)} %bitcast.16, f32[2,1,384,512]{3,2,1,0:T(8,128)S(1)} %copy-done.34, s32[]{:T(128)S(6)} %min.15, f32[]{:T(128)S(6)} %convert_element_type.52, pred[]{:T(512)S(6)} %eq.114), kind=kOutput, calls=%fused_computation.81 | convolution fusion | flops 4838719488 | bytes 8126477 | tf_op jit(solution)/shard_map/dot_general | solution.py:18
  154.9 3.5 fusion.140
  158.4 5.0 bitcast_dynamic-update-slice_fusion
  163.6 5.0 fusion.20
  168.7 6.1 multiply_reduce_fusion.7
  176.9 6.7 multiply_reduce_fusion.1
  183.7 6.5 fusion.74
  190.2 8.7 %fusion.75 = f32[8,64,384]{2,1,0:T(8,128)S(1)} fusion(f32[384,8,64]{0,2,1:T(8,128)S(1)} %copy-done.62, f32[8,384,384]{1,2,0:T(8,128)} %get-tuple-element.97, f32[8,384]{1,0:T(8,128)S(1)} %get-tuple-element.96, f32[8,384,384]{1,2,0:T(8,128)S(1)} %bitcast.357, f32[8,384]{1,0:T(8,128)S(1)} %copy-done.90, f32[8,384]{1,0:T(8,128)S(1)} %copy-done.86, ...), kind=kOutput, calls=%fused_computation.97 | convolution fusion | flops 913244160 | bytes 11194368 | tf_op jit(solution)/shard_map/hqk,qhd->khd/dot_general | solution.py:22
  199.0 6.0 fusion.237
  205.0 6.9 fusion.252
  213.4 3.1 fusion.251
  218.0 3.8 fusion.250
  225.0 3.8 fusion.249
  228.8 3.5 convolution_add_fusion.1
  232.3 9.7 %fusion.63 = f32[2048,512]{1,0:T(8,128)} fusion(f32[384,2048]{1,0:T(8,128)S(1)} %copy-done.36, f32[384,512]{1,0:T(8,128)S(1)} %copy-done.50, f32[]{:T(128)} %bitcast.16), kind=kOutput, calls=%fused_computation.80 | convolution fusion | flops 4838326272 | bytes 8126468 | tf_op jit(solution)/shard_map/dot_general | solution.py:18
  242.1 3.0 multiply_reduce_fusion.5
  245.1 4.9 fusion.14
  250.1 6.8 fusion.253
  256.9 6.3 multiply_reduce_fusion.10
  265.0 5.8 fusion.243
  270.8 7.1 multiply_reduce_fusion
  277.9 8.5 %fusion.73 = f32[8,64,384]{2,1,0:T(8,128)S(1)} fusion(f32[384,8,64]{0,2,1:T(8,128)S(1)} %copy-done.58, f32[8,384,384]{1,2,0:T(8,128)} %get-tuple-element.101, f32[8,384]{1,0:T(8,128)S(1)} %get-tuple-element.100, f32[8,384,384]{1,2,0:T(8,128)S(1)} %bitcast.355, f32[8,384]{1,0:T(8,128)S(1)} %copy-done.88, f32[8,384]{1,0:T(8,128)S(1)} %copy-done.84, ...), kind=kOutput, calls=%fused_computation.95 | convolution fusion | flops 913244160 | bytes 11194368 | tf_op jit(solution)/shard_map/hqk,qhd->khd/dot_general | solution.py:22
  286.5 7.7 %fusion.72 = f32[8,64,384]{2,1,0:T(8,128)} fusion(f32[384,8,64]{0,2,1:T(8,128)S(1)} %copy-done.57, f32[8,384,384]{1,2,0:T(8,128)} %get-tuple-element.101, f32[8,384]{1,0:T(8,128)S(1)} %get-tuple-element.100, f32[8,384,384]{1,2,0:T(8,128)S(1)} %bitcast.355, f32[8,384]{1,0:T(8,128)S(1)} %copy-done.88, f32[8,384]{1,0:T(8,128)S(1)} %copy-done.84, ...), kind=kOutput, calls=%fused_computation.94 | convolution fusion | flops 913244160 | bytes 11194368 | tf_op jit(solution)/shard_map/hqk,khd->qhd/dot_general | solution.py:22
  294.2 3.6 fusion.65
  297.8 2.9 fusion.127
  300.7 2.7 fusion.125
  303.4 2.7 fusion.129
  306.2 9.6 %add_bitcast_fusion = f32[1,2048,512]{2,1,0:T(8,128)} fusion(f32[2048,512]{1,0:T(8,128)S(1)} %fusion.64, f32[2048,512]{1,0:T(8,128)S(1)} %copy-done.37, f32[384,2048]{1,0:T(8,128)S(1)} %copy-done.12, f32[384,512]{1,0:T(8,128)S(1)} %get-tuple-element.73, f32[]{:T(128)} %bitcast.16), kind=kOutput, calls=%fused_computation.18 | convolution fusion | flops 4840423424 | bytes 16515076 | tf_op jit(solution)/shard_map/dot_general | solution.py:18
  315.7 8.6 %add_bitcast_fusion.1 = f32[1,512,2048]{2,1,0:T(8,128)} fusion(f32[512,2048]{1,0:T(8,128)S(1)} %fusion.253, f32[512,2048]{1,0:T(8,128)S(1)} %fusion.252, f32[384,512]{1,0:T(8,128)S(1)} %get-tuple-element.88, f32[384,2048]{1,0:T(8,128)S(1)} %fusion.26), kind=kOutput, calls=%fused_computation.19 | convolution fusion | flops 4833935360 | bytes 16515072 | tf_op jit(solution)/shard_map/dot_general | solution.py:18
  324.3 3.7 fusion.71
  328.0 3.7 fusion.69
  331.7 3.7 fusion.67
  336.7 3.9 fusion.197
  340.5 5.8 fusion.196
  346.4 2.7 copy.82
  349.1 45.8 %all-reduce = (f32[1,2]{1,0:T(1,128)}, f32[3]{0:T(128)S(1)}, f32[]{:T(128)}) all-reduce(f32[1,2]{1,0:T(1,128)S(1)} %fusion.197, f32[3]{0:T(128)S(1)} %fusion.196, f32[]{:T(128)} %convert_reduce_fusion), channel_id=1, replica_groups=mesh['section'=2,'dp'=16] {'dp'}, use_global_device_ids=true, to_apply=%region_21.22 | all-reduce | flops 6 | bytes 48 | tf_op jit(solution)/shard_map/psum | solution.py:183
  396.1 2.9 fusion.157
  399.0 2.7 fusion.152
  404.1 299.1 %all-reduce.4.cloned.1.call-done = (f32[1,512,512]{2,1,0:T(8,128)}, f32[1,512,512]{2,1,0:T(8,128)}, f32[1,512,512]{2,1,0:T(8,128)}, f32[1,512,512]{2,1,0:T(8,128...) async-done(((f32[1,512,512]{2,1,0:T(8,128)}, f32[1,512,512]{2,1,0:T(8,128)}, f32[1,512,512]{2,1,0:T(8,128)}, f32[1,512,512]{2,1,0:T(8,128)}, f32[1,512,2048]{2,1,0:T(8,128)}, ...) | async-done | bytes 12582928 | tf_op jit(solution)/shard_map/psum | solution.py:183
  (245 shorter events, 63.2 us)
Async XLA Ops:
  7.2 35.2 %copy-start = (bf16[1,2048,512]{2,1,0:T(8,128)(2,1)S(1)}, bf16[1,2048,512]{2,1,0:T(8,128)(2,1)}, u32[]{:S(2)}) copy-start(bf16[1,2048,512]{2,1,0:T(8,128)(2,1)} %param.20) | copy-start | bytes 6291460
  7.2 696.0 %all-reduce.4.cloned.1.call-start = ((), (), s32[]{:S(2)}) async-start(), calls=%async_computation | async-start | bytes 25165824 | tf_op jit(solution)/shard_map/psum | solution.py:183
  10.1 9.8 %copy-start.21 = (bf16[1,512,512]{2,1,0:T(8,128)(2,1)S(1)}, bf16[1,512,512]{2,1,0:T(8,128)(2,1)}, u32[]{:S(2)}) copy-start(bf16[1,512,512]{2,1,0:T(8,128)(2,1)} %param.17) | copy-start | bytes 1572868
  13.4 9.7 %copy-start.25 = (bf16[1,512,512]{1,2,0:T(8,128)(2,1)}, bf16[1,512,512]{1,2,0:T(8,128)(2,1)S(1)}, u32[]{:S(2)}) copy-start(bf16[1,512,512]{1,2,0:T(8,128)(2,1)S(1)} %copy.47) | copy-start | bytes 1572868
  16.8 6.4 copy-start.91
  23.2 7.8 %copy-start.78 = (f32[384,8,64]{0,2,1:T(8,128)}, f32[384,8,64]{0,2,1:T(8,128)S(1)}, u32[]{:S(2)}) copy-start(f32[384,8,64]{0,2,1:T(8,128)S(1)} %fusion.123) | copy-start | bytes 2359300
  24.1 7.0 copy-start.71
  30.0 5.2 copy-start.9
  50.6 4.6 collective-permute-start
  55.2 5.8 copy-start.28
  58.6 8.0 %copy-start.63 = (f32[384,8,64]{0,2,1:T(8,128)}, f32[384,8,64]{0,2,1:T(8,128)S(1)}, u32[]{:S(2)}) copy-start(f32[384,8,64]{0,2,1:T(8,128)S(1)} %fusion.113) | copy-start | bytes 2359300
  61.0 5.6 copy-start.61
  62.0 5.6 copy-start.80
  77.1 5.4 copy-start.35
  83.6 7.9 %collective-permute-start.1 = (f32[384,512]{1,0:T(8,128)}, f32[384,512]{1,0:T(8,128)}, u32[]{:S(2)}, u32[]{:S(2)}) collective-permute-start(f32[384,512]{1,0:T(8,128)} %get-tuple-element.70), channel_id=1, source_target_pairs={{0,16},{1,17},{2,18},{3,19},{4,20},{5,21},{6,22},{7,23},{8,24},{9,... | collective-permute-start | bytes 2359304 | tf_op jit(solution)/shard_map/ppermute | solution.py:14
  91.7 12.7 %copy-start.4 = (f32[384,512]{1,0:T(8,128)}, f32[384,512]{1,0:T(8,128)S(1)}, u32[]{:S(2)}) copy-start(f32[384,512]{1,0:T(8,128)S(1)} %bitcast_select_fusion.4) | copy-start | bytes 2359300
  124.6 27.4 %copy-start.43 = (f32[8,64,384]{2,1,0:T(8,128)}, f32[8,64,384]{2,1,0:T(8,128)S(1)}, u32[]{:S(2)}) copy-start(f32[8,64,384]{2,1,0:T(8,128)S(1)} %fusion.231) | copy-start | bytes 2359300
  136.1 14.2 %copy-start.47 = (f32[8,64,384]{2,1,0:T(8,128)}, f32[8,64,384]{2,1,0:T(8,128)S(1)}, u32[]{:S(2)}) copy-start(f32[8,64,384]{2,1,0:T(8,128)S(1)} %fusion.77) | copy-start | bytes 2359300
  140.3 8.5 %copy-start.45 = (f32[8,64,384]{2,1,0:T(8,128)}, f32[8,64,384]{2,1,0:T(8,128)S(1)}, u32[]{:S(2)}) copy-start(f32[8,64,384]{2,1,0:T(8,128)S(1)} %fusion.76) | copy-start | bytes 2359300
  140.3 8.5 %copy-start.23 = (bf16[1,512,512]{2,1,0:T(8,128)(2,1)S(1)}, bf16[1,512,512]{2,1,0:T(8,128)(2,1)}, u32[]{:S(2)}) copy-start(bf16[1,512,512]{2,1,0:T(8,128)(2,1)} %param.15) | copy-start | bytes 1572868
  152.0 6.4 copy-start.33
  152.0 6.4 copy-start.69
  153.5 9.9 %collective-permute-start.2 = (f32[384,512]{1,0:T(8,128)S(1)}, f32[384,512]{1,0:T(8,128)S(1)}, u32[]{:S(2)}, u32[]{:S(2)}) collective-permute-start(f32[384,512]{1,0:T(8,128)S(1)} %get-tuple-element.95), channel_id=1, source_target_pairs={{16,0},{17,1},{18,2},{19,3},{20,4},{21,5},{22,6},{23,7},{24,8},{25... | collective-permute-start | bytes 2359304 | tf_op jit(solution)/shard_map/ppermute | solution.py:14
  158.4 18.5 %slice-start.2 = ((s8[4718592]{0:T(1024)(128)(4,1)}), s8[4194304]{0:T(1024)(128)(4,1)S(1)}, s32[]{:S(2)}) async-start(s8[4718592]{0:T(1024)(128)(4,1)} %bitcast.356), calls=%async_computation.3 | async-start | bytes 8388608
  163.4 5.2 copy-start.70
  163.6 13.3 %slice-start.3 = ((s8[4718592]{0:T(1024)(128)(4,1)}), s8[524288]{0:T(1024)(128)(4,1)S(1)}, s32[]{:S(2)}) async-start(s8[4718592]{0:T(1024)(128)(4,1)} %bitcast.356), calls=%async_computation.4 | async-start | bytes 1048576
  168.7 8.2 %copy-start.81 = (f32[384,8,64]{0,2,1:T(8,128)S(1)}, f32[384,8,64]{0,2,1:T(8,128)}, u32[]{:S(2)}) copy-start(f32[384,8,64]{0,2,1:T(8,128)} %copy-done.80) | copy-start | bytes 2359300
  168.7 8.2 %copy-start.86 = (f32[8,384]{1,0:T(8,128)S(1)}, f32[8,384]{1,0:T(8,128)}, u32[]{:S(2)}) copy-start(f32[8,384]{1,0:T(8,128)} %copy-done.85) | copy-start | bytes 36868
  168.7 8.2 %copy-start.90 = (f32[8,384]{1,0:T(8,128)S(1)}, f32[8,384]{1,0:T(8,128)}, u32[]{:S(2)}) copy-start(f32[8,384]{1,0:T(8,128)} %copy-done.89) | copy-start | bytes 36868
  176.9 6.7 copy-start.64
  183.7 6.6 copy-start.62
  190.2 31.6 %copy-start.51 = (f32[8,64,384]{2,1,0:T(8,128)}, f32[8,64,384]{2,1,0:T(8,128)S(1)}, u32[]{:S(2)}) copy-start(f32[8,64,384]{2,1,0:T(8,128)S(1)} %fusion.74) | copy-start | bytes 2359300
  199.0 17.5 %copy-start.56 = (f32[8,64,384]{2,1,0:T(8,128)}, f32[8,64,384]{2,1,0:T(8,128)S(1)}, u32[]{:S(2)}) copy-start(f32[8,64,384]{2,1,0:T(8,128)S(1)} %fusion.75) | copy-start | bytes 2359300
  199.0 6.0 copy-start.18
  221.8 7.0 copy-start.40
  221.8 7.0 copy-start.68
  223.4 8.9 %copy-start.13 = (f32[2,384,512]{2,1,0:T(8,128)}, f32[2,384,512]{2,1,0:T(8,128)S(1)}, u32[]{:S(2)}) copy-start(f32[2,384,512]{2,1,0:T(8,128)S(1)} %get-tuple-element.98) | copy-start | bytes 4718596
  223.4 8.9 %copy-start.50 = (f32[384,512]{1,0:T(8,128)S(1)}, f32[384,512]{1,0:T(8,128)}, u32[]{:S(2)}) copy-start(f32[384,512]{1,0:T(8,128)} %copy-done.49) | copy-start | bytes 2359300
  223.4 18.6 %collective-permute-start.3 = (f32[384,512]{1,0:T(8,128)S(1)}, f32[384,512]{1,0:T(8,128)S(1)}, u32[]{:S(2)}, u32[]{:S(2)}) collective-permute-start(f32[384,512]{1,0:T(8,128)S(1)} %get-tuple-element.99), channel_id=1, source_target_pairs={{16,0},{17,1},{18,2},{19,3},{20,4},{21,5},{22,6},{23,7},{24,8},{25... | collective-permute-start | bytes 2359304 | tf_op jit(solution)/shard_map/ppermute | solution.py:14
  232.3 9.8 %copy-start.52 = (f32[384,512]{1,0:T(8,128)S(1)}, f32[384,512]{1,0:T(8,128)}, u32[]{:S(2)}) copy-start(f32[384,512]{1,0:T(8,128)} %get-tuple-element.89) | copy-start | bytes 2359300
  232.3 9.8 %copy-start.77 = (f32[384,512]{1,0:T(8,128)S(1)}, f32[384,512]{1,0:T(8,128)}, u32[]{:S(2)}) copy-start(f32[384,512]{1,0:T(8,128)} %get-tuple-element.91) | copy-start | bytes 2359300
  250.0 6.8 copy-start.42
  250.0 6.8 copy-start.75
  250.0 14.9 %slice-start = ((s8[4718592]{0:T(1024)(128)(4,1)}), s8[4194304]{0:T(1024)(128)(4,1)S(1)}, s32[]{:S(2)}) async-start(s8[4718592]{0:T(1024)(128)(4,1)} %bitcast.354), calls=%async_computation.1 | async-start | bytes 8388608
  256.9 8.0 %slice-start.1 = ((s8[4718592]{0:T(1024)(128)(4,1)}), s8[524288]{0:T(1024)(128)(4,1)S(1)}, s32[]{:S(2)}) async-start(s8[4718592]{0:T(1024)(128)(4,1)} %bitcast.354), calls=%async_computation.2 | async-start | bytes 1048576
  256.9 8.0 %copy-start.72 = (pred[384,384]{0,1:T(8,128)(4,1)S(1)}, pred[384,384]{0,1:T(8,128)(4,1)}, u32[]{:S(2)}) copy-start(pred[384,384]{0,1:T(8,128)(4,1)} %copy-done.71) | copy-start | bytes 442372
  256.9 8.0 %copy-start.84 = (f32[8,384]{1,0:T(8,128)S(1)}, f32[8,384]{1,0:T(8,128)}, u32[]{:S(2)}) copy-start(f32[8,384]{1,0:T(8,128)} %copy-done.83) | copy-start | bytes 36868
  256.9 8.0 %copy-start.88 = (f32[8,384]{1,0:T(8,128)S(1)}, f32[8,384]{1,0:T(8,128)}, u32[]{:S(2)}) copy-start(f32[8,384]{1,0:T(8,128)} %copy-done.87) | copy-start | bytes 36868
  264.9 5.8 copy-start.79
  270.7 27.0 %copy-start.54 = (f32[8,64,384]{2,1,0:T(8,128)}, f32[8,64,384]{2,1,0:T(8,128)S(1)}, u32[]{:S(2)}) copy-start(f32[8,64,384]{2,1,0:T(8,128)S(1)} %fusion.243) | copy-start | bytes 2359300
  270.8 7.2 copy-start.58
  277.9 8.5 %copy-start.57 = (f32[384,8,64]{0,2,1:T(8,128)S(1)}, f32[384,8,64]{0,2,1:T(8,128)}, u32[]{:S(2)}) copy-start(f32[384,8,64]{0,2,1:T(8,128)} %fusion.119) | copy-start | bytes 2359300
  286.5 14.2 %copy-start.55 = (f32[8,64,384]{2,1,0:T(8,128)}, f32[8,64,384]{2,1,0:T(8,128)S(1)}, u32[]{:S(2)}) copy-start(f32[8,64,384]{2,1,0:T(8,128)S(1)} %fusion.73) | copy-start | bytes 2359300
  286.5 7.7 %copy-start.41 = (f32[512,512]{1,0:T(8,128)S(1)}, f32[512,512]{1,0:T(8,128)}, u32[]{:S(2)}) copy-start(f32[512,512]{1,0:T(8,128)} %convolution_add_fusion.1) | copy-start | bytes 3145732
  286.5 7.7 %copy-start.60 = (f32[8,64,384]{2,1,0:T(8,128)S(1)}, f32[8,64,384]{2,1,0:T(8,128)}, u32[]{:S(2)}) copy-start(f32[8,64,384]{2,1,0:T(8,128)} %copy-done.59) | copy-start | bytes 2359300
  297.8 5.6 copy-start.65
  300.7 5.5 copy-start.37
  315.7 8.6 %copy-start.5 = (f32[384,512]{1,0:T(8,128)S(1)}, f32[384,512]{1,0:T(8,128)}, u32[]{:S(2)}) copy-start(f32[384,512]{1,0:T(8,128)} %copy-done.4) | copy-start | bytes 2359300
  315.7 8.6 %copy-start.44 = (f32[8,64,384]{2,1,0:T(8,128)S(1)}, f32[8,64,384]{2,1,0:T(8,128)}, u32[]{:S(2)}) copy-start(f32[8,64,384]{2,1,0:T(8,128)} %copy-done.43) | copy-start | bytes 2359300
  336.1 60.0 %copy-start.20 = (bf16[1,512,512]{2,1,0:T(8,128)(2,1)S(1)}, bf16[1,512,512]{2,1,0:T(8,128)(2,1)}, u32[]{:S(2)}) copy-start(bf16[1,512,512]{2,1,0:T(8,128)(2,1)} %param.16) | copy-start | bytes 1572868
  395.5 6.2 copy-start.14
  395.5 6.2 copy-start.24
  395.5 6.2 copy-start.66
  703.2 5.8 copy-start.73
  (37 other events, 133.1 us)
Sparse Core Ops, SparseCore 0:
  335.5 367.6 all-reduce.3
where the time goes:
time: 733 us; the launch traced here: 723 us
  matrix products  301 us (41%)
  waiting for transfers between devices  299 us (41%)
  blocking collectives  45.8 us (6%)
  local copies, waits for them, and re-layouts  28.1 us (4%)
  other arithmetic  22.7 us (3%)
  between operations  16.7 us (2%)
  starting transfers between devices  10 us (1%)
    psum x1, waiting for transfers between devices, shards(): lax.psum((grad_query, grad_key, grad_value, grad_outer, grad_inner, grad_...  299 us
    dot_general x54, matrix products, multiply(): return jnp.dot(left_side, right_side, precision=lax.Precision.HIGHEST)  194 us
    dot_general x18, matrix products, contract(): jnp.einsum(form, left_side, right_side, precision=lax.Precision.HIGHEST)  106 us
    psum x1, blocking collectives, shards(): lax.psum((grad_query, grad_key, grad_value, grad_outer, grad_inner, grad_...  45.8 us
    unnamed x203, local copies, waits for them, and re-layouts  25.6 us
  transfers between devices with their start and end apart: 5, of which 1 were waited for; matrix products, arithmetic and copies ran while one was open for 7% of the time, Pallas kernels for 0%

commit v1 on v0

v1 whole, which is shorter than its diff:
```python
import functools
import math
import jax
import jax.numpy as jnp
from jax import lax
from jax.experimental import pallas as pl
from jax.experimental.pallas import tpu as pltpu
from jax.sharding import PartitionSpec as P

D = 512
HEADS = 8
HEAD_DIM = 64
GELU_A = math.sqrt(2.0 / math.pi)
GELU_B = 0.044715


def start_all(copies):
    for copy in copies:
        copy.start()
    return copies


def wait_all(copies):
    for copy in copies:
        copy.wait()


def split(value):
    high = value.astype(jnp.bfloat16)
    low = (value - high.astype(jnp.float32)).astype(jnp.bfloat16)
    return (high, low)


def stacked(value):
    return jnp.concatenate(split(value), axis=0)


def dot(left_side, right_side):
    return jnp.dot(left_side, right_side, preferred_element_type=jnp.float32)


def dot_rows(left_side, right_side):
    return lax.dot_general(
        left_side, right_side, (((1,), (1,)), ((), ())), preferred_element_type=jnp.float32
    )


def folded(product):
    half = product.shape[0] // 2
    return product[:half] + product[half:]


def gelu_inner(value):
    return jnp.tanh(GELU_A * (value + GELU_B * (value * value * value)))


def tile_of(numbers):
    lane = lax.broadcasted_iota(jnp.int32, (8, 128), 1)
    tile = jnp.zeros((8, 128), jnp.float32)
    for index, number in enumerate(numbers):
        tile = jnp.where(lane == index, number, tile)
    return tile


def fill_bias(bias_ref, segment_row, valid_row):
    blocks = segment_row.shape[1] // 128
    segment_col = jnp.broadcast_to(segment_row, (128, segment_row.shape[1])).T
    valid_col = jnp.broadcast_to(valid_row, (128, valid_row.shape[1])).T
    for kb in range(blocks):
        ks = slice(kb * 128, kb * 128 + 128)
        for qb in range(kb, blocks):
            qs = slice(qb * 128, qb * 128 + 128)
            k_place = lax.broadcasted_iota(jnp.int32, (128, 128), 0) + kb * 128
            q_place = lax.broadcasted_iota(jnp.int32, (128, 128), 1) + qb * 128
            allowed = (segment_col[ks] == segment_row[:, qs]) & (k_place <= q_place)
            allowed = allowed & ((valid_col[ks] > 0) | (k_place == q_place))
            bias_ref[ks, qs] = jnp.where(allowed, 0.0, -1e30)


def halves_of(value):
    lane = lax.broadcasted_iota(jnp.int32, value.shape, 1)
    zero = jnp.zeros_like(value)
    return (jnp.where(lane < HEAD_DIM, value, zero), jnp.where(lane < HEAD_DIM, zero, value))


def pair_scores(keys_cat, queries_high, queries_low):
    sides = []
    for high, low in zip(halves_of(queries_high), halves_of(queries_low)):
        sides.append(jnp.concatenate([high, high, low], axis=1))
    return dot_rows(keys_cat, jnp.concatenate(sides, axis=0))


def three_lanes(value):
    high, low = split(value)
    return jnp.concatenate([high, low, high], axis=1)


def forward_body(tick, *refs):
    (info, alphas, segments, valids, streams, wq, wk, wv, wo, wi, wb) = refs[:11]
    received = streams.at[0] if tick == 0 else refs[11]
    refs = refs[11 + (0 if tick == 0 else 11) :]
    (acts, sent, saved_s, saved_q, saved_k, saved_v, saved_o, saved_l, saved_m, saved_p, sums) = refs[:11]
    (s_v, wq_v, wk_v, wv_v, wo_v, wi_v, wb_v, q_v, k_v, v_v, ot_v, l_v, m_v, p_v, a_v, t_v, bias_v, x_v, in_sem, out_sem) = refs[11:]
    section = info[0]
    micro = tick - section
    rows = s_v.shape[0]
    blocks = rows // 128

    @pl.when((micro >= 0) & (micro < 2))
    def _():
        pairs = [(wq, wq_v), (wk, wk_v), (wv, wv_v), (wo, wo_v), (wi, wi_v), (wb, wb_v)]
        loads = [pltpu.make_async_copy(a, b, in_sem.at[i]) for i, (a, b) in enumerate(pairs)]

        @pl.when(section == 0)
        def _():
            pltpu.make_async_copy(streams.at[micro], s_v, in_sem.at[6]).start()

        @pl.when(section != 0)
        def _():
            pltpu.make_async_copy(received, s_v, in_sem.at[6]).start()

        for load in loads:
            load.start()
        segment_row = segments[micro].astype(jnp.float32)
        valid_row = valids[micro].astype(jnp.float32)
        fill_bias(bias_v, segment_row, valid_row)
        pltpu.make_async_copy(received, s_v, in_sem.at[6]).wait()
        x_v[...] = stacked(s_v[...])
        for index, (weight, target) in enumerate(((wq_v, q_v), (wk_v, k_v), (wv_v, v_v))):
            loads[index].wait()
            value = folded(dot(x_v[...], weight[...]))
            target[...] = value * 0.125 if index == 0 else value

        stores = []

        def store(index, source, target):
            copy = pltpu.make_async_copy(source, target, out_sem.at[index])
            copy.start()
            stores.append(copy)

        store(0, s_v, saved_s.at[micro])
        store(1, q_v, saved_q.at[micro])
        store(2, k_v, saved_k.at[micro])
        store(3, v_v, saved_v.at[micro])

        for pair in range(HEADS // 2):
            lanes = pl.ds(pair * 128, 128)
            keys_cat = three_lanes(k_v[:, lanes])
            queries_high, queries_low = split(q_v[:, lanes])
            values_high, values_low = split(v_v[:, lanes].T)
            for qb in range(blocks):
                qs = slice(qb * 128, qb * 128 + 128)
                ks = (qb + 1) * 128
                scores = pair_scores(keys_cat[:ks], queries_high[qs], queries_low[qs])
                bias = bias_v[:ks, qs]
                for head in range(2):
                    part = scores[:, head * 128 : head * 128 + 128] + bias
                    top = jnp.max(part, axis=0, keepdims=True)
                    probs = jnp.exp(part - top)
                    total = jnp.sum(probs, axis=0, keepdims=True)
                    high, low = split(probs)
                    hs = slice(head * HEAD_DIM, head * HEAD_DIM + HEAD_DIM)
                    both = jnp.concatenate([values_high[hs, :ks], values_low[hs, :ks]], axis=0)
                    mixed = folded(dot(both, high)) + dot(values_high[hs, :ks], low)
                    at = pl.ds(pair * 128 + head * HEAD_DIM, HEAD_DIM)
                    ot_v[at, qs] = mixed / total
                    l_v[pair, head : head + 1, qs] = top + jnp.log(total)

        store(4, ot_v, saved_o.at[micro])
        store(5, l_v, saved_l.at[micro])
        x_v[...] = stacked(ot_v[...].T)
        loads[3].wait()
        attn = folded(dot(x_v[...], wo_v[...])) * alphas[0, 0]
        valid_col = jnp.broadcast_to(valid_row, (128, rows)).T
        weighting = jnp.concatenate([valid_col] * (D // 128), axis=1)
        attn_sum = jnp.sum(attn * attn * weighting)
        middle = s_v[...] + attn
        m_v[...] = middle
        store(6, m_v, saved_m.at[micro])
        x_v[...] = stacked(middle)
        a_v[...] = jnp.zeros_like(a_v)
        loads[4].wait()
        loads[5].wait()

        for part in range(wi_v.shape[1] // 512):
            cols = pl.ds(part * 512, 512)
            before = folded(dot(x_v[...], wi_v[:, cols]))
            p_v[:, cols] = before
            hidden = stacked(0.5 * before * (1.0 + gelu_inner(before)))
            a_v[...] += folded(dot(hidden, wb_v[cols, :]))

        store(7, p_v, saved_p.at[micro])
        ffn = a_v[...] * alphas[0, 1]
        result = m_v[...] + ffn
        a_v[...] = result
        store(8, a_v, acts.at[micro])
        store(9, a_v, sent)
        t_v[...] = tile_of([jnp.sum(result * result * weighting), attn_sum, jnp.sum(ffn * ffn * weighting)])
        store(10, t_v, sums.at[micro])
        for copy in stores:
            copy.wait()


def struct(*shape):
    return pltpu.HBM(shape, jnp.float32)


def loose(*shape):
    return jax.ShapeDtypeStruct(shape, jnp.float32)


def in_hbm(arrays):
    return [pltpu.with_memory_space_constraint(array, pltpu.HBM) for array in arrays]


ANY = pl.BlockSpec(memory_space=pl.ANY)
SCALARS = pl.BlockSpec(memory_space=pltpu.SMEM)
LOCAL = pl.BlockSpec(memory_space=pltpu.VMEM)


def forward_tick(tick, info, alphas, segments, valids, streams, received, weights, state):
    micro_count, rows, width = streams.shape
    inner = weights[4].shape[1]
    whole = struct(micro_count, rows, width)
    shapes = [
        whole,
        struct(rows, width),
        whole,
        whole,
        whole,
        whole,
        struct(micro_count, width, rows),
        struct(micro_count, HEADS // 2, 8, rows),
        whole,
        struct(micro_count, rows, inner),
        struct(micro_count, 8, 128),
    ]
    kept = [0, 2, 3, 4, 5, 6, 7, 8, 9, 10]
    extra = [] if state is None else [received] + in_hbm(state)
    aliases = {} if state is None else {12 + i: out for i, out in enumerate(kept)}
    f32, bf16 = jnp.float32, jnp.bfloat16
    vmem = pltpu.VMEM
    scratch = [vmem((rows, width), f32)] + [vmem(w.shape, bf16) for w in weights]
    scratch += [vmem((rows, width), f32)] * 3 + [vmem((width, rows), f32), vmem((HEADS // 2, 8, rows), f32)]
    scratch += [vmem((rows, width), f32), vmem((rows, inner), f32), vmem((rows, width), f32)]
    scratch += [vmem((8, 128), f32), vmem((rows, rows), f32), vmem((2 * rows, width), bf16)]
    scratch += [pltpu.SemaphoreType.DMA((7,)), pltpu.SemaphoreType.DMA((11,))]
    outs = pl.pallas_call(
        functools.partial(forward_body, tick),
        out_shape=shapes,
        in_specs=[SCALARS, SCALARS, LOCAL, LOCAL] + [ANY] * (7 + len(extra)),
        out_specs=[ANY] * len(shapes),
        scratch_shapes=scratch,
        input_output_aliases=aliases,
        compiler_params=pltpu.CompilerParams(vmem_limit_bytes=28 * 1024 * 1024),
        cost_estimate=pl.CostEstimate(flops=10**10, bytes_accessed=2 * 10**7, transcendentals=10**6),
        name="layer_forward",
    )(info, alphas, segments, valids, *in_hbm([streams, *weights]), *extra)
    return (outs[1], [outs[i] for i in kept])


TOKEN = [None]


def unit_shape(sizes):
    x, y, near, far = sizes
    return (near * far, y, x, 4 * D // (x * y * near * far), D)


def slot_structs(sizes, axis, more=0):
    x, y, near, far = sizes
    shape = [size for index, size in ((3, far), (2, near), (1, y), (0, x)) if index != axis]
    return [struct(*shape, unit_shape(sizes)[3] + more, D)] * sizes[axis]


def put_part(unit, part, value):
    depth = unit.shape[0] // 4
    unit[pl.ds(part * depth, depth)] = value.reshape((depth,) + unit.shape[1:])


def slot_copies(info, sizes, axis, unit, slots, sems, part):
    x, y, near, far = sizes
    depth, rows = near * far // 4, unit.shape[3]
    copies = []
    for by in range(sizes[axis]):
        place = lax.rem(info[1 + axis] + by, sizes[axis])
        if axis == 2:
            pairs = [(unit.at[at * near + place], slots[by].at[at]) for at in range(far) if part * depth < (at + 1) * near <= (part + 1) * depth]
        else:
            pairs = []
            for at in range(part * depth, (part + 1) * depth):
                source = unit.at[at, :, place] if axis == 0 else unit.at[at, place]
                pairs.append((source, slots[by].at[at // near, at % near, :, pl.ds(0, rows)]))
        for source, target in pairs:
            copies.append(pltpu.make_async_copy(source, target, sems.at[part, len(copies)]))
    return copies


def copy_count(sizes, axis):
    return sizes[axis] * max(1, sizes[2] * sizes[3] // 4)


def three_dots(left_high, left_low, right_high, right_low):
    return dot(left_high, right_high) + dot(left_low, right_high) + dot(left_high, right_low)


def back_body(turn, count, sizes, axis, *refs):
    info, alphas = refs[:2]
    upstreams, saved_p = refs[2:4], refs[4]
    slots, refs = refs[6 : 6 + count], refs[7 + count :]
    g_v, gh_v, p_v, w_v, in_sem, out_sem = refs
    parts = p_v.shape[0]
    rows = g_v.shape[1]

    @pl.when(info[0] == 1 - turn)
    def _():
        def load(part, micro):
            cols = pl.ds(part * 512, 512)
            return pltpu.make_async_copy(
                saved_p.at[micro, :, cols], p_v.at[part, pl.ds(micro * rows, rows)], in_sem.at[part, micro]
            )

        firsts = []
        for micro in range(2):
            source = upstreams[micro] if turn else upstreams[micro].at[micro, 0]
            firsts.append(pltpu.make_async_copy(source, g_v.at[micro], in_sem.at[parts, micro]))
        start_all(firsts)
        for part in range(parts):
            for micro in range(2):
                load(part, micro).start()
        wait_all(firsts)
        high, low = split(jnp.concatenate([g_v[0], g_v[1]], axis=0) * alphas[0, 1])
        gh_v[0] = high
        gh_v[1] = low

        stores = []
        for part in range(parts):
            for micro in range(2):
                load(part, micro).wait()
            before = p_v[part].T
            high, low = split(0.5 * before * (1.0 + gelu_inner(before)))
            put_part(w_v, part, three_dots(high, low, gh_v[0], gh_v[1]))
            stores += start_all(slot_copies(info, sizes, axis, w_v, slots, out_sem, part))
        wait_all(stores)


def chain_body(turn, micro, extra, *refs):
    info, alphas, segments, valids, upstream = refs[:5]
    saved_p = refs[5]
    sources = refs[6:11]
    wi, wb = refs[11:13]
    weights = refs[13:17]
    refs = refs[18 + extra :]
    (befores, spreads, firsts, passed, small, sent, _) = refs[:7]
    (g_v, p_v, wi_v, wb_v, gs_v, d_v, b_v) = refs[7:14]
    held = refs[14:19]
    weights_v = refs[19:23]
    (bias_v, do_v, dt_v, dl_v, qt_v, dk_v, dv_v, x_v, f_v, y_v, t_v, in_sem, part_sem, w_sem, out_sem) = refs[23:]
    parts = p_v.shape[0]
    rows = bias_v.shape[0]
    blocks = rows // 128
    (q_v, k_v, v_v, o_v, l_v) = held
    (wq_v, wk_v, wv_v, wo_v) = weights_v

    @pl.when(info[0] == 1 - turn)
    def _():
        def loads(part):
            cols = pl.ds(part * 512, 512)
            return [
                pltpu.make_async_copy(wb.at[cols], wb_v.at[part], part_sem.at[part, 0]),
                pltpu.make_async_copy(saved_p.at[micro, :, cols], p_v.at[part], part_sem.at[part, 1]),
                pltpu.make_async_copy(wi.at[:, cols], wi_v.at[part], part_sem.at[part, 2]),
            ]

        source = upstream if turn else upstream.at[micro, 0]
        first = pltpu.make_async_copy(source, g_v, in_sem.at[5])
        first.start()
        for part in range(parts):
            start_all(loads(part))
        fetches = [pltpu.make_async_copy(a, b, w_sem.at[i]) for i, (a, b) in enumerate(zip(weights, weights_v))]
        start_all(fetches[::-1])
        later = start_all(
            [pltpu.make_async_copy(a.at[micro], b, in_sem.at[i]) for i, (a, b) in enumerate(zip(sources, held))]
        )
        segment_row = segments[micro].astype(jnp.float32)
        valid_row = valids[micro].astype(jnp.float32)
        fill_bias(bias_v, segment_row, valid_row)
        first.wait()
        gs_v[...] = stacked(g_v[...] * alphas[0, 1])
        d_v[...] = jnp.zeros_like(d_v)

        def step(part, total):
            wait_all(loads(part))
            cols = pl.ds(part * 512, 512)
            before = p_v[part]
            grad_hidden = folded(dot_rows(gs_v[...], wb_v[part]))
            inner = gelu_inner(before)
            above = 0.5 * (1.0 + inner)
            total = total + jnp.sum(grad_hidden * (before * above))
            slope = above + 0.5 * before * (1.0 - inner * inner) * (GELU_A * (1.0 + 3.0 * GELU_B * (before * before)))
            high, low = split(grad_hidden * slope)
            b_v[0, :, cols] = high
            b_v[1, :, cols] = low
            d_v[...] += folded(dot_rows(jnp.concatenate([high, low], axis=0), wi_v[part]))
            return total

        total_inner = jnp.float32(0.0)
        for part in range(parts):
            total_inner = step(part, total_inner)
        stores = start_all([pltpu.make_async_copy(b_v, befores.at[micro], out_sem.at[0])])
        middle = g_v[...] + d_v[...]
        d_v[...] = middle
        high, low = split(middle * alphas[0, 0])
        f_v[0] = high
        f_v[1] = low
        stores += start_all([pltpu.make_async_copy(f_v, firsts.at[micro], out_sem.at[1])])
        wait_all(fetches)
        wait_all(later)
        grad_mixed = folded(dot_rows(jnp.concatenate([high, low], axis=0), wo_v[...]))
        do_v[...] = grad_mixed
        dt_v[...] = grad_mixed.T
        total_mixed = jnp.float32(0.0)
        for head in range(HEADS):
            hs = slice(head * HEAD_DIM, head * HEAD_DIM + HEAD_DIM)
            spread = jnp.sum(dt_v[hs, :] * o_v[hs, :], axis=0, keepdims=True)
            dl_v[head // 2, head % 2 : head % 2 + 1, :] = spread
            total_mixed = total_mixed + jnp.sum(spread)

        def pair_step(pair):
            lanes = pl.ds(pair * 128, 128)
            keys = k_v[:, lanes]
            keys_cat = three_lanes(keys)
            values_cat = three_lanes(v_v[:, lanes])
            queries_high, queries_low = split(q_v[:, lanes])
            do_high, do_low = split(do_v[:, lanes])
            turned_high, turned_low = split(keys.T)
            for qb in range(blocks - 1, -1, -1):
                qs = slice(qb * 128, qb * 128 + 128)
                ks = (qb + 1) * 128
                scores = pair_scores(keys_cat[:ks], queries_high[qs], queries_low[qs])
                slopes = pair_scores(values_cat[:ks], do_high[qs], do_low[qs])
                bias = bias_v[:ks, qs]
                sides = [halves_of(x[qs]) for x in (queries_high, queries_low, do_high, do_low)]
                key_part = jnp.zeros((ks, 128), jnp.float32)
                value_part = jnp.zeros((ks, 128), jnp.float32)
                for head in range(2):
                    own = slice(head * 128, head * 128 + 128)
                    at = slice(head, head + 1)
                    probs = jnp.exp((scores[:, own] + bias) - l_v[pair, at, qs])
                    grads = probs * (slopes[:, own] - dl_v[pair, at, qs])
                    q_high, q_low, d_high, d_low = [side[head] for side in sides]
                    none = jnp.zeros_like(q_high)

                    def product(left_high, left_low, right_high, right_low):
                        left_cat = jnp.concatenate([left_high, left_low], axis=1)
                        above = jnp.concatenate([right_high, right_low], axis=1)
                        below = jnp.concatenate([right_high, none], axis=1)
                        value = dot(left_cat, jnp.concatenate([above, below], axis=0))
                        return value[:, :128] + value[:, 128:]

                    value_part = value_part + product(*split(probs), d_high, d_low)
                    high, low = split(grads)
                    key_part = key_part + product(high, low, q_high, q_low)
                    hs = slice(head * HEAD_DIM, head * HEAD_DIM + HEAD_DIM)
                    both = jnp.concatenate([turned_high[hs, :ks], turned_low[hs, :ks]], axis=0)
                    turned = folded(dot(both, high)) + dot(turned_high[hs, :ks], low)
                    rows_at = pl.ds(pair * 128 + head * HEAD_DIM, HEAD_DIM)
                    qt_v[rows_at, qs] = turned * 0.125
                if qb == blocks - 1:
                    dk_v[:, lanes] = key_part
                    dv_v[:, lanes] = value_part
                else:
                    dk_v[:ks, lanes] += key_part
                    dv_v[:ks, lanes] += value_part

        for pair in range(HEADS // 2):
            pair_step(pair)
        result = d_v[...]
        for index, (source, weight) in enumerate(((qt_v, wq_v), (dk_v, wk_v), (dv_v, wv_v))):
            value = source[...].T if index == 0 else source[...]
            high, low = split(value)
            x_v[0, :, pl.ds(index * D, D)] = high
            x_v[1, :, pl.ds(index * D, D)] = low
            result = result + folded(dot_rows(jnp.concatenate([high, low], axis=0), weight[...]))
        y_v[...] = result
        t_v[...] = tile_of([total_mixed / alphas[0, 0], total_inner / alphas[0, 1]])
        stores += start_all(
            [
                pltpu.make_async_copy(y_v, sent, out_sem.at[2]),
                pltpu.make_async_copy(y_v, passed.at[micro], out_sem.at[3]),
                pltpu.make_async_copy(x_v, spreads.at[micro], out_sem.at[4]),
                pltpu.make_async_copy(t_v, small.at[micro], out_sem.at[5]),
            ]
        )
        wait_all(stores)


def rest_body(turn, counts, sizes, axes, extra, *refs):
    info, valids = refs[:2]
    saved_m, saved_s, saved_o, befores, spreads, firsts, sums, small = refs[2:10]
    refs = refs[11 + extra :]
    slots, refs = (refs[: counts[0]], refs[counts[0] : sum(counts)]), refs[sum(counts) + 1 :]
    (m_v, s_v, o_v, lt_v, r_v, w_v, n_v, t_v, in_sem, r_sem, out_sem, n_sem, t_sem) = refs
    rows = m_v.shape[1]

    @pl.when(info[0] == 1 - turn)
    def _():
        def loads(index):
            copies = []
            for micro in range(2):
                for half in range(2):
                    if index < 4:
                        source = befores.at[micro, half, :, pl.ds(index * 512, 512)]
                    elif index < 7:
                        source = spreads.at[micro, half, :, pl.ds((index - 4) * 512, 512)]
                    else:
                        source = firsts.at[micro, half]
                    target = r_v.at[index, half, pl.ds(micro * rows, rows)]
                    copies.append(pltpu.make_async_copy(source, target, r_sem.at[index, micro * 2 + half]))
            return copies

        lefts = [pltpu.make_async_copy(a, b, in_sem.at[i]) for i, (a, b) in enumerate(((saved_m, m_v), (saved_s, s_v), (saved_o, o_v)))]
        tiles = [
            pltpu.make_async_copy(sums, n_v.at[pl.ds(0, 2)], n_sem.at[0]),
            pltpu.make_async_copy(small, n_v.at[pl.ds(2, 2)], n_sem.at[1]),
        ]
        lefts[0].start()
        start_all(loads(0))
        start_all(lefts[1:])
        for index in range(1, 8):
            start_all(loads(index))
        start_all(tiles)

        def turn_left(index, source, transpose):
            for micro in range(2):
                high, low = split(source[micro].T if transpose else source[micro])
                lt_v[index, 0, :, pl.ds(micro * rows, rows)] = high
                lt_v[index, 1, :, pl.ds(micro * rows, rows)] = low

        stores = []
        for index in range(8):
            if index in (0, 4, 7):
                left = (0, 4, 7).index(index)
                lefts[left].wait()
                turn_left(left, (m_v, s_v, o_v)[left], left < 2)
            wait_all(loads(index))
            unit, part = w_v.at[index // 4], index % 4
            put_part(unit, part, three_dots(lt_v[left, 0], lt_v[left, 1], r_v[index, 0], r_v[index, 1]))
            own = index // 4
            stores += start_all(slot_copies(info, sizes, axes[own], unit, slots[own], out_sem.at[own], part))
        wait_all(tiles)
        lane = lax.broadcasted_iota(jnp.int32, (8, 256), 1)
        tile = jnp.where(lane == 3, jnp.sum(valids[...].astype(jnp.float32)), jnp.zeros((8, 256), jnp.float32))
        for index in range(3):
            tile = jnp.where(lane == index, n_v[0, 0, index] + n_v[1, 0, index], tile)
        for index in range(2):
            tile = jnp.where(lane == 4 + index, n_v[2, 0, index] + n_v[3, 0, index], tile)
        t_v[...] = tile
        axis, unit_rows = axes[1], w_v.shape[4]
        for by in range(counts[1]):

            @pl.when(lax.rem(info[1 + axis] + by, sizes[axis]) == 0)
            def _():
                target = slots[1][by].at[0, 0, 0, pl.ds(unit_rows, 8), pl.ds(0, 256)]
                copy = pltpu.make_async_copy(t_v, target, t_sem.at[0])
                copy.start()
                copy.wait()

        wait_all(stores)


def call(body, name, free, inputs, specs, outs, scratch, before, flops, limit):
    extra = list(before) if before is not None else []
    inputs = list(inputs[:free]) + in_hbm(list(inputs[free:])) + [TOKEN[0]]
    results = pl.pallas_call(
        functools.partial(body, len(extra)),
        out_shape=outs + [loose(8, 128)],
        in_specs=specs + [ANY] * (len(inputs) - len(specs) + len(extra)),
        out_specs=[ANY] * (len(outs) + 1),
        scratch_shapes=scratch,
        input_output_aliases={len(inputs) + i: i for i in range(len(extra))},
        compiler_params=pltpu.CompilerParams(vmem_limit_bytes=limit * 1024 * 1024),
        cost_estimate=pl.CostEstimate(flops=flops, bytes_accessed=2 * 10**7, transcendentals=10**6),
        name=name,
    )(*inputs, *in_hbm(extra))
    TOKEN[0] = results[-1]
    return results[:-1]


def backward_back(turn, info, alphas, upstreams, before, sizes, axis):
    micros, rows, inner = before.shape
    parts = inner // 512
    vmem, dma = pltpu.VMEM, pltpu.SemaphoreType.DMA
    f32, bf16 = jnp.float32, jnp.bfloat16
    slots = slot_structs(sizes, axis)
    scratch = [
        vmem((micros, rows, D), f32),
        vmem((2, micros * rows, D), bf16),
        vmem((parts, micros * rows, 512), f32),
        vmem(unit_shape(sizes), f32),
        dma((parts + 1, 2)),
        dma((parts, copy_count(sizes, axis))),
    ]

    def body(extra, *refs):
        back_body(turn, len(slots), sizes, axis, *refs)

    return call(
        body, "grad_back", 4, [info, alphas] + list(upstreams) + [before], [SCALARS, SCALARS], slots, scratch, None,
        5 * 10**9, 24,
    )


def backward_chain(turn, micro, info, alphas, segments, valids, upstream, before, saved, weights, previous):
    micros, rows, inner = before.shape
    parts = inner // 512
    vmem, dma = pltpu.VMEM, pltpu.SemaphoreType.DMA
    f32, bf16 = jnp.float32, jnp.bfloat16
    wq, wk, wv, wo, wi, wb = weights
    outs = [
        pltpu.HBM((micros, 2, rows, inner), bf16),
        pltpu.HBM((micros, 2, rows, 3 * D), bf16),
        pltpu.HBM((micros, 2, rows, D), bf16),
        struct(micros, rows, D),
        struct(micros, 8, 128),
        struct(rows, D),
    ]
    scratch = [
        vmem((rows, D), f32),
        vmem((parts, rows, 512), f32),
        vmem((parts, D, 512), bf16),
        vmem((parts, 512, D), bf16),
        vmem((2 * rows, D), bf16),
        vmem((rows, D), f32),
        vmem((2, rows, inner), bf16),
    ]
    scratch += [vmem(x.shape[1:], f32) for x in saved] + [vmem((D, D), bf16)] * 4
    scratch += [
        vmem((rows, rows), f32),
        vmem((rows, D), f32),
        vmem((D, rows), f32),
        vmem((HEADS // 2, 8, rows), f32),
        vmem((D, rows), f32),
        vmem((rows, D), f32),
        vmem((rows, D), f32),
        vmem((2, rows, 3 * D), bf16),
        vmem((2, rows, D), bf16),
        vmem((rows, D), f32),
        vmem((8, 128), f32),
        dma((6,)),
        dma((parts, 3)),
        dma((4,)),
        dma((6,)),
    ]

    def body(extra, *refs):
        chain_body(turn, micro, extra, *refs)

    inputs = [info, alphas, segments, valids, upstream, before] + list(saved) + [wi, wb, wq, wk, wv, wo]
    return call(
        body, "grad_chain", 5, inputs, [SCALARS, SCALARS, LOCAL, LOCAL], outs, scratch, previous, 2 * 10**10, 36
    )


def backward_rest(turn, info, valids, middle, stream, mixed, chain, sums, previous, sizes, axes):
    micros, rows, _ = middle.shape
    befores, spreads, firsts, _, small = chain
    vmem, dma = pltpu.VMEM, pltpu.SemaphoreType.DMA
    f32, bf16 = jnp.float32, jnp.bfloat16
    slots = [slot_structs(sizes, axes[0]), slot_structs(sizes, axes[1], 8)]
    scratch = [
        vmem(middle.shape, f32),
        vmem(stream.shape, f32),
        vmem(mixed.shape, f32),
        vmem((3, 2, D, micros * rows), bf16),
        vmem((8, 2, micros * rows, 512), bf16),
        vmem((2,) + unit_shape(sizes), f32),
        vmem((4, 8, 128), f32),
        vmem((8, 256), f32),
        dma((3,)),
        dma((8, 4)),
        dma((2, 4, max(copy_count(sizes, axis) for axis in axes))),
        dma((2,)),
        dma((1,)),
    ]

    def body(extra, *refs):
        rest_body(turn, [len(each) for each in slots], sizes, axes, extra, *refs)

    inputs = [info, valids, middle, stream, mixed, befores, spreads, firsts, sums, small]
    return call(body, "grad_rest", 2, inputs, [SCALARS, LOCAL], slots[0] + slots[1], scratch, previous, 10**10, 40)


def local_call(body, name, who, info, inputs, outs, scratch, previous=None, specs=None):
    extra = list(previous) if previous is not None else []
    inputs = [info, TOKEN[0]] + list(inputs)

    def guarded(*refs):
        def run():
            first = len(inputs) + len(extra)
            body(refs[0], refs[2 : len(inputs)], refs[first : first + len(outs)], refs[first + len(outs) + 1 :])

        if who is None:
            run()
        else:
            pl.when(refs[0][0] == who)(run)

    results = pl.pallas_call(
        guarded,
        out_shape=list(outs) + [loose(8, 128)],
        in_specs=[SCALARS] + [ANY] * (len(inputs) - 1 + len(extra)),
        out_specs=(specs or [ANY] * len(outs)) + [ANY],
        scratch_shapes=scratch,
        input_output_aliases={len(inputs) + i: i for i in range(len(extra))},
        compiler_params=pltpu.CompilerParams(vmem_limit_bytes=12 * 1024 * 1024),
        cost_estimate=pl.CostEstimate(flops=10**6, bytes_accessed=6 * 10**6, transcendentals=0),
        name=name,
    )(*inputs, *in_hbm(extra))
    TOKEN[0] = results[-1]
    return results[:-1]


def left_dims(done):
    return [axis for axis in (3, 2, 1, 0) if axis not in done]


def picked(ref, dims, axis, index):
    return ref.at[(slice(None),) * dims.index(axis) + (index,)]


def reduce_stage(sizes, order, step, who, info, arrays):
    shape = arrays[0].shape
    count = len(arrays)
    dims = left_dims(order[:step])
    if step < len(order):
        axis = order[step]
        at = dims.index(axis)
        outs = [loose(*shape[:at], *shape[at + 1 :])] * sizes[axis]
    else:
        outs = [loose(*shape)]

    def body(info, ins, outs, scratch):
        held, sem = scratch
        wait_all(start_all([pltpu.make_async_copy(ref, held.at[i], sem.at[i]) for i, ref in enumerate(ins)]))
        total = held[0]
        for i in range(1, count):
            total = total + held[i]
        held[0] = total
        stores = []
        for by in range(len(outs)):
            source = held.at[0]
            if step < len(order):
                source = picked(source, dims, axis, lax.rem(info[1 + axis] + by, sizes[axis]))
            stores.append(pltpu.make_async_copy(source, outs[by], sem.at[count + by]))
        wait_all(start_all(stores))

    scratch = [pltpu.VMEM((count,) + shape, jnp.float32), pltpu.SemaphoreType.DMA((count + len(outs),))]
    return local_call(body, "reduce_step", who, info, arrays, outs, scratch)


def place_stage(sizes, order, step, who, info, arrays):
    axis = order[step]
    dims = left_dims(order[:step])
    at = dims.index(axis)
    shape = arrays[0].shape
    count = sizes[axis]

    def body(info, ins, outs, scratch):
        copies = []
        for by in range(count):
            target = picked(outs[0], dims, axis, lax.rem(info[1 + axis] + count - by, count))
            copies.append(pltpu.make_async_copy(ins[by], target, scratch[0].at[by]))
        wait_all(start_all(copies))

    out = loose(*shape[:at], count, *shape[at:])
    return local_call(body, "place_step", who, info, arrays, [out], [pltpu.SemaphoreType.DMA((count,))])[0]


def last_stage(sizes, order, who, info, arrays, kind, previous):
    x, y, near, far = sizes
    rows = unit_shape(sizes)[3]
    depth = near * far // 4
    axis = order[0]
    count = sizes[axis]
    specs, scratch = None, [pltpu.SemaphoreType.DMA((near * far * count + 1,))]
    if kind == "rows":
        shapes = [struct(near * far, y, x, rows, D)]
    elif kind == "columns":
        shapes = [struct(depth, y, x, rows, 4 * D)]
    else:
        shapes = [struct(depth, y, x, rows, D)] * 4 + [loose(1, 2), loose(1, 3)]
        specs = [ANY] * 4 + [LOCAL] * 2
        scratch += [pltpu.VMEM((8, 256), jnp.float32)]

    def body(info, ins, outs, scratch):
        sem = scratch[0]
        copies = []

        def put(source, target):
            copies.append(pltpu.make_async_copy(source, target, sem.at[len(copies)]))

        for by in range(count):
            place = lax.rem(info[1 + axis] + count - by, count)
            if axis == 2:
                for at in range(far):
                    put(ins[by].at[at], outs[0].at[at * near + place])
                continue
            for at in range(near * far):
                source = ins[by].at[at // near, at % near, :, pl.ds(0, rows)]
                part, inside = at // depth, at % depth
                out = outs[part] if kind == "four" else outs[0]
                lanes = pl.ds(part * D if kind == "columns" else 0, D)
                inside = at if kind == "rows" else inside
                put(source, out.at[inside, :, place, :, lanes] if axis == 0 else out.at[inside, place, :, :, lanes])
        start_all(copies)
        if kind == "four":
            tile_v = scratch[1]
            for by in range(count):

                @pl.when(info[1 + axis] == by)
                def _():
                    source = ins[by].at[0, 0, 0, pl.ds(rows, 8), pl.ds(0, 256)]
                    copy = pltpu.make_async_copy(source, tile_v, sem.at[len(copies)])
                    copy.start()
                    copy.wait()

            tile = tile_v[0:1, 0:128]
            outs[-2][...] = tile[:, 4:6]
            outs[-1][...] = jnp.sqrt(tile[:, 0:3] / (jnp.maximum(tile[:, 3:4], 1.0) * D))
        wait_all(copies)

    return local_call(body, "place_last", who, info, arrays, shapes, scratch, previous, specs)


def extents(count):
    bits = count.bit_length() - 1
    if 1 << bits != count:
        return (1, 1, 1, count)
    side = 1 << (bits // 3)
    depth = count // (side * side)
    near = 2 if depth > 1 else 1
    return (side, side, near, depth // near)


def shifted(value, axis, by, sizes, who=None):
    count = math.prod(sizes)
    stride, length = math.prod(sizes[:axis]), sizes[axis]
    pairs = []
    for chip in range(count):
        along = (chip // stride) % length
        pairs.append((chip, chip + ((along + by) % length - along) * stride))
    if who is None:
        return lax.ppermute(value, "dp", pairs)
    return lax.ppermute(value, ("section", "dp"), [(who * count + a, who * count + b) for a, b in pairs])


def summing(slots, order, kind, sizes, info, who=None, previous=None):
    pieces = list(slots)
    for step in range(1, len(order) + 1):
        axis = order[step - 1]
        pieces = [pieces[0]] + [shifted(pieces[by], axis, by, sizes, who) for by in range(1, sizes[axis])]
        yield
        pieces = reduce_stage(sizes, order, step, who, info, pieces)
    whole = pieces[0]
    for step in range(len(order) - 1, -1, -1):
        axis = order[step]
        copies = [whole] + [shifted(whole, axis, by, sizes, who) for by in range(1, sizes[axis])]
        yield
        if step:
            whole = place_stage(sizes, order, step, who, info, copies)
    yield last_stage(sizes, order, who, info, copies, kind, previous() if previous else None)


def shards(stream_in, cotangent, segment_ids, pad_mask, w_query, w_key, w_value, w_out, w_in, w_back, alphas):
    weights = [weight[0] for weight in (w_query, w_key, w_value, w_out, w_in, w_back)]
    streams = stream_in[:, 0]
    sizes = extents(lax.axis_size("dp"))
    chip = lax.axis_index("dp")
    section = lax.axis_index("section")
    places, left = [], chip
    for size in sizes:
        places.append(lax.rem(left, size))
        left = lax.div(left, size)
    info = jnp.stack([section] + places).astype(jnp.int32)
    received, state = None, None
    for tick in range(3):
        sent, state = forward_tick(tick, info, alphas, segment_ids, pad_mask, streams, received, weights, state)
        if tick < 2:
            received = lax.ppermute(sent, "section", [(0, 1)])
    acts, saved_s, saved_q, saved_k, saved_v, saved_o, saved_l, saved_m, saved_p, sums = state
    saved = (saved_q, saved_k, saved_v, saved_o, saved_l)
    TOKEN[0] = jnp.zeros((8, 128), jnp.float32)

    def chain_step(turn, micro, upstream, previous):
        return backward_chain(
            turn, micro, info, alphas, segment_ids, pad_mask, upstream, saved_p, saved, weights, previous
        )

    orders = {"back": (2, 0, 1, 3), "inner": (0, 1, 2, 3), "attention": (1, 2, 0, 3)}
    first_axes = [orders["inner"][0], orders["attention"][0]]

    def back_step(turn, upstreams):
        return backward_back(turn, info, alphas, upstreams, saved_p, sizes, orders["back"][0])

    def rest_step(turn, chain, previous):
        return backward_rest(
            turn, info, pad_mask, saved_m, saved_s, saved_o, chain[:5], sums, previous, sizes, first_axes
        )

    late = {}
    early = summing(back_step(0, [cotangent, cotangent]), orders["back"], "rows", sizes, info, who=1)
    next(early)
    chain, upstreams = None, []
    for micro in range(2):
        chain = chain_step(0, micro, cotangent, chain)
        upstreams.append(lax.ppermute(chain[5], "section", [(1, 0)]))
        chain = chain[:5]
        next(early)
    slots = rest_step(0, chain, None)
    next(early)
    for micro in range(2):
        chain = chain_step(1, micro, upstreams[micro], chain)[:5]
    back = summing(
        back_step(1, upstreams), orders["back"], "rows", sizes, info, who=0, previous=lambda: late["back"]
    )
    next(back)
    slots = rest_step(1, chain, slots)
    split_at = sizes[first_axes[0]]
    inner = summing(slots[:split_at], orders["inner"], "columns", sizes, info)
    attention = summing(slots[split_at:], orders["attention"], "four", sizes, info)
    next(inner)
    next(attention)
    next(early)
    next(back)
    next(early)
    next(inner)
    next(attention)
    next(early)
    next(back)
    next(early)
    next(inner)
    next(attention)
    next(back)
    late["back"] = next(early)
    for _ in range(5):
        next(inner)
        next(attention)
        back_out = next(back)
    inner_out = next(inner)
    attention_out = next(attention)
    return (
        acts[None, :, None],
        chain[3][None, :, None],
        attention_out[0].reshape(1, D, D),
        attention_out[1].reshape(1, D, D),
        attention_out[2].reshape(1, D, D),
        attention_out[3].reshape(1, D, D),
        inner_out[0].reshape(1, D, -1),
        back_out[0].reshape(1, -1, D),
        attention_out[4],
        attention_out[5],
    )


def solution(mesh):
    in_specs = (
        P(None, "dp", None, None),
        P(None, "dp", None, None),
        P(None, "dp", None),
        P(None, "dp", None),
        P("section", None, None),
        P("section", None, None),
        P("section", None, None),
        P("section", None, None),
        P("section", None, None),
        P("section", None, None),
        P("section", None),
    )
    out_specs = (
        P("section", None, "dp", None, None),
        P("section", None, "dp", None, None),
        P("section", None, None),
        P("section", None, None),
        P("section", None, None),
        P("section", None, None),
        P("section", None, None),
        P("section", None, None),
        P("section", None),
        P("section", None),
    )
    return jax.shard_map(shards, mesh=mesh, in_specs=in_specs, out_specs=out_specs, check_vma=False)
```

time: 733 us -> 448 us (0.61)
  matrix products: 301 us -> 0 us
  Pallas kernels: 0 us -> 151 us
  waiting for transfers between devices: 299 us -> 228 us
  starting transfers between devices: 10 us -> 58.2 us
  blocking collectives: 45.8 us -> 0 us
  local copies, waits for them, and re-layouts: 28.1 us -> 2.82 us
  other arithmetic: 22.7 us -> 0 us
  between operations: 16.7 us -> 1.64 us
    dot_general x72 -> x0, matrix products: 301 us -> none  [the longest x54 194 us: multiply(): return jnp.dot(left_side, right_side, precision=lax.Precision.HIGHEST)]
    psum x1 -> x0, waiting for transfers between devices: 299 us -> none  [shards(): lax.psum((grad_query, grad_key, grad_value, grad_outer, grad_inner, grad_...]
    ppermute x4 -> x36, waiting for transfers between devices: 0.01 us -> 228 us  [the longest x16 103 us: shifted(): lax.ppermute(value, ('section', 'dp'), [(who * count + a, who * count + b...]
    pallas_call x0 -> x43, Pallas kernels: none -> 151 us  [the longest x8 89.3 us: call(): pl.pallas_call(functools.partial(body, len(extra)), out_shape=outs + [loo...]
    ppermute x4 -> x36, starting transfers between devices: 9.98 us -> 58.2 us  [the longest x16 33.2 us: shifted(): lax.ppermute(value, ('section', 'dp'), [(who * count + a, who * count + b...]
    psum x1 -> x0, blocking collectives: 45.8 us -> none  [shards(): lax.psum((grad_query, grad_key, grad_value, grad_outer, grad_inner, grad_...]
    unnamed x203 -> x22, local copies, waits for them, and re-layouts: 25.6 us -> 2.73 us
  transfers between devices with their start and end apart: 5 -> 36, of which waited for: 1 -> 21; matrix products, arithmetic and copies ran while one was open for 7% -> 0% of each run, Pallas kernels for 0% -> 19%
where the time goes in v1:
time: 448 us; the launch traced here: 441 us
  waiting for transfers between devices  228 us (51%)
  Pallas kernels  151 us (34%)
  starting transfers between devices  58.2 us (13%)
    ppermute x16, waiting for transfers between devices, shifted(): lax.ppermute(value, ('section', 'dp'), [(who * count + a, who * count + b...  103 us
    ppermute x16, waiting for transfers between devices, shifted(): return lax.ppermute(value, 'dp', pairs)  89.7 us
    pallas_call x8, Pallas kernels, call(): pl.pallas_call(functools.partial(body, len(extra)), out_shape=outs + [loo...  89.3 us
    ppermute x16, starting transfers between devices, shifted(): lax.ppermute(value, ('section', 'dp'), [(who * count + a, who * count + b...  33.2 us
    pallas_call x32, Pallas kernels, local_call(): pl.pallas_call(guarded, out_shape=list(outs) + [loose(8, 128)], in_specs=...  30.8 us
    ppermute x2, waiting for transfers between devices, shards(): upstreams.append(lax.ppermute(chain[5], 'section', [(1, 0)]))  30.8 us
    pallas_call x3, Pallas kernels, forward_tick(): pl.pallas_call(functools.partial(forward_body, tick), out_shape=shapes, i...  30.5 us
    ppermute x16, starting transfers between devices, shifted(): return lax.ppermute(value, 'dp', pairs)  18.7 us
  transfers between devices with their start and end apart: 36, of which 21 were waited for; matrix products, arithmetic and copies ran while one was open for 0% of the time, Pallas kernels for 19%

profile of v1, /device:TPU:0, one launch (start us, length us, event | category | flops | bytes accessed | tf_op | source)
XLA Modules:
  0.0 441.2 jit_solution(80864780360318967)
XLA Ops:
  2.8 14.7 %layer_forward.3 = (f32[2,384,512]{2,1,0:T(8,128)}, f32[384,512]{1,0:T(8,128)}, f32[2,384,512]{2,1,0:T(8,128)}, f32[2,384,512]{2,1,0:T(8,128)}, f32[2,384,512]{2...) custom-call(s32[5]{0:T(128)S(1)} %stack.23.refs_0_, ...), custom_call_target="tpu_custom_call" | custom-call | flops 10000000000 | bytes 20000000 | tf_op jit(solution)/shard_map/layer_forward/pallas_call | solution.py:248
  17.5 1.3 collective-permute-start
  18.9 2.1 collective-permute-done.refs_11_
  20.9 15.0 %layer_forward.4 = (f32[2,384,512]{2,1,0:T(8,128)}, f32[384,512]{1,0:T(8,128)}, f32[2,384,512]{2,1,0:T(8,128)}, f32[2,384,512]{2,1,0:T(8,128)}, f32[2,384,512]{2...) custom-call(s32[5]{0:T(128)S(1)} %stack.23.refs_0_, ...), custom_call_target="tpu_custom_call", output_to_operand_aliasing={{0}: (12, {}), {2}: (13, {}), {3}: (14, {}), {4}: (15, {}),... | custom-call | flops 10000000000 | bytes 20000000 | tf_op jit(solution)/shard_map/layer_forward/pallas_call | solution.py:248
  36.0 2.3 collective-permute-start.1
  38.3 2.1 collective-permute-done.1.refs_11_
  41.8 1.2 grad_back.2
  42.9 0.8 collective-permute-start.2
  43.8 7.4 %grad_chain.4 = (bf16[2,2,384,2048]{3,2,1,0:T(8,128)(2,1)}, bf16[2,2,384,1536]{3,2,1,0:T(8,128)(2,1)}, bf16[2,2,384,512]{3,2,1,0:T(8,128)(2,1)}, f32[2,384,512]{...) custom-call(s32[5]{0:T(128)S(1)} %stack.23.refs_0_, f32[1,2]{1,0:T(1,128)S(1)} %copy-done.10, ...), custom_call_target="tpu_custom_call" | custom-call | flops 20000000000 | bytes 20000000 | tf_op jit(solution)/shard_map/grad_chain/pallas_call | solution.py:575
  51.2 1.3 collective-permute-start.4
  53.9 5.6 %grad_chain.5 = (bf16[2,2,384,2048]{3,2,1,0:T(8,128)(2,1)}, bf16[2,2,384,1536]{3,2,1,0:T(8,128)(2,1)}, bf16[2,2,384,512]{3,2,1,0:T(8,128)(2,1)}, f32[2,384,512]{...) custom-call(s32[5]{0:T(128)S(1)} %stack.23.refs_0_, ...), custom_call_target="tpu_custom_call", output_to_operand_aliasing={{0}: (18, {}), {1}: (19, {}), {2}: (20, {}), {3}: (21, {}),... | custom-call | flops 20000000000 | bytes 20000000 | tf_op jit(solution)/shard_map/grad_chain/pallas_call | solution.py:575
  59.5 1.3 collective-permute-start.3
  62.1 9.3 %grad_rest.2 = (f32[2,2,2,128,512]{4,3,2,1,0:T(8,128)}, f32[2,2,2,128,512]{4,3,2,1,0:T(8,128)}, f32[2,2,2,136,512]{4,3,2,1,0:T(8,128)}, f32[2,2,2,136,512]{4,3,2,1,0:T(8,128)}, f32[8,128]{1,0:T(8,128)S(1)}) custom-call(s32[5]{0:T(128)S(1)} %stack.23.refs_0_, s32[2,1,384]{2,1,0:T(1,128)S(1)} %copy-done.8, f32[2,384,512]{2,1,0:T(8,128)} %get-tuple-element.205.refs_2_, ...), custom_call_target="tpu_custom_call" | custom-call | flops 10000000000 | bytes 20000000 | tf_op jit(solution)/shard_map/grad_rest/pallas_call | solution.py:575
  72.0 20.4 %collective-permute-done.4.refs_4_.refs_2_ = f32[384,512]{1,0:T(8,128)S(1)} collective-permute-done((f32[384,512]{1,0:T(8,128)}, f32[384,512]{1,0:T(8,128)S(1)}, u32[]{:S(2)}, u32[]{:S(2)}) %collective-permute-start.4) | collective-permute-done | bytes 786464 | tf_op jit(solution)/shard_map/ppermute | solution.py:916
  92.3 17.8 %grad_chain.6 = (bf16[2,2,384,2048]{3,2,1,0:T(8,128)(2,1)}, bf16[2,2,384,1536]{3,2,1,0:T(8,128)(2,1)}, bf16[2,2,384,512]{3,2,1,0:T(8,128)(2,1)}, f32[2,384,512]{...) custom-call(s32[5]{0:T(128)S(1)} %stack.23.refs_0_, ...), custom_call_target="tpu_custom_call", output_to_operand_aliasing={{0}: (18, {}), {1}: (19, {}), {2}: (20, {}), {3}: (21, {}),... | custom-call | flops 20000000000 | bytes 20000000 | tf_op jit(solution)/shard_map/grad_chain/pallas_call | solution.py:575
  110.2 10.5 %collective-permute-done.3.refs_4_.refs_3_ = f32[384,512]{1,0:T(8,128)S(1)} collective-permute-done((f32[384,512]{1,0:T(8,128)}, f32[384,512]{1,0:T(8,128)S(1)}, u32[]{:S(2)}, u32[]{:S(2)}) %collective-permute-start.3) | collective-permute-done | bytes 786464 | tf_op jit(solution)/shard_map/ppermute | solution.py:916
  120.6 18.2 %grad_chain.7 = (bf16[2,2,384,2048]{3,2,1,0:T(8,128)(2,1)}, bf16[2,2,384,1536]{3,2,1,0:T(8,128)(2,1)}, bf16[2,2,384,512]{3,2,1,0:T(8,128)(2,1)}, f32[2,384,512]{...) custom-call(s32[5]{0:T(128)S(1)} %stack.23.refs_0_, ...), custom_call_target="tpu_custom_call", output_to_operand_aliasing={{0}: (18, {}), {1}: (19, {}), {2}: (20, {}), {3}: (21, {}),... | custom-call | flops 20000000000 | bytes 20000000 | tf_op jit(solution)/shard_map/grad_chain/pallas_call | solution.py:575
  138.8 10.6 %grad_back.3 = (f32[2,2,2,128,512]{4,3,2,1,0:T(8,128)}, f32[2,2,2,128,512]{4,3,2,1,0:T(8,128)}, f32[8,128]{1,0:T(8,128)S(1)}) custom-call(s32[5]{0:T(128)S(1)} %stack.23.refs_0_, f32[1,2]{1,0:T(1,128)S(1)} %copy-done.10, f32[384,512]{1,0:T(8,128)S(1)} %collective-permute-done.4.refs_4_.refs_2_, f32[384,512]{1,0:T(8,128)S(1)} %collective-permute-done.3.refs_4_.refs_3_, ...), custom_call_target="tpu_custom_call" | custom-call | flops 5000000000 | bytes 20000000 | tf_op jit(solution)/shard_map/grad_back/pallas_call | solution.py:575
  149.4 3.5 collective-permute-start.8
  152.9 19.3 %grad_rest.3 = (f32[2,2,2,128,512]{4,3,2,1,0:T(8,128)}, f32[2,2,2,128,512]{4,3,2,1,0:T(8,128)}, f32[2,2,2,136,512]{4,3,2,1,0:T(8,128)}, f32[2,2,2,136,512]{4,3,2,1,0:T(8,128)}, f32[8,128]{1,0:T(8,128)S(1)}) custom-call(s32[5]{0:T(128)S(1)} %stack.23.refs_0_, ...), custom_call_target="tpu_custom_call", output_to_operand_aliasing={{0}: (11, {}), {1}: (12, {}), {2}: (13, {}), {3}: (14, {})} | custom-call | flops 10000000000 | bytes 20000000 | tf_op jit(solution)/shard_map/grad_rest/pallas_call | solution.py:575
  172.2 1.6 collective-permute-start.11
  176.3 6.9 %collective-permute-done.8.refs_3_ = f32[2,2,2,128,512]{4,3,2,1,0:T(8,128)S(1)} collective-permute-done((f32[2,2,2,128,512]{4,3,2,1,0:T(8,128)}, f32[2,2,2,128,512]{4,3,2,1,0:T(8,128)S(1)}, u32[]{:S(2)}, u32[]{:S(2)}) %collective-permute-start.8) | collective-permute-done | bytes 2097184 | tf_op jit(solution)/shard_map/ppermute | solution.py:854
  183.1 1.2 reduce_step.20
  185.9 2.3 collective-permute-start.13
  188.2 15.2 %collective-permute-done.10.refs_3_ = f32[2,2,2,128,512]{4,3,2,1,0:T(8,128)S(1)} collective-permute-done((f32[2,2,2,128,512]{4,3,2,1,0:T(8,128)}, f32[2,2,2,128,512]{4,3,2,1,0:T(8,128)S(1)}, u32[]{:S(2)}, u32[]{:S(2)}) %collective-permute-start.10) | collective-permute-done | bytes 2097184 | tf_op jit(solution)/shard_map/ppermute | solution.py:853
  203.3 1.2 reduce_step.21
  204.6 7.0 %collective-permute-done.11.refs_3_ = f32[2,2,2,136,512]{4,3,2,1,0:T(8,128)S(1)} collective-permute-done((f32[2,2,2,136,512]{4,3,2,1,0:T(8,128)}, f32[2,2,2,136,512]{4,3,2,1,0:T(8,128)S(1)}, u32[]{:S(2)}, u32[]{:S(2)}) %collective-permute-start.11) | collective-permute-done | bytes 2228256 | tf_op jit(solution)/shard_map/ppermute | solution.py:853
  211.5 1.7 reduce_step.22
  214.5 10.1 %collective-permute-done.13.refs_3_ = f32[2,2,128,512]{3,2,1,0:T(8,128)S(1)} collective-permute-done((f32[2,2,128,512]{3,2,1,0:T(8,128)S(1)}, f32[2,2,128,512]{3,2,1,0:T(8,128)S(1)}, u32[]{:S(2)}, u32[]{:S(2)}) %collective-permute-start.13) | collective-permute-done | bytes 1048608 | tf_op jit(solution)/shard_map/ppermute | solution.py:854
  224.6 0.9 reduce_step.23
  226.1 0.8 collective-permute-start.18
  227.4 3.5 collective-permute-start.15
  230.9 23.9 %collective-permute-done.15.refs_3_ = f32[2,2,128,512]{3,2,1,0:T(8,128)S(1)} collective-permute-done((f32[2,2,128,512]{3,2,1,0:T(8,128)S(1)}, f32[2,2,128,512]{3,2,1,0:T(8,128)S(1)}, u32[]{:S(2)}, u32[]{:S(2)}) %collective-permute-start.15) | collective-permute-done | bytes 1048608 | tf_op jit(solution)/shard_map/ppermute | solution.py:853
  254.8 0.9 reduce_step.24
  255.8 1.1 reduce_step.25
  257.4 3.4 collective-permute-start.17
  260.8 1.3 collective-permute-start.19
  262.1 6.3 %collective-permute-done.17.refs_3_ = f32[2,128,512]{2,1,0:T(8,128)S(1)} collective-permute-done((f32[2,128,512]{2,1,0:T(8,128)S(1)}, f32[2,128,512]{2,1,0:T(8,128)S(1)}, u32[]{:S(2)}, u32[]{:S(2)}) %collective-permute-start.17) | collective-permute-done | bytes 524320 | tf_op jit(solution)/shard_map/ppermute | solution.py:854
  269.9 5.9 %collective-permute-done.19.refs_3_ = f32[2,128,512]{2,1,0:T(8,128)S(1)} collective-permute-done((f32[2,128,512]{2,1,0:T(8,128)S(1)}, f32[2,128,512]{2,1,0:T(8,128)S(1)}, u32[]{:S(2)}, u32[]{:S(2)}) %collective-permute-start.19) | collective-permute-done | bytes 524320 | tf_op jit(solution)/shard_map/ppermute | solution.py:853
  276.5 0.9 reduce_step.28
  277.4 2.6 collective-permute-start.23
  280.1 2.2 collective-permute-start.21
  282.3 2.6 collective-permute-start.22
  285.0 11.5 %collective-permute-done.21.refs_3_ = f32[128,512]{1,0:T(8,128)S(1)} collective-permute-done((f32[128,512]{1,0:T(8,128)S(1)}, f32[128,512]{1,0:T(8,128)S(1)}, u32[]{:S(2)}, u32[]{:S(2)}) %collective-permute-start.21) | collective-permute-done | bytes 262176 | tf_op jit(solution)/shard_map/ppermute | solution.py:854
  297.1 2.1 collective-permute-done.22.refs_3_
  300.7 4.8 %collective-permute-start.24 = (f32[128,512]{1,0:T(8,128)S(1)}, f32[128,512]{1,0:T(8,128)S(1)}, u32[]{:S(2)}, u32[]{:S(2)}) collective-permute-start(f32[128,512]{1,0:T(8,128)S(1)} %get-tuple-element.286.refs_2_), channel_id=1, source_target_pairs={{0,8},{1,9},{2,10},{3,11},{4,12},{5,13},{6,14},{7,15},{8,0},{9,1},... | collective-permute-start | bytes 786440 | tf_op jit(solution)/shard_map/ppermute | solution.py:854
  305.7 25.1 %collective-permute-done.24.refs_3_ = f32[128,512]{1,0:T(8,128)S(1)} collective-permute-done((f32[128,512]{1,0:T(8,128)S(1)}, f32[128,512]{1,0:T(8,128)S(1)}, u32[]{:S(2)}, u32[]{:S(2)}) %collective-permute-start.24) | collective-permute-done | bytes 262176 | tf_op jit(solution)/shard_map/ppermute | solution.py:854
  331.4 2.6 collective-permute-done.25.refs_3_
  335.3 1.6 collective-permute-start.29
  336.8 2.2 collective-permute-start.27
  339.2 8.7 %collective-permute-done.27.refs_3_ = f32[2,128,512]{2,1,0:T(8,128)S(1)} collective-permute-done((f32[2,128,512]{2,1,0:T(8,128)S(1)}, f32[2,128,512]{2,1,0:T(8,128)S(1)}, u32[]{:S(2)}, u32[]{:S(2)}) %collective-permute-start.27) | collective-permute-done | bytes 524320 | tf_op jit(solution)/shard_map/ppermute | solution.py:854
  348.5 3.4 collective-permute-done.28.refs_3_
  353.4 4.6 %collective-permute-start.30 = (f32[2,2,128,512]{3,2,1,0:T(8,128)S(1)}, f32[2,2,128,512]{3,2,1,0:T(8,128)S(1)}, u32[]{:S(2)}, u32[]{:S(2)}) collective-permute-start(f32[2,2,128,512]{3,2,1,0:T(8,128)S(1)} %get-tuple-element.298.refs_2_), channel_id=1, source_target_pairs={{0,1},{1,0},{2,3},{3,2},{4,5},{5,4},{6,7},{7,6},{8,9},{9,8},{10,11... | collective-permute-start | bytes 3145736 | tf_op jit(solution)/shard_map/ppermute | solution.py:854
  357.9 1.7 collective-permute-start.31
  359.6 11.1 %collective-permute-done.30.refs_3_ = f32[2,2,128,512]{3,2,1,0:T(8,128)S(1)} collective-permute-done((f32[2,2,128,512]{3,2,1,0:T(8,128)S(1)}, f32[2,2,128,512]{3,2,1,0:T(8,128)S(1)}, u32[]{:S(2)}, u32[]{:S(2)}) %collective-permute-start.30) | collective-permute-done | bytes 1048608 | tf_op jit(solution)/shard_map/ppermute | solution.py:854
  371.4 9.7 %collective-permute-done.31.refs_3_ = f32[2,2,128,512]{3,2,1,0:T(8,128)S(1)} collective-permute-done((f32[2,2,128,512]{3,2,1,0:T(8,128)S(1)}, f32[2,2,128,512]{3,2,1,0:T(8,128)S(1)}, u32[]{:S(2)}, u32[]{:S(2)}) %collective-permute-start.31) | collective-permute-done | bytes 1048608 | tf_op jit(solution)/shard_map/ppermute | solution.py:853
  381.8 0.8 place_step.23
  382.6 1.5 collective-permute-start.35
  384.1 4.4 %collective-permute-start.33 = (f32[2,2,2,128,512]{4,3,2,1,0:T(8,128)S(1)}, f32[2,2,2,128,512]{4,3,2,1,0:T(8,128)S(1)}, u32[]{:S(2)}, u32[]{:S(2)}) collective-permute-start(f32[2,2,2,128,512]{4,3,2,1,0:T(8,128)S(1)} %get-tuple-element.304.refs_2_), channel_id=1, source_target_pairs={{0,4},{1,5},{2,6},{3,7},{4,0},{5,1},{6,2},{7,3},{8,12},{9,13},{10,... | collective-permute-start | bytes 6291464 | tf_op jit(solution)/shard_map/ppermute | solution.py:854
  389.0 23.6 %collective-permute-done.33.refs_3_ = f32[2,2,2,128,512]{4,3,2,1,0:T(8,128)S(1)} collective-permute-done((f32[2,2,2,128,512]{4,3,2,1,0:T(8,128)S(1)}, f32[2,2,2,128,512]{4,3,2,1,0:T(8,128)S(1)}, u32[]{:S(2)}, u32[]{:S(2)}) %collective-permute-start.33) | collective-permute-done | bytes 2097184 | tf_op jit(solution)/shard_map/ppermute | solution.py:854
  412.6 2.6 place_last.5
  415.2 20.0 %collective-permute-done.34.refs_3_ = f32[2,2,2,128,512]{4,3,2,1,0:T(8,128)S(1)} collective-permute-done((f32[2,2,2,128,512]{4,3,2,1,0:T(8,128)S(1)}, f32[2,2,2,128,512]{4,3,2,1,0:T(8,128)S(1)}, u32[]{:S(2)}, u32[]{:S(2)}) %collective-permute-start.34) | collective-permute-done | bytes 2097184 | tf_op jit(solution)/shard_map/ppermute | solution.py:853
  435.2 2.6 place_last.6
  437.8 3.1 place_last.7
  (75 shorter events, 23.7 us)
Async XLA Ops:
  0.8 0.7 copy-start.5
  1.4 0.7 copy-start.7
  2.1 0.7 copy-start.9
  17.5 3.4 collective-permute-start
  36.0 4.4 collective-permute-start.1
  40.3 1.4 copy-start.4
  41.8 2.0 copy-start.6
  41.8 2.0 copy-start.8
  41.8 2.0 copy-start.10
  42.9 9.6 %collective-permute-start.2 = (f32[2,2,2,128,512]{4,3,2,1,0:T(8,128)}, f32[2,2,2,128,512]{4,3,2,1,0:T(8,128)S(1)}, u32[]{:S(2)}, u32[]{:S(2)}) collective-permute-start(f32[2,2,2,128,512]{4,3,2,1,0:T(8,128)} %get-tuple-element.196), channel_id=1, source_target_pairs={{16,20},{17,21},{18,22},{19,23},{20,16},{21,17},{22,18},{23,19},{2... | collective-permute-start | bytes 6291464 | tf_op jit(solution)/shard_map/ppermute | solution.py:854
  43.8 8.7 %copy-start.3 = (f32[2,2,2,128,512]{4,3,2,1,0:T(8,128)S(1)}, f32[2,2,2,128,512]{4,3,2,1,0:T(8,128)}, u32[]{:S(2)}) copy-start(f32[2,2,2,128,512]{4,3,2,1,0:T(8,128)} %get-tuple-element.195.refs_2_) | copy-start | bytes 6291460
  51.2 41.1 %collective-permute-start.4 = (f32[384,512]{1,0:T(8,128)}, f32[384,512]{1,0:T(8,128)S(1)}, u32[]{:S(2)}, u32[]{:S(2)}) collective-permute-start(f32[384,512]{1,0:T(8,128)} %get-tuple-element.204), channel_id=1, source_target_pairs={{16,0},{17,1},{18,2},{19,3},{20,4},{21,5},{22,6},{23,7},{24,8},{25... | collective-permute-start | bytes 2359304 | tf_op jit(solution)/shard_map/ppermute | solution.py:916
  53.1 7.6 %collective-permute-start.5 = (f32[2,2,128,512]{3,2,1,0:T(8,128)S(1)}, f32[2,2,128,512]{3,2,1,0:T(8,128)S(1)}, u32[]{:S(2)}, u32[]{:S(2)}) collective-permute-start(f32[2,2,128,512]{3,2,1,0:T(8,128)S(1)} %get-tuple-element.214), channel_id=1, source_target_pairs={{16,17},{17,16},{18,19},{19,18},{20,21},{21,20},{22,23},{23,22},{2... | collective-permute-start | bytes 3145736 | tf_op jit(solution)/shard_map/ppermute | solution.py:854
  59.5 61.1 %collective-permute-start.3 = (f32[384,512]{1,0:T(8,128)}, f32[384,512]{1,0:T(8,128)S(1)}, u32[]{:S(2)}, u32[]{:S(2)}) collective-permute-start(f32[384,512]{1,0:T(8,128)} %get-tuple-element.203), channel_id=1, source_target_pairs={{16,0},{17,1},{18,2},{19,3},{20,4},{21,5},{22,6},{23,7},{24,8},{25... | collective-permute-start | bytes 2359304 | tf_op jit(solution)/shard_map/ppermute | solution.py:916
  61.4 10.0 %collective-permute-start.6 = (f32[2,128,512]{2,1,0:T(8,128)S(1)}, f32[2,128,512]{2,1,0:T(8,128)S(1)}, u32[]{:S(2)}, u32[]{:S(2)}) collective-permute-start(f32[2,128,512]{2,1,0:T(8,128)S(1)} %get-tuple-element.218), channel_id=1, source_target_pairs={{16,18},{17,19},{18,16},{19,17},{20,22},{21,23},{22,20},{23,21},{2... | collective-permute-start | bytes 1572872 | tf_op jit(solution)/shard_map/ppermute | solution.py:854
  149.4 33.8 %collective-permute-start.8 = (f32[2,2,2,128,512]{4,3,2,1,0:T(8,128)}, f32[2,2,2,128,512]{4,3,2,1,0:T(8,128)S(1)}, u32[]{:S(2)}, u32[]{:S(2)}) collective-permute-start(f32[2,2,2,128,512]{4,3,2,1,0:T(8,128)} %get-tuple-element.243), channel_id=1, source_target_pairs={{0,4},{1,5},{2,6},{3,7},{4,0},{5,1},{6,2},{7,3},{8,12},{9,13},{10,... | collective-permute-start | bytes 6291464 | tf_op jit(solution)/shard_map/ppermute | solution.py:854
  152.9 30.3 %copy-start.2 = (f32[2,2,2,128,512]{4,3,2,1,0:T(8,128)S(1)}, f32[2,2,2,128,512]{4,3,2,1,0:T(8,128)}, u32[]{:S(2)}) copy-start(f32[2,2,2,128,512]{4,3,2,1,0:T(8,128)} %get-tuple-element.242.refs_2_) | copy-start | bytes 6291460
  172.2 39.3 %collective-permute-start.11 = (f32[2,2,2,136,512]{4,3,2,1,0:T(8,128)}, f32[2,2,2,136,512]{4,3,2,1,0:T(8,128)S(1)}, u32[]{:S(2)}, u32[]{:S(2)}) collective-permute-start(f32[2,2,2,136,512]{4,3,2,1,0:T(8,128)} %get-tuple-element.251), channel_id=1, source_target_pairs={{0,2},{1,3},{2,0},{3,1},{4,6},{5,7},{6,4},{7,5},{8,10},{9,11},{10,... | collective-permute-start | bytes 6684680 | tf_op jit(solution)/shard_map/ppermute | solution.py:853
  173.8 29.5 %collective-permute-start.10 = (f32[2,2,2,128,512]{4,3,2,1,0:T(8,128)}, f32[2,2,2,128,512]{4,3,2,1,0:T(8,128)S(1)}, u32[]{:S(2)}, u32[]{:S(2)}) collective-permute-start(f32[2,2,2,128,512]{4,3,2,1,0:T(8,128)} %get-tuple-element.248), channel_id=1, source_target_pairs={{0,1},{1,0},{2,3},{3,2},{4,5},{5,4},{6,7},{7,6},{8,9},{9,8},{10,11... | collective-permute-start | bytes 6291464 | tf_op jit(solution)/shard_map/ppermute | solution.py:853
  174.3 0.7 collective-permute-start.7
  175.6 8.8 %collective-permute-start.9 = (f32[128,512]{1,0:T(8,128)S(1)}, f32[128,512]{1,0:T(8,128)S(1)}, u32[]{:S(2)}, u32[]{:S(2)}) collective-permute-start(f32[128,512]{1,0:T(8,128)S(1)} %get-tuple-element.245.refs_2_), channel_id=1, source_target_pairs={{16,24},{17,25},{18,26},{19,27},{20,28},{21,29},{22,30},{23,31},{2... | collective-permute-start | bytes 786440 | tf_op jit(solution)/shard_map/ppermute | solution.py:854
  183.1 20.2 %copy-start.1 = (f32[2,2,2,128,512]{4,3,2,1,0:T(8,128)S(1)}, f32[2,2,2,128,512]{4,3,2,1,0:T(8,128)}, u32[]{:S(2)}) copy-start(f32[2,2,2,128,512]{4,3,2,1,0:T(8,128)} %get-tuple-element.247.refs_2_) | copy-start | bytes 6291460
  185.2 28.0 %collective-permute-start.12 = (f32[2,128,512]{2,1,0:T(8,128)S(1)}, f32[2,128,512]{2,1,0:T(8,128)S(1)}, u32[]{:S(2)}, u32[]{:S(2)}) collective-permute-start(f32[2,128,512]{2,1,0:T(8,128)S(1)} %get-tuple-element.253.refs_2_), channel_id=1, source_target_pairs={{16,18},{17,19},{18,16},{19,17},{20,22},{21,23},{22,20},{23,21},{2... | collective-permute-start | bytes 1572872 | tf_op jit(solution)/shard_map/ppermute | solution.py:854
  185.9 38.7 %collective-permute-start.13 = (f32[2,2,128,512]{3,2,1,0:T(8,128)S(1)}, f32[2,2,128,512]{3,2,1,0:T(8,128)S(1)}, u32[]{:S(2)}, u32[]{:S(2)}) collective-permute-start(f32[2,2,128,512]{3,2,1,0:T(8,128)S(1)} %get-tuple-element.256), channel_id=1, source_target_pairs={{0,1},{1,0},{2,3},{3,2},{4,5},{5,4},{6,7},{7,6},{8,9},{9,8},{10,11... | collective-permute-start | bytes 3145736 | tf_op jit(solution)/shard_map/ppermute | solution.py:854
  203.3 8.2 %copy-start = (f32[2,2,2,136,512]{4,3,2,1,0:T(8,128)S(1)}, f32[2,2,2,136,512]{4,3,2,1,0:T(8,128)}, u32[]{:S(2)}) copy-start(f32[2,2,2,136,512]{4,3,2,1,0:T(8,128)} %get-tuple-element.250.refs_2_) | copy-start | bytes 6684676
  213.8 11.7 %collective-permute-start.14 = (f32[2,2,128,512]{3,2,1,0:T(8,128)S(1)}, f32[2,2,128,512]{3,2,1,0:T(8,128)S(1)}, u32[]{:S(2)}, u32[]{:S(2)}) collective-permute-start(f32[2,2,128,512]{3,2,1,0:T(8,128)S(1)} %get-tuple-element.258.refs_2_), channel_id=1, source_target_pairs={{16,17},{17,16},{18,19},{19,18},{20,21},{21,20},{22,23},{23,22},{2... | collective-permute-start | bytes 3145736 | tf_op jit(solution)/shard_map/ppermute | solution.py:854
  226.1 43.2 %collective-permute-start.18 = (f32[2,2,2,128,512]{4,3,2,1,0:T(8,128)S(1)}, f32[2,2,2,128,512]{4,3,2,1,0:T(8,128)S(1)}, u32[]{:S(2)}, u32[]{:S(2)}) collective-permute-start(f32[2,2,2,128,512]{4,3,2,1,0:T(8,128)S(1)} %get-tuple-element.269.refs_2_), channel_id=1, source_target_pairs={{16,20},{17,21},{18,22},{19,23},{20,16},{21,17},{22,18},{23,19},{2... | collective-permute-start | bytes 6291464 | tf_op jit(solution)/shard_map/ppermute | solution.py:854
  226.9 28.9 %collective-permute-start.16 = (f32[2,2,136,512]{3,2,1,0:T(8,128)S(1)}, f32[2,2,136,512]{3,2,1,0:T(8,128)S(1)}, u32[]{:S(2)}, u32[]{:S(2)}) collective-permute-start(f32[2,2,136,512]{3,2,1,0:T(8,128)S(1)} %get-tuple-element.264), channel_id=1, source_target_pairs={{0,4},{1,5},{2,6},{3,7},{4,0},{5,1},{6,2},{7,3},{8,12},{9,13},{10,... | collective-permute-start | bytes 3342344 | tf_op jit(solution)/shard_map/ppermute | solution.py:853
  227.4 27.5 %collective-permute-start.15 = (f32[2,2,128,512]{3,2,1,0:T(8,128)S(1)}, f32[2,2,128,512]{3,2,1,0:T(8,128)S(1)}, u32[]{:S(2)}, u32[]{:S(2)}) collective-permute-start(f32[2,2,128,512]{3,2,1,0:T(8,128)S(1)} %get-tuple-element.261), channel_id=1, source_target_pairs={{0,2},{1,3},{2,0},{3,1},{4,6},{5,7},{6,4},{7,5},{8,10},{9,11},{10,... | collective-permute-start | bytes 3145736 | tf_op jit(solution)/shard_map/ppermute | solution.py:853
  256.9 19.6 %collective-permute-start.20 = (f32[2,136,512]{2,1,0:T(8,128)S(1)}, f32[2,136,512]{2,1,0:T(8,128)S(1)}, u32[]{:S(2)}, u32[]{:S(2)}) collective-permute-start(f32[2,136,512]{2,1,0:T(8,128)S(1)} %get-tuple-element.275), channel_id=1, source_target_pairs={{0,1},{1,0},{2,3},{3,2},{4,5},{5,4},{6,7},{7,6},{8,9},{9,8},{10,11... | collective-permute-start | bytes 1671176 | tf_op jit(solution)/shard_map/ppermute | solution.py:853
  257.4 11.1 %collective-permute-start.17 = (f32[2,128,512]{2,1,0:T(8,128)S(1)}, f32[2,128,512]{2,1,0:T(8,128)S(1)}, u32[]{:S(2)}, u32[]{:S(2)}) collective-permute-start(f32[2,128,512]{2,1,0:T(8,128)S(1)} %get-tuple-element.267), channel_id=1, source_target_pairs={{0,2},{1,3},{2,0},{3,1},{4,6},{5,7},{6,4},{7,5},{8,10},{9,11},{10,... | collective-permute-start | bytes 1572872 | tf_op jit(solution)/shard_map/ppermute | solution.py:854
  260.8 14.9 %collective-permute-start.19 = (f32[2,128,512]{2,1,0:T(8,128)S(1)}, f32[2,128,512]{2,1,0:T(8,128)S(1)}, u32[]{:S(2)}, u32[]{:S(2)}) collective-permute-start(f32[2,128,512]{2,1,0:T(8,128)S(1)} %get-tuple-element.272), channel_id=1, source_target_pairs={{0,4},{1,5},{2,6},{3,7},{4,0},{5,1},{6,2},{7,3},{8,12},{9,13},{10,... | collective-permute-start | bytes 1572872 | tf_op jit(solution)/shard_map/ppermute | solution.py:853
  277.4 22.5 %collective-permute-start.23 = (f32[136,512]{1,0:T(8,128)S(1)}, f32[136,512]{1,0:T(8,128)S(1)}, u32[]{:S(2)}, u32[]{:S(2)}) collective-permute-start(f32[136,512]{1,0:T(8,128)S(1)} %get-tuple-element.284), channel_id=1, source_target_pairs={{0,8},{1,9},{2,10},{3,11},{4,12},{5,13},{6,14},{7,15},{8,0},{9,1},... | collective-permute-start | bytes 835592 | tf_op jit(solution)/shard_map/ppermute | solution.py:853
  280.1 16.4 %collective-permute-start.21 = (f32[128,512]{1,0:T(8,128)S(1)}, f32[128,512]{1,0:T(8,128)S(1)}, u32[]{:S(2)}, u32[]{:S(2)}) collective-permute-start(f32[128,512]{1,0:T(8,128)S(1)} %get-tuple-element.278), channel_id=1, source_target_pairs={{0,8},{1,9},{2,10},{3,11},{4,12},{5,13},{6,14},{7,15},{8,0},{9,1},... | collective-permute-start | bytes 786440 | tf_op jit(solution)/shard_map/ppermute | solution.py:854
  282.3 16.9 %collective-permute-start.22 = (f32[128,512]{1,0:T(8,128)S(1)}, f32[128,512]{1,0:T(8,128)S(1)}, u32[]{:S(2)}, u32[]{:S(2)}) collective-permute-start(f32[128,512]{1,0:T(8,128)S(1)} %get-tuple-element.281), channel_id=1, source_target_pairs={{0,8},{1,9},{2,10},{3,11},{4,12},{5,13},{6,14},{7,15},{8,0},{9,1},... | collective-permute-start | bytes 786440 | tf_op jit(solution)/shard_map/ppermute | solution.py:853
  300.7 33.9 %collective-permute-start.26 = (f32[136,512]{1,0:T(8,128)S(1)}, f32[136,512]{1,0:T(8,128)S(1)}, u32[]{:S(2)}, u32[]{:S(2)}) collective-permute-start(f32[136,512]{1,0:T(8,128)S(1)} %get-tuple-element.290.refs_2_), channel_id=1, source_target_pairs={{0,8},{1,9},{2,10},{3,11},{4,12},{5,13},{6,14},{7,15},{8,0},{9,1},... | collective-permute-start | bytes 835592 | tf_op jit(solution)/shard_map/ppermute | solution.py:853
  300.7 30.0 %collective-permute-start.24 = (f32[128,512]{1,0:T(8,128)S(1)}, f32[128,512]{1,0:T(8,128)S(1)}, u32[]{:S(2)}, u32[]{:S(2)}) collective-permute-start(f32[128,512]{1,0:T(8,128)S(1)} %get-tuple-element.286.refs_2_), channel_id=1, source_target_pairs={{0,8},{1,9},{2,10},{3,11},{4,12},{5,13},{6,14},{7,15},{8,0},{9,1},... | collective-permute-start | bytes 786440 | tf_op jit(solution)/shard_map/ppermute | solution.py:854
  305.6 28.4 %collective-permute-start.25 = (f32[128,512]{1,0:T(8,128)S(1)}, f32[128,512]{1,0:T(8,128)S(1)}, u32[]{:S(2)}, u32[]{:S(2)}) collective-permute-start(f32[128,512]{1,0:T(8,128)S(1)} %get-tuple-element.288.refs_2_), channel_id=1, source_target_pairs={{0,8},{1,9},{2,10},{3,11},{4,12},{5,13},{6,14},{7,15},{8,0},{9,1},... | collective-permute-start | bytes 786440 | tf_op jit(solution)/shard_map/ppermute | solution.py:853
  335.3 17.3 %collective-permute-start.29 = (f32[2,136,512]{2,1,0:T(8,128)S(1)}, f32[2,136,512]{2,1,0:T(8,128)S(1)}, u32[]{:S(2)}, u32[]{:S(2)}) collective-permute-start(f32[2,136,512]{2,1,0:T(8,128)S(1)} %get-tuple-element.296.refs_2_), channel_id=1, source_target_pairs={{0,1},{1,0},{2,3},{3,2},{4,5},{5,4},{6,7},{7,6},{8,9},{9,8},{10,11... | collective-permute-start | bytes 1671176 | tf_op jit(solution)/shard_map/ppermute | solution.py:853
  336.8 11.1 %collective-permute-start.27 = (f32[2,128,512]{2,1,0:T(8,128)S(1)}, f32[2,128,512]{2,1,0:T(8,128)S(1)}, u32[]{:S(2)}, u32[]{:S(2)}) collective-permute-start(f32[2,128,512]{2,1,0:T(8,128)S(1)} %get-tuple-element.292.refs_2_), channel_id=1, source_target_pairs={{0,2},{1,3},{2,0},{3,1},{4,6},{5,7},{6,4},{7,5},{8,10},{9,11},{10,... | collective-permute-start | bytes 1572872 | tf_op jit(solution)/shard_map/ppermute | solution.py:854
  339.1 12.9 %collective-permute-start.28 = (f32[2,128,512]{2,1,0:T(8,128)S(1)}, f32[2,128,512]{2,1,0:T(8,128)S(1)}, u32[]{:S(2)}, u32[]{:S(2)}) collective-permute-start(f32[2,128,512]{2,1,0:T(8,128)S(1)} %get-tuple-element.294.refs_2_), channel_id=1, source_target_pairs={{0,4},{1,5},{2,6},{3,7},{4,0},{5,1},{6,2},{7,3},{8,12},{9,13},{10,... | collective-permute-start | bytes 1572872 | tf_op jit(solution)/shard_map/ppermute | solution.py:853
  353.3 28.5 %collective-permute-start.32 = (f32[2,2,136,512]{3,2,1,0:T(8,128)S(1)}, f32[2,2,136,512]{3,2,1,0:T(8,128)S(1)}, u32[]{:S(2)}, u32[]{:S(2)}) collective-permute-start(f32[2,2,136,512]{3,2,1,0:T(8,128)S(1)} %get-tuple-element.302.refs_2_), channel_id=1, source_target_pairs={{0,4},{1,5},{2,6},{3,7},{4,0},{5,1},{6,2},{7,3},{8,12},{9,13},{10,... | collective-permute-start | bytes 3342344 | tf_op jit(solution)/shard_map/ppermute | solution.py:853
  353.4 17.3 %collective-permute-start.30 = (f32[2,2,128,512]{3,2,1,0:T(8,128)S(1)}, f32[2,2,128,512]{3,2,1,0:T(8,128)S(1)}, u32[]{:S(2)}, u32[]{:S(2)}) collective-permute-start(f32[2,2,128,512]{3,2,1,0:T(8,128)S(1)} %get-tuple-element.298.refs_2_), channel_id=1, source_target_pairs={{0,1},{1,0},{2,3},{3,2},{4,5},{5,4},{6,7},{7,6},{8,9},{9,8},{10,11... | collective-permute-start | bytes 3145736 | tf_op jit(solution)/shard_map/ppermute | solution.py:854
  357.9 23.1 %collective-permute-start.31 = (f32[2,2,128,512]{3,2,1,0:T(8,128)S(1)}, f32[2,2,128,512]{3,2,1,0:T(8,128)S(1)}, u32[]{:S(2)}, u32[]{:S(2)}) collective-permute-start(f32[2,2,128,512]{3,2,1,0:T(8,128)S(1)} %get-tuple-element.300.refs_2_), channel_id=1, source_target_pairs={{0,2},{1,3},{2,0},{3,1},{4,6},{5,7},{6,4},{7,5},{8,10},{9,11},{10,... | collective-permute-start | bytes 3145736 | tf_op jit(solution)/shard_map/ppermute | solution.py:853
  382.6 55.2 %collective-permute-start.35 = (f32[2,2,2,136,512]{4,3,2,1,0:T(8,128)S(1)}, f32[2,2,2,136,512]{4,3,2,1,0:T(8,128)S(1)}, u32[]{:S(2)}, u32[]{:S(2)}) collective-permute-start(f32[2,2,2,136,512]{4,3,2,1,0:T(8,128)S(1)} %get-tuple-element.309.refs_2_), channel_id=1, source_target_pairs={{0,2},{1,3},{2,0},{3,1},{4,6},{5,7},{6,4},{7,5},{8,10},{9,11},{10,... | collective-permute-start | bytes 6684680 | tf_op jit(solution)/shard_map/ppermute | solution.py:853
  384.1 28.4 %collective-permute-start.33 = (f32[2,2,2,128,512]{4,3,2,1,0:T(8,128)S(1)}, f32[2,2,2,128,512]{4,3,2,1,0:T(8,128)S(1)}, u32[]{:S(2)}, u32[]{:S(2)}) collective-permute-start(f32[2,2,2,128,512]{4,3,2,1,0:T(8,128)S(1)} %get-tuple-element.304.refs_2_), channel_id=1, source_target_pairs={{0,4},{1,5},{2,6},{3,7},{4,0},{5,1},{6,2},{7,3},{8,12},{9,13},{10,... | collective-permute-start | bytes 6291464 | tf_op jit(solution)/shard_map/ppermute | solution.py:854
  388.6 46.6 %collective-permute-start.34 = (f32[2,2,2,128,512]{4,3,2,1,0:T(8,128)S(1)}, f32[2,2,2,128,512]{4,3,2,1,0:T(8,128)S(1)}, u32[]{:S(2)}, u32[]{:S(2)}) collective-permute-start(f32[2,2,2,128,512]{4,3,2,1,0:T(8,128)S(1)} %get-tuple-element.307.refs_2_), channel_id=1, source_target_pairs={{0,1},{1,0},{2,3},{3,2},{4,5},{5,4},{6,7},{7,6},{8,9},{9,8},{10,11... | collective-permute-start | bytes 6291464 | tf_op jit(solution)/shard_map/ppermute | solution.py:853

commit v2 on v1

--- a/solution.py
+++ b/solution.py
@@ -48,6 +48,16 @@
 def folded(product):
     half = product.shape[0] // 2
     return product[:half] + product[half:]
+
+
+def put_split(target, value):
+    high, low = split(value)
+    target[0] = high
+    target[1] = low
+
+
+def two_dots(left_side, right_side):
+    return dot(left_side[0], right_side) + dot(left_side[1], right_side)
 
 
 def gelu_inner(value):
@@ -125,10 +135,10 @@
         valid_row = valids[micro].astype(jnp.float32)
         fill_bias(bias_v, segment_row, valid_row)
         pltpu.make_async_copy(received, s_v, in_sem.at[6]).wait()
-        x_v[...] = stacked(s_v[...])
+        put_split(x_v, s_v[...])
         for index, (weight, target) in enumerate(((wq_v, q_v), (wk_v, k_v), (wv_v, v_v))):
             loads[index].wait()
-            value = folded(dot(x_v[...], weight[...]))
+            value = two_dots(x_v, weight[...])
             target[...] = value * 0.125 if index == 0 else value
 
         stores = []
@@ -168,26 +178,26 @@
 
         store(4, ot_v, saved_o.at[micro])
         store(5, l_v, saved_l.at[micro])
-        x_v[...] = stacked(ot_v[...].T)
+        put_split(x_v, ot_v[...].T)
         loads[3].wait()
-        attn = folded(dot(x_v[...], wo_v[...])) * alphas[0, 0]
+        attn = two_dots(x_v, wo_v[...]) * alphas[0, 0]
         valid_col = jnp.broadcast_to(valid_row, (128, rows)).T
         weighting = jnp.concatenate([valid_col] * (D // 128), axis=1)
         attn_sum = jnp.sum(attn * attn * weighting)
         middle = s_v[...] + attn
         m_v[...] = middle
         store(6, m_v, saved_m.at[micro])
-        x_v[...] = stacked(middle)
+        put_split(x_v, middle)
         a_v[...] = jnp.zeros_like(a_v)
         loads[4].wait()
         loads[5].wait()
 
         for part in range(wi_v.shape[1] // 512):
             cols = pl.ds(part * 512, 512)
-            before = folded(dot(x_v[...], wi_v[:, cols]))
+            before = two_dots(x_v, wi_v[:, cols])
             p_v[:, cols] = before
-            hidden = stacked(0.5 * before * (1.0 + gelu_inner(before)))
-            a_v[...] += folded(dot(hidden, wb_v[cols, :]))
+            high, low = split(0.5 * before * (1.0 + gelu_inner(before)))
+            a_v[...] += dot(high, wb_v[cols, :]) + dot(low, wb_v[cols, :])
 
         store(7, p_v, saved_p.at[micro])
         ffn = a_v[...] * alphas[0, 1]
@@ -243,7 +253,7 @@
     scratch = [vmem((rows, width), f32)] + [vmem(w.shape, bf16) for w in weights]
     scratch += [vmem((rows, width), f32)] * 3 + [vmem((width, rows), f32), vmem((HEADS // 2, 8, rows), f32)]
     scratch += [vmem((rows, width), f32), vmem((rows, inner), f32), vmem((rows, width), f32)]
-    scratch += [vmem((8, 128), f32), vmem((rows, rows), f32), vmem((2 * rows, width), bf16)]
+    scratch += [vmem((8, 128), f32), vmem((rows, rows), f32), vmem((2, rows, width), bf16)]
     scratch += [pltpu.SemaphoreType.DMA((7,)), pltpu.SemaphoreType.DMA((11,))]
     outs = pl.pallas_call(
         functools.partial(forward_body, tick),
@@ -304,44 +314,47 @@
     return dot(left_high, right_high) + dot(left_low, right_high) + dot(left_high, right_low)
 
 
-def back_body(turn, count, sizes, axis, *refs):
+def back_body(count, sizes, axis, *refs):
     info, alphas = refs[:2]
-    upstreams, saved_p = refs[2:4], refs[4]
-    slots, refs = refs[6 : 6 + count], refs[7 + count :]
+    upstreams, targets, saved_p = refs[2:4], refs[4], refs[5]
+    slots, refs = refs[7 : 7 + count], refs[8 + count :]
     g_v, gh_v, p_v, w_v, in_sem, out_sem = refs
     parts = p_v.shape[0]
     rows = g_v.shape[1]
 
-    @pl.when(info[0] == 1 - turn)
-    def _():
-        def load(part, micro):
-            cols = pl.ds(part * 512, 512)
-            return pltpu.make_async_copy(
-                saved_p.at[micro, :, cols], p_v.at[part, pl.ds(micro * rows, rows)], in_sem.at[part, micro]
-            )
-
-        firsts = []
+    def load(part, micro):
+        cols = pl.ds(part * 512, 512)
+        return pltpu.make_async_copy(
+            saved_p.at[micro, :, cols], p_v.at[part, pl.ds(micro * rows, rows)], in_sem.at[part, micro]
+        )
+
+    for micro in range(2):
+
+        @pl.when(info[0] == 0)
+        def _():
+            pltpu.make_async_copy(upstreams[micro], g_v.at[micro], in_sem.at[parts, micro]).start()
+
+        @pl.when(info[0] != 0)
+        def _():
+            pltpu.make_async_copy(targets.at[micro, 0], g_v.at[micro], in_sem.at[parts, micro]).start()
+
+    for part in range(parts):
         for micro in range(2):
-            source = upstreams[micro] if turn else upstreams[micro].at[micro, 0]
-            firsts.append(pltpu.make_async_copy(source, g_v.at[micro], in_sem.at[parts, micro]))
-        start_all(firsts)
-        for part in range(parts):
-            for micro in range(2):
-                load(part, micro).start()
-        wait_all(firsts)
-        high, low = split(jnp.concatenate([g_v[0], g_v[1]], axis=0) * alphas[0, 1])
-        gh_v[0] = high
-        gh_v[1] = low
-
-        stores = []
-        for part in range(parts):
-            for micro in range(2):
-                load(part, micro).wait()
-            before = p_v[part].T
-            high, low = split(0.5 * before * (1.0 + gelu_inner(before)))
-            put_part(w_v, part, three_dots(high, low, gh_v[0], gh_v[1]))
-            stores += start_all(slot_copies(info, sizes, axis, w_v, slots, out_sem, part))
-        wait_all(stores)
+            load(part, micro).start()
+    for micro in range(2):
+        pltpu.make_async_copy(targets.at[micro, 0], g_v.at[micro], in_sem.at[parts, micro]).wait()
+    high, low = split(jnp.concatenate([g_v[0], g_v[1]], axis=0) * alphas[0, 1])
+    gh_v[0] = high
+    gh_v[1] = low
+    stores = []
+    for part in range(parts):
+        for micro in range(2):
+            load(part, micro).wait()
+        before = p_v[part].T
+        high, low = split(0.5 * before * (1.0 + gelu_inner(before)))
+        put_part(w_v, part, three_dots(high, low, gh_v[0], gh_v[1]))
+        stores += start_all(slot_copies(info, sizes, axis, w_v, slots, out_sem, part))
+    wait_all(stores)
 
 
 def chain_body(turn, micro, extra, *refs):
@@ -495,78 +508,99 @@
         wait_all(stores)
 
 
-def rest_body(turn, counts, sizes, axes, extra, *refs):
-    info, valids = refs[:2]
-    saved_m, saved_s, saved_o, befores, spreads, firsts, sums, small = refs[2:10]
-    refs = refs[11 + extra :]
-    slots, refs = (refs[: counts[0]], refs[counts[0] : sum(counts)]), refs[sum(counts) + 1 :]
-    (m_v, s_v, o_v, lt_v, r_v, w_v, n_v, t_v, in_sem, r_sem, out_sem, n_sem, t_sem) = refs
+def inner_body(count, sizes, axis, *refs):
+    info, saved_m, befores = refs[:3]
+    slots, refs = refs[4 : 4 + count], refs[5 + count :]
+    m_v, lt_v, r_v, w_v, in_sem, r_sem, out_sem = refs
     rows = m_v.shape[1]
 
-    @pl.when(info[0] == 1 - turn)
-    def _():
-        def loads(index):
-            copies = []
-            for micro in range(2):
-                for half in range(2):
-                    if index < 4:
-                        source = befores.at[micro, half, :, pl.ds(index * 512, 512)]
-                    elif index < 7:
-                        source = spreads.at[micro, half, :, pl.ds((index - 4) * 512, 512)]
-                    else:
-                        source = firsts.at[micro, half]
-                    target = r_v.at[index, half, pl.ds(micro * rows, rows)]
-                    copies.append(pltpu.make_async_copy(source, target, r_sem.at[index, micro * 2 + half]))
-            return copies
-
-        lefts = [pltpu.make_async_copy(a, b, in_sem.at[i]) for i, (a, b) in enumerate(((saved_m, m_v), (saved_s, s_v), (saved_o, o_v)))]
-        tiles = [
-            pltpu.make_async_copy(sums, n_v.at[pl.ds(0, 2)], n_sem.at[0]),
-            pltpu.make_async_copy(small, n_v.at[pl.ds(2, 2)], n_sem.at[1]),
-        ]
-        lefts[0].start()
-        start_all(loads(0))
-        start_all(lefts[1:])
-        for index in range(1, 8):
-            start_all(loads(index))
-        start_all(tiles)
-
-        def turn_left(index, source, transpose):
-            for micro in range(2):
-                high, low = split(source[micro].T if transpose else source[micro])
-                lt_v[index, 0, :, pl.ds(micro * rows, rows)] = high
-                lt_v[index, 1, :, pl.ds(micro * rows, rows)] = low
-
-        stores = []
-        for index in range(8):
-            if index in (0, 4, 7):
-                left = (0, 4, 7).index(index)
-                lefts[left].wait()
-                turn_left(left, (m_v, s_v, o_v)[left], left < 2)
-            wait_all(loads(index))
-            unit, part = w_v.at[index // 4], index % 4
-            put_part(unit, part, three_dots(lt_v[left, 0], lt_v[left, 1], r_v[index, 0], r_v[index, 1]))
-            own = index // 4
-            stores += start_all(slot_copies(info, sizes, axes[own], unit, slots[own], out_sem.at[own], part))
-        wait_all(tiles)
-        lane = lax.broadcasted_iota(jnp.int32, (8, 256), 1)
-        tile = jnp.where(lane == 3, jnp.sum(valids[...].astype(jnp.float32)), jnp.zeros((8, 256), jnp.float32))
-        for index in range(3):
-            tile = jnp.where(lane == index, n_v[0, 0, index] + n_v[1, 0, index], tile)
-        for index in range(2):
-            tile = jnp.where(lane == 4 + index, n_v[2, 0, index] + n_v[3, 0, index], tile)
-        t_v[...] = tile
-        axis, unit_rows = axes[1], w_v.shape[4]
-        for by in range(counts[1]):
-
-            @pl.when(lax.rem(info[1 + axis] + by, sizes[axis]) == 0)
-            def _():
-                target = slots[1][by].at[0, 0, 0, pl.ds(unit_rows, 8), pl.ds(0, 256)]
-                copy = pltpu.make_async_copy(t_v, target, t_sem.at[0])
-                copy.start()
-                copy.wait()
-
-        wait_all(stores)
+    def loads(part):
+        copies = []
+        for micro in range(2):
+            for half in range(2):
+                source = befores.at[micro, half, :, pl.ds(part * 512, 512)]
+                target = r_v.at[part, half, pl.ds(micro * rows, rows)]
+                copies.append(pltpu.make_async_copy(source, target, r_sem.at[part, micro * 2 + half]))
+        return copies
+
+    first = pltpu.make_async_copy(saved_m, m_v, in_sem.at[0])
+    first.start()
+    for part in range(4):
+        start_all(loads(part))
+    first.wait()
+    turn_left(lt_v, m_v, True)
+    stores = []
+    for part in range(4):
+        wait_all(loads(part))
+        put_part(w_v, part, three_dots(lt_v[0], lt_v[1], r_v[part, 0], r_v[part, 1]))
+        stores += start_all(slot_copies(info, sizes, axis, w_v, slots, out_sem, part))
+    wait_all(stores)
+
+
+def turn_left(target, source, transpose):
+    rows = target.shape[2] // 2
+    for micro in range(2):
+        high, low = split(source[micro].T if transpose else source[micro])
+        target[0, :, micro * rows : (micro + 1) * rows] = high
+        target[1, :, micro * rows : (micro + 1) * rows] = low
+
+
+def attention_body(count, sizes, axis, *refs):
+    info, valids, saved_s, saved_o, spreads, firsts, sums, small = refs[:8]
+    slots, refs = refs[9 : 9 + count], refs[10 + count :]
+    (s_v, o_v, st_v, lo_v, r_v, w_v, n_v, t_v, in_sem, r_sem, out_sem) = refs
+    rows = s_v.shape[1]
+
+    def loads(part):
+        copies = []
+        for micro in range(2):
+            for half in range(2):
+                if part < 3:
+                    source = spreads.at[micro, half, :, pl.ds(part * 512, 512)]
+                else:
+                    source = firsts.at[micro, half]
+                target = r_v.at[part, half, pl.ds(micro * rows, rows)]
+                copies.append(pltpu.make_async_copy(source, target, r_sem.at[part, micro * 2 + half]))
+        return copies
+
+    lefts = [pltpu.make_async_copy(saved_s, s_v, in_sem.at[0]), pltpu.make_async_copy(saved_o, o_v, in_sem.at[1])]
+    tiles = [
+        pltpu.make_async_copy(sums, n_v.at[pl.ds(0, 2)], in_sem.at[2]),
+        pltpu.make_async_copy(small, n_v.at[pl.ds(2, 2)], in_sem.at[3]),
+    ]
+    start_all(lefts + tiles)
+    for part in range(4):
+        start_all(loads(part))
+    lefts[0].wait()
+    turn_left(st_v, s_v, True)
+    stores = []
+    for part in range(4):
+        if part == 3:
+            lefts[1].wait()
+            turn_left(lo_v, o_v, False)
+        left = lo_v if part == 3 else st_v
+        wait_all(loads(part))
+        put_part(w_v, part, three_dots(left[0], left[1], r_v[part, 0], r_v[part, 1]))
+        stores += start_all(slot_copies(info, sizes, axis, w_v, slots, out_sem, part))
+    wait_all(tiles)
+    lane = lax.broadcasted_iota(jnp.int32, (8, 256), 1)
+    tile = jnp.where(lane == 3, jnp.sum(valids[...].astype(jnp.float32)), jnp.zeros((8, 256), jnp.float32))
+    for index in range(3):
+        tile = jnp.where(lane == index, n_v[0, 0, index] + n_v[1, 0, index], tile)
+    for index in range(2):
+        tile = jnp.where(lane == 4 + index, n_v[2, 0, index] + n_v[3, 0, index], tile)
+    t_v[...] = tile
+    unit_rows = w_v.shape[3]
+    for by in range(count):
+
+        @pl.when(lax.rem(info[1 + axis] + by, sizes[axis]) == 0)
+        def _():
+            target = slots[by].at[0, 0, 0, pl.ds(unit_rows, 8), pl.ds(0, 256)]
+            copy = pltpu.make_async_copy(t_v, target, in_sem.at[0])
+            copy.start()
+            copy.wait()
+
+    wait_all(stores)
 
 
 def call(body, name, free, inputs, specs, outs, scratch, before, flops, limit):
@@ -587,7 +621,7 @@
     return results[:-1]
 
 
-def backward_back(turn, info, alphas, upstreams, before, sizes, axis):
+def backward_back(info, alphas, upstreams, targets, before, sizes, axis):
     micros, rows, inner = before.shape
     parts = inner // 512
     vmem, dma = pltpu.VMEM, pltpu.SemaphoreType.DMA
@@ -603,12 +637,57 @@
     ]
 
     def body(extra, *refs):
-        back_body(turn, len(slots), sizes, axis, *refs)
-
-    return call(
-        body, "grad_back", 4, [info, alphas] + list(upstreams) + [before], [SCALARS, SCALARS], slots, scratch, None,
-        5 * 10**9, 24,
-    )
+        back_body(len(slots), sizes, axis, *refs)
+
+    inputs = [info, alphas] + list(upstreams) + [targets, before]
+    return call(body, "grad_back", 4, inputs, [SCALARS, SCALARS], slots, scratch, None, 5 * 10**9, 24)
+
+
+def backward_inner(info, middle, befores, sizes, axis):
+    micros, rows, _ = middle.shape
+    vmem, dma = pltpu.VMEM, pltpu.SemaphoreType.DMA
+    f32, bf16 = jnp.float32, jnp.bfloat16
+    slots = slot_structs(sizes, axis)
+    scratch = [
+        vmem(middle.shape, f32),
+        vmem((2, D, micros * rows), bf16),
+        vmem((4, 2, micros * rows, 512), bf16),
+        vmem(unit_shape(sizes), f32),
+        dma((1,)),
+        dma((4, 4)),
+        dma((4, copy_count(sizes, axis))),
+    ]
+
+    def body(extra, *refs):
+        inner_body(len(slots), sizes, axis, *refs)
+
+    return call(body, "grad_inner", 1, [info, middle, befores], [SCALARS], slots, scratch, None, 5 * 10**9, 24)
+
+
+def backward_attention(info, valids, stream, mixed, spreads, firsts, sums, small, sizes, axis):
+    micros, rows, _ = stream.shape
+    vmem, dma = pltpu.VMEM, pltpu.SemaphoreType.DMA
+    f32, bf16 = jnp.float32, jnp.bfloat16
+    slots = slot_structs(sizes, axis, 8)
+    scratch = [
+        vmem(stream.shape, f32),
+        vmem(mixed.shape, f32),
+        vmem((2, D, micros * rows), bf16),
+        vmem((2, D, micros * rows), bf16),
+        vmem((4, 2, micros * rows, 512), bf16),
+        vmem(unit_shape(sizes), f32),
+        vmem((4, 8, 128), f32),
+        vmem((8, 256), f32),
+        dma((4,)),
+        dma((4, 4)),
+        dma((4, copy_count(sizes, axis))),
+    ]
+
+    def body(extra, *refs):
+        attention_body(len(slots), sizes, axis, *refs)
+
+    inputs = [info, valids, stream, mixed, spreads, firsts, sums, small]
+    return call(body, "grad_attention", 2, inputs, [SCALARS, LOCAL], slots, scratch, None, 5 * 10**9, 28)
 
 
 def backward_chain(turn, micro, info, alphas, segments, valids, upstream, before, saved, weights, previous):
@@ -662,60 +741,23 @@
     )
 
 
-def backward_rest(turn, info, valids, middle, stream, mixed, chain, sums, previous, sizes, axes):
-    micros, rows, _ = middle.shape
-    befores, spreads, firsts, _, small = chain
-    vmem, dma = pltpu.VMEM, pltpu.SemaphoreType.DMA
-    f32, bf16 = jnp.float32, jnp.bfloat16
-    slots = [slot_structs(sizes, axes[0]), slot_structs(sizes, axes[1], 8)]
-    scratch = [
-        vmem(middle.shape, f32),
-        vmem(stream.shape, f32),
-        vmem(mixed.shape, f32),
-        vmem((3, 2, D, micros * rows), bf16),
-        vmem((8, 2, micros * rows, 512), bf16),
-        vmem((2,) + unit_shape(sizes), f32),
-        vmem((4, 8, 128), f32),
-        vmem((8, 256), f32),
-        dma((3,)),
-        dma((8, 4)),
-        dma((2, 4, max(copy_count(sizes, axis) for axis in axes))),
-        dma((2,)),
-        dma((1,)),
-    ]
-
-    def body(extra, *refs):
-        rest_body(turn, [len(each) for each in slots], sizes, axes, extra, *refs)
-
-    inputs = [info, valids, middle, stream, mixed, befores, spreads, firsts, sums, small]
-    return call(body, "grad_rest", 2, inputs, [SCALARS, LOCAL], slots[0] + slots[1], scratch, previous, 10**10, 40)
-
-
-def local_call(body, name, who, info, inputs, outs, scratch, previous=None, specs=None):
-    extra = list(previous) if previous is not None else []
+def local_call(body, name, info, inputs, outs, scratch, specs=None):
     inputs = [info, TOKEN[0]] + list(inputs)
 
-    def guarded(*refs):
-        def run():
-            first = len(inputs) + len(extra)
-            body(refs[0], refs[2 : len(inputs)], refs[first : first + len(outs)], refs[first + len(outs) + 1 :])
-
-        if who is None:
-            run()
-        else:
-            pl.when(refs[0][0] == who)(run)
+    def parted(*refs):
+        first = len(inputs)
+        body(refs[0], refs[2:first], refs[first : first + len(outs)], refs[first + len(outs) + 1 :])
 
     results = pl.pallas_call(
-        guarded,
+        parted,
         out_shape=list(outs) + [loose(8, 128)],
-        in_specs=[SCALARS] + [ANY] * (len(inputs) - 1 + len(extra)),
+        in_specs=[SCALARS] + [ANY] * (len(inputs) - 1),
         out_specs=(specs or [ANY] * len(outs)) + [ANY],
         scratch_shapes=scratch,
-        input_output_aliases={len(inputs) + i: i for i in range(len(extra))},
         compiler_params=pltpu.CompilerParams(vmem_limit_bytes=12 * 1024 * 1024),
         cost_estimate=pl.CostEstimate(flops=10**6, bytes_accessed=6 * 10**6, transcendentals=0),
         name=name,
-    )(*inputs, *in_hbm(extra))
+    )(*inputs)
     TOKEN[0] = results[-1]
     return results[:-1]
 
@@ -728,11 +770,12 @@
     return ref.at[(slice(None),) * dims.index(axis) + (index,)]
 
 
-def reduce_stage(sizes, order, step, who, info, arrays):
+def reduce_stage(sizes, order, step, info, arrays):
     shape = arrays[0].shape
     count = len(arrays)
     dims = left_dims(order[:step])
-    if step < len(order):
+    parting = step < len(order) - 1
+    if parting:
         axis = order[step]
         at = dims.index(axis)
         outs = [loose(*shape[:at], *shape[at + 1 :])] * sizes[axis]
@@ -749,16 +792,16 @@
         stores = []
         for by in range(len(outs)):
             source = held.at[0]
-            if step < len(order):
+            if parting:
                 source = picked(source, dims, axis, lax.rem(info[1 + axis] + by, sizes[axis]))
             stores.append(pltpu.make_async_copy(source, outs[by], sem.at[count + by]))
         wait_all(start_all(stores))
 
     scratch = [pltpu.VMEM((count,) + shape, jnp.float32), pltpu.SemaphoreType.DMA((count + len(outs),))]
-    return local_call(body, "reduce_step", who, info, arrays, outs, scratch)
-
-
-def place_stage(sizes, order, step, who, info, arrays):
+    return local_call(body, "reduce_step", info, arrays, outs, scratch)
+
+
+def place_stage(sizes, order, step, info, arrays):
     axis = order[step]
     dims = left_dims(order[:step])
     at = dims.index(axis)
@@ -773,10 +816,10 @@
         wait_all(start_all(copies))
 
     out = loose(*shape[:at], count, *shape[at:])
-    return local_call(body, "place_step", who, info, arrays, [out], [pltpu.SemaphoreType.DMA((count,))])[0]
-
-
-def last_stage(sizes, order, who, info, arrays, kind, previous):
+    return local_call(body, "place_step", info, arrays, [out], [pltpu.SemaphoreType.DMA((count,))])[0]
+
+
+def last_stage(sizes, order, info, arrays, kind):
     x, y, near, far = sizes
     rows = unit_shape(sizes)[3]
     depth = near * far // 4
@@ -829,7 +872,7 @@
             outs[-1][...] = jnp.sqrt(tile[:, 0:3] / (jnp.maximum(tile[:, 3:4], 1.0) * D))
         wait_all(copies)
 
-    return local_call(body, "place_last", who, info, arrays, shapes, scratch, previous, specs)
+    return local_call(body, "place_last", info, arrays, shapes, scratch, specs)
 
 
 def extents(count):
@@ -842,33 +885,34 @@
     return (side, side, near, depth // near)
 
 
-def shifted(value, axis, by, sizes, who=None):
+def shifted(value, axis, by, sizes):
     count = math.prod(sizes)
     stride, length = math.prod(sizes[:axis]), sizes[axis]
     pairs = []
     for chip in range(count):
         along = (chip // stride) % length
         pairs.append((chip, chip + ((along + by) % length - along) * stride))
-    if who is None:
-        return lax.ppermute(value, "dp", pairs)
-    return lax.ppermute(value, ("section", "dp"), [(who * count + a, who * count + b) for a, b in pairs])
-
-
-def summing(slots, order, kind, sizes, info, who=None, previous=None):
+    return lax.ppermute(value, "dp", pairs)
+
+
+def summing(slots, order, kind, sizes, info):
     pieces = list(slots)
-    for step in range(1, len(order) + 1):
+    steps = len(order)
+    for step in range(1, steps + 1):
         axis = order[step - 1]
-        pieces = [pieces[0]] + [shifted(pieces[by], axis, by, sizes, who) for by in range(1, sizes[axis])]
+        pieces = [pieces[0]] + [
+            shifted(pieces[by if step < steps else 0], axis, by, sizes) for by in range(1, sizes[axis])
+        ]
         yield
-        pieces = reduce_stage(sizes, order, step, who, info, pieces)
+        pieces = reduce_stage(sizes, order, step, info, pieces)
     whole = pieces[0]
-    for step in range(len(order) - 1, -1, -1):
+    for step in range(steps - 2, -1, -1):
         axis = order[step]
-        copies = [whole] + [shifted(whole, axis, by, sizes, who) for by in range(1, sizes[axis])]
+        copies = [whole] + [shifted(whole, axis, by, sizes) for by in range(1, sizes[axis])]
         yield
         if step:
-            whole = place_stage(sizes, order, step, who, info, copies)
-    yield last_stage(sizes, order, who, info, copies, kind, previous() if previous else None)
+            whole = place_stage(sizes, order, step, info, copies)
+    yield last_stage(sizes, order, info, copies, kind)
 
 
 def shards(stream_in, cotangent, segment_ids, pad_mask, w_query, w_key, w_value, w_out, w_in, w_back, alphas):
@@ -897,60 +941,33 @@
         )
 
     orders = {"back": (2, 0, 1, 3), "inner": (0, 1, 2, 3), "attention": (1, 2, 0, 3)}
-    first_axes = [orders["inner"][0], orders["attention"][0]]
-
-    def back_step(turn, upstreams):
-        return backward_back(turn, info, alphas, upstreams, saved_p, sizes, orders["back"][0])
-
-    def rest_step(turn, chain, previous):
-        return backward_rest(
-            turn, info, pad_mask, saved_m, saved_s, saved_o, chain[:5], sums, previous, sizes, first_axes
-        )
-
-    late = {}
-    early = summing(back_step(0, [cotangent, cotangent]), orders["back"], "rows", sizes, info, who=1)
-    next(early)
     chain, upstreams = None, []
     for micro in range(2):
         chain = chain_step(0, micro, cotangent, chain)
         upstreams.append(lax.ppermute(chain[5], "section", [(1, 0)]))
         chain = chain[:5]
-        next(early)
-    slots = rest_step(0, chain, None)
-    next(early)
     for micro in range(2):
         chain = chain_step(1, micro, upstreams[micro], chain)[:5]
-    back = summing(
-        back_step(1, upstreams), orders["back"], "rows", sizes, info, who=0, previous=lambda: late["back"]
-    )
+    befores, spreads, firsts, passed, small = chain
+    order = orders["back"]
+    slots = backward_back(info, alphas, upstreams, cotangent, saved_p, sizes, order[0])
+    back = summing(slots, order, "rows", sizes, info)
     next(back)
-    slots = rest_step(1, chain, slots)
-    split_at = sizes[first_axes[0]]
-    inner = summing(slots[:split_at], orders["inner"], "columns", sizes, info)
-    attention = summing(slots[split_at:], orders["attention"], "four", sizes, info)
+    order = orders["inner"]
+    slots = backward_inner(info, saved_m, befores, sizes, order[0])
+    inner = summing(slots, order, "columns", sizes, info)
     next(inner)
+    order = orders["attention"]
+    slots = backward_attention(info, pad_mask, saved_s, saved_o, spreads, firsts, sums, small, sizes, order[0])
+    attention = summing(slots, order, "four", sizes, info)
     next(attention)
-    next(early)
-    next(back)
-    next(early)
-    next(inner)
-    next(attention)
-    next(early)
-    next(back)
-    next(early)
-    next(inner)
-    next(attention)
-    next(back)
-    late["back"] = next(early)
-    for _ in range(5):
-        next(inner)
-        next(attention)
+    for _ in range(7):
         back_out = next(back)
-    inner_out = next(inner)
-    attention_out = next(attention)
+        inner_out = next(inner)
+        attention_out = next(attention)
     return (
         acts[None, :, None],
-        chain[3][None, :, None],
+        passed[None, :, None],
         attention_out[0].reshape(1, D, D),
         attention_out[1].reshape(1, D, D),
         attention_out[2].reshape(1, D, D),

time: 448 us -> 401 us (0.90)
  starting transfers between devices: 58.2 us -> 33.5 us
  Pallas kernels: 151 us -> 134 us
  waiting for transfers between devices: 228 us -> 223 us
    ppermute x16 -> x21, waiting for transfers between devices: 89.7 us -> 193 us  [shifted(): return lax.ppermute(value, 'dp', pairs)]
    ppermute x16 -> x0, waiting for transfers between devices: 103 us -> none  [shifted(): lax.ppermute(value, ('section', 'dp'), [(who * count + a, who * count + b...]
    ppermute x16 -> x0, starting transfers between devices: 33.2 us -> none  [shifted(): lax.ppermute(value, ('section', 'dp'), [(who * count + a, who * count + b...]
    pallas_call x8 -> x7, Pallas kernels: 89.3 us -> 77.9 us  [call(): pl.pallas_call(functools.partial(body, len(extra)), out_shape=outs + [loo...]
    ppermute x16 -> x21, starting transfers between devices: 18.7 us -> 27.3 us  [shifted(): return lax.ppermute(value, 'dp', pairs)]
    pallas_call x32 -> x21, Pallas kernels: 30.8 us -> 24.5 us  [local_call(): pl.pallas_call(parted, out_shape=list(outs) + [loose(8, 128)], in_specs=[...]
    ppermute x2, waiting for transfers between devices: 30.8 us -> 25.3 us  [shards(): upstreams.append(lax.ppermute(chain[5], 'section', [(1, 0)]))]
  transfers between devices with their start and end apart: 36 -> 25, of which waited for: 21 -> 15; matrix products, arithmetic and copies ran while one was open for 0% -> 0% of each run, Pallas kernels for 19% -> 10%
where the time goes in v2:
time: 401 us; the launch traced here: 395 us
  waiting for transfers between devices  223 us (56%)
  Pallas kernels  134 us (33%)
  starting transfers between devices  33.5 us (8%)
    ppermute x21, waiting for transfers between devices, shifted(): return lax.ppermute(value, 'dp', pairs)  193 us
    pallas_call x7, Pallas kernels, call(): pl.pallas_call(functools.partial(body, len(extra)), out_shape=outs + [loo...  77.9 us
    pallas_call x3, Pallas kernels, forward_tick(): pl.pallas_call(functools.partial(forward_body, tick), out_shape=shapes, i...  31.3 us
    ppermute x21, starting transfers between devices, shifted(): return lax.ppermute(value, 'dp', pairs)  27.3 us
    ppermute x2, waiting for transfers between devices, shards(): upstreams.append(lax.ppermute(chain[5], 'section', [(1, 0)]))  25.3 us
    pallas_call x21, Pallas kernels, local_call(): pl.pallas_call(parted, out_shape=list(outs) + [loose(8, 128)], in_specs=[...  24.5 us
  transfers between devices with their start and end apart: 25, of which 15 were waited for; matrix products, arithmetic and copies ran while one was open for 0% of the time, Pallas kernels for 10%

profile of v2, /device:TPU:0, one launch (start us, length us, event | category | flops | bytes accessed | tf_op | source)
XLA Modules:
  0.0 394.5 jit_solution(17367064330876273925)
XLA Ops:
  0.8 0.7 copy-done.4
  1.4 0.7 copy-done.6
  2.1 0.7 copy-done.8
  2.8 15.0 %layer_forward.3 = (f32[2,384,512]{2,1,0:T(8,128)}, f32[384,512]{1,0:T(8,128)}, f32[2,384,512]{2,1,0:T(8,128)}, f32[2,384,512]{2,1,0:T(8,128)}, f32[2,384,512]{2...) custom-call(s32[5]{0:T(128)S(1)} %stack.23.refs_0_, ...), custom_call_target="tpu_custom_call" | custom-call | flops 10000000000 | bytes 20000000 | tf_op jit(solution)/shard_map/layer_forward/pallas_call | solution.py:258
  17.8 1.3 collective-permute-start
  19.1 2.1 collective-permute-done.refs_11_
  21.2 15.5 %layer_forward.4 = (f32[2,384,512]{2,1,0:T(8,128)}, f32[384,512]{1,0:T(8,128)}, f32[2,384,512]{2,1,0:T(8,128)}, f32[2,384,512]{2,1,0:T(8,128)}, f32[2,384,512]{2...) custom-call(s32[5]{0:T(128)S(1)} %stack.23.refs_0_, ...), custom_call_target="tpu_custom_call", output_to_operand_aliasing={{0}: (12, {}), {2}: (13, {}), {3}: (14, {}), {4}: (15, {}),... | custom-call | flops 10000000000 | bytes 20000000 | tf_op jit(solution)/shard_map/layer_forward/pallas_call | solution.py:258
  36.7 2.3 collective-permute-start.1
  39.0 2.1 collective-permute-done.1.refs_11_
  41.1 0.8 layer_forward.5
  42.5 2.2 grad_chain.4
  44.7 1.3 collective-permute-start.3
  46.0 6.8 %grad_chain.5 = (bf16[2,2,384,2048]{3,2,1,0:T(8,128)(2,1)}, bf16[2,2,384,1536]{3,2,1,0:T(8,128)(2,1)}, bf16[2,2,384,512]{3,2,1,0:T(8,128)(2,1)}, f32[2,384,512]{...) custom-call(s32[5]{0:T(128)S(1)} %stack.23.refs_0_, ...), custom_call_target="tpu_custom_call", output_to_operand_aliasing={{0}: (18, {}), {1}: (19, {}), {2}: (20, {}), {3}: (21, {}),... | custom-call | flops 20000000000 | bytes 20000000 | tf_op jit(solution)/shard_map/grad_chain/pallas_call | solution.py:609
  52.7 1.3 collective-permute-start.2
  54.0 23.6 %collective-permute-done.3.refs_4_.refs_2_ = f32[384,512]{1,0:T(8,128)S(1)} collective-permute-done((f32[384,512]{1,0:T(8,128)}, f32[384,512]{1,0:T(8,128)S(1)}, u32[]{:S(2)}, u32[]{:S(2)}) %collective-permute-start.3) | collective-permute-done | bytes 786464 | tf_op jit(solution)/shard_map/ppermute | solution.py:947
  77.7 17.9 %grad_chain.6 = (bf16[2,2,384,2048]{3,2,1,0:T(8,128)(2,1)}, bf16[2,2,384,1536]{3,2,1,0:T(8,128)(2,1)}, bf16[2,2,384,512]{3,2,1,0:T(8,128)(2,1)}, f32[2,384,512]{...) custom-call(s32[5]{0:T(128)S(1)} %stack.23.refs_0_, ...), custom_call_target="tpu_custom_call", output_to_operand_aliasing={{0}: (18, {}), {1}: (19, {}), {2}: (20, {}), {3}: (21, {}),... | custom-call | flops 20000000000 | bytes 20000000 | tf_op jit(solution)/shard_map/grad_chain/pallas_call | solution.py:609
  95.5 1.7 collective-permute-done.2.refs_4_.refs_3_
  97.2 18.0 %grad_chain.7 = (bf16[2,2,384,2048]{3,2,1,0:T(8,128)(2,1)}, bf16[2,2,384,1536]{3,2,1,0:T(8,128)(2,1)}, bf16[2,2,384,512]{3,2,1,0:T(8,128)(2,1)}, f32[2,384,512]{...) custom-call(s32[5]{0:T(128)S(1)} %stack.23.refs_0_, ...), custom_call_target="tpu_custom_call", output_to_operand_aliasing={{0}: (18, {}), {1}: (19, {}), {2}: (20, {}), {3}: (21, {}),... | custom-call | flops 20000000000 | bytes 20000000 | tf_op jit(solution)/shard_map/grad_chain/pallas_call | solution.py:609
  115.2 10.9 %grad_back.1 = (f32[2,2,2,128,512]{4,3,2,1,0:T(8,128)}, f32[2,2,2,128,512]{4,3,2,1,0:T(8,128)}, f32[8,128]{1,0:T(8,128)S(1)}) custom-call(s32[5]{0:T(128)S(1)} %stack.23.refs_0_, f32[1,2]{1,0:T(1,128)S(1)} %copy-done.9, f32[384,512]{1,0:T(8,128)S(1)} %collective-permute-done.3.refs_4_.refs_2_, f32[384,512]{1,0:T(8,128)S(1)} %collective-permute-done.2.refs_4_.refs_3_, ...), custom_call_target="tpu_custom_call" | custom-call | flops 5000000000 | bytes 20000000 | tf_op jit(solution)/shard_map/grad_back/pallas_call | solution.py:609
  126.1 11.1 %grad_inner.1 = (f32[2,2,2,128,512]{4,3,2,1,0:T(8,128)}, f32[2,2,2,128,512]{4,3,2,1,0:T(8,128)}, f32[8,128]{1,0:T(8,128)S(1)}) custom-call(s32[5]{0:T(128)S(1)} %stack.23.refs_0_, f32[2,384,512]{2,1,0:T(8,128)} %get-tuple-element.184.refs_1_, bf16[2,2,384,2048]{3,2,1,0:T(8,128)(2,1)} %get-tuple-element.185.refs_2_, f32[8,128]{1,0:T(8,128)S(1)} %get-tuple-element.187.refs_3_), custom_call_target="tpu_custom_call" | custom-call | flops 5000000000 | bytes 20000000 | tf_op jit(solution)/shard_map/grad_inner/pallas_call | solution.py:609
  137.2 11.1 %grad_attention.1 = (f32[2,2,2,136,512]{4,3,2,1,0:T(8,128)}, f32[2,2,2,136,512]{4,3,2,1,0:T(8,128)}, f32[8,128]{1,0:T(8,128)S(1)}) custom-call(s32[5]{0:T(128)S(1)} %stack.23.refs_0_, s32[2,1,384]{2,1,0:T(1,128)S(1)} %copy-done.7, f32[2,384,512]{2,1,0:T(8,128)} %get-tuple-element.179.refs_2_, f32[2,512,384]{2,1,0:T(8,128)} %get-tuple-element.156.refs_9_.refs_3_, ...), custom_call_target="tpu_custom_call" | custom-call | flops 5000000000 | bytes 20000000 | tf_op jit(solution)/shard_map/grad_attention/pallas_call | solution.py:609
  148.3 3.0 collective-permute-start.6
  151.4 1.6 collective-permute-start.4
  152.9 1.5 collective-permute-start.5
  154.4 40.4 %collective-permute-done.4.refs_3_ = f32[2,2,2,128,512]{4,3,2,1,0:T(8,128)S(1)} collective-permute-done((f32[2,2,2,128,512]{4,3,2,1,0:T(8,128)S(1)}, f32[2,2,2,128,512]{4,3,2,1,0:T(8,128)S(1)}, u32[]{:S(2)}, u32[]{:S(2)}) %collective-permute-start.4) | collective-permute-done | bytes 2097184 | tf_op jit(solution)/shard_map/ppermute | solution.py:895
  194.8 1.4 reduce_step.12
  196.4 1.2 reduce_step.13
  198.1 1.7 reduce_step.14
  199.7 1.6 collective-permute-start.9
  201.4 1.5 collective-permute-start.7
  203.4 18.3 %collective-permute-done.7.refs_3_ = f32[2,2,128,512]{3,2,1,0:T(8,128)S(1)} collective-permute-done((f32[2,2,128,512]{3,2,1,0:T(8,128)S(1)}, f32[2,2,128,512]{3,2,1,0:T(8,128)S(1)}, u32[]{:S(2)}, u32[]{:S(2)}) %collective-permute-start.7) | collective-permute-done | bytes 1048608 | tf_op jit(solution)/shard_map/ppermute | solution.py:895
  221.7 0.9 reduce_step.15
  222.9 0.9 reduce_step.16
  223.8 1.1 reduce_step.17
  224.9 1.3 collective-permute-start.12
  227.2 8.2 %collective-permute-done.10.refs_3_ = f32[2,128,512]{2,1,0:T(8,128)S(1)} collective-permute-done((f32[2,128,512]{2,1,0:T(8,128)S(1)}, f32[2,128,512]{2,1,0:T(8,128)S(1)}, u32[]{:S(2)}, u32[]{:S(2)}) %collective-permute-start.10) | collective-permute-done | bytes 524320 | tf_op jit(solution)/shard_map/ppermute | solution.py:895
  235.4 0.7 reduce_step.18
  236.1 1.9 collective-permute-done.11.refs_3_
  238.0 0.7 reduce_step.19
  238.7 0.9 reduce_step.20
  239.6 4.8 %collective-permute-start.15 = (f32[2,136,512]{2,1,0:T(8,128)S(1)}, f32[2,136,512]{2,1,0:T(8,128)S(1)}, u32[]{:S(2)}, u32[]{:S(2)}) collective-permute-start(f32[2,136,512]{2,1,0:T(8,128)S(1)} %get-tuple-element.221.refs_2_), channel_id=1, source_target_pairs={{0,8},{1,9},{2,10},{3,11},{4,12},{5,13},{6,14},{7,15},{8,0},{9,1},... | collective-permute-start | bytes 1671176 | tf_op jit(solution)/shard_map/ppermute | solution.py:895
  244.5 2.8 collective-permute-start.14
  247.3 48.4 %collective-permute-done.13.refs_3_ = f32[2,128,512]{2,1,0:T(8,128)S(1)} collective-permute-done((f32[2,128,512]{2,1,0:T(8,128)S(1)}, f32[2,128,512]{2,1,0:T(8,128)S(1)}, u32[]{:S(2)}, u32[]{:S(2)}) %collective-permute-start.13) | collective-permute-done | bytes 524320 | tf_op jit(solution)/shard_map/ppermute | solution.py:895
  295.7 0.7 reduce_step.21
  296.4 6.2 %collective-permute-done.14.refs_3_ = f32[2,128,512]{2,1,0:T(8,128)S(1)} collective-permute-done((f32[2,128,512]{2,1,0:T(8,128)S(1)}, f32[2,128,512]{2,1,0:T(8,128)S(1)}, u32[]{:S(2)}, u32[]{:S(2)}) %collective-permute-start.14) | collective-permute-done | bytes 524320 | tf_op jit(solution)/shard_map/ppermute | solution.py:895
  302.6 0.7 reduce_step.22
  303.3 0.9 reduce_step.23
  305.4 8.7 %collective-permute-done.16.refs_3_ = f32[2,128,512]{2,1,0:T(8,128)S(1)} collective-permute-done((f32[2,128,512]{2,1,0:T(8,128)S(1)}, f32[2,128,512]{2,1,0:T(8,128)S(1)}, u32[]{:S(2)}, u32[]{:S(2)}) %collective-permute-start.16) | collective-permute-done | bytes 524320 | tf_op jit(solution)/shard_map/ppermute | solution.py:895
  314.7 0.6 place_step.7
  315.3 0.7 place_step.8
  316.0 2.3 collective-permute-start.21
  318.4 1.4 collective-permute-start.19
  319.8 1.1 collective-permute-start.20
  320.9 19.1 %collective-permute-done.19.refs_3_ = f32[2,2,128,512]{3,2,1,0:T(8,128)S(1)} collective-permute-done((f32[2,2,128,512]{3,2,1,0:T(8,128)S(1)}, f32[2,2,128,512]{3,2,1,0:T(8,128)S(1)}, u32[]{:S(2)}, u32[]{:S(2)}) %collective-permute-start.19) | collective-permute-done | bytes 1048608 | tf_op jit(solution)/shard_map/ppermute | solution.py:895
  340.0 0.7 place_step.9
  340.7 0.8 collective-permute-done.20.refs_3_
  341.5 0.7 place_step.10
  342.2 0.8 place_step.11
  343.1 0.9 collective-permute-start.24
  344.0 0.7 collective-permute-start.23
  344.7 41.1 %collective-permute-done.22.refs_3_ = f32[2,2,2,128,512]{4,3,2,1,0:T(8,128)S(1)} collective-permute-done((f32[2,2,2,128,512]{4,3,2,1,0:T(8,128)S(1)}, f32[2,2,2,128,512]{4,3,2,1,0:T(8,128)S(1)}, u32[]{:S(2)}, u32[]{:S(2)}) %collective-permute-start.22) | collective-permute-done | bytes 2097184 | tf_op jit(solution)/shard_map/ppermute | solution.py:895
  385.9 2.6 place_last.3
  388.5 2.6 place_last.4
  391.2 3.1 place_last.5
  (43 shorter events, 5.0 us)
Async XLA Ops:
  0.8 0.7 copy-start.4
  1.4 0.7 copy-start.6
  2.1 0.7 copy-start.8
  17.8 3.4 collective-permute-start
  36.7 4.4 %collective-permute-start.1 = (f32[384,512]{1,0:T(8,128)}, f32[384,512]{1,0:T(8,128)S(1)}, u32[]{:S(2)}, u32[]{:S(2)}) collective-permute-start(f32[384,512]{1,0:T(8,128)} %get-tuple-element.140), channel_id=1, source_target_pairs={{0,16},{1,17},{2,18},{3,19},{4,20},{5,21},{6,22},{7,23},{8,24},{9,... | collective-permute-start | bytes 2359304 | tf_op jit(solution)/shard_map/ppermute | solution.py:933
  41.1 1.4 copy-start.3
  41.1 1.4 copy-start.5
  41.1 1.4 copy-start.7
  41.1 1.4 copy-start.9
  44.7 33.0 %collective-permute-start.3 = (f32[384,512]{1,0:T(8,128)}, f32[384,512]{1,0:T(8,128)S(1)}, u32[]{:S(2)}, u32[]{:S(2)}) collective-permute-start(f32[384,512]{1,0:T(8,128)} %get-tuple-element.165), channel_id=1, source_target_pairs={{16,0},{17,1},{18,2},{19,3},{20,4},{21,5},{22,6},{23,7},{24,8},{25... | collective-permute-start | bytes 2359304 | tf_op jit(solution)/shard_map/ppermute | solution.py:947
  52.7 44.5 %collective-permute-start.2 = (f32[384,512]{1,0:T(8,128)}, f32[384,512]{1,0:T(8,128)S(1)}, u32[]{:S(2)}, u32[]{:S(2)}) collective-permute-start(f32[384,512]{1,0:T(8,128)} %get-tuple-element.164), channel_id=1, source_target_pairs={{16,0},{17,1},{18,2},{19,3},{20,4},{21,5},{22,6},{23,7},{24,8},{25... | collective-permute-start | bytes 2359304 | tf_op jit(solution)/shard_map/ppermute | solution.py:947
  137.1 14.2 %copy-start.11 = (f32[2,2,2,128,512]{4,3,2,1,0:T(8,128)S(1)}, f32[2,2,2,128,512]{4,3,2,1,0:T(8,128)}, u32[]{:S(2)}) copy-start(f32[2,2,2,128,512]{4,3,2,1,0:T(8,128)} %get-tuple-element.191) | copy-start | bytes 6291460
  137.2 15.8 %copy-start.10 = (f32[2,2,2,128,512]{4,3,2,1,0:T(8,128)S(1)}, f32[2,2,2,128,512]{4,3,2,1,0:T(8,128)}, u32[]{:S(2)}) copy-start(f32[2,2,2,128,512]{4,3,2,1,0:T(8,128)} %get-tuple-element.194) | copy-start | bytes 6291460
  137.2 57.7 %copy-start.2 = (f32[2,2,2,128,512]{4,3,2,1,0:T(8,128)S(1)}, f32[2,2,2,128,512]{4,3,2,1,0:T(8,128)}, u32[]{:S(2)}) copy-start(f32[2,2,2,128,512]{4,3,2,1,0:T(8,128)} %get-tuple-element.190.refs_2_) | copy-start | bytes 6291460
  148.3 49.3 %collective-permute-start.6 = (f32[2,2,2,136,512]{4,3,2,1,0:T(8,128)}, f32[2,2,2,136,512]{4,3,2,1,0:T(8,128)S(1)}, u32[]{:S(2)}, u32[]{:S(2)}) collective-permute-start(f32[2,2,2,136,512]{4,3,2,1,0:T(8,128)} %get-tuple-element.197), channel_id=1, source_target_pairs={{0,2},{1,3},{2,0},{3,1},{4,6},{5,7},{6,4},{7,5},{8,10},{9,11},{10,... | collective-permute-start | bytes 6684680 | tf_op jit(solution)/shard_map/ppermute | solution.py:895
  151.4 43.5 %collective-permute-start.4 = (f32[2,2,2,128,512]{4,3,2,1,0:T(8,128)S(1)}, f32[2,2,2,128,512]{4,3,2,1,0:T(8,128)S(1)}, u32[]{:S(2)}, u32[]{:S(2)}) collective-permute-start(f32[2,2,2,128,512]{4,3,2,1,0:T(8,128)S(1)} %copy-done.11), channel_id=1, source_target_pairs={{0,4},{1,5},{2,6},{3,7},{4,0},{5,1},{6,2},{7,3},{8,12},{9,13},{10,... | collective-permute-start | bytes 6291464 | tf_op jit(solution)/shard_map/ppermute | solution.py:895
  152.9 43.3 %collective-permute-start.5 = (f32[2,2,2,128,512]{4,3,2,1,0:T(8,128)S(1)}, f32[2,2,2,128,512]{4,3,2,1,0:T(8,128)S(1)}, u32[]{:S(2)}, u32[]{:S(2)}) collective-permute-start(f32[2,2,2,128,512]{4,3,2,1,0:T(8,128)S(1)} %copy-done.10), channel_id=1, source_target_pairs={{0,1},{1,0},{2,3},{3,2},{4,5},{5,4},{6,7},{7,6},{8,9},{9,8},{10,11... | collective-permute-start | bytes 6291464 | tf_op jit(solution)/shard_map/ppermute | solution.py:895
  194.8 1.6 copy-start.1
  196.4 1.6 copy-start
  199.7 24.0 %collective-permute-start.9 = (f32[2,2,136,512]{3,2,1,0:T(8,128)S(1)}, f32[2,2,136,512]{3,2,1,0:T(8,128)S(1)}, u32[]{:S(2)}, u32[]{:S(2)}) collective-permute-start(f32[2,2,136,512]{3,2,1,0:T(8,128)S(1)} %get-tuple-element.206), channel_id=1, source_target_pairs={{0,4},{1,5},{2,6},{3,7},{4,0},{5,1},{6,2},{7,3},{8,12},{9,13},{10,... | collective-permute-start | bytes 3342344 | tf_op jit(solution)/shard_map/ppermute | solution.py:895
  201.4 20.3 %collective-permute-start.7 = (f32[2,2,128,512]{3,2,1,0:T(8,128)S(1)}, f32[2,2,128,512]{3,2,1,0:T(8,128)S(1)}, u32[]{:S(2)}, u32[]{:S(2)}) collective-permute-start(f32[2,2,128,512]{3,2,1,0:T(8,128)S(1)} %get-tuple-element.200), channel_id=1, source_target_pairs={{0,1},{1,0},{2,3},{3,2},{4,5},{5,4},{6,7},{7,6},{8,9},{9,8},{10,11... | collective-permute-start | bytes 3145736 | tf_op jit(solution)/shard_map/ppermute | solution.py:895
  202.9 20.0 %collective-permute-start.8 = (f32[2,2,128,512]{3,2,1,0:T(8,128)S(1)}, f32[2,2,128,512]{3,2,1,0:T(8,128)S(1)}, u32[]{:S(2)}, u32[]{:S(2)}) collective-permute-start(f32[2,2,128,512]{3,2,1,0:T(8,128)S(1)} %get-tuple-element.203), channel_id=1, source_target_pairs={{0,2},{1,3},{2,0},{3,1},{4,6},{5,7},{6,4},{7,5},{8,10},{9,11},{10,... | collective-permute-start | bytes 3145736 | tf_op jit(solution)/shard_map/ppermute | solution.py:895
  224.9 13.8 %collective-permute-start.12 = (f32[2,136,512]{2,1,0:T(8,128)S(1)}, f32[2,136,512]{2,1,0:T(8,128)S(1)}, u32[]{:S(2)}, u32[]{:S(2)}) collective-permute-start(f32[2,136,512]{2,1,0:T(8,128)S(1)} %get-tuple-element.215), channel_id=1, source_target_pairs={{0,1},{1,0},{2,3},{3,2},{4,5},{5,4},{6,7},{7,6},{8,9},{9,8},{10,11... | collective-permute-start | bytes 1671176 | tf_op jit(solution)/shard_map/ppermute | solution.py:895
  226.2 9.2 %collective-permute-start.10 = (f32[2,128,512]{2,1,0:T(8,128)S(1)}, f32[2,128,512]{2,1,0:T(8,128)S(1)}, u32[]{:S(2)}, u32[]{:S(2)}) collective-permute-start(f32[2,128,512]{2,1,0:T(8,128)S(1)} %get-tuple-element.209), channel_id=1, source_target_pairs={{0,2},{1,3},{2,0},{3,1},{4,6},{5,7},{6,4},{7,5},{8,10},{9,11},{10,... | collective-permute-start | bytes 1572872 | tf_op jit(solution)/shard_map/ppermute | solution.py:895
  226.7 11.3 %collective-permute-start.11 = (f32[2,128,512]{2,1,0:T(8,128)S(1)}, f32[2,128,512]{2,1,0:T(8,128)S(1)}, u32[]{:S(2)}, u32[]{:S(2)}) collective-permute-start(f32[2,128,512]{2,1,0:T(8,128)S(1)} %get-tuple-element.212), channel_id=1, source_target_pairs={{0,4},{1,5},{2,6},{3,7},{4,0},{5,1},{6,2},{7,3},{8,12},{9,13},{10,... | collective-permute-start | bytes 1572872 | tf_op jit(solution)/shard_map/ppermute | solution.py:895
  239.6 63.7 %collective-permute-start.15 = (f32[2,136,512]{2,1,0:T(8,128)S(1)}, f32[2,136,512]{2,1,0:T(8,128)S(1)}, u32[]{:S(2)}, u32[]{:S(2)}) collective-permute-start(f32[2,136,512]{2,1,0:T(8,128)S(1)} %get-tuple-element.221.refs_2_), channel_id=1, source_target_pairs={{0,8},{1,9},{2,10},{3,11},{4,12},{5,13},{6,14},{7,15},{8,0},{9,1},... | collective-permute-start | bytes 1671176 | tf_op jit(solution)/shard_map/ppermute | solution.py:895
  244.4 51.3 %collective-permute-start.13 = (f32[2,128,512]{2,1,0:T(8,128)S(1)}, f32[2,128,512]{2,1,0:T(8,128)S(1)}, u32[]{:S(2)}, u32[]{:S(2)}) collective-permute-start(f32[2,128,512]{2,1,0:T(8,128)S(1)} %get-tuple-element.217.refs_2_), channel_id=1, source_target_pairs={{0,8},{1,9},{2,10},{3,11},{4,12},{5,13},{6,14},{7,15},{8,0},{9,1},... | collective-permute-start | bytes 1572872 | tf_op jit(solution)/shard_map/ppermute | solution.py:895
  244.5 58.1 %collective-permute-start.14 = (f32[2,128,512]{2,1,0:T(8,128)S(1)}, f32[2,128,512]{2,1,0:T(8,128)S(1)}, u32[]{:S(2)}, u32[]{:S(2)}) collective-permute-start(f32[2,128,512]{2,1,0:T(8,128)S(1)} %get-tuple-element.219.refs_2_), channel_id=1, source_target_pairs={{0,8},{1,9},{2,10},{3,11},{4,12},{5,13},{6,14},{7,15},{8,0},{9,1},... | collective-permute-start | bytes 1572872 | tf_op jit(solution)/shard_map/ppermute | solution.py:895
  304.2 11.1 %collective-permute-start.18 = (f32[2,136,512]{2,1,0:T(8,128)S(1)}, f32[2,136,512]{2,1,0:T(8,128)S(1)}, u32[]{:S(2)}, u32[]{:S(2)}) collective-permute-start(f32[2,136,512]{2,1,0:T(8,128)S(1)} %get-tuple-element.227.refs_2_), channel_id=1, source_target_pairs={{0,1},{1,0},{2,3},{3,2},{4,5},{5,4},{6,7},{7,6},{8,9},{9,8},{10,11... | collective-permute-start | bytes 1671176 | tf_op jit(solution)/shard_map/ppermute | solution.py:895
  304.8 9.2 %collective-permute-start.16 = (f32[2,128,512]{2,1,0:T(8,128)S(1)}, f32[2,128,512]{2,1,0:T(8,128)S(1)}, u32[]{:S(2)}, u32[]{:S(2)}) collective-permute-start(f32[2,128,512]{2,1,0:T(8,128)S(1)} %get-tuple-element.223.refs_2_), channel_id=1, source_target_pairs={{0,2},{1,3},{2,0},{3,1},{4,6},{5,7},{6,4},{7,5},{8,10},{9,11},{10,... | collective-permute-start | bytes 1572872 | tf_op jit(solution)/shard_map/ppermute | solution.py:895
  305.4 9.3 %collective-permute-start.17 = (f32[2,128,512]{2,1,0:T(8,128)S(1)}, f32[2,128,512]{2,1,0:T(8,128)S(1)}, u32[]{:S(2)}, u32[]{:S(2)}) collective-permute-start(f32[2,128,512]{2,1,0:T(8,128)S(1)} %get-tuple-element.225.refs_2_), channel_id=1, source_target_pairs={{0,4},{1,5},{2,6},{3,7},{4,0},{5,1},{6,2},{7,3},{8,12},{9,13},{10,... | collective-permute-start | bytes 1572872 | tf_op jit(solution)/shard_map/ppermute | solution.py:895
  316.0 26.2 %collective-permute-start.21 = (f32[2,2,136,512]{3,2,1,0:T(8,128)S(1)}, f32[2,2,136,512]{3,2,1,0:T(8,128)S(1)}, u32[]{:S(2)}, u32[]{:S(2)}) collective-permute-start(f32[2,2,136,512]{3,2,1,0:T(8,128)S(1)} %get-tuple-element.233.refs_2_), channel_id=1, source_target_pairs={{0,4},{1,5},{2,6},{3,7},{4,0},{5,1},{6,2},{7,3},{8,12},{9,13},{10,... | collective-permute-start | bytes 3342344 | tf_op jit(solution)/shard_map/ppermute | solution.py:895
  318.4 21.6 %collective-permute-start.19 = (f32[2,2,128,512]{3,2,1,0:T(8,128)S(1)}, f32[2,2,128,512]{3,2,1,0:T(8,128)S(1)}, u32[]{:S(2)}, u32[]{:S(2)}) collective-permute-start(f32[2,2,128,512]{3,2,1,0:T(8,128)S(1)} %get-tuple-element.229.refs_2_), channel_id=1, source_target_pairs={{0,1},{1,0},{2,3},{3,2},{4,5},{5,4},{6,7},{7,6},{8,9},{9,8},{10,11... | collective-permute-start | bytes 3145736 | tf_op jit(solution)/shard_map/ppermute | solution.py:895
  319.8 21.7 %collective-permute-start.20 = (f32[2,2,128,512]{3,2,1,0:T(8,128)S(1)}, f32[2,2,128,512]{3,2,1,0:T(8,128)S(1)}, u32[]{:S(2)}, u32[]{:S(2)}) collective-permute-start(f32[2,2,128,512]{3,2,1,0:T(8,128)S(1)} %get-tuple-element.231.refs_2_), channel_id=1, source_target_pairs={{0,2},{1,3},{2,0},{3,1},{4,6},{5,7},{6,4},{7,5},{8,10},{9,11},{10,... | collective-permute-start | bytes 3145736 | tf_op jit(solution)/shard_map/ppermute | solution.py:895
  343.1 48.1 %collective-permute-start.24 = (f32[2,2,2,136,512]{4,3,2,1,0:T(8,128)S(1)}, f32[2,2,2,136,512]{4,3,2,1,0:T(8,128)S(1)}, u32[]{:S(2)}, u32[]{:S(2)}) collective-permute-start(f32[2,2,2,136,512]{4,3,2,1,0:T(8,128)S(1)} %get-tuple-element.239.refs_2_), channel_id=1, source_target_pairs={{0,2},{1,3},{2,0},{3,1},{4,6},{5,7},{6,4},{7,5},{8,10},{9,11},{10,... | collective-permute-start | bytes 6684680 | tf_op jit(solution)/shard_map/ppermute | solution.py:895
  343.9 42.0 %collective-permute-start.22 = (f32[2,2,2,128,512]{4,3,2,1,0:T(8,128)S(1)}, f32[2,2,2,128,512]{4,3,2,1,0:T(8,128)S(1)}, u32[]{:S(2)}, u32[]{:S(2)}) collective-permute-start(f32[2,2,2,128,512]{4,3,2,1,0:T(8,128)S(1)} %get-tuple-element.235.refs_2_), channel_id=1, source_target_pairs={{0,4},{1,5},{2,6},{3,7},{4,0},{5,1},{6,2},{7,3},{8,12},{9,13},{10,... | collective-permute-start | bytes 6291464 | tf_op jit(solution)/shard_map/ppermute | solution.py:895
  344.0 44.5 %collective-permute-start.23 = (f32[2,2,2,128,512]{4,3,2,1,0:T(8,128)S(1)}, f32[2,2,2,128,512]{4,3,2,1,0:T(8,128)S(1)}, u32[]{:S(2)}, u32[]{:S(2)}) collective-permute-start(f32[2,2,2,128,512]{4,3,2,1,0:T(8,128)S(1)} %get-tuple-element.237.refs_2_), channel_id=1, source_target_pairs={{0,1},{1,0},{2,3},{3,2},{4,5},{5,4},{6,7},{7,6},{8,9},{9,8},{10,11... | collective-permute-start | bytes 6291464 | tf_op jit(solution)/shard_map/ppermute | solution.py:895

commit v3 on v2

v3 whole, which is shorter than its diff:
```python
import functools
import math
import jax
import jax.numpy as jnp
from jax import lax
from jax.experimental import pallas as pl
from jax.experimental.pallas import tpu as pltpu
from jax.sharding import PartitionSpec as P

D = 512
HEADS = 8
HEAD_DIM = 64
GELU_A = math.sqrt(2.0 / math.pi)
GELU_B = 0.044715
ORDERS = {"B": "nxyf", "b": "xnyf", "I": "yxnf", "i": "nyxf", "A": "xnyf", "a": "xynf"}
PROGRAM = "|Bb|Bb|IaibBbBAaIaBbiaIbABiIbaiAIAaBiIAaiAIBiAbaIiA"


TOKEN = [None]


def start_all(copies):
    for copy in copies:
        copy.start()
    return copies


def wait_all(copies):
    for copy in copies:
        copy.wait()


def split(value):
    high = value.astype(jnp.bfloat16)
    low = (value - high.astype(jnp.float32)).astype(jnp.bfloat16)
    return (high, low)


def stacked(value):
    return jnp.concatenate(split(value), axis=0)


def dot(left_side, right_side):
    return jnp.dot(left_side, right_side, preferred_element_type=jnp.float32)


def dot_rows(left_side, right_side):
    return lax.dot_general(
        left_side, right_side, (((1,), (1,)), ((), ())), preferred_element_type=jnp.float32
    )


def folded(product):
    half = product.shape[0] // 2
    return product[:half] + product[half:]


def put_split(target, value):
    high, low = split(value)
    target[0] = high
    target[1] = low


def two_dots(left_side, right_side):
    return dot(left_side[0], right_side) + dot(left_side[1], right_side)


def gelu_inner(value):
    return jnp.tanh(GELU_A * (value + GELU_B * (value * value * value)))


def tile_of(numbers):
    lane = lax.broadcasted_iota(jnp.int32, (8, 128), 1)
    tile = jnp.zeros((8, 128), jnp.float32)
    for index, number in enumerate(numbers):
        tile = jnp.where(lane == index, number, tile)
    return tile


def fill_bias(bias_ref, segment_row, valid_row):
    blocks = segment_row.shape[1] // 128
    segment_col = jnp.broadcast_to(segment_row, (128, segment_row.shape[1])).T
    valid_col = jnp.broadcast_to(valid_row, (128, valid_row.shape[1])).T
    for kb in range(blocks):
        ks = slice(kb * 128, kb * 128 + 128)
        for qb in range(kb, blocks):
            qs = slice(qb * 128, qb * 128 + 128)
            k_place = lax.broadcasted_iota(jnp.int32, (128, 128), 0) + kb * 128
            q_place = lax.broadcasted_iota(jnp.int32, (128, 128), 1) + qb * 128
            allowed = (segment_col[ks] == segment_row[:, qs]) & (k_place <= q_place)
            allowed = allowed & ((valid_col[ks] > 0) | (k_place == q_place))
            bias_ref[ks, qs] = jnp.where(allowed, 0.0, -1e30)


def halves_of(value):
    lane = lax.broadcasted_iota(jnp.int32, value.shape, 1)
    zero = jnp.zeros_like(value)
    return (jnp.where(lane < HEAD_DIM, value, zero), jnp.where(lane < HEAD_DIM, zero, value))


def pair_scores(keys_cat, queries_high, queries_low):
    sides = []
    for high, low in zip(halves_of(queries_high), halves_of(queries_low)):
        sides.append(jnp.concatenate([high, high, low], axis=1))
    return dot_rows(keys_cat, jnp.concatenate(sides, axis=0))


def three_lanes(value):
    high, low = split(value)
    return jnp.concatenate([high, low, high], axis=1)


def fetch_rows(alphas, segments, valids, alphas_s, rows_v, sem):
    return start_all(
        [
            pltpu.make_async_copy(alphas, alphas_s, sem.at[0]),
            pltpu.make_async_copy(segments, rows_v.at[0], sem.at[1]),
            pltpu.make_async_copy(valids, rows_v.at[1], sem.at[2]),
        ]
    )


def forward_body(tick, *refs):
    (info, alphas, segments, valids, streams, wq, wk, wv, wo, wi, wb) = refs[:11]
    received = streams.at[0, 0] if tick == 0 else refs[12]
    refs = refs[12 + (0 if tick == 0 else 11) :]
    (acts, sent, saved_s, saved_q, saved_k, saved_v, saved_o, saved_l, saved_m, saved_p, sums, _) = refs[:12]
    (s_v, wq_v, wk_v, wv_v, wo_v, wi_v, wb_v, q_v, k_v, v_v, ot_v, l_v, m_v, p_v, a_v, t_v, bias_v, x_v, alphas_s, rows_v, in_sem, out_sem, row_sem) = refs[12:]
    section = info[0]
    micro = tick - section
    rows = s_v.shape[0]
    blocks = rows // 128
    parts = wi_v.shape[1] // 512

    @pl.when((micro >= 0) & (micro < 2))
    def _():
        pairs = [(wq, wq_v), (wk, wk_v), (wv, wv_v), (wo, wo_v), (wi, wi_v), (wb, wb_v)]
        loads = [pltpu.make_async_copy(a, b, in_sem.at[i]) for i, (a, b) in enumerate(pairs)]

        @pl.when(section == 0)
        def _():
            pltpu.make_async_copy(streams.at[micro, 0], s_v, in_sem.at[6]).start()

        @pl.when(section != 0)
        def _():
            pltpu.make_async_copy(received, s_v, in_sem.at[6]).start()

        loads[0].start()
        small = fetch_rows(alphas, segments, valids, alphas_s, rows_v, row_sem)
        pltpu.make_async_copy(received, s_v, in_sem.at[6]).wait()
        start_all(loads[1:])
        put_split(x_v, s_v[...])
        for index, (weight, target) in enumerate(((wq_v, q_v), (wk_v, k_v), (wv_v, v_v))):
            loads[index].wait()
            value = two_dots(x_v, weight[...])
            target[...] = value * 0.125 if index == 0 else value
        wait_all(small)
        segment_row = rows_v[0, micro].astype(jnp.float32)
        valid_row = rows_v[1, micro].astype(jnp.float32)
        fill_bias(bias_v, segment_row, valid_row)

        stores = []

        def store(source, target):
            copy = pltpu.make_async_copy(source, target, out_sem.at[len(stores)])
            copy.start()
            stores.append(copy)

        store(s_v, saved_s.at[micro])
        store(q_v, saved_q.at[micro])
        store(k_v, saved_k.at[micro])
        store(v_v, saved_v.at[micro])
        made = {}

        def scores_of(pair, qb):
            lanes = pl.ds(pair * 128, 128)
            if pair not in made:
                made.clear()
                made[pair] = (three_lanes(k_v[:, lanes]), split(q_v[:, lanes]), split(v_v[:, lanes].T))
            keys_cat, queries, values = made[pair]
            qs = slice(qb * 128, qb * 128 + 128)
            return pair_scores(keys_cat[: (qb + 1) * 128], queries[0][qs], queries[1][qs]), values

        units = [(pair, qb) for pair in range(HEADS // 2) for qb in range(blocks)]
        ahead = scores_of(*units[0])
        for index, (pair, qb) in enumerate(units):
            scores, (values_high, values_low) = ahead
            if index + 1 < len(units):
                ahead = scores_of(*units[index + 1])
            qs = slice(qb * 128, qb * 128 + 128)
            ks = (qb + 1) * 128
            bias = bias_v[:ks, qs]
            for head in range(2):
                part = scores[:, head * 128 : head * 128 + 128] + bias
                top = jnp.max(part, axis=0, keepdims=True)
                probs = jnp.exp(part - top)
                total = jnp.sum(probs, axis=0, keepdims=True)
                high, low = split(probs)
                hs = slice(head * HEAD_DIM, head * HEAD_DIM + HEAD_DIM)
                both = jnp.concatenate([values_high[hs, :ks], values_low[hs, :ks]], axis=0)
                mixed = folded(dot(both, high)) + dot(values_high[hs, :ks], low)
                at = slice(pair * 128 + head * HEAD_DIM, pair * 128 + head * HEAD_DIM + HEAD_DIM)
                ot_v[at, qs] = mixed / total
                l_v[pair, head : head + 1, qs] = top + jnp.log(total)
        store(ot_v, saved_o.at[micro])
        store(l_v, saved_l.at[micro])
        put_split(x_v, ot_v[...].T)
        loads[3].wait()
        attn = two_dots(x_v, wo_v[...]) * alphas_s[0, 0]
        valid_col = jnp.broadcast_to(valid_row, (128, rows)).T
        weighting = jnp.concatenate([valid_col] * (D // 128), axis=1)
        attn_sum = jnp.sum(attn * attn * weighting)
        middle = s_v[...] + attn
        m_v[...] = middle
        store(m_v, saved_m.at[micro])
        put_split(x_v, middle)
        loads[4].wait()

        def before_of(part):
            return two_dots(x_v, wi_v[:, part * 512 : part * 512 + 512])

        ahead = before_of(0)
        loads[5].wait()
        for part in range(parts):
            cols = slice(part * 512, part * 512 + 512)
            before = ahead
            p_v[:, cols] = before
            store(p_v.at[:, pl.ds(part * 512, 512)], saved_p.at[micro, :, pl.ds(part * 512, 512)])
            if part + 1 < parts:
                ahead = before_of(part + 1)
            high, low = split(0.5 * before * (1.0 + gelu_inner(before)))
            more = dot(high, wb_v[cols, :]) + dot(low, wb_v[cols, :])
            a_v[...] = a_v[...] + more if part else more
        ffn = a_v[...] * alphas_s[0, 1]
        result = m_v[...] + ffn
        a_v[...] = result
        store(a_v, sent)
        store(a_v, acts.at[micro])
        t_v[...] = tile_of([jnp.sum(result * result * weighting), attn_sum, jnp.sum(ffn * ffn * weighting)])
        store(t_v, sums.at[micro])
        wait_all(stores)


def struct(*shape):
    return pltpu.HBM(shape, jnp.float32)


def loose(*shape):
    return jax.ShapeDtypeStruct(shape, jnp.float32)


def in_hbm(arrays):
    return [pltpu.with_memory_space_constraint(array, pltpu.HBM) for array in arrays]


ANY = pl.BlockSpec(memory_space=pl.ANY)
SCALARS = pl.BlockSpec(memory_space=pltpu.SMEM)
LOCAL = pl.BlockSpec(memory_space=pltpu.VMEM)


def forward_tick(tick, info, alphas, segments, valids, streams, received, weights, state):
    micro_count, _, rows, width = streams.shape
    inner = weights[4].shape[1]
    whole = struct(micro_count, rows, width)
    shapes = [
        whole,
        struct(rows, width),
        whole,
        whole,
        whole,
        whole,
        struct(micro_count, width, rows),
        struct(micro_count, HEADS // 2, 8, rows),
        whole,
        struct(micro_count, rows, inner),
        struct(micro_count, 8, 128),
        loose(8, 128),
    ]
    kept = [0, 2, 3, 4, 5, 6, 7, 8, 9, 10]
    extra = [] if state is None else [received] + in_hbm(state)
    aliases = {} if state is None else {13 + i: out for i, out in enumerate(kept)}
    f32, bf16 = jnp.float32, jnp.bfloat16
    vmem, dma = pltpu.VMEM, pltpu.SemaphoreType.DMA
    scratch = [vmem((rows, width), f32)] + [vmem(w.shape, bf16) for w in weights]
    scratch += [vmem((rows, width), f32)] * 3 + [vmem((width, rows), f32), vmem((HEADS // 2, 8, rows), f32)]
    scratch += [vmem((rows, width), f32), vmem((rows, inner), f32), vmem((rows, width), f32)]
    scratch += [vmem((8, 128), f32), vmem((rows, rows), f32), vmem((2, rows, width), bf16)]
    scratch += [pltpu.SMEM(alphas.shape, f32), vmem((2,) + segments.shape, jnp.int32)]
    scratch += [dma((7,)), dma((10 + inner // 512,)), dma((3,))]
    outs = pl.pallas_call(
        functools.partial(forward_body, tick),
        out_shape=shapes,
        in_specs=[SCALARS] + [ANY] * (11 + len(extra)),
        out_specs=[ANY] * len(shapes),
        scratch_shapes=scratch,
        input_output_aliases=aliases,
        compiler_params=pltpu.CompilerParams(vmem_limit_bytes=28 * 1024 * 1024),
        cost_estimate=pl.CostEstimate(flops=10**10, bytes_accessed=2 * 10**7, transcendentals=10**6),
        name="layer_forward",
    )(info, *in_hbm([alphas, segments, valids, streams, *weights]), TOKEN[0], *extra)
    TOKEN[0] = outs[-1]
    return (outs[1], [outs[i] for i in kept])


def unit_shape(sizes):
    x, y, near, far = sizes
    return (near * far, y, x, 4 * D // (x * y * near * far), D)


def slot_structs(sizes, axes, more=0):
    x, y, near, far = sizes
    structs = []
    for axis in axes:
        shape = [size for index, size in ((3, far), (2, near), (1, y), (0, x)) if index != axis]
        structs += [struct(*shape, unit_shape(sizes)[3] + (0 if structs else more), D // len(axes))] * sizes[axis]
    return structs


def put_part(unit, part, value):
    depth = unit.shape[0] // 4
    unit[pl.ds(part * depth, depth)] = value.reshape((depth,) + unit.shape[1:])


def slot_copies(info, sizes, axes, unit, slots, sems, part):
    x, y, near, far = sizes
    depth, rows = near * far // 4, unit.shape[3]
    copies, first = [], 0
    for half, axis in enumerate(axes):
        lanes = pl.ds(half * (D // len(axes)), D // len(axes))
        for by in range(sizes[axis]):
            place = lax.rem(info[1 + axis] + by, sizes[axis])
            slot = slots[first + by]
            if axis == 2:
                pairs = [
                    (unit.at[at * near + place, :, :, :, lanes], slot.at[at, :, :, pl.ds(0, rows)])
                    for at in range(far)
                    if part * depth < (at + 1) * near <= (part + 1) * depth
                ]
            else:
                pairs = []
                for at in range(part * depth, (part + 1) * depth):
                    source = unit.at[at, :, place, :, lanes] if axis == 0 else unit.at[at, place, :, :, lanes]
                    pairs.append((source, slot.at[at // near, at % near, :, pl.ds(0, rows)]))
            for source, target in pairs:
                copies.append(pltpu.make_async_copy(source, target, sems.at[part, len(copies)]))
        first += sizes[axis]
    return copies


def copy_count(sizes, axes):
    return sum(sizes[axis] for axis in axes) * max(1, sizes[2] * sizes[3] // 4)


def three_dots(left_high, left_low, right_high, right_low):
    return dot(left_high, right_high) + dot(left_low, right_high) + dot(left_high, right_low)


def back_body(count, sizes, axes, *refs):
    info, alphas = refs[:2]
    upstreams, targets, saved_p = refs[2:4], refs[4], refs[5]
    slots, refs = refs[7 : 7 + count], refs[8 + count :]
    g_v, gh_v, p_v, w_v, in_sem, out_sem = refs
    parts = p_v.shape[0]
    rows = g_v.shape[1]

    def load(part, micro):
        cols = pl.ds(part * 512, 512)
        return pltpu.make_async_copy(
            saved_p.at[micro, :, cols], p_v.at[part, pl.ds(micro * rows, rows)], in_sem.at[part, micro]
        )

    for micro in range(2):

        @pl.when(info[0] == 0)
        def _():
            pltpu.make_async_copy(upstreams[micro], g_v.at[micro], in_sem.at[parts, micro]).start()

        @pl.when(info[0] != 0)
        def _():
            pltpu.make_async_copy(targets.at[micro, 0], g_v.at[micro], in_sem.at[parts, micro]).start()

    start_all([load(0, micro) for micro in range(2)])
    for micro in range(2):
        pltpu.make_async_copy(targets.at[micro, 0], g_v.at[micro], in_sem.at[parts, micro]).wait()
    for part in range(1, parts):
        start_all([load(part, micro) for micro in range(2)])
    high, low = split(jnp.concatenate([g_v[0], g_v[1]], axis=0) * alphas[0, 1])
    gh_v[0] = high
    gh_v[1] = low

    def left_of(part):
        for micro in range(2):
            load(part, micro).wait()
        before = p_v[part].T
        return split(0.5 * before * (1.0 + gelu_inner(before)))

    stores = []
    ahead = left_of(0)
    for part in range(parts):
        high, low = ahead
        if part + 1 < parts:
            ahead = left_of(part + 1)
        put_part(w_v, part, three_dots(high, low, gh_v[0], gh_v[1]))
        stores += start_all(slot_copies(info, sizes, axes, w_v, slots, out_sem, part))
    wait_all(stores)


def chain_body(tick, extra, *refs):
    info, received = refs[:2]
    alphas, segments, valids, targets, saved_p = refs[2:7]
    sources = refs[7:12]
    wi, wb = refs[12:14]
    weights = refs[14:18]
    refs = refs[19 + extra :]
    (befores, spreads, firsts, passed, small, sent, _) = refs[:7]
    (g_v, p_v, wi_v, wb_v, gs_v, d_v, b_v) = refs[7:14]
    held = refs[14:19]
    weights_v = refs[19:23]
    (bias_v, do_v, dt_v, dl_v, qt_v, dk_v, dv_v, x_v, f_v, y_v, t_v, alphas_s, rows_v, in_sem, part_sem, w_sem, out_sem, row_sem) = refs[23:]
    parts = p_v.shape[0]
    rows = bias_v.shape[0]
    blocks = rows // 128
    (q_v, k_v, v_v, o_v, l_v) = held
    (wq_v, wk_v, wv_v, wo_v) = weights_v
    section = info[0]
    micro = tick - (1 - section)

    @pl.when((micro >= 0) & (micro < 2))
    def _():
        def loads(part):
            cols = pl.ds(part * 512, 512)
            return [
                pltpu.make_async_copy(wb.at[cols], wb_v.at[part], part_sem.at[part, 0]),
                pltpu.make_async_copy(saved_p.at[micro, :, cols], p_v.at[part], part_sem.at[part, 1]),
                pltpu.make_async_copy(wi.at[:, cols], wi_v.at[part], part_sem.at[part, 2]),
            ]

        @pl.when(section == 0)
        def _():
            pltpu.make_async_copy(received if tick else targets.at[micro, 0], g_v, in_sem.at[5]).start()

        @pl.when(section != 0)
        def _():
            pltpu.make_async_copy(targets.at[micro, 0], g_v, in_sem.at[5]).start()

        rows_in = fetch_rows(alphas, segments, valids, alphas_s, rows_v, row_sem)
        start_all(loads(0))
        fetches = [pltpu.make_async_copy(a, b, w_sem.at[i]) for i, (a, b) in enumerate(zip(weights, weights_v))]
        later = [pltpu.make_async_copy(a.at[micro], b, in_sem.at[i]) for i, (a, b) in enumerate(zip(sources, held))]
        wait_all(rows_in)
        segment_row = rows_v[0, micro].astype(jnp.float32)
        valid_row = rows_v[1, micro].astype(jnp.float32)
        fill_bias(bias_v, segment_row, valid_row)
        pltpu.make_async_copy(targets.at[micro, 0], g_v, in_sem.at[5]).wait()
        for part in range(1, parts):
            start_all(loads(part))
        start_all(fetches[::-1])
        start_all(later)
        gs_v[...] = stacked(g_v[...] * alphas_s[0, 1])

        def hidden_of(part):
            wait_all(loads(part))
            return folded(dot_rows(gs_v[...], wb_v[part]))

        total_inner = jnp.float32(0.0)
        ahead = hidden_of(0)
        for part in range(parts):
            cols = slice(part * 512, part * 512 + 512)
            grad_hidden = ahead
            if part + 1 < parts:
                ahead = hidden_of(part + 1)
            before = p_v[part]
            inner = gelu_inner(before)
            above = 0.5 * (1.0 + inner)
            total_inner = total_inner + jnp.sum(grad_hidden * (before * above))
            slope = above + 0.5 * before * (1.0 - inner * inner) * (GELU_A * (1.0 + 3.0 * GELU_B * (before * before)))
            high, low = split(grad_hidden * slope)
            b_v[0, :, cols] = high
            b_v[1, :, cols] = low
            more = folded(dot_rows(jnp.concatenate([high, low], axis=0), wi_v[part]))
            d_v[...] = d_v[...] + more if part else more
        stores = start_all([pltpu.make_async_copy(b_v, befores.at[micro], out_sem.at[0])])
        middle = g_v[...] + d_v[...]
        d_v[...] = middle
        high, low = split(middle * alphas_s[0, 0])
        f_v[0] = high
        f_v[1] = low
        stores += start_all([pltpu.make_async_copy(f_v, firsts.at[micro], out_sem.at[1])])
        wait_all(fetches)
        wait_all(later)
        grad_mixed = folded(dot_rows(jnp.concatenate([high, low], axis=0), wo_v[...]))
        do_v[...] = grad_mixed
        dt_v[...] = grad_mixed.T
        total_mixed = jnp.float32(0.0)
        for head in range(HEADS):
            hs = slice(head * HEAD_DIM, head * HEAD_DIM + HEAD_DIM)
            spread = jnp.sum(dt_v[hs, :] * o_v[hs, :], axis=0, keepdims=True)
            dl_v[head // 2, head % 2 : head % 2 + 1, :] = spread
            total_mixed = total_mixed + jnp.sum(spread)

        made = {}

        def products_of(pair, qb):
            lanes = slice(pair * 128, pair * 128 + 128)
            if pair not in made:
                made.clear()
                keys = k_v[:, lanes]
                made[pair] = (
                    three_lanes(keys),
                    three_lanes(v_v[:, lanes]),
                    split(q_v[:, lanes]),
                    split(do_v[:, lanes]),
                    split(keys.T),
                )
            keys_cat, values_cat, queries, mixed, turned = made[pair]
            qs = slice(qb * 128, qb * 128 + 128)
            ks = (qb + 1) * 128
            scores = pair_scores(keys_cat[:ks], queries[0][qs], queries[1][qs])
            slopes = pair_scores(values_cat[:ks], mixed[0][qs], mixed[1][qs])
            return scores, slopes, queries, mixed, turned

        def product(left_high, left_low, right_high, right_low):
            left_cat = jnp.concatenate([left_high, left_low], axis=1)
            above = jnp.concatenate([right_high, right_low], axis=1)
            below = jnp.concatenate([right_high, jnp.zeros_like(right_high)], axis=1)
            value = dot(left_cat, jnp.concatenate([above, below], axis=0))
            return value[:, :128] + value[:, 128:]

        units = [(pair, qb) for pair in range(HEADS // 2) for qb in range(blocks - 1, -1, -1)]
        for pair, qb in units:
            scores, slopes, queries, mixed, turned = products_of(pair, qb)
            lanes = slice(pair * 128, pair * 128 + 128)
            qs = slice(qb * 128, qb * 128 + 128)
            ks = (qb + 1) * 128
            bias = bias_v[:ks, qs]
            sides = [halves_of(x[qs]) for x in queries + mixed]
            key_part, value_part = None, None
            for head in range(2):
                own = slice(head * 128, head * 128 + 128)
                at = slice(head, head + 1)
                probs = jnp.exp((scores[:, own] + bias) - l_v[pair, at, qs])
                grads = probs * (slopes[:, own] - dl_v[pair, at, qs])
                q_high, q_low, d_high, d_low = [side[head] for side in sides]
                from_values = product(*split(probs), d_high, d_low)
                high, low = split(grads)
                from_keys = product(high, low, q_high, q_low)
                value_part = from_values if head == 0 else value_part + from_values
                key_part = from_keys if head == 0 else key_part + from_keys
                hs = slice(head * HEAD_DIM, head * HEAD_DIM + HEAD_DIM)
                both = jnp.concatenate([turned[0][hs, :ks], turned[1][hs, :ks]], axis=0)
                back = folded(dot(both, high)) + dot(turned[0][hs, :ks], low)
                qt_v[pair * 128 + head * HEAD_DIM : pair * 128 + head * HEAD_DIM + HEAD_DIM, qs] = back * 0.125
            if qb == blocks - 1:
                dk_v[:, lanes] = key_part
                dv_v[:, lanes] = value_part
            else:
                dk_v[:ks, lanes] += key_part
                dv_v[:ks, lanes] += value_part
        result = d_v[...]
        for index, (source, weight) in enumerate(((qt_v, wq_v), (dk_v, wk_v), (dv_v, wv_v))):
            value = source[...].T if index == 0 else source[...]
            high, low = split(value)
            x_v[0, :, pl.ds(index * D, D)] = high
            x_v[1, :, pl.ds(index * D, D)] = low
            result = result + folded(dot_rows(jnp.concatenate([high, low], axis=0), weight[...]))
        y_v[...] = result
        t_v[...] = tile_of([total_mixed / alphas_s[0, 0], total_inner / alphas_s[0, 1]])
        stores += start_all(
            [
                pltpu.make_async_copy(y_v, sent, out_sem.at[2]),
                pltpu.make_async_copy(y_v, passed.at[micro], out_sem.at[3]),
                pltpu.make_async_copy(x_v, spreads.at[micro], out_sem.at[4]),
                pltpu.make_async_copy(t_v, small.at[micro], out_sem.at[5]),
            ]
        )
        wait_all(stores)


def inner_body(count, sizes, axes, *refs):
    info, saved_m, befores = refs[:3]
    slots, refs = refs[4 : 4 + count], refs[5 + count :]
    m_v, lt_v, r_v, w_v, in_sem, r_sem, out_sem = refs
    rows = m_v.shape[1]

    def loads(part):
        copies = []
        for micro in range(2):
            for half in range(2):
                source = befores.at[micro, half, :, pl.ds(part * 512, 512)]
                target = r_v.at[part, half, pl.ds(micro * rows, rows)]
                copies.append(pltpu.make_async_copy(source, target, r_sem.at[part, len(copies)]))
        return copies

    first = pltpu.make_async_copy(saved_m, m_v, in_sem.at[0])
    first.start()
    start_all(loads(0))
    first.wait()
    for part in range(1, 4):
        start_all(loads(part))
    turn_left(lt_v, m_v, True)
    stores = []
    for part in range(4):
        wait_all(loads(part))
        put_part(w_v, part, three_dots(lt_v[0], lt_v[1], r_v[part, 0], r_v[part, 1]))
        stores += start_all(slot_copies(info, sizes, axes, w_v, slots, out_sem, part))
    wait_all(stores)


def turn_left(target, source, transpose):
    rows = target.shape[2] // 2
    for micro in range(2):
        high, low = split(source[micro].T if transpose else source[micro])
        target[0, :, micro * rows : (micro + 1) * rows] = high
        target[1, :, micro * rows : (micro + 1) * rows] = low


def attention_body(count, sizes, axes, *refs):
    info, valids, saved_s, saved_o, spreads, firsts, sums, small = refs[:8]
    slots, refs = refs[9 : 9 + count], refs[10 + count :]
    (s_v, o_v, st_v, lo_v, r_v, w_v, n_v, t_v, in_sem, r_sem, out_sem) = refs
    rows = s_v.shape[1]

    def loads(part):
        copies = []
        for micro in range(2):
            for half in range(2):
                if part < 3:
                    source = spreads.at[micro, half, :, pl.ds(part * 512, 512)]
                else:
                    source = firsts.at[micro, half]
                target = r_v.at[part, half, pl.ds(micro * rows, rows)]
                copies.append(pltpu.make_async_copy(source, target, r_sem.at[part, micro * 2 + half]))
        return copies

    lefts = [pltpu.make_async_copy(saved_s, s_v, in_sem.at[0]), pltpu.make_async_copy(saved_o, o_v, in_sem.at[1])]
    tiles = [
        pltpu.make_async_copy(sums, n_v.at[pl.ds(0, 2)], in_sem.at[2]),
        pltpu.make_async_copy(small, n_v.at[pl.ds(2, 2)], in_sem.at[3]),
    ]
    lefts[0].start()
    start_all(loads(0))
    lefts[0].wait()
    for part in range(1, 4):
        start_all(loads(part))
    start_all(lefts[1:] + tiles)
    turn_left(st_v, s_v, True)
    stores = []
    for part in range(4):
        if part == 3:
            lefts[1].wait()
            turn_left(lo_v, o_v, False)
        left = lo_v if part == 3 else st_v
        wait_all(loads(part))
        put_part(w_v, part, three_dots(left[0], left[1], r_v[part, 0], r_v[part, 1]))
        stores += start_all(slot_copies(info, sizes, axes, w_v, slots, out_sem, part))
    wait_all(tiles)
    lane = lax.broadcasted_iota(jnp.int32, (8, 256), 1)
    tile = jnp.where(lane == 3, jnp.sum(valids[...].astype(jnp.float32)), jnp.zeros((8, 256), jnp.float32))
    for index in range(3):
        tile = jnp.where(lane == index, n_v[0, 0, index] + n_v[1, 0, index], tile)
    for index in range(2):
        tile = jnp.where(lane == 4 + index, n_v[2, 0, index] + n_v[3, 0, index], tile)
    t_v[...] = tile
    unit_rows = w_v.shape[3]
    axis = axes[0]
    for by in range(sizes[axis]):

        @pl.when(lax.rem(info[1 + axis] + by, sizes[axis]) == 0)
        def _():
            target = slots[by].at[0, 0, 0, pl.ds(unit_rows, 8), pl.ds(0, 256)]
            copy = pltpu.make_async_copy(t_v, target, in_sem.at[0])
            copy.start()
            copy.wait()

    wait_all(stores)


def call(body, name, free, inputs, specs, outs, scratch, before, flops, limit):
    extra = list(before) if before is not None else []
    inputs = list(inputs[:free]) + in_hbm(list(inputs[free:])) + [TOKEN[0]]
    results = pl.pallas_call(
        functools.partial(body, len(extra)),
        out_shape=outs + [loose(8, 128)],
        in_specs=specs + [ANY] * (len(inputs) - len(specs) + len(extra)),
        out_specs=[ANY] * (len(outs) + 1),
        scratch_shapes=scratch,
        input_output_aliases={len(inputs) + i: i for i in range(len(extra))},
        compiler_params=pltpu.CompilerParams(vmem_limit_bytes=limit * 1024 * 1024),
        cost_estimate=pl.CostEstimate(flops=flops, bytes_accessed=2 * 10**7, transcendentals=10**6),
        name=name,
    )(*inputs, *in_hbm(extra))
    TOKEN[0] = results[-1]
    return results[:-1]


def backward_back(info, alphas, upstreams, targets, before, sizes, axes):
    micros, rows, inner = before.shape
    parts = inner // 512
    vmem, dma = pltpu.VMEM, pltpu.SemaphoreType.DMA
    f32, bf16 = jnp.float32, jnp.bfloat16
    slots = slot_structs(sizes, axes)
    scratch = [
        vmem((micros, rows, D), f32),
        vmem((2, micros * rows, D), bf16),
        vmem((parts, micros * rows, 512), f32),
        vmem(unit_shape(sizes), f32),
        dma((parts + 1, 2)),
        dma((parts, copy_count(sizes, axes))),
    ]

    def body(extra, *refs):
        back_body(len(slots), sizes, axes, *refs)

    inputs = [info, alphas] + list(upstreams) + [targets, before]
    return call(body, "grad_back", 4, inputs, [SCALARS, SCALARS], slots, scratch, None, 5 * 10**9, 24)


def backward_inner(info, middle, befores, sizes, axes):
    micros, rows, _ = middle.shape
    vmem, dma = pltpu.VMEM, pltpu.SemaphoreType.DMA
    f32, bf16 = jnp.float32, jnp.bfloat16
    slots = slot_structs(sizes, axes)
    scratch = [
        vmem(middle.shape, f32),
        vmem((2, D, micros * rows), bf16),
        vmem((4, 2, micros * rows, 512), bf16),
        vmem(unit_shape(sizes), f32),
        dma((1,)),
        dma((4, 4)),
        dma((4, copy_count(sizes, axes))),
    ]

    def body(extra, *refs):
        inner_body(len(slots), sizes, axes, *refs)

    return call(body, "grad_inner", 1, [info, middle, befores], [SCALARS], slots, scratch, None, 5 * 10**9, 24)


def backward_attention(info, valids, stream, mixed, spreads, firsts, sums, small, sizes, axes):
    micros, rows, _ = stream.shape
    vmem, dma = pltpu.VMEM, pltpu.SemaphoreType.DMA
    f32, bf16 = jnp.float32, jnp.bfloat16
    slots = slot_structs(sizes, axes, 8)
    scratch = [
        vmem(stream.shape, f32),
        vmem(mixed.shape, f32),
        vmem((2, D, micros * rows), bf16),
        vmem((2, D, micros * rows), bf16),
        vmem((4, 2, micros * rows, 512), bf16),
        vmem(unit_shape(sizes), f32),
        vmem((4, 8, 128), f32),
        vmem((8, 256), f32),
        dma((4,)),
        dma((4, 4)),
        dma((4, copy_count(sizes, axes))),
    ]

    def body(extra, *refs):
        attention_body(len(slots), sizes, axes, *refs)

    inputs = [info, valids, stream, mixed, spreads, firsts, sums, small]
    return call(body, "grad_attention", 2, inputs, [SCALARS, LOCAL], slots, scratch, None, 5 * 10**9, 28)


def backward_chain(tick, info, alphas, segments, valids, targets, received, before, saved, weights, previous):
    micros, rows, inner = before.shape
    parts = inner // 512
    vmem, dma = pltpu.VMEM, pltpu.SemaphoreType.DMA
    f32, bf16 = jnp.float32, jnp.bfloat16
    wq, wk, wv, wo, wi, wb = weights
    outs = [
        pltpu.HBM((micros, 2, rows, inner), bf16),
        pltpu.HBM((micros, 2, rows, 3 * D), bf16),
        pltpu.HBM((micros, 2, rows, D), bf16),
        struct(micros, rows, D),
        struct(micros, 8, 128),
        struct(rows, D),
    ]
    scratch = [
        vmem((rows, D), f32),
        vmem((parts, rows, 512), f32),
        vmem((parts, D, 512), bf16),
        vmem((parts, 512, D), bf16),
        vmem((2 * rows, D), bf16),
        vmem((rows, D), f32),
        vmem((2, rows, inner), bf16),
    ]
    scratch += [vmem(x.shape[1:], f32) for x in saved] + [vmem((D, D), bf16)] * 4
    scratch += [
        vmem((rows, rows), f32),
        vmem((rows, D), f32),
        vmem((D, rows), f32),
        vmem((HEADS // 2, 8, rows), f32),
        vmem((D, rows), f32),
        vmem((rows, D), f32),
        vmem((rows, D), f32),
        vmem((2, rows, 3 * D), bf16),
        vmem((2, rows, D), bf16),
        vmem((rows, D), f32),
        vmem((8, 128), f32),
        pltpu.SMEM(alphas.shape, f32),
        vmem((2,) + segments.shape, jnp.int32),
        dma((6,)),
        dma((parts, 3)),
        dma((4,)),
        dma((6,)),
        dma((3,)),
    ]

    def body(extra, *refs):
        chain_body(tick, extra, *refs)

    inputs = [info, TOKEN[0] if received is None else received, alphas, segments, valids, targets, before]
    inputs += list(saved) + [wi, wb, wq, wk, wv, wo]
    return call(body, "grad_chain", 2, inputs, [SCALARS], outs, scratch, previous, 2 * 10**10, 36)


def local_call(body, name, info, inputs, outs, scratch, specs=None, placed=()):
    inputs = [info, TOKEN[0]] + list(inputs)

    def parted(*refs):
        refs = refs[: len(inputs)] + refs[len(inputs) + len(placed) :]
        first = len(inputs)
        body(refs[0], refs[2:first], refs[first : first + len(outs)], refs[first + len(outs) + 1 :])

    results = pl.pallas_call(
        parted,
        out_shape=list(outs) + [loose(8, 128)],
        in_specs=[SCALARS] + [ANY] * (len(inputs) - 1 + len(placed)),
        out_specs=(specs or [ANY] * len(outs)) + [ANY],
        scratch_shapes=scratch,
        input_output_aliases={len(inputs) + i: i for i in range(len(placed))},
        compiler_params=pltpu.CompilerParams(vmem_limit_bytes=12 * 1024 * 1024),
        cost_estimate=pl.CostEstimate(flops=10**6, bytes_accessed=6 * 10**6, transcendentals=0),
        name=name,
    )(*inputs, *in_hbm(placed))
    TOKEN[0] = results[-1]
    return results[:-1]


def left_dims(done):
    return [axis for axis in (3, 2, 1, 0) if axis not in done]


def picked(ref, dims, axis, index):
    return ref.at[(slice(None),) * dims.index(axis) + (index,)]


def reduce_stage(sizes, order, step, info, arrays):
    shape = arrays[0].shape
    count = len(arrays)
    dims = left_dims(order[:step])
    parting = step < len(order) - 1
    if parting:
        axis = order[step]
        at = dims.index(axis)
        outs = [loose(*shape[:at], *shape[at + 1 :])] * sizes[axis]
    else:
        outs = [loose(*shape)]

    def body(info, ins, outs, scratch):
        held, sem = scratch
        wait_all(start_all([pltpu.make_async_copy(ref, held.at[i], sem.at[i]) for i, ref in enumerate(ins)]))
        total = held[0]
        for i in range(1, count):
            total = total + held[i]
        held[0] = total
        stores = []
        for by in range(len(outs)):
            source = held.at[0]
            if parting:
                source = picked(source, dims, axis, lax.rem(info[1 + axis] + by, sizes[axis]))
            stores.append(pltpu.make_async_copy(source, outs[by], sem.at[count + by]))
        wait_all(start_all(stores))

    scratch = [pltpu.VMEM((count,) + shape, jnp.float32), pltpu.SemaphoreType.DMA((count + len(outs),))]
    return local_call(body, "reduce_step", info, arrays, outs, scratch)


def place_stage(sizes, order, step, info, arrays):
    axis = order[step]
    dims = left_dims(order[:step])
    at = dims.index(axis)
    shape = arrays[0].shape
    count = sizes[axis]

    def body(info, ins, outs, scratch):
        copies = []
        for by in range(count):
            target = picked(outs[0], dims, axis, lax.rem(info[1 + axis] + count - by, count))
            copies.append(pltpu.make_async_copy(ins[by], target, scratch[0].at[by]))
        wait_all(start_all(copies))

    out = loose(*shape[:at], count, *shape[at:])
    return local_call(body, "place_step", info, arrays, [out], [pltpu.SemaphoreType.DMA((count,))])[0]


def out_copies(sizes, axis, info, kind, half, sources, outs, sem):
    x, y, near, far = sizes
    rows = unit_shape(sizes)[3]
    depth = near * far // 4
    count = sizes[axis]
    copies = []

    def put(source, target):
        copies.append(pltpu.make_async_copy(source, target, sem.at[len(copies)]))

    for by, piece in sources:
        place = lax.rem(info[1 + axis] + count - by, count)
        for at in range(near * far if axis < 2 else far):
            if axis == 2:
                source = piece.at[at, :, :, pl.ds(0, rows)]
                z = at * near + place
            else:
                source = piece.at[at // near, at % near, :, pl.ds(0, rows)]
                z = at
            width = piece.shape[-1]
            first = half * width
            if kind == "rows":
                out, inside = outs[0], z
            elif kind == "columns":
                part = lax.div(z, depth) if axis == 2 else z // depth
                first = pl.multiple_of(part * D + first, 128) if axis == 2 else part * D + first
                out, inside = outs[0], lax.rem(z, depth) if axis == 2 else z % depth
            else:
                out, inside = outs[z // depth], z % depth
            lanes = pl.ds(first, width)
            if axis == 0:
                put(source, out.at[inside, :, place, :, lanes])
            elif axis == 1:
                put(source, out.at[inside, place, :, :, lanes])
            else:
                put(source, out.at[inside, :, :, :, lanes])
    return copies


def out_shapes(sizes, kind):
    x, y, near, far = sizes
    rows = unit_shape(sizes)[3]
    depth = near * far // 4
    if kind == "rows":
        return [struct(near * far, y, x, rows, D)]
    if kind == "columns":
        return [struct(depth, y, x, rows, 4 * D)]
    return [struct(depth, y, x, rows, D)] * 4


def own_stage(sizes, axis, info, whole, kind, half, placed):
    def body(info, ins, outs, scratch):
        wait_all(start_all(out_copies(sizes, axis, info, kind, half, [(0, ins[0])], outs, scratch[0])))

    scratch = [pltpu.SemaphoreType.DMA((sizes[2] * sizes[3],))]
    return local_call(body, "place_own", info, [whole], out_shapes(sizes, kind), scratch, None, placed)


def last_stage(sizes, axis, info, arrays, kind, half, placed):
    rows = unit_shape(sizes)[3]
    count = sizes[axis]
    shapes, specs = out_shapes(sizes, kind), None
    scratch = [pltpu.SemaphoreType.DMA((sizes[2] * sizes[3] * count + 1,))]
    has_small = arrays[0].shape[3] > rows
    if has_small:
        specs = [ANY] * len(shapes) + [LOCAL] * 2
        shapes += [loose(1, 2), loose(1, 3)]
        scratch += [pltpu.VMEM((8, 256), jnp.float32)]

    def body(info, ins, outs, scratch):
        sem = scratch[0]
        sources = [(by, ins[by]) for by in range(1, count)]
        copies = start_all(out_copies(sizes, axis, info, kind, half, sources, outs, sem))
        if has_small:
            tile_v = scratch[1]
            for by in range(count):

                @pl.when(info[1 + axis] == by)
                def _():
                    source = ins[by].at[0, 0, 0, pl.ds(rows, 8), pl.ds(0, 256)]
                    copy = pltpu.make_async_copy(source, tile_v, sem.at[len(copies)])
                    copy.start()
                    copy.wait()

            tile = tile_v[0:1, 0:128]
            outs[-2][...] = tile[:, 4:6]
            outs[-1][...] = jnp.sqrt(tile[:, 0:3] / (jnp.maximum(tile[:, 3:4], 1.0) * D))
        wait_all(copies)

    return local_call(body, "place_last", info, arrays, shapes, scratch, specs, placed)


def extents(count):
    bits = count.bit_length() - 1
    if 1 << bits != count:
        return (1, 1, 1, count)
    side = 1 << (bits // 3)
    depth = count // (side * side)
    near = 2 if depth > 1 else 1
    return (side, side, near, depth // near)


def shifted(value, axis, by, sizes):
    count = math.prod(sizes)
    stride, length = math.prod(sizes[:axis]), sizes[axis]
    pairs = []
    for chip in range(count):
        along = (chip // stride) % length
        pairs.append((chip, chip + ((along + by) % length - along) * stride))
    return lax.ppermute(value, "dp", pairs)


def summing(slots, order, kind, half, results, sizes, info):
    pieces = list(slots)
    steps = len(order)
    for step in range(1, steps + 1):
        axis = order[step - 1]
        pieces = [pieces[0]] + [
            shifted(pieces[by if step < steps else 0], axis, by, sizes) for by in range(1, sizes[axis])
        ]
        yield pieces[-1]
        pieces = reduce_stage(sizes, order, step, info, pieces)
    whole = pieces[0]
    for step in range(steps - 2, -1, -1):
        axis = order[step]
        copies = [whole] + [shifted(whole, axis, by, sizes) for by in range(1, sizes[axis])]
        yield copies[-1]
        if step:
            whole = place_stage(sizes, order, step, info, copies)
    placed = results.get(kind, ())
    results[kind] = own_stage(sizes, order[0], info, whole, kind, half, placed)
    yield
    outs = last_stage(sizes, order[0], info, copies, kind, half, results[kind])
    results[kind] = outs[: len(out_shapes(sizes, kind))]
    results["small"] = outs[len(results[kind]) :] or results.get("small")
    yield


def shards(stream_in, cotangent, segment_ids, pad_mask, w_query, w_key, w_value, w_out, w_in, w_back, alphas):
    weights = [weight[0] for weight in (w_query, w_key, w_value, w_out, w_in, w_back)]
    sizes = extents(lax.axis_size("dp"))
    chip = lax.axis_index("dp")
    section = lax.axis_index("section")
    places, left = [], chip
    for size in sizes:
        places.append(lax.rem(left, size))
        left = lax.div(left, size)
    info = jnp.stack([section] + places).astype(jnp.int32)
    TOKEN[0] = jnp.zeros((8, 128), jnp.float32)
    state, chain = None, None

    def forward_step(tick, received):
        return forward_tick(tick, info, alphas, segment_ids, pad_mask, stream_in, received, weights, state)

    def chain_step(tick, received):
        saved = state[2:7]
        return backward_chain(
            tick, info, alphas, segment_ids, pad_mask, cotangent, received, state[8], saved, weights, chain
        )

    received, upstreams = [None], [None]
    for tick in range(2):
        sent, state = forward_step(tick, received[tick])
        received.append(lax.ppermute(sent, "section", [(0, 1)]))
    for tick in range(3):
        *chain, sent = chain_step(tick, upstreams[tick])
        if tick < 2:
            upstreams.append(lax.ppermute(sent, "section", [(1, 0)]))
        if tick == 0:
            _, state = forward_step(2, received[2])
    acts, saved_s, _, _, _, saved_o, _, saved_m, saved_p, sums = state
    befores, spreads, firsts, passed, small = chain
    orders = {key: tuple("xynf".index(axis) for axis in order) for key, order in ORDERS.items()}
    results, streams = {}, {}

    def gradients(index):
        pair, kind = ("Bb", "Ii", "Aa")[index], ("rows", "columns", "four")[index]
        pair = [key for key in pair if key in orders]
        axes = [orders[key][0] for key in pair]
        if index == 0:
            slots = backward_back(info, alphas, upstreams[1:], cotangent, saved_p, sizes, axes)
        elif index == 1:
            slots = backward_inner(info, saved_m, befores, sizes, axes)
        else:
            slots = backward_attention(info, pad_mask, saved_s, saved_o, spreads, firsts, sums, small, sizes, axes)
        for half, key in enumerate(pair):
            count = sizes[axes[half]]
            streams[key] = summing(slots[:count], orders[key], kind, half, results, sizes, info)
            slots = slots[count:]

    made, steps, owned = 0, {}, set()
    for item in PROGRAM:
        if item == "|":
            gradients(made)
            made += 1
            continue
        steps[item] = steps.get(item, 0) + 1
        if steps[item] == 8:
            for key in [key for key in steps if steps[key] in (7, 8) and key not in owned]:
                owned.add(key)
                next(streams[key])
        next(streams[item])
    attention, inner, back = results["four"], results["columns"], results["rows"]
    return (
        acts[None, :, None],
        passed[None, :, None],
        attention[0].reshape(1, D, D),
        attention[1].reshape(1, D, D),
        attention[2].reshape(1, D, D),
        attention[3].reshape(1, D, D),
        inner[0].reshape(1, D, -1),
        back[0].reshape(1, -1, D),
        results["small"][0],
        results["small"][1],
    )


def solution(mesh):
    in_specs = (
        P(None, "dp", None, None),
        P(None, "dp", None, None),
        P(None, "dp", None),
        P(None, "dp", None),
        P("section", None, None),
        P("section", None, None),
        P("section", None, None),
        P("section", None, None),
        P("section", None, None),
        P("section", None, None),
        P("section", None),
    )
    out_specs = (
        P("section", None, "dp", None, None),
        P("section", None, "dp", None, None),
        P("section", None, None),
        P("section", None, None),
        P("section", None, None),
        P("section", None, None),
        P("section", None, None),
        P("section", None, None),
        P("section", None),
        P("section", None),
    )
    return jax.shard_map(shards, mesh=mesh, in_specs=in_specs, out_specs=out_specs, check_vma=False)
```

time: 401 us -> 384 us (0.958)
  waiting for transfers between devices: 223 us -> 169 us
  starting transfers between devices: 33.5 us -> 58.3 us
  Pallas kernels: 134 us -> 149 us
    ppermute x21 -> x42, waiting for transfers between devices: 193 us -> 144 us  [shifted(): return lax.ppermute(value, 'dp', pairs)]
    ppermute x21 -> x42, starting transfers between devices: 27.3 us -> 52.3 us  [shifted(): return lax.ppermute(value, 'dp', pairs)]
    pallas_call x21 -> x48, Pallas kernels: 24.5 us -> 45.4 us  [local_call(): pl.pallas_call(parted, out_shape=list(outs) + [loose(8, 128)], in_specs=[...]
    pallas_call x7 -> x6, Pallas kernels: 77.9 us -> 67.9 us  [call(): pl.pallas_call(functools.partial(body, len(extra)), out_shape=outs + [loo...]
    pallas_call x3, Pallas kernels: 31.3 us -> 35.5 us  [forward_tick(): pl.pallas_call(functools.partial(forward_body, tick), out_shape=shapes, i...]
    ppermute x4, waiting for transfers between devices: 29.4 us -> 25.3 us  [the longest x2 23.3 us: shards(): upstreams.append(lax.ppermute(sent, 'section', [(1, 0)]))]
  transfers between devices with their start and end apart: 25 -> 46, of which waited for: 15 -> 19; matrix products, arithmetic and copies ran while one was open for 0% -> 0% of each run, Pallas kernels for 10% -> 16%
where the time goes in v3:
time: 384 us; the launch traced here: 378 us
  waiting for transfers between devices  169 us (44%)
  Pallas kernels  149 us (39%)
  starting transfers between devices  58.3 us (15%)
    ppermute x42, waiting for transfers between devices, shifted(): return lax.ppermute(value, 'dp', pairs)  144 us
    pallas_call x6, Pallas kernels, call(): pl.pallas_call(functools.partial(body, len(extra)), out_shape=outs + [loo...  67.9 us
    ppermute x42, starting transfers between devices, shifted(): return lax.ppermute(value, 'dp', pairs)  52.3 us
    pallas_call x48, Pallas kernels, local_call(): pl.pallas_call(parted, out_shape=list(outs) + [loose(8, 128)], in_specs=[...  45.4 us
    pallas_call x3, Pallas kernels, forward_tick(): pl.pallas_call(functools.partial(forward_body, tick), out_shape=shapes, i...  35.5 us
    ppermute x2, waiting for transfers between devices, shards(): upstreams.append(lax.ppermute(sent, 'section', [(1, 0)]))  23.3 us
  transfers between devices with their start and end apart: 46, of which 19 were waited for; matrix products, arithmetic and copies ran while one was open for 0% of the time, Pallas kernels for 16%

profile of v3, /device:TPU:0, one launch (start us, length us, event | category | flops | bytes accessed | tf_op | source)
XLA Modules:
  0.0 378.0 jit_solution(13669466108746071757)
XLA Ops:
  0.8 12.9 %layer_forward.3 = (f32[2,384,512]{2,1,0:T(8,128)}, f32[384,512]{1,0:T(8,128)}, f32[2,384,512]{2,1,0:T(8,128)}, f32[2,384,512]{2,1,0:T(8,128)}, f32[2,384,512]{2...) custom-call(s32[5]{0:T(128)S(1)} %stack.23.refs_0_, ...), custom_call_target="tpu_custom_call" | custom-call | flops 10000000000 | bytes 20000000 | tf_op jit(solution)/shard_map/layer_forward/pallas_call | solution.py:290
  13.7 1.3 collective-permute-start
  15.0 2.1 collective-permute-done.refs_12_
  17.1 13.2 %layer_forward.4 = (f32[2,384,512]{2,1,0:T(8,128)}, f32[384,512]{1,0:T(8,128)}, f32[2,384,512]{2,1,0:T(8,128)}, f32[2,384,512]{2,1,0:T(8,128)}, f32[2,384,512]{2...) custom-call(s32[5]{0:T(128)S(1)} %stack.23.refs_0_, ...), custom_call_target="tpu_custom_call", output_to_operand_aliasing={{0}: (13, {}), {2}: (14, {}), {3}: (15, {}), {4}: (16, {}),... | custom-call | flops 10000000000 | bytes 20000000 | tf_op jit(solution)/shard_map/layer_forward/pallas_call | solution.py:290
  30.3 2.0 collective-permute-start.1
  33.1 1.3 collective-permute-start.2
  34.5 9.4 %layer_forward.5 = (f32[2,384,512]{2,1,0:T(8,128)}, f32[384,512]{1,0:T(8,128)}, f32[2,384,512]{2,1,0:T(8,128)}, f32[2,384,512]{2,1,0:T(8,128)}, f32[2,384,512]{2...) custom-call(s32[5]{0:T(128)S(1)} %stack.23.refs_0_, ...), custom_call_target="tpu_custom_call", output_to_operand_aliasing={{0}: (13, {}), {2}: (14, {}), {3}: (15, {}), {4}: (16, {}),... | custom-call | flops 10000000000 | bytes 20000000 | tf_op jit(solution)/shard_map/layer_forward/pallas_call | solution.py:290
  43.9 9.8 %collective-permute-done.2.refs_1_.refs_2_ = f32[384,512]{1,0:T(8,128)S(1)} collective-permute-done((f32[384,512]{1,0:T(8,128)}, f32[384,512]{1,0:T(8,128)S(1)}, u32[]{:S(2)}, u32[]{:S(2)}) %collective-permute-start.2) | collective-permute-done | bytes 786464 | tf_op jit(solution)/shard_map/ppermute | solution.py:1065
  53.6 18.3 %grad_chain.4 = (bf16[2,2,384,2048]{3,2,1,0:T(8,128)(2,1)}, bf16[2,2,384,1536]{3,2,1,0:T(8,128)(2,1)}, bf16[2,2,384,512]{3,2,1,0:T(8,128)(2,1)}, f32[2,384,512]{...) custom-call(s32[5]{0:T(128)S(1)} %stack.23.refs_0_, ...), custom_call_target="tpu_custom_call", output_to_operand_aliasing={{0}: (19, {}), {1}: (20, {}), {2}: (21, {}), {3}: (22, {}),... | custom-call | flops 20000000000 | bytes 20000000 | tf_op jit(solution)/shard_map/grad_chain/pallas_call | solution.py:681
  72.0 1.3 collective-permute-start.3
  73.3 13.5 %collective-permute-done.3.refs_1_.refs_3_ = f32[384,512]{1,0:T(8,128)S(1)} collective-permute-done((f32[384,512]{1,0:T(8,128)}, f32[384,512]{1,0:T(8,128)S(1)}, u32[]{:S(2)}, u32[]{:S(2)}) %collective-permute-start.3) | collective-permute-done | bytes 786464 | tf_op jit(solution)/shard_map/ppermute | solution.py:1065
  86.8 19.0 %grad_chain.5 = (bf16[2,2,384,2048]{3,2,1,0:T(8,128)(2,1)}, bf16[2,2,384,1536]{3,2,1,0:T(8,128)(2,1)}, bf16[2,2,384,512]{3,2,1,0:T(8,128)(2,1)}, f32[2,384,512]{...) custom-call(s32[5]{0:T(128)S(1)} %stack.23.refs_0_, ...), custom_call_target="tpu_custom_call", output_to_operand_aliasing={{0}: (19, {}), {1}: (20, {}), {2}: (21, {}), {3}: (22, {}),... | custom-call | flops 20000000000 | bytes 20000000 | tf_op jit(solution)/shard_map/grad_chain/pallas_call | solution.py:681
  105.8 9.9 %grad_back.1 = (f32[2,2,2,128,256]{4,3,2,1,0:T(8,128)}, f32[2,2,2,128,256]{4,3,2,1,0:T(8,128)}, f32[2,2,2,128,256]{4,3,2,1,0:T(8,128)}, f32[2,2,2,128,256]{4,3,2,1,0:T(8,128)}, f32[8,128]{1,0:T(8,128)S(1)}) custom-call(s32[5]{0:T(128)S(1)} %stack.23.refs_0_, f32[1,2]{1,0:T(1,128)S(1)} %copy-done.7, f32[384,512]{1,0:T(8,128)S(1)} %collective-permute-done.2.refs_1_.refs_2_, ...), custom_call_target="tpu_custom_call" | custom-call | flops 5000000000 | bytes 20000000 | tf_op jit(solution)/shard_map/grad_back/pallas_call | solution.py:681
  115.7 3.1 collective-permute-start.4
  118.8 1.5 collective-permute-start.5
  120.3 9.8 %grad_inner.1 = (f32[2,2,2,128,256]{4,3,2,1,0:T(8,128)}, f32[2,2,2,128,256]{4,3,2,1,0:T(8,128)}, f32[2,2,2,128,256]{4,3,2,1,0:T(8,128)}, f32[2,2,2,128,256]{4,3,2,1,0:T(8,128)}, f32[8,128]{1,0:T(8,128)S(1)}) custom-call(s32[5]{0:T(128)S(1)} %stack.23.refs_0_, f32[2,384,512]{2,1,0:T(8,128)} %get-tuple-element.253.refs_1_, ...), custom_call_target="tpu_custom_call" | custom-call | flops 5000000000 | bytes 20000000 | tf_op jit(solution)/shard_map/grad_inner/pallas_call | solution.py:681
  130.2 1.6 collective-permute-done.4.refs_3_
  134.8 9.9 %grad_attention.1 = (f32[2,2,2,136,256]{4,3,2,1,0:T(8,128)}, f32[2,2,2,136,256]{4,3,2,1,0:T(8,128)}, f32[2,2,2,128,256]{4,3,2,1,0:T(8,128)}, f32[2,2,2,128,256]{4,3,2,1,0:T(8,128)}, f32[8,128]{1,0:T(8,128)S(1)}) custom-call(s32[5]{0:T(128)S(1)} %stack.23.refs_0_, s32[2,1,384]{2,1,0:T(1,128)S(1)} %copy-done.6, f32[2,384,512]{2,1,0:T(8,128)} %get-tuple-element.248.refs_2_, ...), custom_call_target="tpu_custom_call" | custom-call | flops 5000000000 | bytes 20000000 | tf_op jit(solution)/shard_map/grad_attention/pallas_call | solution.py:681
  144.7 1.6 collective-permute-start.10
  148.0 1.5 collective-permute-start.11
  149.5 6.0 %collective-permute-done.6.refs_3_ = f32[2,2,128,256]{3,2,1,0:T(8,128)S(1)} collective-permute-done((f32[2,2,128,256]{3,2,1,0:T(8,128)S(1)}, f32[2,2,128,256]{3,2,1,0:T(8,128)S(1)}, u32[]{:S(2)}, u32[]{:S(2)}) %collective-permute-start.6) | collective-permute-done | bytes 524320 | tf_op jit(solution)/shard_map/ppermute | solution.py:1007
  156.2 1.6 collective-permute-start.8
  157.8 18.9 %collective-permute-done.7.refs_3_ = f32[2,2,128,256]{3,2,1,0:T(8,128)S(1)} collective-permute-done((f32[2,2,128,256]{3,2,1,0:T(8,128)S(1)}, f32[2,2,128,256]{3,2,1,0:T(8,128)S(1)}, u32[]{:S(2)}, u32[]{:S(2)}) %collective-permute-start.7) | collective-permute-done | bytes 524320 | tf_op jit(solution)/shard_map/ppermute | solution.py:1007
  177.4 2.6 collective-permute-start.9
  180.0 1.3 collective-permute-start.15
  181.3 1.5 collective-permute-start.19
  186.0 2.1 collective-permute-start.12
  188.1 2.6 collective-permute-start.14
  191.9 9.0 %collective-permute-done.12.refs_3_ = f32[2,2,128,256]{3,2,1,0:T(8,128)S(1)} collective-permute-done((f32[2,2,128,256]{3,2,1,0:T(8,128)S(1)}, f32[2,2,128,256]{3,2,1,0:T(8,128)S(1)}, u32[]{:S(2)}, u32[]{:S(2)}) %collective-permute-start.12) | collective-permute-done | bytes 524320 | tf_op jit(solution)/shard_map/ppermute | solution.py:1007
  200.9 1.5 collective-permute-start.17
  203.2 5.5 %collective-permute-done.13.refs_3_ = f32[2,128,256]{2,1,0:T(8,128)S(1)} collective-permute-done((f32[2,128,256]{2,1,0:T(8,128)S(1)}, f32[2,128,256]{2,1,0:T(8,128)S(1)}, u32[]{:S(2)}, u32[]{:S(2)}) %collective-permute-start.13) | collective-permute-done | bytes 262176 | tf_op jit(solution)/shard_map/ppermute | solution.py:1007
  208.6 3.7 collective-permute-start.16
  214.7 2.1 collective-permute-start.21
  216.8 2.8 collective-permute-done.16.refs_3_
  222.8 2.1 collective-permute-start.26
  225.1 1.9 collective-permute-start.22
  226.9 4.7 %collective-permute-done.20.refs_3_ = f32[2,128,256]{2,1,0:T(8,128)S(1)} collective-permute-done((f32[2,128,256]{2,1,0:T(8,128)S(1)}, f32[2,128,256]{2,1,0:T(8,128)S(1)}, u32[]{:S(2)}, u32[]{:S(2)}) %collective-permute-start.20) | collective-permute-done | bytes 262176 | tf_op jit(solution)/shard_map/ppermute | solution.py:1007
  233.0 2.6 collective-permute-start.25
  235.6 25.5 %collective-permute-done.22.refs_3_ = f32[2,128,256]{2,1,0:T(8,128)S(1)} collective-permute-done((f32[2,128,256]{2,1,0:T(8,128)S(1)}, f32[2,128,256]{2,1,0:T(8,128)S(1)}, u32[]{:S(2)}, u32[]{:S(2)}) %collective-permute-start.22) | collective-permute-done | bytes 262176 | tf_op jit(solution)/shard_map/ppermute | solution.py:1007
  261.1 2.5 collective-permute-start.30
  267.4 9.1 %collective-permute-done.27.refs_3_ = f32[2,128,256]{2,1,0:T(8,128)S(1)} collective-permute-done((f32[2,128,256]{2,1,0:T(8,128)S(1)}, f32[2,128,256]{2,1,0:T(8,128)S(1)}, u32[]{:S(2)}, u32[]{:S(2)}) %collective-permute-start.27) | collective-permute-done | bytes 262176 | tf_op jit(solution)/shard_map/ppermute | solution.py:1007
  277.9 2.9 collective-permute-start.31
  281.5 2.0 collective-permute-start.34
  284.1 2.1 collective-permute-start.38
  286.2 6.5 %collective-permute-done.31.refs_3_ = f32[2,128,256]{2,1,0:T(8,128)S(1)} collective-permute-done((f32[2,128,256]{2,1,0:T(8,128)S(1)}, f32[2,128,256]{2,1,0:T(8,128)S(1)}, u32[]{:S(2)}, u32[]{:S(2)}) %collective-permute-start.31) | collective-permute-done | bytes 262176 | tf_op jit(solution)/shard_map/ppermute | solution.py:1007
  294.7 2.8 collective-permute-start.36
  298.2 8.6 %collective-permute-done.35.refs_3_ = f32[2,128,256]{2,1,0:T(8,128)S(1)} collective-permute-done((f32[2,128,256]{2,1,0:T(8,128)S(1)}, f32[2,128,256]{2,1,0:T(8,128)S(1)}, u32[]{:S(2)}, u32[]{:S(2)}) %collective-permute-start.35) | collective-permute-done | bytes 262176 | tf_op jit(solution)/shard_map/ppermute | solution.py:1007
  308.3 14.7 %collective-permute-done.37.refs_3_ = f32[2,2,128,256]{3,2,1,0:T(8,128)S(1)} collective-permute-done((f32[2,2,128,256]{3,2,1,0:T(8,128)S(1)}, f32[2,2,128,256]{3,2,1,0:T(8,128)S(1)}, u32[]{:S(2)}, u32[]{:S(2)}) %collective-permute-start.37) | collective-permute-done | bytes 524320 | tf_op jit(solution)/shard_map/ppermute | solution.py:1007
  323.7 1.5 place_own.6
  325.2 1.5 place_own.7
  326.8 1.5 place_own.8
  328.3 1.5 place_own.9
  329.9 1.6 place_last.6
  332.9 2.0 collective-permute-start.41
  335.1 2.0 collective-permute-start.44
  337.1 1.5 place_own.10
  338.6 1.5 place_own.11
  340.2 19.5 %collective-permute-done.41.refs_3_ = f32[2,2,2,128,256]{4,3,2,1,0:T(8,128)S(1)} collective-permute-done((f32[2,2,2,128,256]{4,3,2,1,0:T(8,128)S(1)}, f32[2,2,2,128,256]{4,3,2,1,0:T(8,128)S(1)}, u32[]{:S(2)}, u32[]{:S(2)}) %collective-permute-start.41) | collective-permute-done | bytes 1048608 | tf_op jit(solution)/shard_map/ppermute | solution.py:1007
  359.7 1.6 place_last.7
  361.3 9.6 %collective-permute-done.42.refs_3_ = f32[2,2,2,128,256]{4,3,2,1,0:T(8,128)S(1)} collective-permute-done((f32[2,2,2,128,256]{4,3,2,1,0:T(8,128)S(1)}, f32[2,2,2,128,256]{4,3,2,1,0:T(8,128)S(1)}, u32[]{:S(2)}, u32[]{:S(2)}) %collective-permute-start.42) | collective-permute-done | bytes 1048608 | tf_op jit(solution)/shard_map/ppermute | solution.py:1007
  370.9 1.6 place_last.8
  372.5 1.6 place_last.9
  374.1 1.6 place_last.10
  375.7 2.1 place_last.11
  (109 shorter events, 32.0 us)
Async XLA Ops:
  13.7 3.4 collective-permute-start
  30.3 4.2 %collective-permute-start.1 = (f32[384,512]{1,0:T(8,128)}, f32[384,512]{1,0:T(8,128)S(1)}, u32[]{:S(2)}, u32[]{:S(2)}) collective-permute-start(f32[384,512]{1,0:T(8,128)} %get-tuple-element.221), channel_id=1, source_target_pairs={{0,16},{1,17},{2,18},{3,19},{4,20},{5,21},{6,22},{7,23},{8,24},{9,... | collective-permute-start | bytes 2359304 | tf_op jit(solution)/shard_map/ppermute | solution.py:1061
  33.1 20.5 %collective-permute-start.2 = (f32[384,512]{1,0:T(8,128)}, f32[384,512]{1,0:T(8,128)S(1)}, u32[]{:S(2)}, u32[]{:S(2)}) collective-permute-start(f32[384,512]{1,0:T(8,128)} %get-tuple-element.227), channel_id=1, source_target_pairs={{16,0},{17,1},{18,2},{19,3},{20,4},{21,5},{22,6},{23,7},{24,8},{25... | collective-permute-start | bytes 2359304 | tf_op jit(solution)/shard_map/ppermute | solution.py:1065
  72.0 14.8 %collective-permute-start.3 = (f32[384,512]{1,0:T(8,128)}, f32[384,512]{1,0:T(8,128)S(1)}, u32[]{:S(2)}, u32[]{:S(2)}) collective-permute-start(f32[384,512]{1,0:T(8,128)} %get-tuple-element.240), channel_id=1, source_target_pairs={{16,0},{17,1},{18,2},{19,3},{20,4},{21,5},{22,6},{23,7},{24,8},{25... | collective-permute-start | bytes 2359304 | tf_op jit(solution)/shard_map/ppermute | solution.py:1065
  86.8 19.0 %copy-start.7 = (f32[1,2]{1,0:T(1,128)S(1)}, f32[1,2]{1,0:T(1,128)}, u32[]{:S(2)}) copy-start(f32[1,2]{1,0:T(1,128)} %refs_1_.8) | copy-start | bytes 28
  115.7 16.1 %collective-permute-start.4 = (f32[2,2,2,128,256]{4,3,2,1,0:T(8,128)}, f32[2,2,2,128,256]{4,3,2,1,0:T(8,128)S(1)}, u32[]{:S(2)}, u32[]{:S(2)}) collective-permute-start(f32[2,2,2,128,256]{4,3,2,1,0:T(8,128)} %get-tuple-element.259), channel_id=1, source_target_pairs={{0,4},{1,5},{2,6},{3,7},{4,0},{5,1},{6,2},{7,3},{8,12},{9,13},{10,... | collective-permute-start | bytes 3145736 | tf_op jit(solution)/shard_map/ppermute | solution.py:1007
  118.8 15.0 %collective-permute-start.5 = (f32[2,2,2,128,256]{4,3,2,1,0:T(8,128)}, f32[2,2,2,128,256]{4,3,2,1,0:T(8,128)S(1)}, u32[]{:S(2)}, u32[]{:S(2)}) collective-permute-start(f32[2,2,2,128,256]{4,3,2,1,0:T(8,128)} %get-tuple-element.262), channel_id=1, source_target_pairs={{0,1},{1,0},{2,3},{3,2},{4,5},{5,4},{6,7},{7,6},{8,9},{9,8},{10,11... | collective-permute-start | bytes 3145736 | tf_op jit(solution)/shard_map/ppermute | solution.py:1007
  120.3 11.5 %copy-start.5 = (f32[2,2,2,128,256]{4,3,2,1,0:T(8,128)S(1)}, f32[2,2,2,128,256]{4,3,2,1,0:T(8,128)}, u32[]{:S(2)}) copy-start(f32[2,2,2,128,256]{4,3,2,1,0:T(8,128)} %get-tuple-element.258.refs_2_) | copy-start | bytes 3145732
  130.2 3.7 copy-start.4
  132.9 1.9 copy-start.6
  134.8 13.2 %copy-start.10 = (f32[2,2,2,128,256]{4,3,2,1,0:T(8,128)S(1)}, f32[2,2,2,128,256]{4,3,2,1,0:T(8,128)}, u32[]{:S(2)}) copy-start(f32[2,2,2,128,256]{4,3,2,1,0:T(8,128)} %get-tuple-element.281) | copy-start | bytes 3145732
  134.8 45.3 %copy-start.9 = (f32[2,2,2,128,256]{4,3,2,1,0:T(8,128)S(1)}, f32[2,2,2,128,256]{4,3,2,1,0:T(8,128)}, u32[]{:S(2)}) copy-start(f32[2,2,2,128,256]{4,3,2,1,0:T(8,128)} %get-tuple-element.291) | copy-start | bytes 3145732
  144.7 36.6 %copy-start.8 = (f32[2,2,2,136,256]{4,3,2,1,0:T(8,128)S(1)}, f32[2,2,2,136,256]{4,3,2,1,0:T(8,128)}, u32[]{:S(2)}) copy-start(f32[2,2,2,136,256]{4,3,2,1,0:T(8,128)} %get-tuple-element.302) | copy-start | bytes 3342340
  144.7 40.3 %collective-permute-start.10 = (f32[2,2,2,128,256]{4,3,2,1,0:T(8,128)}, f32[2,2,2,128,256]{4,3,2,1,0:T(8,128)S(1)}, u32[]{:S(2)}, u32[]{:S(2)}) collective-permute-start(f32[2,2,2,128,256]{4,3,2,1,0:T(8,128)} %get-tuple-element.278), channel_id=1, source_target_pairs={{0,1},{1,0},{2,3},{3,2},{4,5},{5,4},{6,7},{7,6},{8,9},{9,8},{10,11... | collective-permute-start | bytes 3145736 | tf_op jit(solution)/shard_map/ppermute | solution.py:1007
  146.3 9.2 %collective-permute-start.6 = (f32[2,2,128,256]{3,2,1,0:T(8,128)S(1)}, f32[2,2,128,256]{3,2,1,0:T(8,128)S(1)}, u32[]{:S(2)}, u32[]{:S(2)}) collective-permute-start(f32[2,2,128,256]{3,2,1,0:T(8,128)S(1)} %get-tuple-element.266), channel_id=1, source_target_pairs={{0,4},{1,5},{2,6},{3,7},{4,0},{5,1},{6,2},{7,3},{8,12},{9,13},{10,... | collective-permute-start | bytes 1572872 | tf_op jit(solution)/shard_map/ppermute | solution.py:1007
  147.4 29.3 %collective-permute-start.7 = (f32[2,2,128,256]{3,2,1,0:T(8,128)S(1)}, f32[2,2,128,256]{3,2,1,0:T(8,128)S(1)}, u32[]{:S(2)}, u32[]{:S(2)}) collective-permute-start(f32[2,2,128,256]{3,2,1,0:T(8,128)S(1)} %get-tuple-element.269), channel_id=1, source_target_pairs={{0,1},{1,0},{2,3},{3,2},{4,5},{5,4},{6,7},{7,6},{8,9},{9,8},{10,11... | collective-permute-start | bytes 1572872 | tf_op jit(solution)/shard_map/ppermute | solution.py:1007
  148.0 42.7 %collective-permute-start.11 = (f32[2,2,2,128,256]{4,3,2,1,0:T(8,128)S(1)}, f32[2,2,2,128,256]{4,3,2,1,0:T(8,128)S(1)}, u32[]{:S(2)}, u32[]{:S(2)}) collective-permute-start(f32[2,2,2,128,256]{4,3,2,1,0:T(8,128)S(1)} %copy-done.10), channel_id=1, source_target_pairs={{0,2},{1,3},{2,0},{3,1},{4,6},{5,7},{6,4},{7,5},{8,10},{9,11},{10,... | collective-permute-start | bytes 3145736 | tf_op jit(solution)/shard_map/ppermute | solution.py:1007
  155.5 29.6 %copy-start.3 = (f32[2,2,2,128,256]{4,3,2,1,0:T(8,128)S(1)}, f32[2,2,2,128,256]{4,3,2,1,0:T(8,128)}, u32[]{:S(2)}) copy-start(f32[2,2,2,128,256]{4,3,2,1,0:T(8,128)} %get-tuple-element.277.refs_2_) | copy-start | bytes 3145732
  156.2 25.1 %collective-permute-start.8 = (f32[2,128,256]{2,1,0:T(8,128)S(1)}, f32[2,128,256]{2,1,0:T(8,128)S(1)}, u32[]{:S(2)}, u32[]{:S(2)}) collective-permute-start(f32[2,128,256]{2,1,0:T(8,128)S(1)} %get-tuple-element.272), channel_id=1, source_target_pairs={{0,2},{1,3},{2,0},{3,1},{4,6},{5,7},{6,4},{7,5},{8,10},{9,11},{10,... | collective-permute-start | bytes 786440 | tf_op jit(solution)/shard_map/ppermute | solution.py:1007
  177.4 6.9 %collective-permute-start.9 = (f32[2,128,256]{2,1,0:T(8,128)S(1)}, f32[2,128,256]{2,1,0:T(8,128)S(1)}, u32[]{:S(2)}, u32[]{:S(2)}) collective-permute-start(f32[2,128,256]{2,1,0:T(8,128)S(1)} %get-tuple-element.275), channel_id=1, source_target_pairs={{0,2},{1,3},{2,0},{3,1},{4,6},{5,7},{6,4},{7,5},{8,10},{9,11},{10,... | collective-permute-start | bytes 786440 | tf_op jit(solution)/shard_map/ppermute | solution.py:1007
  180.0 33.8 %collective-permute-start.15 = (f32[2,2,2,128,256]{4,3,2,1,0:T(8,128)S(1)}, f32[2,2,2,128,256]{4,3,2,1,0:T(8,128)S(1)}, u32[]{:S(2)}, u32[]{:S(2)}) collective-permute-start(f32[2,2,2,128,256]{4,3,2,1,0:T(8,128)S(1)} %copy-done.9), channel_id=1, source_target_pairs={{0,4},{1,5},{2,6},{3,7},{4,0},{5,1},{6,2},{7,3},{8,12},{9,13},{10,... | collective-permute-start | bytes 3145736 | tf_op jit(solution)/shard_map/ppermute | solution.py:1007
  181.3 40.3 %collective-permute-start.19 = (f32[2,2,2,136,256]{4,3,2,1,0:T(8,128)S(1)}, f32[2,2,2,136,256]{4,3,2,1,0:T(8,128)S(1)}, u32[]{:S(2)}, u32[]{:S(2)}) collective-permute-start(f32[2,2,2,136,256]{4,3,2,1,0:T(8,128)S(1)} %copy-done.8), channel_id=1, source_target_pairs={{0,1},{1,0},{2,3},{3,2},{4,5},{5,4},{6,7},{7,6},{8,9},{9,8},{10,11... | collective-permute-start | bytes 3342344 | tf_op jit(solution)/shard_map/ppermute | solution.py:1007
  182.8 8.2 %copy-start.2 = (f32[2,2,2,128,256]{4,3,2,1,0:T(8,128)S(1)}, f32[2,2,2,128,256]{4,3,2,1,0:T(8,128)}, u32[]{:S(2)}) copy-start(f32[2,2,2,128,256]{4,3,2,1,0:T(8,128)} %get-tuple-element.280.refs_2_) | copy-start | bytes 3145732
  186.0 14.9 %collective-permute-start.12 = (f32[2,2,128,256]{3,2,1,0:T(8,128)S(1)}, f32[2,2,128,256]{3,2,1,0:T(8,128)S(1)}, u32[]{:S(2)}, u32[]{:S(2)}) collective-permute-start(f32[2,2,128,256]{3,2,1,0:T(8,128)S(1)} %get-tuple-element.284), channel_id=1, source_target_pairs={{0,2},{1,3},{2,0},{3,1},{4,6},{5,7},{6,4},{7,5},{8,10},{9,11},{10,... | collective-permute-start | bytes 1572872 | tf_op jit(solution)/shard_map/ppermute | solution.py:1007
  188.1 25.0 %collective-permute-start.14 = (f32[2,128,256]{2,1,0:T(8,128)S(1)}, f32[2,128,256]{2,1,0:T(8,128)S(1)}, u32[]{:S(2)}, u32[]{:S(2)}) collective-permute-start(f32[2,128,256]{2,1,0:T(8,128)S(1)} %get-tuple-element.288.refs_2_), channel_id=1, source_target_pairs={{0,8},{1,9},{2,10},{3,11},{4,12},{5,13},{6,14},{7,15},{8,0},{9,1},... | collective-permute-start | bytes 786440 | tf_op jit(solution)/shard_map/ppermute | solution.py:1007
  190.7 18.0 %collective-permute-start.13 = (f32[2,128,256]{2,1,0:T(8,128)S(1)}, f32[2,128,256]{2,1,0:T(8,128)S(1)}, u32[]{:S(2)}, u32[]{:S(2)}) collective-permute-start(f32[2,128,256]{2,1,0:T(8,128)S(1)} %get-tuple-element.286.refs_2_), channel_id=1, source_target_pairs={{0,8},{1,9},{2,10},{3,11},{4,12},{5,13},{6,14},{7,15},{8,0},{9,1},... | collective-permute-start | bytes 786440 | tf_op jit(solution)/shard_map/ppermute | solution.py:1007
  191.9 21.9 %copy-start.1 = (f32[2,2,2,128,256]{4,3,2,1,0:T(8,128)S(1)}, f32[2,2,2,128,256]{4,3,2,1,0:T(8,128)}, u32[]{:S(2)}) copy-start(f32[2,2,2,128,256]{4,3,2,1,0:T(8,128)} %get-tuple-element.290.refs_2_) | copy-start | bytes 3145732
  200.9 19.3 %collective-permute-start.17 = (f32[2,2,128,256]{3,2,1,0:T(8,128)S(1)}, f32[2,2,128,256]{3,2,1,0:T(8,128)S(1)}, u32[]{:S(2)}, u32[]{:S(2)}) collective-permute-start(f32[2,2,128,256]{3,2,1,0:T(8,128)S(1)} %get-tuple-element.297), channel_id=1, source_target_pairs={{0,1},{1,0},{2,3},{3,2},{4,5},{5,4},{6,7},{7,6},{8,9},{9,8},{10,11... | collective-permute-start | bytes 1572872 | tf_op jit(solution)/shard_map/ppermute | solution.py:1007
  208.6 11.0 %collective-permute-start.16 = (f32[2,128,256]{2,1,0:T(8,128)S(1)}, f32[2,128,256]{2,1,0:T(8,128)S(1)}, u32[]{:S(2)}, u32[]{:S(2)}) collective-permute-start(f32[2,128,256]{2,1,0:T(8,128)S(1)} %get-tuple-element.294), channel_id=1, source_target_pairs={{0,4},{1,5},{2,6},{3,7},{4,0},{5,1},{6,2},{7,3},{8,12},{9,13},{10,... | collective-permute-start | bytes 786440 | tf_op jit(solution)/shard_map/ppermute | solution.py:1007
  213.7 7.3 %collective-permute-start.18 = (f32[2,128,256]{2,1,0:T(8,128)S(1)}, f32[2,128,256]{2,1,0:T(8,128)S(1)}, u32[]{:S(2)}, u32[]{:S(2)}) collective-permute-start(f32[2,128,256]{2,1,0:T(8,128)S(1)} %get-tuple-element.299.refs_2_), channel_id=1, source_target_pairs={{0,2},{1,3},{2,0},{3,1},{4,6},{5,7},{6,4},{7,5},{8,10},{9,11},{10,... | collective-permute-start | bytes 786440 | tf_op jit(solution)/shard_map/ppermute | solution.py:1007
  214.7 6.9 %copy-start = (f32[2,2,2,136,256]{4,3,2,1,0:T(8,128)S(1)}, f32[2,2,2,136,256]{4,3,2,1,0:T(8,128)}, u32[]{:S(2)}) copy-start(f32[2,2,2,136,256]{4,3,2,1,0:T(8,128)} %get-tuple-element.301.refs_2_) | copy-start | bytes 3342340
  214.7 17.5 %collective-permute-start.21 = (f32[2,2,128,256]{3,2,1,0:T(8,128)S(1)}, f32[2,2,128,256]{3,2,1,0:T(8,128)S(1)}, u32[]{:S(2)}, u32[]{:S(2)}) collective-permute-start(f32[2,2,128,256]{3,2,1,0:T(8,128)S(1)} %get-tuple-element.307), channel_id=1, source_target_pairs={{0,2},{1,3},{2,0},{3,1},{4,6},{5,7},{6,4},{7,5},{8,10},{9,11},{10,... | collective-permute-start | bytes 1572872 | tf_op jit(solution)/shard_map/ppermute | solution.py:1007
  222.8 43.5 %collective-permute-start.26 = (f32[2,2,136,256]{3,2,1,0:T(8,128)S(1)}, f32[2,2,136,256]{3,2,1,0:T(8,128)S(1)}, u32[]{:S(2)}, u32[]{:S(2)}) collective-permute-start(f32[2,2,136,256]{3,2,1,0:T(8,128)S(1)} %get-tuple-element.320), channel_id=1, source_target_pairs={{0,4},{1,5},{2,6},{3,7},{4,0},{5,1},{6,2},{7,3},{8,12},{9,13},{10,... | collective-permute-start | bytes 1671176 | tf_op jit(solution)/shard_map/ppermute | solution.py:1007
  224.9 6.8 %collective-permute-start.20 = (f32[2,128,256]{2,1,0:T(8,128)S(1)}, f32[2,128,256]{2,1,0:T(8,128)S(1)}, u32[]{:S(2)}, u32[]{:S(2)}) collective-permute-start(f32[2,128,256]{2,1,0:T(8,128)S(1)} %get-tuple-element.304.refs_2_), channel_id=1, source_target_pairs={{0,2},{1,3},{2,0},{3,1},{4,6},{5,7},{6,4},{7,5},{8,10},{9,11},{10,... | collective-permute-start | bytes 786440 | tf_op jit(solution)/shard_map/ppermute | solution.py:1007
  224.9 39.4 %collective-permute-start.23 = (f32[2,2,128,256]{3,2,1,0:T(8,128)S(1)}, f32[2,2,128,256]{3,2,1,0:T(8,128)S(1)}, u32[]{:S(2)}, u32[]{:S(2)}) collective-permute-start(f32[2,2,128,256]{3,2,1,0:T(8,128)S(1)} %get-tuple-element.312.refs_2_), channel_id=1, source_target_pairs={{0,4},{1,5},{2,6},{3,7},{4,0},{5,1},{6,2},{7,3},{8,12},{9,13},{10,... | collective-permute-start | bytes 1572872 | tf_op jit(solution)/shard_map/ppermute | solution.py:1007
  225.1 36.1 %collective-permute-start.22 = (f32[2,128,256]{2,1,0:T(8,128)S(1)}, f32[2,128,256]{2,1,0:T(8,128)S(1)}, u32[]{:S(2)}, u32[]{:S(2)}) collective-permute-start(f32[2,128,256]{2,1,0:T(8,128)S(1)} %get-tuple-element.310), channel_id=1, source_target_pairs={{0,4},{1,5},{2,6},{3,7},{4,0},{5,1},{6,2},{7,3},{8,12},{9,13},{10,... | collective-permute-start | bytes 786440 | tf_op jit(solution)/shard_map/ppermute | solution.py:1007
  231.7 33.3 %collective-permute-start.24 = (f32[2,128,256]{2,1,0:T(8,128)S(1)}, f32[2,128,256]{2,1,0:T(8,128)S(1)}, u32[]{:S(2)}, u32[]{:S(2)}) collective-permute-start(f32[2,128,256]{2,1,0:T(8,128)S(1)} %get-tuple-element.314.refs_2_), channel_id=1, source_target_pairs={{0,8},{1,9},{2,10},{3,11},{4,12},{5,13},{6,14},{7,15},{8,0},{9,1},... | collective-permute-start | bytes 786440 | tf_op jit(solution)/shard_map/ppermute | solution.py:1007
  233.0 32.6 %collective-permute-start.25 = (f32[2,128,256]{2,1,0:T(8,128)S(1)}, f32[2,128,256]{2,1,0:T(8,128)S(1)}, u32[]{:S(2)}, u32[]{:S(2)}) collective-permute-start(f32[2,128,256]{2,1,0:T(8,128)S(1)} %get-tuple-element.317), channel_id=1, source_target_pairs={{0,1},{1,0},{2,3},{3,2},{4,5},{5,4},{6,7},{7,6},{8,9},{9,8},{10,11... | collective-permute-start | bytes 786440 | tf_op jit(solution)/shard_map/ppermute | solution.py:1007
  261.1 22.4 %collective-permute-start.30 = (f32[2,2,128,256]{3,2,1,0:T(8,128)S(1)}, f32[2,2,128,256]{3,2,1,0:T(8,128)S(1)}, u32[]{:S(2)}, u32[]{:S(2)}) collective-permute-start(f32[2,2,128,256]{3,2,1,0:T(8,128)S(1)} %get-tuple-element.329.refs_2_), channel_id=1, source_target_pairs={{0,1},{1,0},{2,3},{3,2},{4,5},{5,4},{6,7},{7,6},{8,9},{9,8},{10,11... | collective-permute-start | bytes 1572872 | tf_op jit(solution)/shard_map/ppermute | solution.py:1007
  267.1 10.0 %collective-permute-start.28 = (f32[2,136,256]{2,1,0:T(8,128)S(1)}, f32[2,136,256]{2,1,0:T(8,128)S(1)}, u32[]{:S(2)}, u32[]{:S(2)}) collective-permute-start(f32[2,136,256]{2,1,0:T(8,128)S(1)} %get-tuple-element.325), channel_id=1, source_target_pairs={{0,2},{1,3},{2,0},{3,1},{4,6},{5,7},{6,4},{7,5},{8,10},{9,11},{10,... | collective-permute-start | bytes 835592 | tf_op jit(solution)/shard_map/ppermute | solution.py:1007
  267.2 9.2 %collective-permute-start.27 = (f32[2,128,256]{2,1,0:T(8,128)S(1)}, f32[2,128,256]{2,1,0:T(8,128)S(1)}, u32[]{:S(2)}, u32[]{:S(2)}) collective-permute-start(f32[2,128,256]{2,1,0:T(8,128)S(1)} %get-tuple-element.322.refs_2_), channel_id=1, source_target_pairs={{0,8},{1,9},{2,10},{3,11},{4,12},{5,13},{6,14},{7,15},{8,0},{9,1},... | collective-permute-start | bytes 786440 | tf_op jit(solution)/shard_map/ppermute | solution.py:1007
  267.3 13.6 %collective-permute-start.29 = (f32[2,128,256]{2,1,0:T(8,128)S(1)}, f32[2,128,256]{2,1,0:T(8,128)S(1)}, u32[]{:S(2)}, u32[]{:S(2)}) collective-permute-start(f32[2,128,256]{2,1,0:T(8,128)S(1)} %get-tuple-element.327.refs_2_), channel_id=1, source_target_pairs={{0,4},{1,5},{2,6},{3,7},{4,0},{5,1},{6,2},{7,3},{8,12},{9,13},{10,... | collective-permute-start | bytes 786440 | tf_op jit(solution)/shard_map/ppermute | solution.py:1007
  277.9 16.1 %collective-permute-start.33 = (f32[2,136,256]{2,1,0:T(8,128)S(1)}, f32[2,136,256]{2,1,0:T(8,128)S(1)}, u32[]{:S(2)}, u32[]{:S(2)}) collective-permute-start(f32[2,136,256]{2,1,0:T(8,128)S(1)} %get-tuple-element.335.refs_2_), channel_id=1, source_target_pairs={{0,8},{1,9},{2,10},{3,11},{4,12},{5,13},{6,14},{7,15},{8,0},{9,1},... | collective-permute-start | bytes 835592 | tf_op jit(solution)/shard_map/ppermute | solution.py:1007
  277.9 14.8 %collective-permute-start.31 = (f32[2,128,256]{2,1,0:T(8,128)S(1)}, f32[2,128,256]{2,1,0:T(8,128)S(1)}, u32[]{:S(2)}, u32[]{:S(2)}) collective-permute-start(f32[2,128,256]{2,1,0:T(8,128)S(1)} %get-tuple-element.331.refs_2_), channel_id=1, source_target_pairs={{0,8},{1,9},{2,10},{3,11},{4,12},{5,13},{6,14},{7,15},{8,0},{9,1},... | collective-permute-start | bytes 786440 | tf_op jit(solution)/shard_map/ppermute | solution.py:1007
  280.9 12.5 %collective-permute-start.32 = (f32[2,128,256]{2,1,0:T(8,128)S(1)}, f32[2,128,256]{2,1,0:T(8,128)S(1)}, u32[]{:S(2)}, u32[]{:S(2)}) collective-permute-start(f32[2,128,256]{2,1,0:T(8,128)S(1)} %get-tuple-element.333.refs_2_), channel_id=1, source_target_pairs={{0,4},{1,5},{2,6},{3,7},{4,0},{5,1},{6,2},{7,3},{8,12},{9,13},{10,... | collective-permute-start | bytes 786440 | tf_op jit(solution)/shard_map/ppermute | solution.py:1007
  281.5 16.0 %collective-permute-start.34 = (f32[2,2,128,256]{3,2,1,0:T(8,128)S(1)}, f32[2,2,128,256]{3,2,1,0:T(8,128)S(1)}, u32[]{:S(2)}, u32[]{:S(2)}) collective-permute-start(f32[2,2,128,256]{3,2,1,0:T(8,128)S(1)} %get-tuple-element.337.refs_2_), channel_id=1, source_target_pairs={{0,2},{1,3},{2,0},{3,1},{4,6},{5,7},{6,4},{7,5},{8,10},{9,11},{10,... | collective-permute-start | bytes 1572872 | tf_op jit(solution)/shard_map/ppermute | solution.py:1007
  284.1 45.7 %collective-permute-start.38 = (f32[2,2,2,128,256]{4,3,2,1,0:T(8,128)S(1)}, f32[2,2,2,128,256]{4,3,2,1,0:T(8,128)S(1)}, u32[]{:S(2)}, u32[]{:S(2)}) collective-permute-start(f32[2,2,2,128,256]{4,3,2,1,0:T(8,128)S(1)} %get-tuple-element.345.refs_2_), channel_id=1, source_target_pairs={{0,4},{1,5},{2,6},{3,7},{4,0},{5,1},{6,2},{7,3},{8,12},{9,13},{10,... | collective-permute-start | bytes 3145736 | tf_op jit(solution)/shard_map/ppermute | solution.py:1007
  294.7 12.6 %collective-permute-start.36 = (f32[2,136,256]{2,1,0:T(8,128)S(1)}, f32[2,136,256]{2,1,0:T(8,128)S(1)}, u32[]{:S(2)}, u32[]{:S(2)}) collective-permute-start(f32[2,136,256]{2,1,0:T(8,128)S(1)} %get-tuple-element.341.refs_2_), channel_id=1, source_target_pairs={{0,2},{1,3},{2,0},{3,1},{4,6},{5,7},{6,4},{7,5},{8,10},{9,11},{10,... | collective-permute-start | bytes 835592 | tf_op jit(solution)/shard_map/ppermute | solution.py:1007
  297.5 9.2 %collective-permute-start.35 = (f32[2,128,256]{2,1,0:T(8,128)S(1)}, f32[2,128,256]{2,1,0:T(8,128)S(1)}, u32[]{:S(2)}, u32[]{:S(2)}) collective-permute-start(f32[2,128,256]{2,1,0:T(8,128)S(1)} %get-tuple-element.339.refs_2_), channel_id=1, source_target_pairs={{0,1},{1,0},{2,3},{3,2},{4,5},{5,4},{6,7},{7,6},{8,9},{9,8},{10,11... | collective-permute-start | bytes 786440 | tf_op jit(solution)/shard_map/ppermute | solution.py:1007
  308.0 24.1 %collective-permute-start.40 = (f32[2,2,136,256]{3,2,1,0:T(8,128)S(1)}, f32[2,2,136,256]{3,2,1,0:T(8,128)S(1)}, u32[]{:S(2)}, u32[]{:S(2)}) collective-permute-start(f32[2,2,136,256]{3,2,1,0:T(8,128)S(1)} %get-tuple-element.358.refs_2_), channel_id=1, source_target_pairs={{0,4},{1,5},{2,6},{3,7},{4,0},{5,1},{6,2},{7,3},{8,12},{9,13},{10,... | collective-permute-start | bytes 1671176 | tf_op jit(solution)/shard_map/ppermute | solution.py:1007
  308.1 14.9 %collective-permute-start.37 = (f32[2,2,128,256]{3,2,1,0:T(8,128)S(1)}, f32[2,2,128,256]{3,2,1,0:T(8,128)S(1)}, u32[]{:S(2)}, u32[]{:S(2)}) collective-permute-start(f32[2,2,128,256]{3,2,1,0:T(8,128)S(1)} %get-tuple-element.343.refs_2_), channel_id=1, source_target_pairs={{0,1},{1,0},{2,3},{3,2},{4,5},{5,4},{6,7},{7,6},{8,9},{9,8},{10,11... | collective-permute-start | bytes 1572872 | tf_op jit(solution)/shard_map/ppermute | solution.py:1007
  308.2 23.3 %collective-permute-start.39 = (f32[2,2,128,256]{3,2,1,0:T(8,128)S(1)}, f32[2,2,128,256]{3,2,1,0:T(8,128)S(1)}, u32[]{:S(2)}, u32[]{:S(2)}) collective-permute-start(f32[2,2,128,256]{3,2,1,0:T(8,128)S(1)} %get-tuple-element.356.refs_2_), channel_id=1, source_target_pairs={{0,2},{1,3},{2,0},{3,1},{4,6},{5,7},{6,4},{7,5},{8,10},{9,11},{10,... | collective-permute-start | bytes 1572872 | tf_op jit(solution)/shard_map/ppermute | solution.py:1007
  332.9 42.9 %collective-permute-start.45 = (f32[2,2,2,136,256]{4,3,2,1,0:T(8,128)S(1)}, f32[2,2,2,136,256]{4,3,2,1,0:T(8,128)S(1)}, u32[]{:S(2)}, u32[]{:S(2)}) collective-permute-start(f32[2,2,2,136,256]{4,3,2,1,0:T(8,128)S(1)} %get-tuple-element.363.refs_2_), channel_id=1, source_target_pairs={{0,1},{1,0},{2,3},{3,2},{4,5},{5,4},{6,7},{7,6},{8,9},{9,8},{10,11... | collective-permute-start | bytes 3342344 | tf_op jit(solution)/shard_map/ppermute | solution.py:1007
  332.9 26.7 %collective-permute-start.41 = (f32[2,2,2,128,256]{4,3,2,1,0:T(8,128)S(1)}, f32[2,2,2,128,256]{4,3,2,1,0:T(8,128)S(1)}, u32[]{:S(2)}, u32[]{:S(2)}) collective-permute-start(f32[2,2,2,128,256]{4,3,2,1,0:T(8,128)S(1)} %get-tuple-element.347.refs_2_), channel_id=1, source_target_pairs={{0,1},{1,0},{2,3},{3,2},{4,5},{5,4},{6,7},{7,6},{8,9},{9,8},{10,11... | collective-permute-start | bytes 3145736 | tf_op jit(solution)/shard_map/ppermute | solution.py:1007
  335.0 35.9 %collective-permute-start.42 = (f32[2,2,2,128,256]{4,3,2,1,0:T(8,128)S(1)}, f32[2,2,2,128,256]{4,3,2,1,0:T(8,128)S(1)}, u32[]{:S(2)}, u32[]{:S(2)}) collective-permute-start(f32[2,2,2,128,256]{4,3,2,1,0:T(8,128)S(1)} %get-tuple-element.352.refs_2_), channel_id=1, source_target_pairs={{0,1},{1,0},{2,3},{3,2},{4,5},{5,4},{6,7},{7,6},{8,9},{9,8},{10,11... | collective-permute-start | bytes 3145736 | tf_op jit(solution)/shard_map/ppermute | solution.py:1007
  335.0 37.5 %collective-permute-start.43 = (f32[2,2,2,128,256]{4,3,2,1,0:T(8,128)S(1)}, f32[2,2,2,128,256]{4,3,2,1,0:T(8,128)S(1)}, u32[]{:S(2)}, u32[]{:S(2)}) collective-permute-start(f32[2,2,2,128,256]{4,3,2,1,0:T(8,128)S(1)} %get-tuple-element.350.refs_2_), channel_id=1, source_target_pairs={{0,2},{1,3},{2,0},{3,1},{4,6},{5,7},{6,4},{7,5},{8,10},{9,11},{10,... | collective-permute-start | bytes 3145736 | tf_op jit(solution)/shard_map/ppermute | solution.py:1007
  335.1 39.0 %collective-permute-start.44 = (f32[2,2,2,128,256]{4,3,2,1,0:T(8,128)S(1)}, f32[2,2,2,128,256]{4,3,2,1,0:T(8,128)S(1)}, u32[]{:S(2)}, u32[]{:S(2)}) collective-permute-start(f32[2,2,2,128,256]{4,3,2,1,0:T(8,128)S(1)} %get-tuple-element.360.refs_2_), channel_id=1, source_target_pairs={{0,4},{1,5},{2,6},{3,7},{4,0},{5,1},{6,2},{7,3},{8,12},{9,13},{10,... | collective-permute-start | bytes 3145736 | tf_op jit(solution)/shard_map/ppermute | solution.py:1007

commit v4 on v3

--- a/solution.py
+++ b/solution.py
@@ -55,10 +55,22 @@
     return product[:half] + product[half:]
 
 
-def put_split(target, value):
-    high, low = split(value)
-    target[0] = high
-    target[1] = low
+def bands(rows, step=32):
+    return [slice(at, at + step) for at in range(0, rows, step)]
+
+
+def put_split(target, source, factor=None):
+    for band in bands(source.shape[0]):
+        high, low = split(source[band, :] if factor is None else source[band, :] * factor)
+        target[0, band, :] = high
+        target[1, band, :] = low
+
+
+def turned(target, source):
+    rows, cols = source.shape
+    for row in bands(rows, 128):
+        for col in bands(cols, 128):
+            target[col, row] = source[row, col].T
 
 
 def two_dots(left_side, right_side):
@@ -66,7 +78,7 @@
 
 
 def gelu_inner(value):
-    return jnp.tanh(GELU_A * (value + GELU_B * (value * value * value)))
+    return jnp.tanh(value * (GELU_A + (GELU_A * GELU_B) * (value * value)))
 
 
 def tile_of(numbers):
@@ -125,7 +137,7 @@
     received = streams.at[0, 0] if tick == 0 else refs[12]
     refs = refs[12 + (0 if tick == 0 else 11) :]
     (acts, sent, saved_s, saved_q, saved_k, saved_v, saved_o, saved_l, saved_m, saved_p, sums, _) = refs[:12]
-    (s_v, wq_v, wk_v, wv_v, wo_v, wi_v, wb_v, q_v, k_v, v_v, ot_v, l_v, m_v, p_v, a_v, t_v, bias_v, x_v, alphas_s, rows_v, in_sem, out_sem, row_sem) = refs[12:]
+    (s_v, wq_v, wk_v, wv_v, wo_v, wi_v, wb_v, q_v, k_v, v_v, ot_v, l_v, m_v, p_v, a_v, t_v, bias_v, x_v, w_v, c_v, h_v, alphas_s, rows_v, in_sem, out_sem, row_sem) = refs[12:]
     section = info[0]
     micro = tick - section
     rows = s_v.shape[0]
@@ -149,7 +161,7 @@
         small = fetch_rows(alphas, segments, valids, alphas_s, rows_v, row_sem)
         pltpu.make_async_copy(received, s_v, in_sem.at[6]).wait()
         start_all(loads[1:])
-        put_split(x_v, s_v[...])
+        put_split(x_v, s_v)
         for index, (weight, target) in enumerate(((wq_v, q_v), (wk_v, k_v), (wv_v, v_v))):
             loads[index].wait()
             value = two_dots(x_v, weight[...])
@@ -172,71 +184,94 @@
         store(v_v, saved_v.at[micro])
         made = {}
 
-        def scores_of(pair, qb):
-            lanes = pl.ds(pair * 128, 128)
+        def put_scores(index):
+            pair, qb = units[index]
+            lanes = slice(pair * 128, pair * 128 + 128)
             if pair not in made:
-                made.clear()
                 made[pair] = (three_lanes(k_v[:, lanes]), split(q_v[:, lanes]), split(v_v[:, lanes].T))
-            keys_cat, queries, values = made[pair]
-            qs = slice(qb * 128, qb * 128 + 128)
-            return pair_scores(keys_cat[: (qb + 1) * 128], queries[0][qs], queries[1][qs]), values
-
-        units = [(pair, qb) for pair in range(HEADS // 2) for qb in range(blocks)]
-        ahead = scores_of(*units[0])
-        for index, (pair, qb) in enumerate(units):
-            scores, (values_high, values_low) = ahead
-            if index + 1 < len(units):
-                ahead = scores_of(*units[index + 1])
+            keys_cat, queries, _ = made[pair]
             qs = slice(qb * 128, qb * 128 + 128)
             ks = (qb + 1) * 128
-            bias = bias_v[:ks, qs]
+            w_v[index % 2, :ks, :] = pair_scores(keys_cat[:ks], queries[0][qs], queries[1][qs])
+
+        units = [(pair, qb) for pair in range(HEADS // 2) for qb in range(blocks)]
+        put_scores(0)
+        for index, (pair, qb) in enumerate(units):
+            if index + 1 < len(units):
+                put_scores(index + 1)
+            values_high, values_low = made[pair][2]
+            qs = slice(qb * 128, qb * 128 + 128)
+            ks = (qb + 1) * 128
             for head in range(2):
-                part = scores[:, head * 128 : head * 128 + 128] + bias
-                top = jnp.max(part, axis=0, keepdims=True)
-                probs = jnp.exp(part - top)
-                total = jnp.sum(probs, axis=0, keepdims=True)
-                high, low = split(probs)
+                own = slice(head * 128, head * 128 + 128)
+                top = None
+                for band in bands(ks, 128):
+                    part = w_v[index % 2, band, own] + bias_v[band, qs]
+                    w_v[index % 2, band, own] = part
+                    most = jnp.max(part, axis=0, keepdims=True)
+                    top = most if top is None else jnp.maximum(top, most)
+                total = None
+                for band in bands(ks, 128):
+                    probs = jnp.exp(w_v[index % 2, band, own] - top)
+                    more = jnp.sum(probs, axis=0, keepdims=True)
+                    total = more if total is None else total + more
+                    high, low = split(probs)
+                    c_v[head, band, :128] = high
+                    c_v[head, band, 128:] = low
                 hs = slice(head * HEAD_DIM, head * HEAD_DIM + HEAD_DIM)
                 both = jnp.concatenate([values_high[hs, :ks], values_low[hs, :ks]], axis=0)
-                mixed = folded(dot(both, high)) + dot(values_high[hs, :ks], low)
+                mixed = folded(dot(both, c_v[head, :ks, :128])) + dot(values_high[hs, :ks], c_v[head, :ks, 128:])
                 at = slice(pair * 128 + head * HEAD_DIM, pair * 128 + head * HEAD_DIM + HEAD_DIM)
                 ot_v[at, qs] = mixed / total
                 l_v[pair, head : head + 1, qs] = top + jnp.log(total)
         store(ot_v, saved_o.at[micro])
         store(l_v, saved_l.at[micro])
-        put_split(x_v, ot_v[...].T)
+        turned(m_v, ot_v)
+        put_split(x_v, m_v)
         loads[3].wait()
-        attn = two_dots(x_v, wo_v[...]) * alphas_s[0, 0]
+        a_v[...] = two_dots(x_v, wo_v[...])
         valid_col = jnp.broadcast_to(valid_row, (128, rows)).T
-        weighting = jnp.concatenate([valid_col] * (D // 128), axis=1)
-        attn_sum = jnp.sum(attn * attn * weighting)
-        middle = s_v[...] + attn
-        m_v[...] = middle
+        attn_sum = jnp.zeros((32, D), jnp.float32)
+        for band in bands(rows):
+            attn = a_v[band, :] * alphas_s[0, 0]
+            attn_sum = attn_sum + attn * attn * jnp.concatenate([valid_col[band]] * (D // 128), axis=1)
+            middle = s_v[band, :] + attn
+            m_v[band, :] = middle
+            high, low = split(middle)
+            x_v[0, band, :] = high
+            x_v[1, band, :] = low
         store(m_v, saved_m.at[micro])
-        put_split(x_v, middle)
         loads[4].wait()
 
-        def before_of(part):
-            return two_dots(x_v, wi_v[:, part * 512 : part * 512 + 512])
-
-        ahead = before_of(0)
+        def put_before(part):
+            p_v[:, part * 512 : part * 512 + 512] = two_dots(x_v, wi_v[:, part * 512 : part * 512 + 512])
+
+        put_before(0)
         loads[5].wait()
         for part in range(parts):
             cols = slice(part * 512, part * 512 + 512)
-            before = ahead
-            p_v[:, cols] = before
             store(p_v.at[:, pl.ds(part * 512, 512)], saved_p.at[micro, :, pl.ds(part * 512, 512)])
             if part + 1 < parts:
-                ahead = before_of(part + 1)
-            high, low = split(0.5 * before * (1.0 + gelu_inner(before)))
-            more = dot(high, wb_v[cols, :]) + dot(low, wb_v[cols, :])
+                put_before(part + 1)
+            for band in bands(rows):
+                before = p_v[band, cols]
+                high, low = split(0.5 * before * (1.0 + gelu_inner(before)))
+                h_v[part % 2, 0, band, :] = high
+                h_v[part % 2, 1, band, :] = low
+            more = two_dots(h_v.at[part % 2], wb_v[cols, :])
             a_v[...] = a_v[...] + more if part else more
-        ffn = a_v[...] * alphas_s[0, 1]
-        result = m_v[...] + ffn
-        a_v[...] = result
+        result_sum = jnp.zeros((32, D), jnp.float32)
+        ffn_sum = jnp.zeros((32, D), jnp.float32)
+        for band in bands(rows):
+            weighting = jnp.concatenate([valid_col[band]] * (D // 128), axis=1)
+            ffn = a_v[band, :] * alphas_s[0, 1]
+            result = m_v[band, :] + ffn
+            a_v[band, :] = result
+            result_sum = result_sum + result * result * weighting
+            ffn_sum = ffn_sum + ffn * ffn * weighting
         store(a_v, sent)
         store(a_v, acts.at[micro])
-        t_v[...] = tile_of([jnp.sum(result * result * weighting), attn_sum, jnp.sum(ffn * ffn * weighting)])
+        t_v[...] = tile_of([jnp.sum(result_sum), jnp.sum(attn_sum), jnp.sum(ffn_sum)])
         store(t_v, sums.at[micro])
         wait_all(stores)
 
@@ -285,6 +320,7 @@
     scratch += [vmem((rows, width), f32)] * 3 + [vmem((width, rows), f32), vmem((HEADS // 2, 8, rows), f32)]
     scratch += [vmem((rows, width), f32), vmem((rows, inner), f32), vmem((rows, width), f32)]
     scratch += [vmem((8, 128), f32), vmem((rows, rows), f32), vmem((2, rows, width), bf16)]
+    scratch += [vmem((2, rows, 256), f32), vmem((2, rows, 256), bf16), vmem((2, 2, rows, 512), bf16)]
     scratch += [pltpu.SMEM(alphas.shape, f32), vmem((2,) + segments.shape, jnp.int32)]
     scratch += [dma((7,)), dma((10 + inner // 512,)), dma((3,))]
     outs = pl.pallas_call(
@@ -359,7 +395,7 @@
     info, alphas = refs[:2]
     upstreams, targets, saved_p = refs[2:4], refs[4], refs[5]
     slots, refs = refs[7 : 7 + count], refs[8 + count :]
-    g_v, gh_v, p_v, w_v, in_sem, out_sem = refs
+    g_v, gh_v, p_v, h_v, w_v, in_sem, out_sem = refs
     parts = p_v.shape[0]
     rows = g_v.shape[1]
 
@@ -384,23 +420,26 @@
         pltpu.make_async_copy(targets.at[micro, 0], g_v.at[micro], in_sem.at[parts, micro]).wait()
     for part in range(1, parts):
         start_all([load(part, micro) for micro in range(2)])
-    high, low = split(jnp.concatenate([g_v[0], g_v[1]], axis=0) * alphas[0, 1])
-    gh_v[0] = high
-    gh_v[1] = low
-
-    def left_of(part):
+    for micro in range(2):
+        put_split(gh_v.at[:, pl.ds(micro * rows, rows)], g_v.at[micro], alphas[0, 1])
+
+    def put_left(part):
         for micro in range(2):
             load(part, micro).wait()
-        before = p_v[part].T
-        return split(0.5 * before * (1.0 + gelu_inner(before)))
+        for row in bands(2 * rows, 128):
+            for col in bands(512, 128):
+                before = p_v[part, row, col].T
+                high, low = split(0.5 * before * (1.0 + gelu_inner(before)))
+                h_v[part % 2, 0, col, row] = high
+                h_v[part % 2, 1, col, row] = low
 
     stores = []
-    ahead = left_of(0)
+    put_left(0)
     for part in range(parts):
-        high, low = ahead
         if part + 1 < parts:
-            ahead = left_of(part + 1)
-        put_part(w_v, part, three_dots(high, low, gh_v[0], gh_v[1]))
+            put_left(part + 1)
+        left = h_v.at[part % 2]
+        put_part(w_v, part, three_dots(left[0], left[1], gh_v[0], gh_v[1]))
         stores += start_all(slot_copies(info, sizes, axes, w_v, slots, out_sem, part))
     wait_all(stores)
 
@@ -416,7 +455,7 @@
     (g_v, p_v, wi_v, wb_v, gs_v, d_v, b_v) = refs[7:14]
     held = refs[14:19]
     weights_v = refs[19:23]
-    (bias_v, do_v, dt_v, dl_v, qt_v, dk_v, dv_v, x_v, f_v, y_v, t_v, alphas_s, rows_v, in_sem, part_sem, w_sem, out_sem, row_sem) = refs[23:]
+    (bias_v, do_v, dt_v, dl_v, qt_v, dk_v, dv_v, x_v, f_v, y_v, t_v, h_v, s_v, c_v, alphas_s, rows_v, in_sem, part_sem, w_sem, out_sem, row_sem) = refs[23:]
     parts = p_v.shape[0]
     rows = bias_v.shape[0]
     blocks = rows // 128
@@ -456,54 +495,56 @@
             start_all(loads(part))
         start_all(fetches[::-1])
         start_all(later)
-        gs_v[...] = stacked(g_v[...] * alphas_s[0, 1])
-
-        def hidden_of(part):
+        put_split(gs_v, g_v, alphas_s[0, 1])
+
+        def put_hidden(part):
             wait_all(loads(part))
-            return folded(dot_rows(gs_v[...], wb_v[part]))
-
-        total_inner = jnp.float32(0.0)
-        ahead = hidden_of(0)
+            h_v[part % 2] = dot_rows(gs_v[0], wb_v[part]) + dot_rows(gs_v[1], wb_v[part])
+
+        inner_sum = jnp.zeros((32, 512), jnp.float32)
+        put_hidden(0)
         for part in range(parts):
             cols = slice(part * 512, part * 512 + 512)
-            grad_hidden = ahead
             if part + 1 < parts:
-                ahead = hidden_of(part + 1)
-            before = p_v[part]
-            inner = gelu_inner(before)
-            above = 0.5 * (1.0 + inner)
-            total_inner = total_inner + jnp.sum(grad_hidden * (before * above))
-            slope = above + 0.5 * before * (1.0 - inner * inner) * (GELU_A * (1.0 + 3.0 * GELU_B * (before * before)))
-            high, low = split(grad_hidden * slope)
-            b_v[0, :, cols] = high
-            b_v[1, :, cols] = low
-            more = folded(dot_rows(jnp.concatenate([high, low], axis=0), wi_v[part]))
+                put_hidden(part + 1)
+            for band in bands(rows):
+                grad_hidden = h_v[part % 2, band, :]
+                before = p_v[part, band, :]
+                square = before * before
+                inner = jnp.tanh(before * (GELU_A + (GELU_A * GELU_B) * square))
+                above = 0.5 + 0.5 * inner
+                inner_sum = inner_sum + grad_hidden * (before * above)
+                slope = above + before * (1.0 - inner * inner) * (0.5 * GELU_A + (1.5 * GELU_A * GELU_B) * square)
+                high, low = split(grad_hidden * slope)
+                b_v[0, band, cols] = high
+                b_v[1, band, cols] = low
+            more = dot_rows(b_v[0, :, cols], wi_v[part]) + dot_rows(b_v[1, :, cols], wi_v[part])
             d_v[...] = d_v[...] + more if part else more
+        total_inner = jnp.sum(inner_sum)
         stores = start_all([pltpu.make_async_copy(b_v, befores.at[micro], out_sem.at[0])])
-        middle = g_v[...] + d_v[...]
-        d_v[...] = middle
-        high, low = split(middle * alphas_s[0, 0])
-        f_v[0] = high
-        f_v[1] = low
+        for band in bands(rows):
+            middle = g_v[band, :] + d_v[band, :]
+            d_v[band, :] = middle
+            high, low = split(middle * alphas_s[0, 0])
+            f_v[0, band, :] = high
+            f_v[1, band, :] = low
         stores += start_all([pltpu.make_async_copy(f_v, firsts.at[micro], out_sem.at[1])])
         wait_all(fetches)
         wait_all(later)
-        grad_mixed = folded(dot_rows(jnp.concatenate([high, low], axis=0), wo_v[...]))
-        do_v[...] = grad_mixed
-        dt_v[...] = grad_mixed.T
+        do_v[...] = dot_rows(f_v[0], wo_v[...]) + dot_rows(f_v[1], wo_v[...])
+        turned(dt_v, do_v)
         total_mixed = jnp.float32(0.0)
         for head in range(HEADS):
             hs = slice(head * HEAD_DIM, head * HEAD_DIM + HEAD_DIM)
             spread = jnp.sum(dt_v[hs, :] * o_v[hs, :], axis=0, keepdims=True)
             dl_v[head // 2, head % 2 : head % 2 + 1, :] = spread
             total_mixed = total_mixed + jnp.sum(spread)
-
         made = {}
 
-        def products_of(pair, qb):
+        def put_products(index):
+            pair, qb = units[index]
             lanes = slice(pair * 128, pair * 128 + 128)
             if pair not in made:
-                made.clear()
                 keys = k_v[:, lanes]
                 made[pair] = (
                     three_lanes(keys),
@@ -512,57 +553,58 @@
                     split(do_v[:, lanes]),
                     split(keys.T),
                 )
-            keys_cat, values_cat, queries, mixed, turned = made[pair]
+            keys_cat, values_cat, queries, mixed, _ = made[pair]
             qs = slice(qb * 128, qb * 128 + 128)
             ks = (qb + 1) * 128
-            scores = pair_scores(keys_cat[:ks], queries[0][qs], queries[1][qs])
-            slopes = pair_scores(values_cat[:ks], mixed[0][qs], mixed[1][qs])
-            return scores, slopes, queries, mixed, turned
-
-        def product(left_high, left_low, right_high, right_low):
-            left_cat = jnp.concatenate([left_high, left_low], axis=1)
+            s_v[index % 2, 0, :ks, :] = pair_scores(keys_cat[:ks], queries[0][qs], queries[1][qs])
+            s_v[index % 2, 1, :ks, :] = pair_scores(values_cat[:ks], mixed[0][qs], mixed[1][qs])
+
+        def product(left_cat, right_high, right_low):
             above = jnp.concatenate([right_high, right_low], axis=1)
             below = jnp.concatenate([right_high, jnp.zeros_like(right_high)], axis=1)
             value = dot(left_cat, jnp.concatenate([above, below], axis=0))
             return value[:, :128] + value[:, 128:]
 
         units = [(pair, qb) for pair in range(HEADS // 2) for qb in range(blocks - 1, -1, -1)]
-        for pair, qb in units:
-            scores, slopes, queries, mixed, turned = products_of(pair, qb)
+        put_products(0)
+        for index, (pair, qb) in enumerate(units):
+            if index + 1 < len(units):
+                put_products(index + 1)
+            _, _, queries, mixed, keys_turned = made[pair]
             lanes = slice(pair * 128, pair * 128 + 128)
             qs = slice(qb * 128, qb * 128 + 128)
             ks = (qb + 1) * 128
-            bias = bias_v[:ks, qs]
             sides = [halves_of(x[qs]) for x in queries + mixed]
-            key_part, value_part = None, None
             for head in range(2):
                 own = slice(head * 128, head * 128 + 128)
                 at = slice(head, head + 1)
-                probs = jnp.exp((scores[:, own] + bias) - l_v[pair, at, qs])
-                grads = probs * (slopes[:, own] - dl_v[pair, at, qs])
+                for band in bands(ks, 128):
+                    probs = jnp.exp((s_v[index % 2, 0, band, own] + bias_v[band, qs]) - l_v[pair, at, qs])
+                    grads = probs * (s_v[index % 2, 1, band, own] - dl_v[pair, at, qs])
+                    for place, value in enumerate((probs, grads)):
+                        high, low = split(value)
+                        c_v[head, place, band, :128] = high
+                        c_v[head, place, band, 128:] = low
                 q_high, q_low, d_high, d_low = [side[head] for side in sides]
-                from_values = product(*split(probs), d_high, d_low)
-                high, low = split(grads)
-                from_keys = product(high, low, q_high, q_low)
-                value_part = from_values if head == 0 else value_part + from_values
-                key_part = from_keys if head == 0 else key_part + from_keys
+                from_values = product(c_v[head, 0, :ks, :], d_high, d_low)
+                from_keys = product(c_v[head, 1, :ks, :], q_high, q_low)
+                if qb == blocks - 1 and head == 0:
+                    dv_v[:, lanes] = from_values
+                    dk_v[:, lanes] = from_keys
+                else:
+                    dv_v[:ks, lanes] += from_values
+                    dk_v[:ks, lanes] += from_keys
                 hs = slice(head * HEAD_DIM, head * HEAD_DIM + HEAD_DIM)
-                both = jnp.concatenate([turned[0][hs, :ks], turned[1][hs, :ks]], axis=0)
-                back = folded(dot(both, high)) + dot(turned[0][hs, :ks], low)
+                both = jnp.concatenate([keys_turned[0][hs, :ks], keys_turned[1][hs, :ks]], axis=0)
+                back = folded(dot(both, c_v[head, 1, :ks, :128])) + dot(keys_turned[0][hs, :ks], c_v[head, 1, :ks, 128:])
                 qt_v[pair * 128 + head * HEAD_DIM : pair * 128 + head * HEAD_DIM + HEAD_DIM, qs] = back * 0.125
-            if qb == blocks - 1:
-                dk_v[:, lanes] = key_part
-                dv_v[:, lanes] = value_part
-            else:
-                dk_v[:ks, lanes] += key_part
-                dv_v[:ks, lanes] += value_part
+
+        turned(do_v, qt_v)
         result = d_v[...]
-        for index, (source, weight) in enumerate(((qt_v, wq_v), (dk_v, wk_v), (dv_v, wv_v))):
-            value = source[...].T if index == 0 else source[...]
-            high, low = split(value)
-            x_v[0, :, pl.ds(index * D, D)] = high
-            x_v[1, :, pl.ds(index * D, D)] = low
-            result = result + folded(dot_rows(jnp.concatenate([high, low], axis=0), weight[...]))
+        for index, (source, weight) in enumerate(((do_v, wq_v), (dk_v, wk_v), (dv_v, wv_v))):
+            cols = pl.ds(index * D, D)
+            put_split(x_v.at[:, :, cols], source)
+            result = result + dot_rows(x_v[0, :, cols], weight[...]) + dot_rows(x_v[1, :, cols], weight[...])
         y_v[...] = result
         t_v[...] = tile_of([total_mixed / alphas_s[0, 0], total_inner / alphas_s[0, 1]])
         stores += start_all(
@@ -609,9 +651,14 @@
 def turn_left(target, source, transpose):
     rows = target.shape[2] // 2
     for micro in range(2):
-        high, low = split(source[micro].T if transpose else source[micro])
-        target[0, :, micro * rows : (micro + 1) * rows] = high
-        target[1, :, micro * rows : (micro + 1) * rows] = low
+        for row in bands(source.shape[1], 128):
+            for col in bands(source.shape[2], 128):
+                value = source[micro, row, col]
+                high, low = split(value.T if transpose else value)
+                lines, lanes = (col, row) if transpose else (row, col)
+                lanes = slice(micro * rows + lanes.start, micro * rows + lanes.stop)
+                target[0, lines, lanes] = high
+                target[1, lines, lanes] = low
 
 
 def attention_body(count, sizes, axes, *refs):
@@ -703,6 +750,7 @@
         vmem((micros, rows, D), f32),
         vmem((2, micros * rows, D), bf16),
         vmem((parts, micros * rows, 512), f32),
+        vmem((2, 2, 512, micros * rows), bf16),
         vmem(unit_shape(sizes), f32),
         dma((parts + 1, 2)),
         dma((parts, copy_count(sizes, axes))),
@@ -781,7 +829,7 @@
         vmem((parts, rows, 512), f32),
         vmem((parts, D, 512), bf16),
         vmem((parts, 512, D), bf16),
-        vmem((2 * rows, D), bf16),
+        vmem((2, rows, D), bf16),
         vmem((rows, D), f32),
         vmem((2, rows, inner), bf16),
     ]
@@ -798,6 +846,9 @@
         vmem((2, rows, D), bf16),
         vmem((rows, D), f32),
         vmem((8, 128), f32),
+        vmem((2, rows, 512), f32),
+        vmem((2, 2, rows, 256), f32),
+        vmem((2, 2, rows, 256), bf16),
         pltpu.SMEM(alphas.shape, f32),
         vmem((2,) + segments.shape, jnp.int32),
         dma((6,)),
@@ -831,7 +882,7 @@
         scratch_shapes=scratch,
         input_output_aliases={len(inputs) + i: i for i in range(len(placed))},
         compiler_params=pltpu.CompilerParams(vmem_limit_bytes=12 * 1024 * 1024),
-        cost_estimate=pl.CostEstimate(flops=10**6, bytes_accessed=6 * 10**6, transcendentals=0),
+        cost_estimate=pl.CostEstimate(flops=10**10, bytes_accessed=10**8, transcendentals=0),
         name=name,
     )(*inputs, *in_hbm(placed))
     TOKEN[0] = results[-1]
@@ -895,7 +946,7 @@
     return local_call(body, "place_step", info, arrays, [out], [pltpu.SemaphoreType.DMA((count,))])[0]
 
 
-def out_copies(sizes, axis, info, kind, half, sources, outs, sem):
+def out_copies(sizes, axis, info, kind, half, sources, outs, stage, sem):
     x, y, near, far = sizes
     rows = unit_shape(sizes)[3]
     depth = near * far // 4
@@ -903,7 +954,9 @@
     copies = []
 
     def put(source, target):
-        copies.append(pltpu.make_async_copy(source, target, sem.at[len(copies)]))
+        at = len(copies)
+        load = pltpu.make_async_copy(source, stage.at[at], sem.at[0, at])
+        copies.append((load, pltpu.make_async_copy(stage.at[at], target, sem.at[1, at])))
 
     for by, piece in sources:
         place = lax.rem(info[1 + axis] + count - by, count)
@@ -931,7 +984,17 @@
                 put(source, out.at[inside, place, :, :, lanes])
             else:
                 put(source, out.at[inside, :, :, :, lanes])
-    return copies
+    start_all([load for load, _ in copies])
+    for load, store in copies:
+        load.wait()
+        store.start()
+    return [store for _, store in copies]
+
+
+def out_scratch(sizes, axis, shape, pieces):
+    rows, count = unit_shape(sizes)[3], pieces * (sizes[3] if axis == 2 else sizes[2] * sizes[3])
+    inner = shape[1:3] if axis == 2 else shape[2:3]
+    return [pltpu.VMEM((count, *inner, rows, shape[-1]), jnp.float32), pltpu.SemaphoreType.DMA((2, count))]
 
 
 def out_shapes(sizes, kind):
@@ -947,9 +1010,9 @@
 
 def own_stage(sizes, axis, info, whole, kind, half, placed):
     def body(info, ins, outs, scratch):
-        wait_all(start_all(out_copies(sizes, axis, info, kind, half, [(0, ins[0])], outs, scratch[0])))
-
-    scratch = [pltpu.SemaphoreType.DMA((sizes[2] * sizes[3],))]
+        wait_all(out_copies(sizes, axis, info, kind, half, [(0, ins[0])], outs, *scratch))
+
+    scratch = out_scratch(sizes, axis, whole.shape, 1)
     return local_call(body, "place_own", info, [whole], out_shapes(sizes, kind), scratch, None, placed)
 
 
@@ -957,25 +1020,24 @@
     rows = unit_shape(sizes)[3]
     count = sizes[axis]
     shapes, specs = out_shapes(sizes, kind), None
-    scratch = [pltpu.SemaphoreType.DMA((sizes[2] * sizes[3] * count + 1,))]
+    scratch = out_scratch(sizes, axis, arrays[0].shape, count - 1)
     has_small = arrays[0].shape[3] > rows
     if has_small:
         specs = [ANY] * len(shapes) + [LOCAL] * 2
         shapes += [loose(1, 2), loose(1, 3)]
-        scratch += [pltpu.VMEM((8, 256), jnp.float32)]
+        scratch += [pltpu.VMEM((8, 256), jnp.float32), pltpu.SemaphoreType.DMA((1,))]
 
     def body(info, ins, outs, scratch):
-        sem = scratch[0]
         sources = [(by, ins[by]) for by in range(1, count)]
-        copies = start_all(out_copies(sizes, axis, info, kind, half, sources, outs, sem))
+        copies = out_copies(sizes, axis, info, kind, half, sources, outs, *scratch[:2])
         if has_small:
-            tile_v = scratch[1]
+            tile_v, sem = scratch[2:]
             for by in range(count):
 
                 @pl.when(info[1 + axis] == by)
                 def _():
                     source = ins[by].at[0, 0, 0, pl.ds(rows, 8), pl.ds(0, 256)]
-                    copy = pltpu.make_async_copy(source, tile_v, sem.at[len(copies)])
+                    copy = pltpu.make_async_copy(source, tile_v, sem.at[0])
                     copy.start()
                     copy.wait()
 

time: 384 us -> 333 us (0.87)
  waiting for transfers between devices: 169 us -> 115 us
    ppermute x42, waiting for transfers between devices: 144 us -> 90.7 us  [shifted(): return lax.ppermute(value, 'dp', pairs)]
  transfers between devices with their start and end apart: 46 -> 46, of which waited for: 19 -> 22; matrix products, arithmetic and copies ran while one was open for 0% -> 0% of each run, Pallas kernels for 16% -> 23%
where the time goes in v4:
time: 333 us; the launch traced here: 327 us
  Pallas kernels  151 us (45%)
  waiting for transfers between devices  115 us (35%)
  starting transfers between devices  58.2 us (17%)
    ppermute x42, waiting for transfers between devices, shifted(): return lax.ppermute(value, 'dp', pairs)  90.7 us
    pallas_call x6, Pallas kernels, call(): pl.pallas_call(functools.partial(body, len(extra)), out_shape=outs + [loo...  66.5 us
    ppermute x42, starting transfers between devices, shifted(): return lax.ppermute(value, 'dp', pairs)  52.2 us
    pallas_call x48, Pallas kernels, local_call(): pl.pallas_call(parted, out_shape=list(outs) + [loose(8, 128)], in_specs=[...  48.9 us
    pallas_call x3, Pallas kernels, forward_tick(): pl.pallas_call(functools.partial(forward_body, tick), out_shape=shapes, i...  35.9 us
    ppermute x2, waiting for transfers between devices, shards(): upstreams.append(lax.ppermute(sent, 'section', [(1, 0)]))  22.6 us
  transfers between devices with their start and end apart: 46, of which 22 were waited for; matrix products, arithmetic and copies ran while one was open for 0% of the time, Pallas kernels for 23%

profile of v4, /device:TPU:0, one launch (start us, length us, event | category | flops | bytes accessed | tf_op | source)
XLA Modules:
  0.0 326.8 jit_solution(9313657534712563193)
XLA Ops:
  0.8 13.1 %layer_forward.3 = (f32[2,384,512]{2,1,0:T(8,128)}, f32[384,512]{1,0:T(8,128)}, f32[2,384,512]{2,1,0:T(8,128)}, f32[2,384,512]{2,1,0:T(8,128)}, f32[2,384,512]{2...) custom-call(s32[5]{0:T(128)S(1)} %stack.23.refs_0_, ...), custom_call_target="tpu_custom_call" | custom-call | flops 10000000000 | bytes 20000000 | tf_op jit(solution)/shard_map/layer_forward/pallas_call | solution.py:326
  13.9 1.3 collective-permute-start
  15.3 2.1 collective-permute-done.refs_12_
  17.3 13.3 %layer_forward.4 = (f32[2,384,512]{2,1,0:T(8,128)}, f32[384,512]{1,0:T(8,128)}, f32[2,384,512]{2,1,0:T(8,128)}, f32[2,384,512]{2,1,0:T(8,128)}, f32[2,384,512]{2...) custom-call(s32[5]{0:T(128)S(1)} %stack.23.refs_0_, ...), custom_call_target="tpu_custom_call", output_to_operand_aliasing={{0}: (13, {}), {2}: (14, {}), {3}: (15, {}), {4}: (16, {}),... | custom-call | flops 10000000000 | bytes 20000000 | tf_op jit(solution)/shard_map/layer_forward/pallas_call | solution.py:326
  30.7 2.0 collective-permute-start.1
  34.9 9.5 %layer_forward.5 = (f32[2,384,512]{2,1,0:T(8,128)}, f32[384,512]{1,0:T(8,128)}, f32[2,384,512]{2,1,0:T(8,128)}, f32[2,384,512]{2,1,0:T(8,128)}, f32[2,384,512]{2...) custom-call(s32[5]{0:T(128)S(1)} %stack.23.refs_0_, ...), custom_call_target="tpu_custom_call", output_to_operand_aliasing={{0}: (13, {}), {2}: (14, {}), {3}: (15, {}), {4}: (16, {}),... | custom-call | flops 10000000000 | bytes 20000000 | tf_op jit(solution)/shard_map/layer_forward/pallas_call | solution.py:326
  44.3 9.0 %collective-permute-done.2.refs_1_.refs_2_ = f32[384,512]{1,0:T(8,128)S(1)} collective-permute-done((f32[384,512]{1,0:T(8,128)}, f32[384,512]{1,0:T(8,128)S(1)}, u32[]{:S(2)}, u32[]{:S(2)}) %collective-permute-start.2) | collective-permute-done | bytes 786464 | tf_op jit(solution)/shard_map/ppermute | solution.py:1127
  53.3 17.6 %grad_chain.4 = (bf16[2,2,384,2048]{3,2,1,0:T(8,128)(2,1)}, bf16[2,2,384,1536]{3,2,1,0:T(8,128)(2,1)}, bf16[2,2,384,512]{3,2,1,0:T(8,128)(2,1)}, f32[2,384,512]{...) custom-call(s32[5]{0:T(128)S(1)} %stack.23.refs_0_, ...), custom_call_target="tpu_custom_call", output_to_operand_aliasing={{0}: (19, {}), {1}: (20, {}), {2}: (21, {}), {3}: (22, {}),... | custom-call | flops 20000000000 | bytes 20000000 | tf_op jit(solution)/shard_map/grad_chain/pallas_call | solution.py:728
  72.2 13.6 %collective-permute-done.3.refs_1_.refs_3_ = f32[384,512]{1,0:T(8,128)S(1)} collective-permute-done((f32[384,512]{1,0:T(8,128)}, f32[384,512]{1,0:T(8,128)S(1)}, u32[]{:S(2)}, u32[]{:S(2)}) %collective-permute-start.3) | collective-permute-done | bytes 786464 | tf_op jit(solution)/shard_map/ppermute | solution.py:1127
  85.9 18.2 %grad_chain.5 = (bf16[2,2,384,2048]{3,2,1,0:T(8,128)(2,1)}, bf16[2,2,384,1536]{3,2,1,0:T(8,128)(2,1)}, bf16[2,2,384,512]{3,2,1,0:T(8,128)(2,1)}, f32[2,384,512]{...) custom-call(s32[5]{0:T(128)S(1)} %stack.23.refs_0_, ...), custom_call_target="tpu_custom_call", output_to_operand_aliasing={{0}: (19, {}), {1}: (20, {}), {2}: (21, {}), {3}: (22, {}),... | custom-call | flops 20000000000 | bytes 20000000 | tf_op jit(solution)/shard_map/grad_chain/pallas_call | solution.py:728
  104.1 10.2 %grad_back.1 = (f32[2,2,2,128,256]{4,3,2,1,0:T(8,128)}, f32[2,2,2,128,256]{4,3,2,1,0:T(8,128)}, f32[2,2,2,128,256]{4,3,2,1,0:T(8,128)}, f32[2,2,2,128,256]{4,3,2,1,0:T(8,128)}, f32[8,128]{1,0:T(8,128)S(1)}) custom-call(s32[5]{0:T(128)S(1)} %stack.23.refs_0_, f32[1,2]{1,0:T(1,128)S(1)} %copy-done.1, f32[384,512]{1,0:T(8,128)S(1)} %collective-permute-done.2.refs_1_.refs_2_, ...), custom_call_target="tpu_custom_call" | custom-call | flops 5000000000 | bytes 20000000 | tf_op jit(solution)/shard_map/grad_back/pallas_call | solution.py:728
  114.3 3.1 collective-permute-start.4
  117.4 1.5 collective-permute-start.5
  118.9 9.8 %grad_inner.1 = (f32[2,2,2,128,256]{4,3,2,1,0:T(8,128)}, f32[2,2,2,128,256]{4,3,2,1,0:T(8,128)}, f32[2,2,2,128,256]{4,3,2,1,0:T(8,128)}, f32[2,2,2,128,256]{4,3,2,1,0:T(8,128)}, f32[8,128]{1,0:T(8,128)S(1)}) custom-call(s32[5]{0:T(128)S(1)} %stack.23.refs_0_, f32[2,384,512]{2,1,0:T(8,128)} %get-tuple-element.253.refs_1_, ...), custom_call_target="tpu_custom_call" | custom-call | flops 5000000000 | bytes 20000000 | tf_op jit(solution)/shard_map/grad_inner/pallas_call | solution.py:728
  128.7 8.0 %collective-permute-done.4.refs_3_ = f32[2,2,2,128,256]{4,3,2,1,0:T(8,128)S(1)} collective-permute-done((f32[2,2,2,128,256]{4,3,2,1,0:T(8,128)}, f32[2,2,2,128,256]{4,3,2,1,0:T(8,128)S(1)}, u32[]{:S(2)}, u32[]{:S(2)}) %collective-permute-start.4) | collective-permute-done | bytes 1048608 | tf_op jit(solution)/shard_map/ppermute | solution.py:1069
  138.8 2.3 collective-permute-start.6
  141.2 1.5 collective-permute-start.11
  142.9 1.5 collective-permute-start.7
  144.4 9.9 %grad_attention.1 = (f32[2,2,2,136,256]{4,3,2,1,0:T(8,128)}, f32[2,2,2,136,256]{4,3,2,1,0:T(8,128)}, f32[2,2,2,128,256]{4,3,2,1,0:T(8,128)}, f32[2,2,2,128,256]{4,3,2,1,0:T(8,128)}, f32[8,128]{1,0:T(8,128)S(1)}) custom-call(s32[5]{0:T(128)S(1)} %stack.23.refs_0_, s32[2,1,384]{2,1,0:T(1,128)S(1)} %copy-done, f32[2,384,512]{2,1,0:T(8,128)} %get-tuple-element.248.refs_2_, ...), custom_call_target="tpu_custom_call" | custom-call | flops 5000000000 | bytes 20000000 | tf_op jit(solution)/shard_map/grad_attention/pallas_call | solution.py:728
  154.9 1.5 collective-permute-start.19
  159.0 8.0 %collective-permute-done.8.refs_3_ = f32[2,128,256]{2,1,0:T(8,128)S(1)} collective-permute-done((f32[2,128,256]{2,1,0:T(8,128)S(1)}, f32[2,128,256]{2,1,0:T(8,128)S(1)}, u32[]{:S(2)}, u32[]{:S(2)}) %collective-permute-start.8) | collective-permute-done | bytes 262176 | tf_op jit(solution)/shard_map/ppermute | solution.py:1069
  168.2 5.2 %collective-permute-done.9.refs_3_ = f32[2,128,256]{2,1,0:T(8,128)S(1)} collective-permute-done((f32[2,128,256]{2,1,0:T(8,128)S(1)}, f32[2,128,256]{2,1,0:T(8,128)S(1)}, u32[]{:S(2)}, u32[]{:S(2)}) %collective-permute-start.9) | collective-permute-done | bytes 262176 | tf_op jit(solution)/shard_map/ppermute | solution.py:1069
  173.4 2.6 collective-permute-start.14
  176.7 4.1 %collective-permute-done.10.refs_3_ = f32[2,2,2,128,256]{4,3,2,1,0:T(8,128)S(1)} collective-permute-done((f32[2,2,2,128,256]{4,3,2,1,0:T(8,128)}, f32[2,2,2,128,256]{4,3,2,1,0:T(8,128)S(1)}, u32[]{:S(2)}, u32[]{:S(2)}) %collective-permute-start.10) | collective-permute-done | bytes 1048608 | tf_op jit(solution)/shard_map/ppermute | solution.py:1069
  180.7 2.6 collective-permute-start.13
  185.7 8.5 %collective-permute-done.12.refs_3_ = f32[2,2,128,256]{3,2,1,0:T(8,128)S(1)} collective-permute-done((f32[2,2,128,256]{3,2,1,0:T(8,128)S(1)}, f32[2,2,128,256]{3,2,1,0:T(8,128)S(1)}, u32[]{:S(2)}, u32[]{:S(2)}) %collective-permute-start.12) | collective-permute-done | bytes 524320 | tf_op jit(solution)/shard_map/ppermute | solution.py:1069
  196.7 1.5 collective-permute-start.18
  198.8 1.8 collective-permute-start.16
  201.4 6.6 %collective-permute-done.16.refs_3_ = f32[2,128,256]{2,1,0:T(8,128)S(1)} collective-permute-done((f32[2,128,256]{2,1,0:T(8,128)S(1)}, f32[2,128,256]{2,1,0:T(8,128)S(1)}, u32[]{:S(2)}, u32[]{:S(2)}) %collective-permute-start.16) | collective-permute-done | bytes 262176 | tf_op jit(solution)/shard_map/ppermute | solution.py:1069
  208.0 1.4 collective-permute-start.21
  211.8 1.4 collective-permute-start.24
  216.2 4.1 %collective-permute-start.30 = (f32[2,2,128,256]{3,2,1,0:T(8,128)S(1)}, f32[2,2,128,256]{3,2,1,0:T(8,128)S(1)}, u32[]{:S(2)}, u32[]{:S(2)}) collective-permute-start(f32[2,2,128,256]{3,2,1,0:T(8,128)S(1)} %get-tuple-element.329.refs_2_), channel_id=1, source_target_pairs={{0,1},{1,0},{2,3},{3,2},{4,5},{5,4},{6,7},{7,6},{8,9},{9,8},{10,11... | collective-permute-start | bytes 1572872 | tf_op jit(solution)/shard_map/ppermute | solution.py:1069
  221.6 3.3 collective-permute-done.22.refs_3_
  226.2 7.8 %collective-permute-done.23.refs_3_ = f32[2,2,128,256]{3,2,1,0:T(8,128)S(1)} collective-permute-done((f32[2,2,128,256]{3,2,1,0:T(8,128)S(1)}, f32[2,2,128,256]{3,2,1,0:T(8,128)S(1)}, u32[]{:S(2)}, u32[]{:S(2)}) %collective-permute-start.23) | collective-permute-done | bytes 524320 | tf_op jit(solution)/shard_map/ppermute | solution.py:1069
  234.1 1.6 place_step.14
  237.0 1.7 collective-permute-done.25.refs_3_
  239.4 2.5 collective-permute-start.31
  242.0 4.0 %collective-permute-done.26.refs_3_ = f32[2,2,136,256]{3,2,1,0:T(8,128)S(1)} collective-permute-done((f32[2,2,136,256]{3,2,1,0:T(8,128)S(1)}, f32[2,2,136,256]{3,2,1,0:T(8,128)S(1)}, u32[]{:S(2)}, u32[]{:S(2)}) %collective-permute-start.26) | collective-permute-done | bytes 557088 | tf_op jit(solution)/shard_map/ppermute | solution.py:1069
  246.8 2.8 collective-permute-start.28
  250.3 6.8 %collective-permute-done.28.refs_3_ = f32[2,136,256]{2,1,0:T(8,128)S(1)} collective-permute-done((f32[2,136,256]{2,1,0:T(8,128)S(1)}, f32[2,136,256]{2,1,0:T(8,128)S(1)}, u32[]{:S(2)}, u32[]{:S(2)}) %collective-permute-start.28) | collective-permute-done | bytes 278560 | tf_op jit(solution)/shard_map/ppermute | solution.py:1069
  261.3 4.1 %collective-permute-done.32.refs_3_ = f32[2,128,256]{2,1,0:T(8,128)S(1)} collective-permute-done((f32[2,128,256]{2,1,0:T(8,128)S(1)}, f32[2,128,256]{2,1,0:T(8,128)S(1)}, u32[]{:S(2)}, u32[]{:S(2)}) %collective-permute-start.32) | collective-permute-done | bytes 262176 | tf_op jit(solution)/shard_map/ppermute | solution.py:1069
  266.0 1.7 collective-permute-start.37
  267.8 1.4 collective-permute-start.34
  269.2 2.2 collective-permute-done.33.refs_3_
  272.2 7.6 %collective-permute-done.34.refs_3_ = f32[2,2,128,256]{3,2,1,0:T(8,128)S(1)} collective-permute-done((f32[2,2,128,256]{3,2,1,0:T(8,128)S(1)}, f32[2,2,128,256]{3,2,1,0:T(8,128)S(1)}, u32[]{:S(2)}, u32[]{:S(2)}) %collective-permute-start.34) | collective-permute-done | bytes 524320 | tf_op jit(solution)/shard_map/ppermute | solution.py:1069
  279.7 1.7 collective-permute-start.36
  283.1 3.2 collective-permute-done.36.refs_3_
  286.3 1.6 collective-permute-start.42
  289.2 1.9 collective-permute-start.43
  291.1 1.6 place_own.6
  292.7 2.5 place_own.7
  295.3 1.7 place_own.8
  296.9 1.7 place_own.9
  299.0 1.6 place_last.6
  301.3 1.7 collective-permute-start.44
  303.0 5.2 %collective-permute-done.40.refs_3_ = f32[2,2,136,256]{3,2,1,0:T(8,128)S(1)} collective-permute-done((f32[2,2,136,256]{3,2,1,0:T(8,128)S(1)}, f32[2,2,136,256]{3,2,1,0:T(8,128)S(1)}, u32[]{:S(2)}, u32[]{:S(2)}) %collective-permute-start.40) | collective-permute-done | bytes 557088 | tf_op jit(solution)/shard_map/ppermute | solution.py:1069
  309.7 1.6 place_own.10
  311.4 1.7 place_own.11
  313.0 2.5 place_last.7
  315.6 1.7 place_last.8
  317.3 1.7 place_last.9
  319.4 1.6 place_last.10
  321.1 3.4 %collective-permute-done.45.refs_3_ = f32[2,2,2,136,256]{4,3,2,1,0:T(8,128)S(1)} collective-permute-done((f32[2,2,2,136,256]{4,3,2,1,0:T(8,128)S(1)}, f32[2,2,2,136,256]{4,3,2,1,0:T(8,128)S(1)}, u32[]{:S(2)}, u32[]{:S(2)}) %collective-permute-start.45) | collective-permute-done | bytes 1114144 | tf_op jit(solution)/shard_map/ppermute | solution.py:1069
  324.4 2.2 place_last.11
  (107 shorter events, 40.1 us)
Async XLA Ops:
  13.9 3.4 %collective-permute-start = (f32[384,512]{1,0:T(8,128)}, f32[384,512]{1,0:T(8,128)S(1)}, u32[]{:S(2)}, u32[]{:S(2)}) collective-permute-start(f32[384,512]{1,0:T(8,128)} %get-tuple-element.202), channel_id=1, source_target_pairs={{0,16},{1,17},{2,18},{3,19},{4,20},{5,21},{6,22},{7,23},{8,24},{9,... | collective-permute-start | bytes 2359304 | tf_op jit(solution)/shard_map/ppermute | solution.py:1123
  30.7 4.2 %collective-permute-start.1 = (f32[384,512]{1,0:T(8,128)}, f32[384,512]{1,0:T(8,128)S(1)}, u32[]{:S(2)}, u32[]{:S(2)}) collective-permute-start(f32[384,512]{1,0:T(8,128)} %get-tuple-element.221), channel_id=1, source_target_pairs={{0,16},{1,17},{2,18},{3,19},{4,20},{5,21},{6,22},{7,23},{8,24},{9,... | collective-permute-start | bytes 2359304 | tf_op jit(solution)/shard_map/ppermute | solution.py:1123
  33.6 19.8 %collective-permute-start.2 = (f32[384,512]{1,0:T(8,128)}, f32[384,512]{1,0:T(8,128)S(1)}, u32[]{:S(2)}, u32[]{:S(2)}) collective-permute-start(f32[384,512]{1,0:T(8,128)} %get-tuple-element.227), channel_id=1, source_target_pairs={{16,0},{17,1},{18,2},{19,3},{20,4},{21,5},{22,6},{23,7},{24,8},{25... | collective-permute-start | bytes 2359304 | tf_op jit(solution)/shard_map/ppermute | solution.py:1127
  70.9 14.9 %collective-permute-start.3 = (f32[384,512]{1,0:T(8,128)}, f32[384,512]{1,0:T(8,128)S(1)}, u32[]{:S(2)}, u32[]{:S(2)}) collective-permute-start(f32[384,512]{1,0:T(8,128)} %get-tuple-element.240), channel_id=1, source_target_pairs={{16,0},{17,1},{18,2},{19,3},{20,4},{21,5},{22,6},{23,7},{24,8},{25... | collective-permute-start | bytes 2359304 | tf_op jit(solution)/shard_map/ppermute | solution.py:1127
  85.9 18.2 %copy-start.1 = (f32[1,2]{1,0:T(1,128)S(1)}, f32[1,2]{1,0:T(1,128)}, u32[]{:S(2)}) copy-start(f32[1,2]{1,0:T(1,128)} %refs_1_.8) | copy-start | bytes 28
  114.3 22.4 %collective-permute-start.4 = (f32[2,2,2,128,256]{4,3,2,1,0:T(8,128)}, f32[2,2,2,128,256]{4,3,2,1,0:T(8,128)S(1)}, u32[]{:S(2)}, u32[]{:S(2)}) collective-permute-start(f32[2,2,2,128,256]{4,3,2,1,0:T(8,128)} %get-tuple-element.259), channel_id=1, source_target_pairs={{0,4},{1,5},{2,6},{3,7},{4,0},{5,1},{6,2},{7,3},{8,12},{9,13},{10,... | collective-permute-start | bytes 3145736 | tf_op jit(solution)/shard_map/ppermute | solution.py:1069
  117.4 20.4 %collective-permute-start.5 = (f32[2,2,2,128,256]{4,3,2,1,0:T(8,128)}, f32[2,2,2,128,256]{4,3,2,1,0:T(8,128)S(1)}, u32[]{:S(2)}, u32[]{:S(2)}) collective-permute-start(f32[2,2,2,128,256]{4,3,2,1,0:T(8,128)} %get-tuple-element.262), channel_id=1, source_target_pairs={{0,1},{1,0},{2,3},{3,2},{4,5},{5,4},{6,7},{7,6},{8,9},{9,8},{10,11... | collective-permute-start | bytes 3145736 | tf_op jit(solution)/shard_map/ppermute | solution.py:1069
  118.9 17.8 %copy-start.5 = (f32[2,2,2,128,256]{4,3,2,1,0:T(8,128)S(1)}, f32[2,2,2,128,256]{4,3,2,1,0:T(8,128)}, u32[]{:S(2)}) copy-start(f32[2,2,2,128,256]{4,3,2,1,0:T(8,128)} %get-tuple-element.258.refs_2_) | copy-start | bytes 3145732
  136.7 1.2 copy-start.4
  137.9 3.3 copy-start.9
  137.9 4.8 %copy-start.8 = (f32[2,2,2,128,256]{4,3,2,1,0:T(8,128)S(1)}, f32[2,2,2,128,256]{4,3,2,1,0:T(8,128)}, u32[]{:S(2)}) copy-start(f32[2,2,2,128,256]{4,3,2,1,0:T(8,128)} %get-tuple-element.291) | copy-start | bytes 3145732
  137.9 6.6 %copy-start = (s32[2,1,384]{2,1,0:T(1,128)S(1)}, s32[2,1,384]{2,1,0:T(1,128)}, u32[]{:S(2)}) copy-start(s32[2,1,384]{2,1,0:T(1,128)} %refs_1_.9) | copy-start | bytes 9220
  138.8 16.1 %collective-permute-start.6 = (f32[2,2,128,256]{3,2,1,0:T(8,128)S(1)}, f32[2,2,128,256]{3,2,1,0:T(8,128)S(1)}, u32[]{:S(2)}, u32[]{:S(2)}) collective-permute-start(f32[2,2,128,256]{3,2,1,0:T(8,128)S(1)} %get-tuple-element.266), channel_id=1, source_target_pairs={{0,4},{1,5},{2,6},{3,7},{4,0},{5,1},{6,2},{7,3},{8,12},{9,13},{10,... | collective-permute-start | bytes 1572872 | tf_op jit(solution)/shard_map/ppermute | solution.py:1069
  141.2 43.1 %collective-permute-start.11 = (f32[2,2,2,128,256]{4,3,2,1,0:T(8,128)S(1)}, f32[2,2,2,128,256]{4,3,2,1,0:T(8,128)S(1)}, u32[]{:S(2)}, u32[]{:S(2)}) collective-permute-start(f32[2,2,2,128,256]{4,3,2,1,0:T(8,128)S(1)} %copy-done.9), channel_id=1, source_target_pairs={{0,2},{1,3},{2,0},{3,1},{4,6},{5,7},{6,4},{7,5},{8,10},{9,11},{10,... | collective-permute-start | bytes 3145736 | tf_op jit(solution)/shard_map/ppermute | solution.py:1069
  142.7 56.1 %collective-permute-start.15 = (f32[2,2,2,128,256]{4,3,2,1,0:T(8,128)S(1)}, f32[2,2,2,128,256]{4,3,2,1,0:T(8,128)S(1)}, u32[]{:S(2)}, u32[]{:S(2)}) collective-permute-start(f32[2,2,2,128,256]{4,3,2,1,0:T(8,128)S(1)} %copy-done.8), channel_id=1, source_target_pairs={{0,4},{1,5},{2,6},{3,7},{4,0},{5,1},{6,2},{7,3},{8,12},{9,13},{10,... | collective-permute-start | bytes 3145736 | tf_op jit(solution)/shard_map/ppermute | solution.py:1069
  142.9 14.9 %collective-permute-start.7 = (f32[2,2,128,256]{3,2,1,0:T(8,128)S(1)}, f32[2,2,128,256]{3,2,1,0:T(8,128)S(1)}, u32[]{:S(2)}, u32[]{:S(2)}) collective-permute-start(f32[2,2,128,256]{3,2,1,0:T(8,128)S(1)} %get-tuple-element.269), channel_id=1, source_target_pairs={{0,1},{1,0},{2,3},{3,2},{4,5},{5,4},{6,7},{7,6},{8,9},{9,8},{10,11... | collective-permute-start | bytes 1572872 | tf_op jit(solution)/shard_map/ppermute | solution.py:1069
  154.4 26.4 %collective-permute-start.10 = (f32[2,2,2,128,256]{4,3,2,1,0:T(8,128)}, f32[2,2,2,128,256]{4,3,2,1,0:T(8,128)S(1)}, u32[]{:S(2)}, u32[]{:S(2)}) collective-permute-start(f32[2,2,2,128,256]{4,3,2,1,0:T(8,128)} %get-tuple-element.278), channel_id=1, source_target_pairs={{0,1},{1,0},{2,3},{3,2},{4,5},{5,4},{6,7},{7,6},{8,9},{9,8},{10,11... | collective-permute-start | bytes 3145736 | tf_op jit(solution)/shard_map/ppermute | solution.py:1069
  154.9 58.9 %collective-permute-start.19 = (f32[2,2,2,136,256]{4,3,2,1,0:T(8,128)}, f32[2,2,2,136,256]{4,3,2,1,0:T(8,128)S(1)}, u32[]{:S(2)}, u32[]{:S(2)}) collective-permute-start(f32[2,2,2,136,256]{4,3,2,1,0:T(8,128)} %get-tuple-element.302), channel_id=1, source_target_pairs={{0,1},{1,0},{2,3},{3,2},{4,5},{5,4},{6,7},{7,6},{8,9},{9,8},{10,11... | collective-permute-start | bytes 3342344 | tf_op jit(solution)/shard_map/ppermute | solution.py:1069
  157.8 9.2 %collective-permute-start.8 = (f32[2,128,256]{2,1,0:T(8,128)S(1)}, f32[2,128,256]{2,1,0:T(8,128)S(1)}, u32[]{:S(2)}, u32[]{:S(2)}) collective-permute-start(f32[2,128,256]{2,1,0:T(8,128)S(1)} %get-tuple-element.272), channel_id=1, source_target_pairs={{0,2},{1,3},{2,0},{3,1},{4,6},{5,7},{6,4},{7,5},{8,10},{9,11},{10,... | collective-permute-start | bytes 786440 | tf_op jit(solution)/shard_map/ppermute | solution.py:1069
  167.0 6.4 %collective-permute-start.9 = (f32[2,128,256]{2,1,0:T(8,128)S(1)}, f32[2,128,256]{2,1,0:T(8,128)S(1)}, u32[]{:S(2)}, u32[]{:S(2)}) collective-permute-start(f32[2,128,256]{2,1,0:T(8,128)S(1)} %get-tuple-element.275), channel_id=1, source_target_pairs={{0,2},{1,3},{2,0},{3,1},{4,6},{5,7},{6,4},{7,5},{8,10},{9,11},{10,... | collective-permute-start | bytes 786440 | tf_op jit(solution)/shard_map/ppermute | solution.py:1069
  173.4 22.6 %collective-permute-start.14 = (f32[2,128,256]{2,1,0:T(8,128)S(1)}, f32[2,128,256]{2,1,0:T(8,128)S(1)}, u32[]{:S(2)}, u32[]{:S(2)}) collective-permute-start(f32[2,128,256]{2,1,0:T(8,128)S(1)} %get-tuple-element.288.refs_2_), channel_id=1, source_target_pairs={{0,8},{1,9},{2,10},{3,11},{4,12},{5,13},{6,14},{7,15},{8,0},{9,1},... | collective-permute-start | bytes 786440 | tf_op jit(solution)/shard_map/ppermute | solution.py:1069
  176.0 7.3 %copy-start.3 = (f32[2,2,2,128,256]{4,3,2,1,0:T(8,128)S(1)}, f32[2,2,2,128,256]{4,3,2,1,0:T(8,128)}, u32[]{:S(2)}) copy-start(f32[2,2,2,128,256]{4,3,2,1,0:T(8,128)} %get-tuple-element.277.refs_2_) | copy-start | bytes 3145732
  180.7 14.6 %collective-permute-start.13 = (f32[2,128,256]{2,1,0:T(8,128)S(1)}, f32[2,128,256]{2,1,0:T(8,128)S(1)}, u32[]{:S(2)}, u32[]{:S(2)}) collective-permute-start(f32[2,128,256]{2,1,0:T(8,128)S(1)} %get-tuple-element.286.refs_2_), channel_id=1, source_target_pairs={{0,8},{1,9},{2,10},{3,11},{4,12},{5,13},{6,14},{7,15},{8,0},{9,1},... | collective-permute-start | bytes 786440 | tf_op jit(solution)/shard_map/ppermute | solution.py:1069
  183.3 1.5 copy-start.7
  184.3 9.9 %collective-permute-start.12 = (f32[2,2,128,256]{3,2,1,0:T(8,128)S(1)}, f32[2,2,128,256]{3,2,1,0:T(8,128)S(1)}, u32[]{:S(2)}, u32[]{:S(2)}) collective-permute-start(f32[2,2,128,256]{3,2,1,0:T(8,128)S(1)} %get-tuple-element.284), channel_id=1, source_target_pairs={{0,2},{1,3},{2,0},{3,1},{4,6},{5,7},{6,4},{7,5},{8,10},{9,11},{10,... | collective-permute-start | bytes 1572872 | tf_op jit(solution)/shard_map/ppermute | solution.py:1069
  194.2 15.9 %collective-permute-start.17 = (f32[2,2,128,256]{3,2,1,0:T(8,128)S(1)}, f32[2,2,128,256]{3,2,1,0:T(8,128)S(1)}, u32[]{:S(2)}, u32[]{:S(2)}) collective-permute-start(f32[2,2,128,256]{3,2,1,0:T(8,128)S(1)} %get-tuple-element.297), channel_id=1, source_target_pairs={{0,1},{1,0},{2,3},{3,2},{4,5},{5,4},{6,7},{7,6},{8,9},{9,8},{10,11... | collective-permute-start | bytes 1572872 | tf_op jit(solution)/shard_map/ppermute | solution.py:1069
  196.0 4.5 %copy-start.6 = (f32[2,2,2,128,256]{4,3,2,1,0:T(8,128)S(1)}, f32[2,2,2,128,256]{4,3,2,1,0:T(8,128)}, u32[]{:S(2)}) copy-start(f32[2,2,2,128,256]{4,3,2,1,0:T(8,128)} %get-tuple-element.290.refs_2_) | copy-start | bytes 3145732
  196.7 15.1 %collective-permute-start.18 = (f32[2,128,256]{2,1,0:T(8,128)S(1)}, f32[2,128,256]{2,1,0:T(8,128)S(1)}, u32[]{:S(2)}, u32[]{:S(2)}) collective-permute-start(f32[2,128,256]{2,1,0:T(8,128)S(1)} %get-tuple-element.299.refs_2_), channel_id=1, source_target_pairs={{0,2},{1,3},{2,0},{3,1},{4,6},{5,7},{6,4},{7,5},{8,10},{9,11},{10,... | collective-permute-start | bytes 786440 | tf_op jit(solution)/shard_map/ppermute | solution.py:1069
  198.1 17.5 %collective-permute-start.20 = (f32[2,128,256]{2,1,0:T(8,128)S(1)}, f32[2,128,256]{2,1,0:T(8,128)S(1)}, u32[]{:S(2)}, u32[]{:S(2)}) collective-permute-start(f32[2,128,256]{2,1,0:T(8,128)S(1)} %get-tuple-element.304.refs_2_), channel_id=1, source_target_pairs={{0,2},{1,3},{2,0},{3,1},{4,6},{5,7},{6,4},{7,5},{8,10},{9,11},{10,... | collective-permute-start | bytes 786440 | tf_op jit(solution)/shard_map/ppermute | solution.py:1069
  198.8 9.2 %collective-permute-start.16 = (f32[2,128,256]{2,1,0:T(8,128)S(1)}, f32[2,128,256]{2,1,0:T(8,128)S(1)}, u32[]{:S(2)}, u32[]{:S(2)}) collective-permute-start(f32[2,128,256]{2,1,0:T(8,128)S(1)} %get-tuple-element.294), channel_id=1, source_target_pairs={{0,4},{1,5},{2,6},{3,7},{4,0},{5,1},{6,2},{7,3},{8,12},{9,13},{10,... | collective-permute-start | bytes 786440 | tf_op jit(solution)/shard_map/ppermute | solution.py:1069
  208.0 12.3 %collective-permute-start.21 = (f32[2,2,128,256]{3,2,1,0:T(8,128)S(1)}, f32[2,2,128,256]{3,2,1,0:T(8,128)S(1)}, u32[]{:S(2)}, u32[]{:S(2)}) collective-permute-start(f32[2,2,128,256]{3,2,1,0:T(8,128)S(1)} %get-tuple-element.307), channel_id=1, source_target_pairs={{0,2},{1,3},{2,0},{3,1},{4,6},{5,7},{6,4},{7,5},{8,10},{9,11},{10,... | collective-permute-start | bytes 1572872 | tf_op jit(solution)/shard_map/ppermute | solution.py:1069
  210.8 14.0 %collective-permute-start.22 = (f32[2,128,256]{2,1,0:T(8,128)S(1)}, f32[2,128,256]{2,1,0:T(8,128)S(1)}, u32[]{:S(2)}, u32[]{:S(2)}) collective-permute-start(f32[2,128,256]{2,1,0:T(8,128)S(1)} %get-tuple-element.310), channel_id=1, source_target_pairs={{0,4},{1,5},{2,6},{3,7},{4,0},{5,1},{6,2},{7,3},{8,12},{9,13},{10,... | collective-permute-start | bytes 786440 | tf_op jit(solution)/shard_map/ppermute | solution.py:1069
  211.8 23.9 %collective-permute-start.24 = (f32[2,128,256]{2,1,0:T(8,128)S(1)}, f32[2,128,256]{2,1,0:T(8,128)S(1)}, u32[]{:S(2)}, u32[]{:S(2)}) collective-permute-start(f32[2,128,256]{2,1,0:T(8,128)S(1)} %get-tuple-element.314.refs_2_), channel_id=1, source_target_pairs={{0,8},{1,9},{2,10},{3,11},{4,12},{5,13},{6,14},{7,15},{8,0},{9,1},... | collective-permute-start | bytes 786440 | tf_op jit(solution)/shard_map/ppermute | solution.py:1069
  213.2 1.2 copy-start.2
  213.8 20.1 %collective-permute-start.23 = (f32[2,2,128,256]{3,2,1,0:T(8,128)S(1)}, f32[2,2,128,256]{3,2,1,0:T(8,128)S(1)}, u32[]{:S(2)}, u32[]{:S(2)}) collective-permute-start(f32[2,2,128,256]{3,2,1,0:T(8,128)S(1)} %get-tuple-element.312.refs_2_), channel_id=1, source_target_pairs={{0,4},{1,5},{2,6},{3,7},{4,0},{5,1},{6,2},{7,3},{8,12},{9,13},{10,... | collective-permute-start | bytes 1572872 | tf_op jit(solution)/shard_map/ppermute | solution.py:1069
  216.2 43.2 %collective-permute-start.30 = (f32[2,2,128,256]{3,2,1,0:T(8,128)S(1)}, f32[2,2,128,256]{3,2,1,0:T(8,128)S(1)}, u32[]{:S(2)}, u32[]{:S(2)}) collective-permute-start(f32[2,2,128,256]{3,2,1,0:T(8,128)S(1)} %get-tuple-element.329.refs_2_), channel_id=1, source_target_pairs={{0,1},{1,0},{2,3},{3,2},{4,5},{5,4},{6,7},{7,6},{8,9},{9,8},{10,11... | collective-permute-start | bytes 1572872 | tf_op jit(solution)/shard_map/ppermute | solution.py:1069
  220.3 25.6 %collective-permute-start.26 = (f32[2,2,136,256]{3,2,1,0:T(8,128)S(1)}, f32[2,2,136,256]{3,2,1,0:T(8,128)S(1)}, u32[]{:S(2)}, u32[]{:S(2)}) collective-permute-start(f32[2,2,136,256]{3,2,1,0:T(8,128)S(1)} %get-tuple-element.320), channel_id=1, source_target_pairs={{0,4},{1,5},{2,6},{3,7},{4,0},{5,1},{6,2},{7,3},{8,12},{9,13},{10,... | collective-permute-start | bytes 1671176 | tf_op jit(solution)/shard_map/ppermute | solution.py:1069
  224.9 13.9 %collective-permute-start.25 = (f32[2,128,256]{2,1,0:T(8,128)S(1)}, f32[2,128,256]{2,1,0:T(8,128)S(1)}, u32[]{:S(2)}, u32[]{:S(2)}) collective-permute-start(f32[2,128,256]{2,1,0:T(8,128)S(1)} %get-tuple-element.317), channel_id=1, source_target_pairs={{0,1},{1,0},{2,3},{3,2},{4,5},{5,4},{6,7},{7,6},{8,9},{9,8},{10,11... | collective-permute-start | bytes 786440 | tf_op jit(solution)/shard_map/ppermute | solution.py:1069
  234.0 12.9 %collective-permute-start.27 = (f32[2,128,256]{2,1,0:T(8,128)S(1)}, f32[2,128,256]{2,1,0:T(8,128)S(1)}, u32[]{:S(2)}, u32[]{:S(2)}) collective-permute-start(f32[2,128,256]{2,1,0:T(8,128)S(1)} %get-tuple-element.322.refs_2_), channel_id=1, source_target_pairs={{0,8},{1,9},{2,10},{3,11},{4,12},{5,13},{6,14},{7,15},{8,0},{9,1},... | collective-permute-start | bytes 786440 | tf_op jit(solution)/shard_map/ppermute | solution.py:1069
  236.3 22.4 %collective-permute-start.29 = (f32[2,128,256]{2,1,0:T(8,128)S(1)}, f32[2,128,256]{2,1,0:T(8,128)S(1)}, u32[]{:S(2)}, u32[]{:S(2)}) collective-permute-start(f32[2,128,256]{2,1,0:T(8,128)S(1)} %get-tuple-element.327.refs_2_), channel_id=1, source_target_pairs={{0,4},{1,5},{2,6},{3,7},{4,0},{5,1},{6,2},{7,3},{8,12},{9,13},{10,... | collective-permute-start | bytes 786440 | tf_op jit(solution)/shard_map/ppermute | solution.py:1069
  239.4 20.6 %collective-permute-start.31 = (f32[2,128,256]{2,1,0:T(8,128)S(1)}, f32[2,128,256]{2,1,0:T(8,128)S(1)}, u32[]{:S(2)}, u32[]{:S(2)}) collective-permute-start(f32[2,128,256]{2,1,0:T(8,128)S(1)} %get-tuple-element.331.refs_2_), channel_id=1, source_target_pairs={{0,8},{1,9},{2,10},{3,11},{4,12},{5,13},{6,14},{7,15},{8,0},{9,1},... | collective-permute-start | bytes 786440 | tf_op jit(solution)/shard_map/ppermute | solution.py:1069
  246.0 67.1 %collective-permute-start.41 = (f32[2,2,2,128,256]{4,3,2,1,0:T(8,128)}, f32[2,2,2,128,256]{4,3,2,1,0:T(8,128)}, u32[]{:S(2)}, u32[]{:S(2)}) collective-permute-start(f32[2,2,2,128,256]{4,3,2,1,0:T(8,128)} %get-tuple-element.347.refs_2_), channel_id=1, source_target_pairs={{0,1},{1,0},{2,3},{3,2},{4,5},{5,4},{6,7},{7,6},{8,9},{9,8},{10,11... | collective-permute-start | bytes 3145736 | tf_op jit(solution)/shard_map/ppermute | solution.py:1069
  246.8 10.3 %collective-permute-start.28 = (f32[2,136,256]{2,1,0:T(8,128)S(1)}, f32[2,136,256]{2,1,0:T(8,128)S(1)}, u32[]{:S(2)}, u32[]{:S(2)}) collective-permute-start(f32[2,136,256]{2,1,0:T(8,128)S(1)} %get-tuple-element.325), channel_id=1, source_target_pairs={{0,2},{1,3},{2,0},{3,1},{4,6},{5,7},{6,4},{7,5},{8,10},{9,11},{10,... | collective-permute-start | bytes 835592 | tf_op jit(solution)/shard_map/ppermute | solution.py:1069
  257.1 8.3 %collective-permute-start.32 = (f32[2,128,256]{2,1,0:T(8,128)S(1)}, f32[2,128,256]{2,1,0:T(8,128)S(1)}, u32[]{:S(2)}, u32[]{:S(2)}) collective-permute-start(f32[2,128,256]{2,1,0:T(8,128)S(1)} %get-tuple-element.333.refs_2_), channel_id=1, source_target_pairs={{0,4},{1,5},{2,6},{3,7},{4,0},{5,1},{6,2},{7,3},{8,12},{9,13},{10,... | collective-permute-start | bytes 786440 | tf_op jit(solution)/shard_map/ppermute | solution.py:1069
  260.7 21.4 %collective-permute-start.35 = (f32[2,128,256]{2,1,0:T(8,128)S(1)}, f32[2,128,256]{2,1,0:T(8,128)S(1)}, u32[]{:S(2)}, u32[]{:S(2)}) collective-permute-start(f32[2,128,256]{2,1,0:T(8,128)S(1)} %get-tuple-element.339.refs_2_), channel_id=1, source_target_pairs={{0,1},{1,0},{2,3},{3,2},{4,5},{5,4},{6,7},{7,6},{8,9},{9,8},{10,11... | collective-permute-start | bytes 786440 | tf_op jit(solution)/shard_map/ppermute | solution.py:1069
  261.0 10.4 %collective-permute-start.33 = (f32[2,136,256]{2,1,0:T(8,128)S(1)}, f32[2,136,256]{2,1,0:T(8,128)S(1)}, u32[]{:S(2)}, u32[]{:S(2)}) collective-permute-start(f32[2,136,256]{2,1,0:T(8,128)S(1)} %get-tuple-element.335.refs_2_), channel_id=1, source_target_pairs={{0,8},{1,9},{2,10},{3,11},{4,12},{5,13},{6,14},{7,15},{8,0},{9,1},... | collective-permute-start | bytes 835592 | tf_op jit(solution)/shard_map/ppermute | solution.py:1069
  266.0 22.5 %collective-permute-start.37 = (f32[2,2,128,256]{3,2,1,0:T(8,128)S(1)}, f32[2,2,128,256]{3,2,1,0:T(8,128)S(1)}, u32[]{:S(2)}, u32[]{:S(2)}) collective-permute-start(f32[2,2,128,256]{3,2,1,0:T(8,128)S(1)} %get-tuple-element.343.refs_2_), channel_id=1, source_target_pairs={{0,1},{1,0},{2,3},{3,2},{4,5},{5,4},{6,7},{7,6},{8,9},{9,8},{10,11... | collective-permute-start | bytes 1572872 | tf_op jit(solution)/shard_map/ppermute | solution.py:1069
  267.8 12.0 %collective-permute-start.34 = (f32[2,2,128,256]{3,2,1,0:T(8,128)S(1)}, f32[2,2,128,256]{3,2,1,0:T(8,128)S(1)}, u32[]{:S(2)}, u32[]{:S(2)}) collective-permute-start(f32[2,2,128,256]{3,2,1,0:T(8,128)S(1)} %get-tuple-element.337.refs_2_), channel_id=1, source_target_pairs={{0,2},{1,3},{2,0},{3,1},{4,6},{5,7},{6,4},{7,5},{8,10},{9,11},{10,... | collective-permute-start | bytes 1572872 | tf_op jit(solution)/shard_map/ppermute | solution.py:1069
  271.4 27.2 %collective-permute-start.38 = (f32[2,2,2,128,256]{4,3,2,1,0:T(8,128)S(1)}, f32[2,2,2,128,256]{4,3,2,1,0:T(8,128)S(1)}, u32[]{:S(2)}, u32[]{:S(2)}) collective-permute-start(f32[2,2,2,128,256]{4,3,2,1,0:T(8,128)S(1)} %get-tuple-element.345.refs_2_), channel_id=1, source_target_pairs={{0,4},{1,5},{2,6},{3,7},{4,0},{5,1},{6,2},{7,3},{8,12},{9,13},{10,... | collective-permute-start | bytes 3145736 | tf_op jit(solution)/shard_map/ppermute | solution.py:1069
  279.7 6.5 %collective-permute-start.36 = (f32[2,136,256]{2,1,0:T(8,128)S(1)}, f32[2,136,256]{2,1,0:T(8,128)S(1)}, u32[]{:S(2)}, u32[]{:S(2)}) collective-permute-start(f32[2,136,256]{2,1,0:T(8,128)S(1)} %get-tuple-element.341.refs_2_), channel_id=1, source_target_pairs={{0,2},{1,3},{2,0},{3,1},{4,6},{5,7},{6,4},{7,5},{8,10},{9,11},{10,... | collective-permute-start | bytes 835592 | tf_op jit(solution)/shard_map/ppermute | solution.py:1069
  282.7 17.9 %collective-permute-start.39 = (f32[2,2,128,256]{3,2,1,0:T(8,128)S(1)}, f32[2,2,128,256]{3,2,1,0:T(8,128)S(1)}, u32[]{:S(2)}, u32[]{:S(2)}) collective-permute-start(f32[2,2,128,256]{3,2,1,0:T(8,128)S(1)} %get-tuple-element.356.refs_2_), channel_id=1, source_target_pairs={{0,2},{1,3},{2,0},{3,1},{4,6},{5,7},{6,4},{7,5},{8,10},{9,11},{10,... | collective-permute-start | bytes 1572872 | tf_op jit(solution)/shard_map/ppermute | solution.py:1069
  286.3 29.3 %collective-permute-start.42 = (f32[2,2,2,128,256]{4,3,2,1,0:T(8,128)S(1)}, f32[2,2,2,128,256]{4,3,2,1,0:T(8,128)S(1)}, u32[]{:S(2)}, u32[]{:S(2)}) collective-permute-start(f32[2,2,2,128,256]{4,3,2,1,0:T(8,128)S(1)} %get-tuple-element.352.refs_2_), channel_id=1, source_target_pairs={{0,1},{1,0},{2,3},{3,2},{4,5},{5,4},{6,7},{7,6},{8,9},{9,8},{10,11... | collective-permute-start | bytes 3145736 | tf_op jit(solution)/shard_map/ppermute | solution.py:1069
  289.2 28.1 %collective-permute-start.43 = (f32[2,2,2,128,256]{4,3,2,1,0:T(8,128)S(1)}, f32[2,2,2,128,256]{4,3,2,1,0:T(8,128)S(1)}, u32[]{:S(2)}, u32[]{:S(2)}) collective-permute-start(f32[2,2,2,128,256]{4,3,2,1,0:T(8,128)S(1)} %get-tuple-element.350.refs_2_), channel_id=1, source_target_pairs={{0,2},{1,3},{2,0},{3,1},{4,6},{5,7},{6,4},{7,5},{8,10},{9,11},{10,... | collective-permute-start | bytes 3145736 | tf_op jit(solution)/shard_map/ppermute | solution.py:1069
  298.6 9.6 %collective-permute-start.40 = (f32[2,2,136,256]{3,2,1,0:T(8,128)S(1)}, f32[2,2,136,256]{3,2,1,0:T(8,128)S(1)}, u32[]{:S(2)}, u32[]{:S(2)}) collective-permute-start(f32[2,2,136,256]{3,2,1,0:T(8,128)S(1)} %get-tuple-element.358.refs_2_), channel_id=1, source_target_pairs={{0,4},{1,5},{2,6},{3,7},{4,0},{5,1},{6,2},{7,3},{8,12},{9,13},{10,... | collective-permute-start | bytes 1671176 | tf_op jit(solution)/shard_map/ppermute | solution.py:1069
  301.3 18.1 %collective-permute-start.44 = (f32[2,2,2,128,256]{4,3,2,1,0:T(8,128)S(1)}, f32[2,2,2,128,256]{4,3,2,1,0:T(8,128)S(1)}, u32[]{:S(2)}, u32[]{:S(2)}) collective-permute-start(f32[2,2,2,128,256]{4,3,2,1,0:T(8,128)S(1)} %get-tuple-element.360.refs_2_), channel_id=1, source_target_pairs={{0,4},{1,5},{2,6},{3,7},{4,0},{5,1},{6,2},{7,3},{8,12},{9,13},{10,... | collective-permute-start | bytes 3145736 | tf_op jit(solution)/shard_map/ppermute | solution.py:1069
  308.9 15.6 %collective-permute-start.45 = (f32[2,2,2,136,256]{4,3,2,1,0:T(8,128)S(1)}, f32[2,2,2,136,256]{4,3,2,1,0:T(8,128)S(1)}, u32[]{:S(2)}, u32[]{:S(2)}) collective-permute-start(f32[2,2,2,136,256]{4,3,2,1,0:T(8,128)S(1)} %get-tuple-element.363.refs_2_), channel_id=1, source_target_pairs={{0,1},{1,0},{2,3},{3,2},{4,5},{5,4},{6,7},{7,6},{8,9},{9,8},{10,11... | collective-permute-start | bytes 3342344 | tf_op jit(solution)/shard_map/ppermute | solution.py:1069

commit v5 on v4

--- a/solution.py
+++ b/solution.py
@@ -12,8 +12,8 @@
 HEAD_DIM = 64
 GELU_A = math.sqrt(2.0 / math.pi)
 GELU_B = 0.044715
-ORDERS = {"B": "nxyf", "b": "xnyf", "I": "yxnf", "i": "nyxf", "A": "xnyf", "a": "xynf"}
-PROGRAM = "|Bb|Bb|IaibBbBAaIaBbiaIbABiIbaiAIAaBiIAaiAIBiAbaIiA"
+ORDERS = {"B": "nxyf", "b": "xynf", "I": "yxnf", "i": "nyxf", "A": "xnyf", "a": "xynf"}
+PROGRAM = "|Bb|Bb|IbaiIBbBAaaBbiaIbABiIbaiAIAaBiIAaiAIBiAbaIiA"
 
 
 TOKEN = [None]
@@ -733,7 +733,7 @@
         scratch_shapes=scratch,
         input_output_aliases={len(inputs) + i: i for i in range(len(extra))},
         compiler_params=pltpu.CompilerParams(vmem_limit_bytes=limit * 1024 * 1024),
-        cost_estimate=pl.CostEstimate(flops=flops, bytes_accessed=2 * 10**7, transcendentals=10**6),
+        cost_estimate=pl.CostEstimate(flops=10**12, bytes_accessed=10**9, transcendentals=0),
         name=name,
     )(*inputs, *in_hbm(extra))
     TOKEN[0] = results[-1]

time: 333 us -> 356 us (1.069)
  waiting for transfers between devices: 115 us -> 129 us
  Pallas kernels: 151 us -> 157 us
    ppermute x42, waiting for transfers between devices: 90.7 us -> 103 us  [shifted(): return lax.ppermute(value, 'dp', pairs)]
    pallas_call x48, Pallas kernels: 48.9 us -> 55.9 us  [local_call(): pl.pallas_call(parted, out_shape=list(outs) + [loose(8, 128)], in_specs=[...]
  transfers between devices with their start and end apart: 46 -> 46, of which waited for: 22 -> 20; matrix products, arithmetic and copies ran while one was open for 0% -> 0% of each run, Pallas kernels for 23% -> 23%
where the time goes in v5:
time: 356 us; the launch traced here: 350 us
  Pallas kernels  157 us (44%)
  waiting for transfers between devices  129 us (36%)
  starting transfers between devices  61.6 us (17%)
    ppermute x42, waiting for transfers between devices, shifted(): return lax.ppermute(value, 'dp', pairs)  103 us
    pallas_call x6, Pallas kernels, call(): pl.pallas_call(functools.partial(body, len(extra)), out_shape=outs + [loo...  66.5 us
    pallas_call x48, Pallas kernels, local_call(): pl.pallas_call(parted, out_shape=list(outs) + [loose(8, 128)], in_specs=[...  55.9 us
    ppermute x42, starting transfers between devices, shifted(): return lax.ppermute(value, 'dp', pairs)  54.7 us
    pallas_call x3, Pallas kernels, forward_tick(): pl.pallas_call(functools.partial(forward_body, tick), out_shape=shapes, i...  34.1 us
    ppermute x2, waiting for transfers between devices, shards(): upstreams.append(lax.ppermute(sent, 'section', [(1, 0)]))  23.9 us
  transfers between devices with their start and end apart: 46, of which 20 were waited for; matrix products, arithmetic and copies ran while one was open for 0% of the time, Pallas kernels for 23%

profile of v5, /device:TPU:0, one launch (start us, length us, event | category | flops | bytes accessed | tf_op | source)
XLA Modules:
  0.0 349.8 jit_solution(13277305270802825620)
XLA Ops:
  0.8 13.1 %layer_forward.3 = (f32[2,384,512]{2,1,0:T(8,128)}, f32[384,512]{1,0:T(8,128)}, f32[2,384,512]{2,1,0:T(8,128)}, f32[2,384,512]{2,1,0:T(8,128)}, f32[2,384,512]{2...) custom-call(s32[5]{0:T(128)S(1)} %stack.23.refs_0_, ...), custom_call_target="tpu_custom_call" | custom-call | flops 10000000000 | bytes 20000000 | tf_op jit(solution)/shard_map/layer_forward/pallas_call | solution.py:326
  15.3 2.1 collective-permute-done.refs_12_
  17.3 13.6 %layer_forward.4 = (f32[2,384,512]{2,1,0:T(8,128)}, f32[384,512]{1,0:T(8,128)}, f32[2,384,512]{2,1,0:T(8,128)}, f32[2,384,512]{2,1,0:T(8,128)}, f32[2,384,512]{2...) custom-call(s32[5]{0:T(128)S(1)} %stack.23.refs_0_, ...), custom_call_target="tpu_custom_call", output_to_operand_aliasing={{0}: (13, {}), {2}: (14, {}), {3}: (15, {}), {4}: (16, {}),... | custom-call | flops 10000000000 | bytes 20000000 | tf_op jit(solution)/shard_map/layer_forward/pallas_call | solution.py:326
  30.9 2.9 collective-permute-start.1
  35.9 7.4 %layer_forward.5 = (f32[2,384,512]{2,1,0:T(8,128)}, f32[384,512]{1,0:T(8,128)}, f32[2,384,512]{2,1,0:T(8,128)}, f32[2,384,512]{2,1,0:T(8,128)}, f32[2,384,512]{2...) custom-call(s32[5]{0:T(128)S(1)} %stack.23.refs_0_, ...), custom_call_target="tpu_custom_call", output_to_operand_aliasing={{0}: (13, {}), {2}: (14, {}), {3}: (15, {}), {4}: (16, {}),... | custom-call | flops 10000000000 | bytes 20000000 | tf_op jit(solution)/shard_map/layer_forward/pallas_call | solution.py:326
  43.3 10.2 %collective-permute-done.2.refs_1_.refs_2_ = f32[384,512]{1,0:T(8,128)S(1)} collective-permute-done((f32[384,512]{1,0:T(8,128)}, f32[384,512]{1,0:T(8,128)S(1)}, u32[]{:S(2)}, u32[]{:S(2)}) %collective-permute-start.2) | collective-permute-done | bytes 786464 | tf_op jit(solution)/shard_map/ppermute | solution.py:1127
  53.5 18.0 %grad_chain.4 = (bf16[2,2,384,2048]{3,2,1,0:T(8,128)(2,1)}, bf16[2,2,384,1536]{3,2,1,0:T(8,128)(2,1)}, bf16[2,2,384,512]{3,2,1,0:T(8,128)(2,1)}, f32[2,384,512]{...) custom-call(s32[5]{0:T(128)S(1)} %stack.23.refs_0_, ...), custom_call_target="tpu_custom_call", output_to_operand_aliasing={{0}: (19, {}), {1}: (20, {}), {2}: (21, {}), {3}: (22, {}),... | custom-call | flops 999999995904 | bytes 1000000000 | tf_op jit(solution)/shard_map/grad_chain/pallas_call | solution.py:728
  72.8 13.7 %collective-permute-done.3.refs_1_.refs_3_ = f32[384,512]{1,0:T(8,128)S(1)} collective-permute-done((f32[384,512]{1,0:T(8,128)}, f32[384,512]{1,0:T(8,128)S(1)}, u32[]{:S(2)}, u32[]{:S(2)}) %collective-permute-start.3) | collective-permute-done | bytes 786464 | tf_op jit(solution)/shard_map/ppermute | solution.py:1127
  86.5 17.6 %grad_chain.5 = (bf16[2,2,384,2048]{3,2,1,0:T(8,128)(2,1)}, bf16[2,2,384,1536]{3,2,1,0:T(8,128)(2,1)}, bf16[2,2,384,512]{3,2,1,0:T(8,128)(2,1)}, f32[2,384,512]{...) custom-call(s32[5]{0:T(128)S(1)} %stack.23.refs_0_, ...), custom_call_target="tpu_custom_call", output_to_operand_aliasing={{0}: (19, {}), {1}: (20, {}), {2}: (21, {}), {3}: (22, {}),... | custom-call | flops 999999995904 | bytes 1000000000 | tf_op jit(solution)/shard_map/grad_chain/pallas_call | solution.py:728
  104.2 10.3 %grad_back.1 = (f32[2,2,2,128,256]{4,3,2,1,0:T(8,128)}, f32[2,2,2,128,256]{4,3,2,1,0:T(8,128)}, f32[2,2,2,128,256]{4,3,2,1,0:T(8,128)}, f32[2,2,2,128,256]{4,3,2,1,0:T(8,128)}, f32[8,128]{1,0:T(8,128)S(1)}) custom-call(s32[5]{0:T(128)S(1)} %stack.23.refs_0_, f32[1,2]{1,0:T(1,128)S(1)} %copy-done.1, f32[384,512]{1,0:T(8,128)S(1)} %collective-permute-done.2.refs_1_.refs_2_, ...), custom_call_target="tpu_custom_call" | custom-call | flops 999999995904 | bytes 1000000000 | tf_op jit(solution)/shard_map/grad_back/pallas_call | solution.py:728
  114.5 3.1 collective-permute-start.4
  117.6 1.5 collective-permute-start.5
  119.1 9.8 %grad_inner.1 = (f32[2,2,2,128,256]{4,3,2,1,0:T(8,128)}, f32[2,2,2,128,256]{4,3,2,1,0:T(8,128)}, f32[2,2,2,128,256]{4,3,2,1,0:T(8,128)}, f32[2,2,2,128,256]{4,3,2,1,0:T(8,128)}, f32[8,128]{1,0:T(8,128)S(1)}) custom-call(s32[5]{0:T(128)S(1)} %stack.23.refs_0_, f32[2,384,512]{2,1,0:T(8,128)} %get-tuple-element.253.refs_1_, ...), custom_call_target="tpu_custom_call" | custom-call | flops 999999995904 | bytes 1000000000 | tf_op jit(solution)/shard_map/grad_inner/pallas_call | solution.py:728
  129.0 1.6 collective-permute-start.7
  130.7 3.0 reduce_step.24
  133.8 7.0 %collective-permute-done.5.refs_3_ = f32[2,2,2,128,256]{4,3,2,1,0:T(8,128)} collective-permute-done((f32[2,2,2,128,256]{4,3,2,1,0:T(8,128)}, f32[2,2,2,128,256]{4,3,2,1,0:T(8,128)}, u32[]{:S(2)}, u32[]{:S(2)}) %collective-permute-start.5) | collective-permute-done | bytes 1048608 | tf_op jit(solution)/shard_map/ppermute | solution.py:1069
  140.7 2.8 reduce_step.25
  143.6 2.6 collective-permute-start.6
  147.6 9.9 %grad_attention.1 = (f32[2,2,2,136,256]{4,3,2,1,0:T(8,128)}, f32[2,2,2,136,256]{4,3,2,1,0:T(8,128)}, f32[2,2,2,128,256]{4,3,2,1,0:T(8,128)}, f32[2,2,2,128,256]{4,3,2,1,0:T(8,128)}, f32[8,128]{1,0:T(8,128)S(1)}) custom-call(s32[5]{0:T(128)S(1)} %stack.23.refs_0_, s32[2,1,384]{2,1,0:T(1,128)S(1)} %copy-done, f32[2,384,512]{2,1,0:T(8,128)} %get-tuple-element.248.refs_2_, ...), custom_call_target="tpu_custom_call" | custom-call | flops 999999995904 | bytes 1000000000 | tf_op jit(solution)/shard_map/grad_attention/pallas_call | solution.py:728
  158.2 1.7 reduce_step.26
  160.1 2.1 reduce_step.27
  162.1 1.7 reduce_step.28
  164.0 7.5 %collective-permute-done.9.refs_3_ = f32[2,128,256]{2,1,0:T(8,128)S(1)} collective-permute-done((f32[2,128,256]{2,1,0:T(8,128)S(1)}, f32[2,128,256]{2,1,0:T(8,128)S(1)}, u32[]{:S(2)}, u32[]{:S(2)}) %collective-permute-start.9) | collective-permute-done | bytes 262176 | tf_op jit(solution)/shard_map/ppermute | solution.py:1069
  172.8 11.1 %collective-permute-done.11.refs_3_ = f32[2,2,2,128,256]{4,3,2,1,0:T(8,128)S(1)} collective-permute-done((f32[2,2,2,128,256]{4,3,2,1,0:T(8,128)}, f32[2,2,2,128,256]{4,3,2,1,0:T(8,128)S(1)}, u32[]{:S(2)}, u32[]{:S(2)}) %collective-permute-start.11) | collective-permute-done | bytes 1048608 | tf_op jit(solution)/shard_map/ppermute | solution.py:1069
  186.1 1.5 collective-permute-start.17
  187.5 2.6 collective-permute-start.14
  190.1 9.5 %collective-permute-done.12.refs_3_ = f32[2,2,128,256]{3,2,1,0:T(8,128)S(1)} collective-permute-done((f32[2,2,128,256]{3,2,1,0:T(8,128)S(1)}, f32[2,2,128,256]{3,2,1,0:T(8,128)S(1)}, u32[]{:S(2)}, u32[]{:S(2)}) %collective-permute-start.12) | collective-permute-done | bytes 524320 | tf_op jit(solution)/shard_map/ppermute | solution.py:1069
  199.7 2.7 collective-permute-start.13
  203.1 14.2 %collective-permute-done.13.refs_3_ = f32[2,128,256]{2,1,0:T(8,128)S(1)} collective-permute-done((f32[2,128,256]{2,1,0:T(8,128)S(1)}, f32[2,128,256]{2,1,0:T(8,128)S(1)}, u32[]{:S(2)}, u32[]{:S(2)}) %collective-permute-start.13) | collective-permute-done | bytes 262176 | tf_op jit(solution)/shard_map/ppermute | solution.py:1069
  218.7 7.7 %collective-permute-start.18 = (f32[2,128,256]{2,1,0:T(8,128)S(1)}, f32[2,128,256]{2,1,0:T(8,128)S(1)}, u32[]{:S(2)}, u32[]{:S(2)}) collective-permute-start(f32[2,128,256]{2,1,0:T(8,128)S(1)} %get-tuple-element.299.refs_2_), channel_id=1, source_target_pairs={{0,4},{1,5},{2,6},{3,7},{4,0},{5,1},{6,2},{7,3},{8,12},{9,13},{10,... | collective-permute-start | bytes 786440 | tf_op jit(solution)/shard_map/ppermute | solution.py:1069
  226.4 1.8 collective-permute-start.20
  229.2 10.0 %collective-permute-done.16.refs_3_ = f32[2,128,256]{2,1,0:T(8,128)S(1)} collective-permute-done((f32[2,128,256]{2,1,0:T(8,128)S(1)}, f32[2,128,256]{2,1,0:T(8,128)S(1)}, u32[]{:S(2)}, u32[]{:S(2)}) %collective-permute-start.16) | collective-permute-done | bytes 262176 | tf_op jit(solution)/shard_map/ppermute | solution.py:1069
  239.2 1.9 collective-permute-start.21
  247.3 5.2 %collective-permute-done.21.refs_3_ = f32[2,2,128,256]{3,2,1,0:T(8,128)S(1)} collective-permute-done((f32[2,2,128,256]{3,2,1,0:T(8,128)S(1)}, f32[2,2,128,256]{3,2,1,0:T(8,128)S(1)}, u32[]{:S(2)}, u32[]{:S(2)}) %collective-permute-start.21) | collective-permute-done | bytes 524320 | tf_op jit(solution)/shard_map/ppermute | solution.py:1069
  255.4 7.2 %collective-permute-done.23.refs_3_ = f32[2,2,128,256]{3,2,1,0:T(8,128)S(1)} collective-permute-done((f32[2,2,128,256]{3,2,1,0:T(8,128)S(1)}, f32[2,2,128,256]{3,2,1,0:T(8,128)S(1)}, u32[]{:S(2)}, u32[]{:S(2)}) %collective-permute-start.23) | collective-permute-done | bytes 524320 | tf_op jit(solution)/shard_map/ppermute | solution.py:1069
  262.5 1.6 place_step.14
  264.8 1.8 collective-permute-start.29
  267.3 3.0 collective-permute-start.31
  271.1 1.6 collective-permute-done.27.refs_3_
  272.7 1.9 collective-permute-start.28
  275.3 5.6 %collective-permute-done.28.refs_3_ = f32[2,136,256]{2,1,0:T(8,128)S(1)} collective-permute-done((f32[2,136,256]{2,1,0:T(8,128)S(1)}, f32[2,136,256]{2,1,0:T(8,128)S(1)}, u32[]{:S(2)}, u32[]{:S(2)}) %collective-permute-start.28) | collective-permute-done | bytes 278560 | tf_op jit(solution)/shard_map/ppermute | solution.py:1069
  284.7 1.8 collective-permute-start.33
  286.4 6.2 %collective-permute-done.32.refs_3_ = f32[2,128,256]{2,1,0:T(8,128)S(1)} collective-permute-done((f32[2,128,256]{2,1,0:T(8,128)S(1)}, f32[2,128,256]{2,1,0:T(8,128)S(1)}, u32[]{:S(2)}, u32[]{:S(2)}) %collective-permute-start.32) | collective-permute-done | bytes 262176 | tf_op jit(solution)/shard_map/ppermute | solution.py:1069
  294.3 2.6 collective-permute-start.34
  297.9 6.1 %collective-permute-done.34.refs_3_ = f32[2,2,128,256]{3,2,1,0:T(8,128)S(1)} collective-permute-done((f32[2,2,128,256]{3,2,1,0:T(8,128)S(1)}, f32[2,2,128,256]{3,2,1,0:T(8,128)S(1)}, u32[]{:S(2)}, u32[]{:S(2)}) %collective-permute-start.34) | collective-permute-done | bytes 524320 | tf_op jit(solution)/shard_map/ppermute | solution.py:1069
  304.0 2.0 collective-permute-start.36
  307.4 3.2 collective-permute-done.36.refs_3_
  312.4 1.7 collective-permute-start.43
  314.0 1.6 place_own.6
  315.7 2.5 place_own.7
  318.2 1.7 place_own.8
  319.9 1.7 place_own.9
  321.6 1.6 place_last.6
  323.9 2.1 collective-permute-start.44
  326.0 5.2 %collective-permute-done.40.refs_3_ = f32[2,2,136,256]{3,2,1,0:T(8,128)S(1)} collective-permute-done((f32[2,2,136,256]{3,2,1,0:T(8,128)S(1)}, f32[2,2,136,256]{3,2,1,0:T(8,128)S(1)}, u32[]{:S(2)}, u32[]{:S(2)}) %collective-permute-start.40) | collective-permute-done | bytes 557088 | tf_op jit(solution)/shard_map/ppermute | solution.py:1069
  331.8 2.0 collective-permute-start.45
  333.8 1.6 place_own.10
  335.5 1.7 place_own.11
  337.1 2.5 place_last.7
  339.7 1.7 place_last.8
  341.4 1.7 place_last.9
  343.0 1.6 place_last.10
  344.7 2.7 collective-permute-done.45.refs_3_
  347.4 2.2 place_last.11
  (107 shorter events, 36.5 us)
Async XLA Ops:
  13.9 3.4 collective-permute-start
  30.9 5.1 %collective-permute-start.1 = (f32[384,512]{1,0:T(8,128)}, f32[384,512]{1,0:T(8,128)}, u32[]{:S(2)}, u32[]{:S(2)}) collective-permute-start(f32[384,512]{1,0:T(8,128)} %get-tuple-element.221), channel_id=1, source_target_pairs={{0,16},{1,17},{2,18},{3,19},{4,20},{5,21},{6,22},{7,23},{8,24},{9,... | collective-permute-start | bytes 2359304 | tf_op jit(solution)/shard_map/ppermute | solution.py:1123
  34.6 18.9 %collective-permute-start.2 = (f32[384,512]{1,0:T(8,128)}, f32[384,512]{1,0:T(8,128)S(1)}, u32[]{:S(2)}, u32[]{:S(2)}) collective-permute-start(f32[384,512]{1,0:T(8,128)} %get-tuple-element.227), channel_id=1, source_target_pairs={{16,0},{17,1},{18,2},{19,3},{20,4},{21,5},{22,6},{23,7},{24,8},{25... | collective-permute-start | bytes 2359304 | tf_op jit(solution)/shard_map/ppermute | solution.py:1127
  71.5 15.0 %collective-permute-start.3 = (f32[384,512]{1,0:T(8,128)}, f32[384,512]{1,0:T(8,128)S(1)}, u32[]{:S(2)}, u32[]{:S(2)}) collective-permute-start(f32[384,512]{1,0:T(8,128)} %get-tuple-element.240), channel_id=1, source_target_pairs={{16,0},{17,1},{18,2},{19,3},{20,4},{21,5},{22,6},{23,7},{24,8},{25... | collective-permute-start | bytes 2359304 | tf_op jit(solution)/shard_map/ppermute | solution.py:1127
  86.5 17.6 %copy-start.1 = (f32[1,2]{1,0:T(1,128)S(1)}, f32[1,2]{1,0:T(1,128)}, u32[]{:S(2)}) copy-start(f32[1,2]{1,0:T(1,128)} %refs_1_.8) | copy-start | bytes 28
  114.5 16.2 %collective-permute-start.4 = (f32[2,2,2,128,256]{4,3,2,1,0:T(8,128)}, f32[2,2,2,128,256]{4,3,2,1,0:T(8,128)}, u32[]{:S(2)}, u32[]{:S(2)}) collective-permute-start(f32[2,2,2,128,256]{4,3,2,1,0:T(8,128)} %get-tuple-element.259), channel_id=1, source_target_pairs={{0,4},{1,5},{2,6},{3,7},{4,0},{5,1},{6,2},{7,3},{8,12},{9,13},{10,... | collective-permute-start | bytes 3145736 | tf_op jit(solution)/shard_map/ppermute | solution.py:1069
  117.6 23.1 %collective-permute-start.5 = (f32[2,2,2,128,256]{4,3,2,1,0:T(8,128)}, f32[2,2,2,128,256]{4,3,2,1,0:T(8,128)}, u32[]{:S(2)}, u32[]{:S(2)}) collective-permute-start(f32[2,2,2,128,256]{4,3,2,1,0:T(8,128)} %get-tuple-element.262), channel_id=1, source_target_pairs={{0,1},{1,0},{2,3},{3,2},{4,5},{5,4},{6,7},{7,6},{8,9},{9,8},{10,11... | collective-permute-start | bytes 3145736 | tf_op jit(solution)/shard_map/ppermute | solution.py:1069
  119.1 11.6 %copy-start.7 = (f32[2,2,2,128,256]{4,3,2,1,0:T(8,128)S(1)}, f32[2,2,2,128,256]{4,3,2,1,0:T(8,128)}, u32[]{:S(2)}) copy-start(f32[2,2,2,128,256]{4,3,2,1,0:T(8,128)} %get-tuple-element.258.refs_2_) | copy-start | bytes 3145732
  129.0 31.1 %collective-permute-start.7 = (f32[2,2,2,128,256]{4,3,2,1,0:T(8,128)}, f32[2,2,2,128,256]{4,3,2,1,0:T(8,128)}, u32[]{:S(2)}, u32[]{:S(2)}) collective-permute-start(f32[2,2,2,128,256]{4,3,2,1,0:T(8,128)} %get-tuple-element.269), channel_id=1, source_target_pairs={{0,2},{1,3},{2,0},{3,1},{4,6},{5,7},{6,4},{7,5},{8,10},{9,11},{10,... | collective-permute-start | bytes 3145736 | tf_op jit(solution)/shard_map/ppermute | solution.py:1069
  130.7 10.0 %copy-start.6 = (f32[2,2,2,128,256]{4,3,2,1,0:T(8,128)S(1)}, f32[2,2,2,128,256]{4,3,2,1,0:T(8,128)}, u32[]{:S(2)}) copy-start(f32[2,2,2,128,256]{4,3,2,1,0:T(8,128)} %get-tuple-element.261.refs_2_) | copy-start | bytes 3145732
  140.7 6.9 %copy-start = (s32[2,1,384]{2,1,0:T(1,128)S(1)}, s32[2,1,384]{2,1,0:T(1,128)}, u32[]{:S(2)}) copy-start(s32[2,1,384]{2,1,0:T(1,128)} %refs_1_.9) | copy-start | bytes 9220
  143.6 14.6 %collective-permute-start.6 = (f32[2,2,128,256]{3,2,1,0:T(8,128)}, f32[2,2,128,256]{3,2,1,0:T(8,128)}, u32[]{:S(2)}, u32[]{:S(2)}) collective-permute-start(f32[2,2,128,256]{3,2,1,0:T(8,128)} %get-tuple-element.266), channel_id=1, source_target_pairs={{0,2},{1,3},{2,0},{3,1},{4,6},{5,7},{6,4},{7,5},{8,10},{9,11},{10,... | collective-permute-start | bytes 1572872 | tf_op jit(solution)/shard_map/ppermute | solution.py:1069
  146.2 15.9 %collective-permute-start.8 = (f32[2,2,128,256]{3,2,1,0:T(8,128)}, f32[2,2,128,256]{3,2,1,0:T(8,128)}, u32[]{:S(2)}, u32[]{:S(2)}) collective-permute-start(f32[2,2,128,256]{3,2,1,0:T(8,128)} %get-tuple-element.272), channel_id=1, source_target_pairs={{0,1},{1,0},{2,3},{3,2},{4,5},{5,4},{6,7},{7,6},{8,9},{9,8},{10,11... | collective-permute-start | bytes 1572872 | tf_op jit(solution)/shard_map/ppermute | solution.py:1069
  157.6 26.4 %collective-permute-start.11 = (f32[2,2,2,128,256]{4,3,2,1,0:T(8,128)}, f32[2,2,2,128,256]{4,3,2,1,0:T(8,128)S(1)}, u32[]{:S(2)}, u32[]{:S(2)}) collective-permute-start(f32[2,2,2,128,256]{4,3,2,1,0:T(8,128)} %get-tuple-element.281), channel_id=1, source_target_pairs={{0,1},{1,0},{2,3},{3,2},{4,5},{5,4},{6,7},{7,6},{8,9},{9,8},{10,11... | collective-permute-start | bytes 3145736 | tf_op jit(solution)/shard_map/ppermute | solution.py:1069
  158.2 1.8 copy-start.5
  160.0 11.5 %collective-permute-start.9 = (f32[2,128,256]{2,1,0:T(8,128)S(1)}, f32[2,128,256]{2,1,0:T(8,128)S(1)}, u32[]{:S(2)}, u32[]{:S(2)}) collective-permute-start(f32[2,128,256]{2,1,0:T(8,128)S(1)} %get-tuple-element.275), channel_id=1, source_target_pairs={{0,4},{1,5},{2,6},{3,7},{4,0},{5,1},{6,2},{7,3},{8,12},{9,13},{10,... | collective-permute-start | bytes 786440 | tf_op jit(solution)/shard_map/ppermute | solution.py:1069
  163.9 8.3 %collective-permute-start.10 = (f32[2,128,256]{2,1,0:T(8,128)S(1)}, f32[2,128,256]{2,1,0:T(8,128)S(1)}, u32[]{:S(2)}, u32[]{:S(2)}) collective-permute-start(f32[2,128,256]{2,1,0:T(8,128)S(1)} %get-tuple-element.278), channel_id=1, source_target_pairs={{0,2},{1,3},{2,0},{3,1},{4,6},{5,7},{6,4},{7,5},{8,10},{9,11},{10,... | collective-permute-start | bytes 786440 | tf_op jit(solution)/shard_map/ppermute | solution.py:1069
  172.2 11.8 %copy-start.4 = (f32[2,2,2,128,256]{4,3,2,1,0:T(8,128)S(1)}, f32[2,2,2,128,256]{4,3,2,1,0:T(8,128)}, u32[]{:S(2)}) copy-start(f32[2,2,2,128,256]{4,3,2,1,0:T(8,128)} %get-tuple-element.280.refs_2_) | copy-start | bytes 3145732
  183.9 1.2 copy-start.9
  183.9 1.6 copy-start.8
  184.9 14.8 %collective-permute-start.12 = (f32[2,2,128,256]{3,2,1,0:T(8,128)S(1)}, f32[2,2,128,256]{3,2,1,0:T(8,128)S(1)}, u32[]{:S(2)}, u32[]{:S(2)}) collective-permute-start(f32[2,2,128,256]{3,2,1,0:T(8,128)S(1)} %get-tuple-element.284), channel_id=1, source_target_pairs={{0,2},{1,3},{2,0},{3,1},{4,6},{5,7},{6,4},{7,5},{8,10},{9,11},{10,... | collective-permute-start | bytes 1572872 | tf_op jit(solution)/shard_map/ppermute | solution.py:1069
  185.2 43.0 %collective-permute-start.15 = (f32[2,2,2,128,256]{4,3,2,1,0:T(8,128)S(1)}, f32[2,2,2,128,256]{4,3,2,1,0:T(8,128)S(1)}, u32[]{:S(2)}, u32[]{:S(2)}) collective-permute-start(f32[2,2,2,128,256]{4,3,2,1,0:T(8,128)S(1)} %copy-done.9), channel_id=1, source_target_pairs={{0,4},{1,5},{2,6},{3,7},{4,0},{5,1},{6,2},{7,3},{8,12},{9,13},{10,... | collective-permute-start | bytes 3145736 | tf_op jit(solution)/shard_map/ppermute | solution.py:1069
  185.5 59.3 %collective-permute-start.19 = (f32[2,2,2,136,256]{4,3,2,1,0:T(8,128)S(1)}, f32[2,2,2,136,256]{4,3,2,1,0:T(8,128)S(1)}, u32[]{:S(2)}, u32[]{:S(2)}) collective-permute-start(f32[2,2,2,136,256]{4,3,2,1,0:T(8,128)S(1)} %copy-done.8), channel_id=1, source_target_pairs={{0,1},{1,0},{2,3},{3,2},{4,5},{5,4},{6,7},{7,6},{8,9},{9,8},{10,11... | collective-permute-start | bytes 3342344 | tf_op jit(solution)/shard_map/ppermute | solution.py:1069
  186.1 55.7 %collective-permute-start.17 = (f32[2,2,128,256]{3,2,1,0:T(8,128)S(1)}, f32[2,2,128,256]{3,2,1,0:T(8,128)S(1)}, u32[]{:S(2)}, u32[]{:S(2)}) collective-permute-start(f32[2,2,128,256]{3,2,1,0:T(8,128)S(1)} %get-tuple-element.297), channel_id=1, source_target_pairs={{0,1},{1,0},{2,3},{3,2},{4,5},{5,4},{6,7},{7,6},{8,9},{9,8},{10,11... | collective-permute-start | bytes 1572872 | tf_op jit(solution)/shard_map/ppermute | solution.py:1069
  187.5 30.5 %collective-permute-start.14 = (f32[2,128,256]{2,1,0:T(8,128)S(1)}, f32[2,128,256]{2,1,0:T(8,128)S(1)}, u32[]{:S(2)}, u32[]{:S(2)}) collective-permute-start(f32[2,128,256]{2,1,0:T(8,128)S(1)} %get-tuple-element.288.refs_2_), channel_id=1, source_target_pairs={{0,8},{1,9},{2,10},{3,11},{4,12},{5,13},{6,14},{7,15},{8,0},{9,1},... | collective-permute-start | bytes 786440 | tf_op jit(solution)/shard_map/ppermute | solution.py:1069
  199.7 17.7 %collective-permute-start.13 = (f32[2,128,256]{2,1,0:T(8,128)S(1)}, f32[2,128,256]{2,1,0:T(8,128)S(1)}, u32[]{:S(2)}, u32[]{:S(2)}) collective-permute-start(f32[2,128,256]{2,1,0:T(8,128)S(1)} %get-tuple-element.286.refs_2_), channel_id=1, source_target_pairs={{0,8},{1,9},{2,10},{3,11},{4,12},{5,13},{6,14},{7,15},{8,0},{9,1},... | collective-permute-start | bytes 786440 | tf_op jit(solution)/shard_map/ppermute | solution.py:1069
  218.0 10.2 %copy-start.3 = (f32[2,2,2,128,256]{4,3,2,1,0:T(8,128)S(1)}, f32[2,2,2,128,256]{4,3,2,1,0:T(8,128)}, u32[]{:S(2)}) copy-start(f32[2,2,2,128,256]{4,3,2,1,0:T(8,128)} %get-tuple-element.290.refs_2_) | copy-start | bytes 3145732
  218.7 25.1 %collective-permute-start.18 = (f32[2,128,256]{2,1,0:T(8,128)S(1)}, f32[2,128,256]{2,1,0:T(8,128)S(1)}, u32[]{:S(2)}, u32[]{:S(2)}) collective-permute-start(f32[2,128,256]{2,1,0:T(8,128)S(1)} %get-tuple-element.299.refs_2_), channel_id=1, source_target_pairs={{0,4},{1,5},{2,6},{3,7},{4,0},{5,1},{6,2},{7,3},{8,12},{9,13},{10,... | collective-permute-start | bytes 786440 | tf_op jit(solution)/shard_map/ppermute | solution.py:1069
  226.4 20.2 %collective-permute-start.20 = (f32[2,128,256]{2,1,0:T(8,128)S(1)}, f32[2,128,256]{2,1,0:T(8,128)S(1)}, u32[]{:S(2)}, u32[]{:S(2)}) collective-permute-start(f32[2,128,256]{2,1,0:T(8,128)S(1)} %get-tuple-element.304.refs_2_), channel_id=1, source_target_pairs={{0,2},{1,3},{2,0},{3,1},{4,6},{5,7},{6,4},{7,5},{8,10},{9,11},{10,... | collective-permute-start | bytes 786440 | tf_op jit(solution)/shard_map/ppermute | solution.py:1069
  228.2 11.0 %collective-permute-start.16 = (f32[2,128,256]{2,1,0:T(8,128)S(1)}, f32[2,128,256]{2,1,0:T(8,128)S(1)}, u32[]{:S(2)}, u32[]{:S(2)}) collective-permute-start(f32[2,128,256]{2,1,0:T(8,128)S(1)} %get-tuple-element.294), channel_id=1, source_target_pairs={{0,4},{1,5},{2,6},{3,7},{4,0},{5,1},{6,2},{7,3},{8,12},{9,13},{10,... | collective-permute-start | bytes 786440 | tf_op jit(solution)/shard_map/ppermute | solution.py:1069
  239.2 13.3 %collective-permute-start.21 = (f32[2,2,128,256]{3,2,1,0:T(8,128)S(1)}, f32[2,2,128,256]{3,2,1,0:T(8,128)S(1)}, u32[]{:S(2)}, u32[]{:S(2)}) collective-permute-start(f32[2,2,128,256]{3,2,1,0:T(8,128)S(1)} %get-tuple-element.307), channel_id=1, source_target_pairs={{0,2},{1,3},{2,0},{3,1},{4,6},{5,7},{6,4},{7,5},{8,10},{9,11},{10,... | collective-permute-start | bytes 1572872 | tf_op jit(solution)/shard_map/ppermute | solution.py:1069
  242.6 12.1 %collective-permute-start.22 = (f32[2,128,256]{2,1,0:T(8,128)S(1)}, f32[2,128,256]{2,1,0:T(8,128)S(1)}, u32[]{:S(2)}, u32[]{:S(2)}) collective-permute-start(f32[2,128,256]{2,1,0:T(8,128)S(1)} %get-tuple-element.310), channel_id=1, source_target_pairs={{0,4},{1,5},{2,6},{3,7},{4,0},{5,1},{6,2},{7,3},{8,12},{9,13},{10,... | collective-permute-start | bytes 786440 | tf_op jit(solution)/shard_map/ppermute | solution.py:1069
  243.8 20.3 %collective-permute-start.24 = (f32[2,128,256]{2,1,0:T(8,128)S(1)}, f32[2,128,256]{2,1,0:T(8,128)S(1)}, u32[]{:S(2)}, u32[]{:S(2)}) collective-permute-start(f32[2,128,256]{2,1,0:T(8,128)S(1)} %get-tuple-element.314.refs_2_), channel_id=1, source_target_pairs={{0,8},{1,9},{2,10},{3,11},{4,12},{5,13},{6,14},{7,15},{8,0},{9,1},... | collective-permute-start | bytes 786440 | tf_op jit(solution)/shard_map/ppermute | solution.py:1069
  244.2 1.2 copy-start.2
  244.8 17.7 %collective-permute-start.23 = (f32[2,2,128,256]{3,2,1,0:T(8,128)S(1)}, f32[2,2,128,256]{3,2,1,0:T(8,128)S(1)}, u32[]{:S(2)}, u32[]{:S(2)}) collective-permute-start(f32[2,2,128,256]{3,2,1,0:T(8,128)S(1)} %get-tuple-element.312.refs_2_), channel_id=1, source_target_pairs={{0,2},{1,3},{2,0},{3,1},{4,6},{5,7},{6,4},{7,5},{8,10},{9,11},{10,... | collective-permute-start | bytes 1572872 | tf_op jit(solution)/shard_map/ppermute | solution.py:1069
  247.2 35.1 %collective-permute-start.30 = (f32[2,2,128,256]{3,2,1,0:T(8,128)S(1)}, f32[2,2,128,256]{3,2,1,0:T(8,128)S(1)}, u32[]{:S(2)}, u32[]{:S(2)}) collective-permute-start(f32[2,2,128,256]{3,2,1,0:T(8,128)S(1)} %get-tuple-element.329.refs_2_), channel_id=1, source_target_pairs={{0,1},{1,0},{2,3},{3,2},{4,5},{5,4},{6,7},{7,6},{8,9},{9,8},{10,11... | collective-permute-start | bytes 1572872 | tf_op jit(solution)/shard_map/ppermute | solution.py:1069
  252.5 17.8 %collective-permute-start.26 = (f32[2,2,136,256]{3,2,1,0:T(8,128)S(1)}, f32[2,2,136,256]{3,2,1,0:T(8,128)S(1)}, u32[]{:S(2)}, u32[]{:S(2)}) collective-permute-start(f32[2,2,136,256]{3,2,1,0:T(8,128)S(1)} %get-tuple-element.320), channel_id=1, source_target_pairs={{0,4},{1,5},{2,6},{3,7},{4,0},{5,1},{6,2},{7,3},{8,12},{9,13},{10,... | collective-permute-start | bytes 1671176 | tf_op jit(solution)/shard_map/ppermute | solution.py:1069
  254.7 11.9 %collective-permute-start.25 = (f32[2,128,256]{2,1,0:T(8,128)S(1)}, f32[2,128,256]{2,1,0:T(8,128)S(1)}, u32[]{:S(2)}, u32[]{:S(2)}) collective-permute-start(f32[2,128,256]{2,1,0:T(8,128)S(1)} %get-tuple-element.317), channel_id=1, source_target_pairs={{0,1},{1,0},{2,3},{3,2},{4,5},{5,4},{6,7},{7,6},{8,9},{9,8},{10,11... | collective-permute-start | bytes 786440 | tf_op jit(solution)/shard_map/ppermute | solution.py:1069
  262.5 10.2 %collective-permute-start.27 = (f32[2,128,256]{2,1,0:T(8,128)S(1)}, f32[2,128,256]{2,1,0:T(8,128)S(1)}, u32[]{:S(2)}, u32[]{:S(2)}) collective-permute-start(f32[2,128,256]{2,1,0:T(8,128)S(1)} %get-tuple-element.322.refs_2_), channel_id=1, source_target_pairs={{0,8},{1,9},{2,10},{3,11},{4,12},{5,13},{6,14},{7,15},{8,0},{9,1},... | collective-permute-start | bytes 786440 | tf_op jit(solution)/shard_map/ppermute | solution.py:1069
  264.8 16.9 %collective-permute-start.29 = (f32[2,128,256]{2,1,0:T(8,128)S(1)}, f32[2,128,256]{2,1,0:T(8,128)S(1)}, u32[]{:S(2)}, u32[]{:S(2)}) collective-permute-start(f32[2,128,256]{2,1,0:T(8,128)S(1)} %get-tuple-element.327.refs_2_), channel_id=1, source_target_pairs={{0,4},{1,5},{2,6},{3,7},{4,0},{5,1},{6,2},{7,3},{8,12},{9,13},{10,... | collective-permute-start | bytes 786440 | tf_op jit(solution)/shard_map/ppermute | solution.py:1069
  267.3 15.7 %collective-permute-start.31 = (f32[2,128,256]{2,1,0:T(8,128)S(1)}, f32[2,128,256]{2,1,0:T(8,128)S(1)}, u32[]{:S(2)}, u32[]{:S(2)}) collective-permute-start(f32[2,128,256]{2,1,0:T(8,128)S(1)} %get-tuple-element.331.refs_2_), channel_id=1, source_target_pairs={{0,8},{1,9},{2,10},{3,11},{4,12},{5,13},{6,14},{7,15},{8,0},{9,1},... | collective-permute-start | bytes 786440 | tf_op jit(solution)/shard_map/ppermute | solution.py:1069
  270.3 66.9 %collective-permute-start.41 = (f32[2,2,2,128,256]{4,3,2,1,0:T(8,128)}, f32[2,2,2,128,256]{4,3,2,1,0:T(8,128)}, u32[]{:S(2)}, u32[]{:S(2)}) collective-permute-start(f32[2,2,2,128,256]{4,3,2,1,0:T(8,128)} %get-tuple-element.347.refs_2_), channel_id=1, source_target_pairs={{0,1},{1,0},{2,3},{3,2},{4,5},{5,4},{6,7},{7,6},{8,9},{9,8},{10,11... | collective-permute-start | bytes 3145736 | tf_op jit(solution)/shard_map/ppermute | solution.py:1069
  272.7 8.2 %collective-permute-start.28 = (f32[2,136,256]{2,1,0:T(8,128)S(1)}, f32[2,136,256]{2,1,0:T(8,128)S(1)}, u32[]{:S(2)}, u32[]{:S(2)}) collective-permute-start(f32[2,136,256]{2,1,0:T(8,128)S(1)} %get-tuple-element.325), channel_id=1, source_target_pairs={{0,2},{1,3},{2,0},{3,1},{4,6},{5,7},{6,4},{7,5},{8,10},{9,11},{10,... | collective-permute-start | bytes 835592 | tf_op jit(solution)/shard_map/ppermute | solution.py:1069
  280.9 11.7 %collective-permute-start.32 = (f32[2,128,256]{2,1,0:T(8,128)S(1)}, f32[2,128,256]{2,1,0:T(8,128)S(1)}, u32[]{:S(2)}, u32[]{:S(2)}) collective-permute-start(f32[2,128,256]{2,1,0:T(8,128)S(1)} %get-tuple-element.333.refs_2_), channel_id=1, source_target_pairs={{0,4},{1,5},{2,6},{3,7},{4,0},{5,1},{6,2},{7,3},{8,12},{9,13},{10,... | collective-permute-start | bytes 786440 | tf_op jit(solution)/shard_map/ppermute | solution.py:1069
  283.6 23.1 %collective-permute-start.35 = (f32[2,128,256]{2,1,0:T(8,128)S(1)}, f32[2,128,256]{2,1,0:T(8,128)S(1)}, u32[]{:S(2)}, u32[]{:S(2)}) collective-permute-start(f32[2,128,256]{2,1,0:T(8,128)S(1)} %get-tuple-element.339.refs_2_), channel_id=1, source_target_pairs={{0,1},{1,0},{2,3},{3,2},{4,5},{5,4},{6,7},{7,6},{8,9},{9,8},{10,11... | collective-permute-start | bytes 786440 | tf_op jit(solution)/shard_map/ppermute | solution.py:1069
  284.7 12.2 %collective-permute-start.33 = (f32[2,136,256]{2,1,0:T(8,128)S(1)}, f32[2,136,256]{2,1,0:T(8,128)S(1)}, u32[]{:S(2)}, u32[]{:S(2)}) collective-permute-start(f32[2,136,256]{2,1,0:T(8,128)S(1)} %get-tuple-element.335.refs_2_), channel_id=1, source_target_pairs={{0,8},{1,9},{2,10},{3,11},{4,12},{5,13},{6,14},{7,15},{8,0},{9,1},... | collective-permute-start | bytes 835592 | tf_op jit(solution)/shard_map/ppermute | solution.py:1069
  293.2 18.5 %collective-permute-start.37 = (f32[2,2,128,256]{3,2,1,0:T(8,128)S(1)}, f32[2,2,128,256]{3,2,1,0:T(8,128)S(1)}, u32[]{:S(2)}, u32[]{:S(2)}) collective-permute-start(f32[2,2,128,256]{3,2,1,0:T(8,128)S(1)} %get-tuple-element.343.refs_2_), channel_id=1, source_target_pairs={{0,1},{1,0},{2,3},{3,2},{4,5},{5,4},{6,7},{7,6},{8,9},{9,8},{10,11... | collective-permute-start | bytes 1572872 | tf_op jit(solution)/shard_map/ppermute | solution.py:1069
  294.3 9.7 %collective-permute-start.34 = (f32[2,2,128,256]{3,2,1,0:T(8,128)S(1)}, f32[2,2,128,256]{3,2,1,0:T(8,128)S(1)}, u32[]{:S(2)}, u32[]{:S(2)}) collective-permute-start(f32[2,2,128,256]{3,2,1,0:T(8,128)S(1)} %get-tuple-element.337.refs_2_), channel_id=1, source_target_pairs={{0,2},{1,3},{2,0},{3,1},{4,6},{5,7},{6,4},{7,5},{8,10},{9,11},{10,... | collective-permute-start | bytes 1572872 | tf_op jit(solution)/shard_map/ppermute | solution.py:1069
  296.9 24.7 %collective-permute-start.38 = (f32[2,2,2,128,256]{4,3,2,1,0:T(8,128)S(1)}, f32[2,2,2,128,256]{4,3,2,1,0:T(8,128)S(1)}, u32[]{:S(2)}, u32[]{:S(2)}) collective-permute-start(f32[2,2,2,128,256]{4,3,2,1,0:T(8,128)S(1)} %get-tuple-element.345.refs_2_), channel_id=1, source_target_pairs={{0,4},{1,5},{2,6},{3,7},{4,0},{5,1},{6,2},{7,3},{8,12},{9,13},{10,... | collective-permute-start | bytes 3145736 | tf_op jit(solution)/shard_map/ppermute | solution.py:1069
  304.0 6.5 %collective-permute-start.36 = (f32[2,136,256]{2,1,0:T(8,128)S(1)}, f32[2,136,256]{2,1,0:T(8,128)S(1)}, u32[]{:S(2)}, u32[]{:S(2)}) collective-permute-start(f32[2,136,256]{2,1,0:T(8,128)S(1)} %get-tuple-element.341.refs_2_), channel_id=1, source_target_pairs={{0,2},{1,3},{2,0},{3,1},{4,6},{5,7},{6,4},{7,5},{8,10},{9,11},{10,... | collective-permute-start | bytes 835592 | tf_op jit(solution)/shard_map/ppermute | solution.py:1069
  307.3 15.9 %collective-permute-start.39 = (f32[2,2,128,256]{3,2,1,0:T(8,128)S(1)}, f32[2,2,128,256]{3,2,1,0:T(8,128)S(1)}, u32[]{:S(2)}, u32[]{:S(2)}) collective-permute-start(f32[2,2,128,256]{3,2,1,0:T(8,128)S(1)} %get-tuple-element.356.refs_2_), channel_id=1, source_target_pairs={{0,2},{1,3},{2,0},{3,1},{4,6},{5,7},{6,4},{7,5},{8,10},{9,11},{10,... | collective-permute-start | bytes 1572872 | tf_op jit(solution)/shard_map/ppermute | solution.py:1069
  310.6 29.1 %collective-permute-start.42 = (f32[2,2,2,128,256]{4,3,2,1,0:T(8,128)S(1)}, f32[2,2,2,128,256]{4,3,2,1,0:T(8,128)S(1)}, u32[]{:S(2)}, u32[]{:S(2)}) collective-permute-start(f32[2,2,2,128,256]{4,3,2,1,0:T(8,128)S(1)} %get-tuple-element.352.refs_2_), channel_id=1, source_target_pairs={{0,1},{1,0},{2,3},{3,2},{4,5},{5,4},{6,7},{7,6},{8,9},{9,8},{10,11... | collective-permute-start | bytes 3145736 | tf_op jit(solution)/shard_map/ppermute | solution.py:1069
  312.4 29.0 %collective-permute-start.43 = (f32[2,2,2,128,256]{4,3,2,1,0:T(8,128)S(1)}, f32[2,2,2,128,256]{4,3,2,1,0:T(8,128)S(1)}, u32[]{:S(2)}, u32[]{:S(2)}) collective-permute-start(f32[2,2,2,128,256]{4,3,2,1,0:T(8,128)S(1)} %get-tuple-element.350.refs_2_), channel_id=1, source_target_pairs={{0,2},{1,3},{2,0},{3,1},{4,6},{5,7},{6,4},{7,5},{8,10},{9,11},{10,... | collective-permute-start | bytes 3145736 | tf_op jit(solution)/shard_map/ppermute | solution.py:1069
  321.5 9.6 %collective-permute-start.40 = (f32[2,2,136,256]{3,2,1,0:T(8,128)S(1)}, f32[2,2,136,256]{3,2,1,0:T(8,128)S(1)}, u32[]{:S(2)}, u32[]{:S(2)}) collective-permute-start(f32[2,2,136,256]{3,2,1,0:T(8,128)S(1)} %get-tuple-element.358.refs_2_), channel_id=1, source_target_pairs={{0,4},{1,5},{2,6},{3,7},{4,0},{5,1},{6,2},{7,3},{8,12},{9,13},{10,... | collective-permute-start | bytes 1671176 | tf_op jit(solution)/shard_map/ppermute | solution.py:1069
  323.9 19.1 %collective-permute-start.44 = (f32[2,2,2,128,256]{4,3,2,1,0:T(8,128)S(1)}, f32[2,2,2,128,256]{4,3,2,1,0:T(8,128)S(1)}, u32[]{:S(2)}, u32[]{:S(2)}) collective-permute-start(f32[2,2,2,128,256]{4,3,2,1,0:T(8,128)S(1)} %get-tuple-element.360.refs_2_), channel_id=1, source_target_pairs={{0,4},{1,5},{2,6},{3,7},{4,0},{5,1},{6,2},{7,3},{8,12},{9,13},{10,... | collective-permute-start | bytes 3145736 | tf_op jit(solution)/shard_map/ppermute | solution.py:1069
  331.8 15.6 %collective-permute-start.45 = (f32[2,2,2,136,256]{4,3,2,1,0:T(8,128)S(1)}, f32[2,2,2,136,256]{4,3,2,1,0:T(8,128)S(1)}, u32[]{:S(2)}, u32[]{:S(2)}) collective-permute-start(f32[2,2,2,136,256]{4,3,2,1,0:T(8,128)S(1)} %get-tuple-element.363.refs_2_), channel_id=1, source_target_pairs={{0,1},{1,0},{2,3},{3,2},{4,5},{5,4},{6,7},{7,6},{8,9},{9,8},{10,11... | collective-permute-start | bytes 3342344 | tf_op jit(solution)/shard_map/ppermute | solution.py:1069
